TPU v7x, 32 devices: a whole 2x2x4 slice. The times are simulated.
32 devices in a mesh: section: 2 (over core), dp: 16 (over z, y, x).
Axes of the slice: x: 2, y: 2, z: 4, core: 2. Of those that a mesh axis runs over, the one named last changes fastest.
Arguments:
- patches: bfloat16 [192, 196, 768], P('dp'), may hold values from -6 to 6
- keep: int32 [192], P('dp'), may hold values from 40 to 98, as said below
- perm: int32 [192, 196], P('dp'), may hold values from 0 to 195, as said below
- master: float32 [2, 7673856], P('section', 'dp')
- first: float32 [2, 7673856], P('section', 'dp'), may hold values from -4.7683716e-06 to 4.7683716e-06
- second: float32 [2, 7673856], P('section', 'dp'), may hold values from 8.614131e-15 to 3.4456524e-14
- ema: float32 [2, 7673856], P('section', 'dp')
Outputs:
- new_master: float32 [2, 7673856], P('section', 'dp')
- new_first: float32 [2, 7673856], P('section', 'dp')
- new_second: float32 [2, 7673856], P('section', 'dp')
- new_ema: float32 [2, 7673856], P('section', 'dp')
- grad_norm: float32 [], replicated
- loss_sum: float32 [], replicated
- loss_count: float32 [], replicated
Inputs may be any that keep to these rules, and one draw needn't show every extreme that they name: `keep`: some image keeps exactly 98 patches. `perm`: each row is a permutation of 0 to 195; its first keep entries are the visible patches.
All inputs are finite; a program needn't handle non-finite values.
Results may differ from a plain program's by a relative error of at most 0.00035.
The roundings to bfloat16 on the way count: a program that leaves them out, or rounds other values in their place, can miss the bound.
Values may be sent and summed in bfloat16 or wider, within the bound.
No kernel may reach another device: no remote copies, remote signals or barrier semaphores. Data moves between devices by JAX's collectives and lax.ppermute only.
A program may use at most 704 MiB of HBM per device.

v0:
```python
import math

import jax
import jax.numpy as jnp
from jax import lax
from jax.sharding import PartitionSpec as P

D = 768
HEADS_E = 12
FF_E = 3072
DD = 512
HEADS_D = 16
FF_D = 2048
PIX = 768
NP = 196
SLOTS = 98
IMG = 4
MICRO = 3
STEP = 10


norm_epsilon = 1e-06
clip_limit = 0.01
learn_rate = 0.02
beta_one = 0.9
beta_two = 0.999
adam_epsilon = 1e-08
weight_decay = 0.05
average_keep = 0.8


def passed_along(value, axis, steps):
    count = lax.axis_size(axis)
    leading, last = (max(0, -steps), min(count, count - steps))
    return lax.ppermute(value, axis, [(source, source + steps) for source in range(leading, last)])


def to_bfloat(values):
    return lax.optimization_barrier(values.astype(jnp.bfloat16)).astype(jnp.float32)


def pass_through(values):
    return values


def round_value_keep(values):
    return (to_bfloat(values), None)


def round_value_pass(kept, grad):
    return (grad,)


def round_grad_keep(values):
    return (values, None)


def round_grad_pass(kept, grad):
    return (to_bfloat(grad),)


def round_value(values):
    rounder = jax.custom_vjp(to_bfloat)
    rounder.defvjp(round_value_keep, round_value_pass)
    return rounder(values)


def round_grad(values):
    rounder = jax.custom_vjp(pass_through)
    rounder.defvjp(round_grad_keep, round_grad_pass)
    return rounder(values)


def encoder_layout():
    return [
        (PIX, D),
        (D,),
        (D,),
        (D,),
        (D, 3 * D),
        (D, D),
        (D,),
        (D,),
        (D, FF_E),
        (FF_E, D),
        (D,),
        (D,),
    ]


def decoder_layout():
    return [
        (D, DD),
        (DD,),
        (DD,),
        (DD,),
        (DD, 3 * DD),
        (DD, DD),
        (DD,),
        (DD,),
        (DD, FF_D),
        (FF_D, DD),
        (DD,),
        (DD,),
        (DD, PIX),
    ]


def unpack(flat, layout):
    pieces = []
    offset = 0
    for shape in layout:
        amount = math.prod(shape)
        pieces.append(flat[offset : offset + amount].reshape(shape))
        offset += amount
    return pieces


def sincos(width):
    places = jnp.arange(NP).astype(jnp.float32)[:, None]
    column = jnp.arange(width)
    rates = jnp.exp(-(2.0 * (column // 2).astype(jnp.float32) / width) * math.log(10000.0))
    phases = places * rates[None, :]
    return jnp.where(column[None, :] % 2 == 0, jnp.sin(phases), jnp.cos(phases))


def normalize(values, gain, shift):
    centre = values - jnp.mean(values, axis=-1, keepdims=True)
    spread = jnp.mean(centre * centre, axis=-1, keepdims=True)
    return centre * lax.rsqrt(spread + norm_epsilon) * gain + shift


def block(stream, weights, heads, valid):
    gain_one, bias_one, qkv_w, proj_w, gain_two, bias_two, fc_one, fc_two = weights
    batch, length, width = stream.shape
    size = width // heads
    normed = round_value(normalize(stream, gain_one, bias_one))
    mixed = round_grad(jnp.einsum("blw,wk->blk", normed, qkv_w))
    query = round_value(mixed[..., :width] * (1.0 / math.sqrt(size))).reshape(
        batch, length, heads, size
    )
    keys = round_value(mixed[..., width : 2 * width]).reshape(batch, length, heads, size)
    values = round_value(mixed[..., 2 * width :]).reshape(batch, length, heads, size)
    scores = round_grad(jnp.einsum("bqhd,bkhd->bhqk", query, keys))
    scores = jnp.where(valid[:, None, None, :], scores, -1e30)
    probs = round_value(jax.nn.softmax(scores, axis=-1))
    attended = round_value(round_grad(jnp.einsum("bhqk,bkhd->bqhd", probs, values)))
    attended = attended.reshape(batch, length, width)
    stream = stream + round_grad(jnp.einsum("blw,wk->blk", attended, proj_w))
    normed = round_value(normalize(stream, gain_two, bias_two))
    hidden = round_grad(jnp.einsum("blw,wk->blk", normed, fc_one))
    hidden = round_value(jax.nn.gelu(hidden, approximate=False))
    return stream + round_grad(jnp.einsum("blk,kw->blw", hidden, fc_two))


def encode(flat, pixels, kept_count, order):
    pieces = unpack(flat, encoder_layout())
    chosen = order[:, :SLOTS]
    visible = jnp.take_along_axis(pixels, chosen[:, :, None], axis=1)
    embedded = round_grad(jnp.einsum("bsp,pw->bsw", visible, pieces[0]))
    embedded = embedded + pieces[1] + sincos(D)[chosen]
    valid = jnp.arange(SLOTS)[None, :] < kept_count[:, None]
    stream = block(embedded, pieces[2:10], HEADS_E, valid)
    return normalize(stream, pieces[10], pieces[11])


def decode(flat, latent, pixels, kept_count, order):
    pieces = unpack(flat, decoder_layout())
    embedded = round_grad(jnp.einsum("bsw,wk->bsk", latent, pieces[0]))
    ranks = jnp.argsort(order, axis=1)
    kept = ranks < kept_count[:, None]
    placed = jnp.take_along_axis(embedded, jnp.minimum(ranks, SLOTS - 1)[:, :, None], axis=1)
    tokens = jnp.where(kept[:, :, None], placed, pieces[1]) + sincos(DD)
    stream = block(tokens, pieces[2:10], HEADS_D, jnp.ones(kept.shape, dtype=bool))
    normed = round_value(normalize(stream, pieces[10], pieces[11]))
    predicted = round_grad(jnp.einsum("bpk,kx->bpx", normed, pieces[12]))
    centre = pixels - jnp.mean(pixels, axis=-1, keepdims=True)
    target = centre * lax.rsqrt(jnp.mean(centre * centre, axis=-1, keepdims=True) + norm_epsilon)
    error = jnp.mean((predicted - target) ** 2, axis=-1)
    return jnp.sum(jnp.where(kept, 0.0, error))


def on_device(patches, keep, perm, master, first, second, ema):
    section = lax.axis_index("section")
    gathered = lax.all_gather(master.astype(jnp.bfloat16), "dp", axis=1, tiled=True)
    params = gathered[0].astype(jnp.float32)
    count = lax.psum(jnp.sum(NP - keep).astype(jnp.float32), "dp")
    seed_grad = 1.0 / count
    images = patches.astype(jnp.float32)
    latent_zero = jnp.zeros((IMG, SLOTS, D), jnp.bfloat16)
    flat_zero = jnp.zeros(params.shape, jnp.float32)
    scalar_zero = jnp.zeros((), jnp.float32)
    grad_total = flat_zero
    loss_part = scalar_zero
    for index in range(MICRO):
        pixels = images[index * IMG : (index + 1) * IMG]
        counts = keep[index * IMG : (index + 1) * IMG]
        order = perm[index * IMG : (index + 1) * IMG]

        def encoder_side():
            return encode(params, pixels, counts, order).astype(jnp.bfloat16)

        latent = lax.cond(section == 0, encoder_side, lambda: latent_zero)
        latent = passed_along(latent, "section", 1)

        def decoder_side():
            total, pull = jax.vjp(
                lambda flat, coded: decode(flat, coded, pixels, counts, order),
                params,
                latent.astype(jnp.float32),
            )
            grad_flat, grad_latent = pull(seed_grad)
            return (grad_latent.astype(jnp.bfloat16), grad_flat, total)

        returned, grad_decoder, partial_loss = lax.cond(
            section == 1, decoder_side, lambda: (latent_zero, flat_zero, scalar_zero)
        )
        returned = passed_along(returned, "section", -1)

        def encoder_back():
            _, pull = jax.vjp(lambda flat: encode(flat, pixels, counts, order), params)
            return pull(returned.astype(jnp.float32))[0]

        grad_encoder = lax.cond(section == 0, encoder_back, lambda: flat_zero)
        loss_part = loss_part + partial_loss
        grad_total = grad_total + grad_decoder + grad_encoder
    shard_total = lax.psum_scatter(grad_total, "dp", scatter_dimension=0, tiled=True)
    squares, loss_sum = lax.psum((jnp.sum(shard_total * shard_total), loss_part), ("section", "dp"))
    norm = jnp.sqrt(squares)
    factor = jnp.minimum(1.0, clip_limit / (norm + norm_epsilon))
    clipped = (shard_total * factor).reshape(master.shape)
    new_first = beta_one * first + (1.0 - beta_one) * clipped
    new_second = beta_two * second + (1.0 - beta_two) * clipped * clipped
    first_hat = new_first / (1.0 - beta_one**STEP)
    second_hat = new_second / (1.0 - beta_two**STEP)
    new_master = master - learn_rate * (
        first_hat / (jnp.sqrt(second_hat) + adam_epsilon) + weight_decay * master
    )
    new_ema = average_keep * ema + (1.0 - average_keep) * new_master
    return (new_master, new_first, new_second, new_ema, norm, loss_sum, count)


def solution(mesh):
    return jax.shard_map(
        on_device,
        mesh=mesh,
        in_specs=(
            P("dp", None, None),
            P("dp"),
            P("dp", None),
            P("section", "dp"),
            P("section", "dp"),
            P("section", "dp"),
            P("section", "dp"),
        ),
        out_specs=(
            P("section", "dp"),
            P("section", "dp"),
            P("section", "dp"),
            P("section", "dp"),
            P(),
            P(),
            P(),
        ),
        check_vma=False,
    )
```

profile of v0, /device:TPU:0, one launch (start us, length us, event | category | flops | bytes accessed | tf_op | source)
XLA Modules:
  0.0 2924.1 jit_solution(9693231369364950500)
XLA Ops:
  19.9 10.2 fusion.510
  30.1 308.1 %all-gather.2.cloned.1.call-done = bf16[1,7673856]{1,0:T(2,128)(2,1)} async-done(((bf16[1,479616]{1,0:T(2,128)(2,1)}), bf16[1,7673856]{1,0:T(2,128)(2,1)}) %all-gather.2.cloned.1.call-update) | async-done | bytes 15347728 | tf_op jit(solution)/shard_map/all_gather | solution.py:185
  338.2 35.4 %convert_element_type.662 = f32[1,7673856]{1,0:T(1,128)} convert(bf16[1,7673856]{1,0:T(2,128)(2,1)} %all-gather.2.cloned.1.call-done) | non-fusion elementwise | flops 7673856 | bytes 46043136 | tf_op jit(solution)/shard_map/convert_element_type | solution.py:186
  373.7 109.2 %conditional.9 = (bf16[4,98,768]{2,1,0:T(8,128)(2,1)S(1)}) conditional(s32[]{:T(128)} %convert_element_type.659, () %tuple.89, (s32[4,196]{1,0:T(4,128)S(1)}, f32[4,196,768]{2,0,1:T(4,128)S(1)}, f32[7673856]{0:T(1024)}, s32[4]{0:T(128)S(1)}) %tuple.384), branch_computations={%region_0.0_spmd, %region_1.11_spmd} | conditional | flops 6221844992 | bytes 131762040 | solution.py:203
  433.1 11.0 fusion.433
  452.2 15.0 fusion.3
  467.3 9.2 reshape.2217
  486.1 125.7 %conditional.12 = (bf16[4,98,768]{2,1,0:T(8,128)(2,1)}) conditional(s32[]{:T(128)} %convert_element_type.659, () %tuple.95, (s32[4,196]{1,0:T(4,128)S(1)}, f32[4,196,768]{2,0,1:T(4,128)}, f32[7673856]{0:T(1024)}, s32[4]{0:T(128)S(1)}) %tuple.385), branch_computations={%region_66.69_spmd, %region_67.78_spmd} | conditional | flops 6221844992 | bytes 138987392 | solution.py:203
  560.9 11.0 fusion.442
  580.1 15.2 fusion.138
  595.2 9.2 reshape.2248
  616.1 108.8 %conditional.15 = (bf16[4,98,768]{2,1,0:T(8,128)(2,1)S(1)}) conditional(s32[]{:T(128)} %convert_element_type.659, () %tuple.101, (s32[4,196]{1,0:T(4,128)S(1)}, f32[4,196,768]{2,0,1:T(4,128)S(1)}, f32[7673856]{0:T(1024)}, s32[4]{0:T(128)S(1)}) %tuple.405), branch_computations={%region_130.133_spmd, %region_131.142_spmd} | conditional | flops 6221844992 | bytes 131762040 | solution.py:203
  675.1 11.0 fusion.451
  694.3 15.0 fusion.273
  709.3 9.4 reshape.2279
  729.4 39.4 %psum.21 = f32[]{:T(128)} all-reduce(f32[]{:T(128)S(6)} %convert_element_type.661), channel_id=1, replica_groups=mesh['section'=2,'dp'=16] {'dp'}, use_global_device_ids=true, to_apply=%region_11.13 | all-reduce | flops 1 | bytes 8 | tf_op jit(solution)/shard_map/psum | solution.py:187
  769.5 19.9 conditional.10
  769.5 10.2 broadcast_in_dim.426
  792.9 19.8 conditional.13
  792.9 10.2 broadcast_in_dim.490
  816.2 18.5 conditional.16
  816.2 10.1 broadcast_in_dim.560
  838.1 34.0 %collective-permute-done.1 = bf16[4,98,768]{2,0,1:T(4,128)(2,1)} collective-permute-done((bf16[4,98,768]{2,0,1:T(4,128)(2,1)}, bf16[4,98,768]{2,0,1:T(4,128)(2,1)}, u32[]{:S(2)}, u32[]{:S(2)}) %collective-permute-start.1) | collective-permute-done | bytes 602144 | tf_op jit(solution)/shard_map/ppermute | solution.py:35
  872.1 316.9 %conditional.11 = (f32[7673856]{0:T(1024)}) conditional(s32[]{:T(128)} %convert_element_type.659, () %tuple.92, (bf16[4,98,768]{2,0,1:T(4,128)(2,1)}, s32[4,196]{1,0:T(4,128)S(1)}, f32[4,196,768]{2,0,1:T(4,128)}, f32[7673856]{0:T(1024)}, s32[4]{0:T(128)}) %tuple.411), branch_computations={%region_42.45_spmd, %region_43.68_spmd} | conditional | flops 18148079616 | bytes 518729600 | solution.py:224
  933.5 11.0 fusion.468
  952.7 16.0 multiply_convert_fusion.3
  968.8 9.3 reshape.2236
  994.9 10.9 reshape.1971
  1092.1 96.7 %pad_add_fusion.1 = f32[7673856]{0:T(1024)} fusion(f32[589824]{0:T(1024)} %reshape.1977, f32[768]{0:T(1024)S(1)} %get-tuple-element.490, f32[768]{0:T(1024)S(1)} %get-tuple-element.269, f32[768]{0:T(1024)S(1)} %get-tuple-element.277, f32[1769472]{0:T(1024)} %reshape.1976, f32[589824]{0:T(1024)S(1)} %copy-done.67, f32[768]{0:T(1024)S(1)} %get-tuple-element.267, ...), kind=kLoop, calls=%fused_computation.227 | loop fusion | flops 84412416 | bytes 61387776 | tf_op jit(solution)/shard_map/cond/branch_1_fun/transpose(jvp())/add_any | solution.py:114
  1189.0 110.0 %collective-permute-done.3 = bf16[4,98,768]{2,0,1:T(4,128)(2,1)} collective-permute-done((bf16[4,98,768]{2,0,1:T(4,128)(2,1)}, bf16[4,98,768]{2,0,1:T(4,128)(2,1)}, u32[]{:S(2)}, u32[]{:S(2)}) %collective-permute-start.3) | collective-permute-done | bytes 602144 | tf_op jit(solution)/shard_map/ppermute | solution.py:35
  1299.0 333.9 %conditional.14 = (f32[7673856]{0:T(1024)}) conditional(s32[]{:T(128)} %convert_element_type.659, () %tuple.98, (bf16[4,98,768]{2,0,1:T(4,128)(2,1)}, s32[4,196]{1,0:T(4,128)S(1)}, f32[4,196,768]{2,0,1:T(4,128)}, f32[7673856]{0:T(1024)}, s32[4]{0:T(128)S(1)}) %tuple.409), branch_computations={%region_106.109_spmd, %region_107.132_spmd} | conditional | flops 18148079616 | bytes 499658368 | solution.py:224
  1374.2 11.0 fusion.485
  1393.4 16.0 multiply_convert_fusion.7
  1409.4 9.4 reshape.2267
  1436.1 10.8 reshape.2004
  1446.9 8.7 add_convert_fusion.23
  1536.3 96.5 %pad_add_fusion.3 = f32[7673856]{0:T(1024)} fusion(f32[589824]{0:T(1024)} %reshape.2010, f32[768]{0:T(1024)S(1)} %get-tuple-element.555, f32[768]{0:T(1024)S(1)} %get-tuple-element.291, f32[768]{0:T(1024)S(1)} %get-tuple-element.299, f32[1769472]{0:T(1024)} %reshape.2009, f32[589824]{0:T(1024)} %reshape.2006, f32[768]{0:T(1024)S(1)} %get-tuple-element.289, ...), kind=kLoop, calls=%fused_computation.561 | loop fusion | flops 84412416 | bytes 61387776 | tf_op jit(solution)/shard_map/cond/branch_1_fun/transpose(jvp())/add_any | solution.py:114
  1632.9 48.1 %collective-permute-done.5 = bf16[4,98,768]{2,0,1:T(4,128)(2,1)} collective-permute-done((bf16[4,98,768]{2,0,1:T(4,128)(2,1)}, bf16[4,98,768]{2,0,1:T(4,128)(2,1)}, u32[]{:S(2)}, u32[]{:S(2)}) %collective-permute-start.5) | collective-permute-done | bytes 602144 | tf_op jit(solution)/shard_map/ppermute | solution.py:35
  1681.0 316.5 %conditional.17 = (f32[7673856]{0:T(1024)}) conditional(s32[]{:T(128)} %convert_element_type.659, () %tuple.104, (bf16[4,98,768]{2,0,1:T(4,128)(2,1)}, s32[4,196]{1,0:T(4,128)S(1)}, f32[4,196,768]{2,0,1:T(4,128)S(1)}, f32[7673856]{0:T(1024)}, s32[4]{0:T(128)S(1)}) %tuple.407), branch_computations={%region_170.173_spmd, %region_171.196_spmd} | conditional | flops 18148079616 | bytes 509095680 | solution.py:224
  1742.2 11.0 fusion.502
  1761.4 16.0 multiply_convert_fusion.11
  1777.5 9.4 reshape.2298
  1803.7 10.8 reshape.2037
  1900.7 96.7 %pad_add_fusion.5 = f32[7673856]{0:T(1024)} fusion(f32[589824]{0:T(1024)} %reshape.2043, f32[768]{0:T(1024)S(1)} %get-tuple-element.620, f32[768]{0:T(1024)S(1)} %get-tuple-element.313, f32[768]{0:T(1024)S(1)} %get-tuple-element.321, f32[1769472]{0:T(1024)} %reshape.2042, f32[589824]{0:T(1024)S(1)} %copy-done.68, f32[768]{0:T(1024)S(1)} %get-tuple-element.311, ...), kind=kLoop, calls=%fused_computation.895 | loop fusion | flops 84412416 | bytes 61387776 | tf_op jit(solution)/shard_map/cond/branch_1_fun/transpose(jvp())/add_any | solution.py:114
  1997.5 66.4 %add_add_fusion.30 = f32[7673856]{0:T(1024)} fusion(f32[7673856]{0:T(1024)} %get-tuple-element.675, f32[7673856]{0:T(1024)} %get-tuple-element.183, f32[7673856]{0:T(1024)} %get-tuple-element.673, f32[7673856]{0:T(1024)} %get-tuple-element.181, f32[7673856]{0:T(1024)} %get-tuple-element.179, f32[7673856]{0:T(1024)} %get-tuple-element.671), kind=kLoop, calls=%fused_computation.1020 | loop fusion | flops 38369280 | bytes 214867968 | tf_op jit(solution)/shard_map/add | solution.py:226
  2065.8 786.5 %all-reduce.97.cloned.1.call-done = f32[7673856]{0:T(1024)} async-done(((f32[7673856]{0:T(1024)}), f32[7673856]{0:T(1024)}) %all-reduce.97.cloned.1.call-update) | async-done | bytes 30695440
  2855.1 39.6 %all-reduce.94 = (f32[]{:T(128)}, f32[]{:T(128)}) all-reduce(f32[]{:T(128)} %multiply_reduce_fusion.69, f32[]{:T(128)S(6)} %add.1025), channel_id=1, replica_groups=mesh['section'=2,'dp'=16] {'section','dp'}, use_global_device_ids=true, to_apply=%region_196.199 | all-reduce | flops 2 | bytes 16 | tf_op jit(solution)/shard_map/psum | solution.py:228
  2898.7 17.2 multiply_add_fusion.18
  (633 shorter events, 805.7 us)
Async XLA Ops:
  7.2 331.0 %all-gather.2.cloned.1.call-start = ((), (), s32[]{:S(2)}) async-start(), calls=%async_computation | async-start | bytes 32613888 | tf_op jit(solution)/shard_map/all_gather | solution.py:185
  11.6 2840.8 %all-reduce.97.cloned.1.call-start = ((), (), s32[]{:S(2)}) async-start(), calls=%async_computation.1 | async-start | bytes 61390848
  12.3 361.4 %copy-start.222 = (s32[4]{0:T(128)}, s32[4]{0:T(128)S(1)}, u32[]{:S(2)}) copy-start(s32[4]{0:T(128)S(1)} %get-tuple-element.649) | copy-start | bytes 52
  12.3 473.8 %copy-start.219 = (s32[4]{0:T(128)}, s32[4]{0:T(128)S(1)}, u32[]{:S(2)}) copy-start(s32[4]{0:T(128)S(1)} %get-tuple-element.651) | copy-start | bytes 52
  12.9 360.8 %copy-start.171 = (s32[4,196]{1,0:T(4,128)}, s32[4,196]{1,0:T(4,128)S(1)}, u32[]{:S(2)}) copy-start(s32[4,196]{1,0:T(4,128)S(1)} %get-tuple-element.646) | copy-start | bytes 9412
  12.9 473.2 %copy-start.168 = (s32[4,196]{1,0:T(4,128)}, s32[4,196]{1,0:T(4,128)S(1)}, u32[]{:S(2)}) copy-start(s32[4,196]{1,0:T(4,128)S(1)} %get-tuple-element.648) | copy-start | bytes 9412
  30.1 343.6 %copy-start.3 = (f32[4,196,768]{2,0,1:T(4,128)}, f32[4,196,768]{2,0,1:T(4,128)S(1)}, u32[]{:S(2)}) copy-start(f32[4,196,768]{2,0,1:T(4,128)S(1)} %get-tuple-element.643) | copy-start | bytes 7225348
  483.9 285.5 %collective-permute-start = (bf16[4,98,768]{2,0,1:T(4,128)(2,1)}, bf16[4,98,768]{2,0,1:T(4,128)(2,1)}, u32[]{:S(2)}, u32[]{:S(2)}) collective-permute-start(bf16[4,98,768]{2,0,1:T(4,128)(2,1)} %copy.335), channel_id=1, source_target_pairs={{0,16},{1,17},{2,18},{3,19},{4,20},{5,21},{6,22},{7,23},{8,24},{9,... | collective-permute-start | bytes 1806344 | tf_op jit(solution)/shard_map/ppermute | solution.py:35
  486.1 130.0 %copy-start = (f32[4,196,768]{2,0,1:T(4,128)S(1)}, f32[4,196,768]{2,0,1:T(4,128)}, u32[]{:S(2)}) copy-start(f32[4,196,768]{2,0,1:T(4,128)} %get-tuple-element.644) | copy-start | bytes 7225348
  486.1 130.0 %copy-start.165 = (s32[4,196]{1,0:T(4,128)S(1)}, s32[4,196]{1,0:T(4,128)}, u32[]{:S(2)}) copy-start(s32[4,196]{1,0:T(4,128)} %get-tuple-element.647) | copy-start | bytes 9412
  486.1 130.0 %copy-start.216 = (s32[4]{0:T(128)S(1)}, s32[4]{0:T(128)}, u32[]{:S(2)}) copy-start(s32[4]{0:T(128)} %get-tuple-element.650) | copy-start | bytes 52
  613.9 178.9 %collective-permute-start.2 = (bf16[4,98,768]{2,0,1:T(4,128)(2,1)}, bf16[4,98,768]{2,0,1:T(4,128)(2,1)}, u32[]{:S(2)}, u32[]{:S(2)}) collective-permute-start(bf16[4,98,768]{2,0,1:T(4,128)(2,1)} %copy.340), channel_id=1, source_target_pairs={{0,16},{1,17},{2,18},{3,19},{4,20},{5,21},{6,22},{7,23},{8,24},{9,... | collective-permute-start | bytes 1806344 | tf_op jit(solution)/shard_map/ppermute | solution.py:35
  616.1 112.0 %copy-start.207 = (s32[12]{0:T(128)S(1)}, s32[12]{0:T(128)}, u32[]{:S(2)}) copy-start(s32[12]{0:T(128)} %param.30) | copy-start | bytes 148
  616.1 153.4 %copy-start.172 = (s32[4,196]{1,0:T(4,128)S(1)}, s32[4,196]{1,0:T(4,128)}, u32[]{:S(2)}) copy-start(s32[4,196]{1,0:T(4,128)} %copy-done.171) | copy-start | bytes 9412
  726.0 90.1 %collective-permute-start.4 = (bf16[4,98,768]{2,0,1:T(4,128)(2,1)}, bf16[4,98,768]{2,0,1:T(4,128)(2,1)}, u32[]{:S(2)}, u32[]{:S(2)}) collective-permute-start(bf16[4,98,768]{2,0,1:T(4,128)(2,1)} %copy.345), channel_id=1, source_target_pairs={{0,16},{1,17},{2,18},{3,19},{4,20},{5,21},{6,22},{7,23},{8,24},{9,... | collective-permute-start | bytes 1806344 | tf_op jit(solution)/shard_map/ppermute | solution.py:35
  769.5 23.3 copy-start.169
  791.5 80.6 %collective-permute-start.1 = (bf16[4,98,768]{2,0,1:T(4,128)(2,1)}, bf16[4,98,768]{2,0,1:T(4,128)(2,1)}, u32[]{:S(2)}, u32[]{:S(2)}) collective-permute-start(bf16[4,98,768]{2,0,1:T(4,128)(2,1)} %copy.338), channel_id=1, source_target_pairs={{16,0},{17,1},{18,2},{19,3},{20,4},{21,5},{22,6},{23,7},{24,8},{25... | collective-permute-start | bytes 1806344 | tf_op jit(solution)/shard_map/ppermute | solution.py:35
  792.8 23.3 copy-start.1
  792.8 23.3 copy-start.166
  792.9 23.3 copy-start.217
  814.8 484.2 %collective-permute-start.3 = (bf16[4,98,768]{2,0,1:T(4,128)(2,1)}, bf16[4,98,768]{2,0,1:T(4,128)(2,1)}, u32[]{:S(2)}, u32[]{:S(2)}) collective-permute-start(bf16[4,98,768]{2,0,1:T(4,128)(2,1)} %copy.343), channel_id=1, source_target_pairs={{16,0},{17,1},{18,2},{19,3},{20,4},{21,5},{22,6},{23,7},{24,8},{25... | collective-permute-start | bytes 1806344 | tf_op jit(solution)/shard_map/ppermute | solution.py:35
  816.2 56.0 %copy-start.173 = (s32[4,196]{1,0:T(4,128)S(1)}, s32[4,196]{1,0:T(4,128)}, u32[]{:S(2)}) copy-start(s32[4,196]{1,0:T(4,128)} %copy-done.171) | copy-start | bytes 9412
  836.9 844.1 %collective-permute-start.5 = (bf16[4,98,768]{2,0,1:T(4,128)(2,1)}, bf16[4,98,768]{2,0,1:T(4,128)(2,1)}, u32[]{:S(2)}, u32[]{:S(2)}) collective-permute-start(bf16[4,98,768]{2,0,1:T(4,128)(2,1)} %copy.348), channel_id=1, source_target_pairs={{16,0},{17,1},{18,2},{19,3},{20,4},{21,5},{22,6},{23,7},{24,8},{25... | collective-permute-start | bytes 1806344 | tf_op jit(solution)/shard_map/ppermute | solution.py:35
  872.1 426.9 %copy-start.170 = (s32[4,196]{1,0:T(4,128)S(1)}, s32[4,196]{1,0:T(4,128)}, u32[]{:S(2)}) copy-start(s32[4,196]{1,0:T(4,128)} %copy-done.168) | copy-start | bytes 9412
  872.1 426.9 %copy-start.220 = (s32[4]{0:T(128)S(1)}, s32[4]{0:T(128)}, u32[]{:S(2)}) copy-start(s32[4]{0:T(128)} %copy-done.219) | copy-start | bytes 52
  872.9 7.6 copy-start.5
  886.2 5.5 copy-start.88
  894.7 12.8 copy-start.130
  914.4 6.8 copy-start.116
  1005.8 10.2 copy-start.162
  1016.1 8.6 slice-start.12
  1018.7 5.9 slice-start.13
  1039.3 5.9 copy-start.49
  1299.0 382.0 %copy-start.2 = (f32[4,196,768]{2,0,1:T(4,128)S(1)}, f32[4,196,768]{2,0,1:T(4,128)}, u32[]{:S(2)}) copy-start(f32[4,196,768]{2,0,1:T(4,128)} %get-tuple-element.644) | copy-start | bytes 7225348
  1299.0 382.0 %copy-start.167 = (s32[4,196]{1,0:T(4,128)S(1)}, s32[4,196]{1,0:T(4,128)}, u32[]{:S(2)}) copy-start(s32[4,196]{1,0:T(4,128)} %get-tuple-element.647) | copy-start | bytes 9412
  1299.0 382.0 %copy-start.218 = (s32[4]{0:T(128)S(1)}, s32[4]{0:T(128)}, u32[]{:S(2)}) copy-start(s32[4]{0:T(128)} %get-tuple-element.650) | copy-start | bytes 52
  1446.9 10.2 copy-start.163
  1457.1 8.5 slice-start.14
  1459.8 5.8 copy-start.16
  1459.8 5.8 slice-start.15
  1694.9 5.5 copy-start.91
  1703.5 12.8 copy-start.133
  1723.1 6.7 copy-start.118
  1814.5 10.2 copy-start.164
  1824.6 8.6 slice-start.16
  1827.3 5.9 slice-start.17
  1847.9 6.0 copy-start.52
  2063.9 833.8 %copy-start.143 = (f32[1,479616]{1,0:T(1,128)S(1)}, f32[1,479616]{1,0:T(1,128)}, u32[]{:S(2)}) copy-start(f32[1,479616]{1,0:T(1,128)} %param.34) | copy-start | bytes 5755396
  (70 other events, 174.2 us)
Sparse Core Ops, SparseCore 0:
  11.7 326.4 all-gather.1
  2064.1 788.2 all-reduce.96
where the time goes:
time: 2940 us; the launch traced here: 2920 us
  waiting for transfers between devices  1290 us (44%)
  local copies, waits for them, and re-layouts  625 us (21%)
  other arithmetic  518 us (18%)
  matrix products  358 us (12%)
  blocking collectives  79 us (3%)
    unnamed x3, waiting for transfers between devices  787 us
    all_gather x1, waiting for transfers between devices, on_device(): lax.all_gather(master.astype(jnp.bfloat16), 'dp', axis=1, tiled=True)  308 us
    add_any x3, other arithmetic, unpack(): pieces.append(flat[offset:offset + amount].reshape(shape))  290 us
    slice x42, local copies, waits for them, and re-layouts, unpack(): pieces.append(flat[offset:offset + amount].reshape(shape))  219 us
    ppermute x6, waiting for transfers between devices, passed_along(): lax.ppermute(value, axis, [(source, source + steps) for source in range(l...  192 us
    reshape x24, local copies, waits for them, and re-layouts, unpack(): pieces.append(flat[offset:offset + amount].reshape(shape))  173 us
    dot_general x12, matrix products, block(): hidden = round_grad(jnp.einsum('blw,wk->blk', normed, fc_one))  114 us
    dot_general x12, matrix products, block(): return stream + round_grad(jnp.einsum('blk,kw->blw', hidden, fc_two))  74.3 us
  transfers between devices with their start and end apart: 8, of which 5 were waited for; matrix products, arithmetic and copies ran while one was open for 32% of the time, Pallas kernels for 0%

commit v1 on v0

v1 whole, which is shorter than its diff:
```python
import math

import jax
import jax.numpy as jnp
import numpy as np
from jax import lax
from jax.experimental import pallas as pl
from jax.experimental.pallas import tpu as pltpu
from jax.sharding import PartitionSpec as P

D = 768
HEADS_E = 12
FF_E = 3072
DD = 512
HEADS_D = 16
FF_D = 2048
PIX = 768
NP = 196
SLOTS = 98
STEP = 10

norm_epsilon = 1e-06
clip_limit = 0.01
learn_rate = 0.02
beta_one = 0.9
beta_two = 0.999
adam_epsilon = 1e-08
weight_decay = 0.05
average_keep = 0.8

F32 = jnp.float32
BF16 = jnp.bfloat16
ROWS_E = 112
ROWS_D = 208
GROUP = 16
VEC_UNITS = 2
VMEM_BYTES = 60 * 1024 * 1024

ENC = [
    ("patch", (PIX, D)),
    ("patch_b", (D,)),
    ("g1", (D,)),
    ("b1", (D,)),
    ("qkv", (D, 3 * D)),
    ("proj", (D, D)),
    ("g2", (D,)),
    ("b2", (D,)),
    ("fc1", (D, FF_E)),
    ("fc2", (FF_E, D)),
    ("gf", (D,)),
    ("bf", (D,)),
]
DEC = [
    ("embed", (D, DD)),
    ("mask", (DD,)),
    ("g1", (DD,)),
    ("b1", (DD,)),
    ("qkv", (DD, 3 * DD)),
    ("proj", (DD, DD)),
    ("g2", (DD,)),
    ("b2", (DD,)),
    ("fc1", (DD, FF_D)),
    ("fc2", (FF_D, DD)),
    ("gf", (DD,)),
    ("bf", (DD,)),
    ("head", (DD, PIX)),
]


class Section:
    def __init__(self, layout, dp, shard_rows):
        self.dp = dp
        self.shard_rows = shard_rows
        self.groups = []
        self.vectors = {}
        self.panels = {}
        fill = [0] * dp
        vector_fill = [0] * dp
        row = 0
        for name, shape in layout:
            panels = shape[-1] // 128
            self.panels[name] = panels
            if len(shape) == 2:
                for group in range(shape[0] // GROUP):
                    block = row // shard_rows
                    self.groups.append((name, group, row, panels, block, fill[block]))
                    fill[block] += panels
                    row += GROUP * panels
            else:
                block = row // shard_rows
                self.vectors[name] = (row, panels, block, vector_fill[block])
                vector_fill[block] += panels
                row += panels
        self.rows = row
        self.fill = fill
        assert max(vector_fill) <= 16 * VEC_UNITS
        self.blocks_used = max(b for b in range(dp) if fill[b] or vector_fill[b]) + 1

    def pieces(self, name, first=0, count=None):
        out = []
        for tensor, group, _, panels, block, unit in self.groups:
            if tensor != name or group < first or (count is not None and group >= first + count):
                continue
            if out and out[-1][0] == block and out[-1][1] + out[-1][3] * panels == unit:
                out[-1][3] += 1
            else:
                out.append([block, unit, group, 1])
        return [tuple(p) for p in out]


class Plan:
    def __init__(self, dp, shard_rows):
        self.dp = dp
        self.shard_rows = shard_rows
        self.sections = [Section(ENC, dp, shard_rows), Section(DEC, dp, shard_rows)]
        units = max(max(s.fill) for s in self.sections)
        units += (units + VEC_UNITS) % 2
        self.vec_unit = units
        self.units = units + VEC_UNITS
        self.half = self.units // 2
        self.head_rows = 8 * -(-max(16 * max(s.panels.values()) for s in self.sections) // 8)
        self.tail_units = max(max(s.panels.values()) for s in self.sections)
        self.pack_rows = shard_rows + self.head_rows
        self.pack_index = np.zeros((2, dp, self.units * 16), np.int32)
        self.tail_rows = 16 * (self.tail_units + VEC_UNITS)
        self.zero_row = self.units * 16 + self.tail_rows
        self.unpack_index = np.full((2, dp, shard_rows), self.zero_row, np.int32)
        self.tail_start = np.zeros((2, dp), np.int32)
        for s, section in enumerate(self.sections):
            for b in range(dp):
                self.tail_start[s, b] = max(section.fill[b] - self.tail_units, 0)
            for name, group, row, panels, block, unit in section.groups:
                for panel in range(panels):
                    for r in range(GROUP):
                        self.place(s, block, (unit + panel) * 16 + r, row + r * panels + panel)
            for row, panels, block, at in section.vectors.values():
                for panel in range(panels):
                    self.place(s, block, self.vec_unit * 16 + at + panel, row + panel)

    def place(self, s, block, block_row, flat_row):
        local = flat_row - block * self.shard_rows
        assert 0 <= local < self.pack_rows
        self.pack_index[s, block, block_row] = local
        owner, at = divmod(flat_row, self.shard_rows)
        if owner == block:
            self.unpack_index[s, owner, at] = block_row
        else:
            assert owner == block + 1
            if block_row >= self.vec_unit * 16:
                source = self.tail_units * 16 + block_row - self.vec_unit * 16
            else:
                source = block_row - int(self.tail_start[s, block]) * 16
                assert 0 <= source < self.tail_units * 16
            self.unpack_index[s, owner, at] = self.units * 16 + source


def factors(dp):
    if dp == 16:
        return (4, 2, 2)
    if dp == 64:
        return (4, 4, 4)
    return (dp, 1, 1)


def move_rows_kernel(index_ref, *refs, count, sizes, zero_at):
    sources, out_ref, held, done = refs[: len(sizes)], refs[-3], refs[-2], refs[-1]
    at = 0
    for source, size in zip(sources, sizes):
        held[pl.ds(at, size), :] = source[...].reshape(size, 128)
        at += size
    if zero_at is not None:
        held[pl.ds(zero_at, 8), :] = jnp.zeros((8, 128), F32)

    def eight(i, carry):
        for j in range(8):
            row = i * 8 + j
            done[pl.ds(row, 1), :] = held[pl.ds(index_ref[row], 1), :]
        return carry

    lax.fori_loop(0, count // 8, eight, 0)
    for row in range(count // 8 * 8, count):
        done[pl.ds(row, 1), :] = held[pl.ds(index_ref[row], 1), :]
    out_ref[...] = done[...].reshape(out_ref.shape).astype(out_ref.dtype)


def move_rows(index, sources, out_shape, dtype, zero_at=None):
    sizes = [math.prod(s.shape) // 128 for s in sources]
    count = math.prod(out_shape) // 128
    total = sum(sizes) + 8
    import functools

    return pl.pallas_call(
        functools.partial(move_rows_kernel, count=count, sizes=sizes, zero_at=zero_at),
        out_shape=jax.ShapeDtypeStruct(out_shape, dtype),
        in_specs=[pl.BlockSpec(memory_space=pltpu.SMEM)]
        + [pl.BlockSpec(memory_space=pltpu.VMEM)] * len(sources),
        out_specs=pl.BlockSpec(memory_space=pltpu.VMEM),
        scratch_shapes=[pltpu.VMEM((total, 128), F32), pltpu.VMEM((count, 128), F32)],
        compiler_params=pltpu.CompilerParams(vmem_limit_bytes=32 * 1024 * 1024),
        name="move_rows",
    )(index, *sources)


def dot(a, b):
    return lax.dot_general(a, b, (((1,), (0,)), ((), ())), preferred_element_type=F32)


def dot_nt(a, b):
    return lax.dot_general(a, b, (((1,), (1,)), ((), ())), preferred_element_type=F32)


def dot_tn(a, b):
    return lax.dot_general(a, b, (((0,), (0,)), ((), ())), preferred_element_type=F32)


def for_rows(count, size, step, unroll=1):
    def body(i, carry):
        step(pl.multiple_of(i * size, size))
        return carry

    lax.fori_loop(0, count // size, body, 0, unroll=unroll)


def columns(weight, panels, depth, pair):
    halves = [
        weight[:, 2 * pair + i].reshape(depth, 128)
        for i in range(2)
    ]
    return jnp.concatenate(halves, axis=1)


def row_band(weight, panels, band):
    parts = [weight[pl.ds(band * 16, 16), i].reshape(256, 128) for i in range(panels)]
    return jnp.concatenate(parts, axis=1)


def times_columns(left, weight, panels, depth, acc, finish):
    def body(pair, carry):
        acc[...] = dot(left[...], columns(weight, panels, depth, pair))
        finish(pair)
        return carry

    lax.fori_loop(0, panels // 2, body, 0)


def lanes(pair):
    return pl.ds(pl.multiple_of(pair * 256, 256), 256)


def norm_rows(x, width):
    mean = jnp.sum(x, axis=1, keepdims=True) * (1.0 / width)
    centre = x - mean
    spread = jnp.sum(centre * centre, axis=1, keepdims=True) * (1.0 / width)
    rstd = lax.rsqrt(spread + norm_epsilon)
    return centre * rstd, rstd


def norm_forward(x_ref, gain, shift, out_ref, count, width, size=16):
    def step(at):
        hat, _ = norm_rows(x_ref[pl.ds(at, size), :], width)
        out_ref[pl.ds(at, size), :] = (hat * gain + shift).astype(out_ref.dtype)

    for_rows(count, size, step, 2)


def norm_backward(x_ref, gain, grad_of, put, count, width, size=16):
    def body(i, carry):
        gain_sum, shift_sum = carry
        at = pl.multiple_of(i * size, size)
        hat, rstd = norm_rows(x_ref[pl.ds(at, size), :], width)
        grad = grad_of(at, size)
        gain_sum = gain_sum + jnp.sum((grad * hat).reshape(size // 8, 8, width), axis=0)
        shift_sum = shift_sum + jnp.sum(grad.reshape(size // 8, 8, width), axis=0)
        scaled = grad * gain
        first = jnp.sum(scaled, axis=1, keepdims=True) * (1.0 / width)
        second = jnp.sum(scaled * hat, axis=1, keepdims=True) * (1.0 / width)
        put(at, size, rstd * (scaled - first - hat * second))
        return gain_sum, shift_sum

    zero = jnp.zeros((8, width), F32)
    gain_sum, shift_sum = lax.fori_loop(0, count // size, body, (zero, zero))
    return jnp.sum(gain_sum, axis=0, keepdims=True), jnp.sum(shift_sum, axis=0, keepdims=True)


def head_masks(size):
    lane = lax.broadcasted_iota(jnp.int32, (1, 128), 1)
    return [
        jnp.where((lane >= h * size) & (lane < (h + 1) * size), 1.0, 0.0).astype(BF16)
        for h in range(128 // size)
    ]


def softmax_rows(scores, limit):
    key = lax.broadcasted_iota(jnp.int32, scores.shape, 1)
    scores = jnp.where(key < limit, scores, -1e30)
    top = jnp.max(scores, axis=1, keepdims=True)
    raised = jnp.exp(scores - top)
    return raised * (1.0 / jnp.sum(raised, axis=1, keepdims=True))


def attention_forward(mixed, out, limit_of, images, rows, width, size):
    panels = width // 128
    masks = head_masks(size)

    def body(step, carry):
        image, panel = step // panels, step % panels
        here = pl.ds(pl.multiple_of(image * rows, 16), rows)

        def part(third):
            return mixed[here, pl.ds(pl.multiple_of((third * panels + panel) * 128, 128), 128)]

        query, keys, values = part(0), part(1), part(2)
        limit = limit_of(image)
        total = jnp.zeros((rows, 128), F32)
        for mask in masks:
            probs = softmax_rows(dot_nt(query * mask, keys), limit).astype(BF16)
            total = total + dot(probs, values * mask)
        out[here, pl.ds(pl.multiple_of(panel * 128, 128), 128)] = total.astype(BF16)
        return carry

    lax.fori_loop(0, images * panels, body, 0)


def attention_backward(mixed, grad_out, grad_mixed, limit_of, images, rows, width, size):
    panels = width // 128
    masks = head_masks(size)

    def body(step, carry):
        image, panel = step // panels, step % panels
        here = pl.ds(pl.multiple_of(image * rows, 16), rows)

        def place(third):
            return pl.ds(pl.multiple_of((third * panels + panel) * 128, 128), 128)

        query, keys, values = (mixed[here, place(third)] for third in range(3))
        grad = grad_out[here, place(0)]
        limit = limit_of(image)
        zero = jnp.zeros((rows, 128), F32)
        grad_query, grad_keys, grad_values = zero, zero, zero
        for mask in masks:
            masked_query = query * mask
            masked_grad = grad * mask
            probs = softmax_rows(dot_nt(masked_query, keys), limit)
            grad_probs = dot_nt(masked_grad, values)
            inner = jnp.sum(probs * grad_probs, axis=1, keepdims=True)
            grad_scores = (probs * (grad_probs - inner)).astype(BF16)
            grad_values = grad_values + dot_tn(probs.astype(BF16), masked_grad)
            grad_query = grad_query + dot(grad_scores, keys * mask)
            grad_keys = grad_keys + dot_tn(grad_scores, masked_query)
        grad_mixed[here, place(0)] = (grad_query * (1.0 / math.sqrt(size))).astype(BF16)
        grad_mixed[here, place(1)] = grad_keys.astype(BF16)
        grad_mixed[here, place(2)] = grad_values.astype(BF16)
        return carry

    lax.fori_loop(0, images * panels, body, 0)


def gelu_parts(value):
    bell = 0.5 * (1.0 + lax.erf(value * math.sqrt(0.5)))
    slope = bell + value * (jnp.exp(value * value * -0.5) * (1.0 / math.sqrt(2.0 * math.pi)))
    return value * bell, slope


class Shape:
    def __init__(self, images, rows, width, heads, hidden):
        self.images, self.rows, self.width = images, rows, width
        self.size = width // heads
        self.hidden = hidden
        self.count = images * rows


def block_forward(sh, x0, n1, mixed, o, x1, n2, g, gp, y, w, vec, limit_of, acc, ready, saved):
    width, hidden, count = sh.width, sh.hidden, sh.count
    panels = width // 128
    norm_forward(x0, vec("g1"), vec("b1"), n1, count, width)
    saved(n1)
    ready("qkv")

    def put_mixed(pair):
        scale = jnp.where(pair < panels // 2, 1.0 / math.sqrt(sh.size), 1.0)

        def step(at):
            mixed[pl.ds(at, 16), lanes(pair)] = (acc[pl.ds(at, 16), :] * scale).astype(BF16)

        for_rows(count, 16, step, 4)

    times_columns(n1, w["qkv"], 3 * panels, width, acc, put_mixed)
    saved(mixed)
    attention_forward(mixed, o, limit_of, sh.images, sh.rows, width, sh.size)
    saved(o)
    ready("proj")

    def put_sum(base, out):
        def finish(pair):
            def step(at):
                here = pl.ds(at, 16)
                out[here, lanes(pair)] = base[here, lanes(pair)] + acc[here, :]

            for_rows(count, 16, step, 4)

        return finish

    times_columns(o, w["proj"], panels, width, acc, put_sum(x0, x1))
    saved(x1)
    norm_forward(x1, vec("g2"), vec("b2"), n2, count, width)
    saved(n2)
    ready("fc1")

    def put_hidden(pair):
        def step(at):
            here = pl.ds(at, 16)
            value, slope = gelu_parts(acc[here, :])
            g[here, lanes(pair)] = value.astype(BF16)
            gp[here, lanes(pair)] = slope

        for_rows(count, 16, step, 2)

    times_columns(n2, w["fc1"], hidden // 128, width, acc, put_hidden)
    saved(g)
    saved(gp)
    ready("fc2")
    times_columns(g, w["fc2"], panels, hidden, acc, put_sum(x1, y))
    saved(y)


class Gradients:
    def __init__(self, section, half, own, stage, sems, keep, send):
        self.section, self.half, self.own = section, half, own
        self.stage, self.sems, self.keep, self.send = stage, sems, keep, send
        self.turn = 0
        self.flying = [[], []]

    def pieces(self, name, first, count):
        panels = self.section.panels[name]
        out = []
        for block, unit, group, groups in self.section.pieces(name, first, count):
            start, left = unit, groups * panels
            at = (group - first) * panels
            while left:
                side = 0 if start < self.half else 1
                take = min(left, self.half - start) if side == 0 else left
                out.append((block, side, start - side * self.half, at, take))
                start, at, left = start + take, at + take, left - take
        return out

    def copy_out(self, source, block, side, unit, take, sem):
        def to(target):
            return pltpu.make_async_copy(source, target.at[block, pl.ds(unit, take)], sem)

        @pl.when(self.own == side)
        def _():
            to(self.keep).start()

        @pl.when(self.own != side)
        def _():
            to(self.send).start()

        return to(self.keep)

    def drain(self, slot):
        for copy in self.flying[slot]:
            copy.wait()
        self.flying[slot] = []

    def weight(self, name, left, depth, right, turned):
        panels = self.section.panels[name]
        for band in range(depth // 256):
            slot = self.turn % 2
            self.turn += 1
            self.drain(slot)
            stage = self.stage.at[slot]
            turned[...] = left[:, band * 256 : band * 256 + 256].T

            def body(pair, carry):
                value = dot(turned[...], right[:, lanes(pair)])
                for i in range(2):
                    stage[pl.ds(2 * pair + i, 16, stride=panels)] = value[
                        :, i * 128 : i * 128 + 128
                    ].reshape(16, 16, 128)
                return carry

            lax.fori_loop(0, panels // 2, body, 0)
            for block, side, unit, at, take in self.pieces(name, band * 16, 16):
                self.flying[slot].append(
                    self.copy_out(
                        stage.at[pl.ds(at, take)], block, side, unit, take, self.sems.at[slot]
                    )
                )

    def vectors(self, values, scratch, vec_unit):
        blocks = sorted({v[2] for v in self.section.vectors.values()})
        for k, block in enumerate(blocks):
            scratch[k] = jnp.zeros((16 * VEC_UNITS, 128), F32).reshape(VEC_UNITS, 16, 128)
            for name, (_, panels, at_block, at) in self.section.vectors.items():
                if at_block != block:
                    continue
                for panel in range(panels):
                    unit, row = divmod(at + panel, 16)
                    scratch[k, unit, row : row + 1, :] = values[name][
                        :, panel * 128 : panel * 128 + 128
                    ]
        copies = [
            self.copy_out(
                scratch.at[k], block, 1, vec_unit - self.half, VEC_UNITS, self.sems.at[2]
            )
            for k, block in enumerate(blocks)
        ]
        for copy in copies:
            copy.wait()
        self.drain(0)
        self.drain(1)


def block_backward(sh, dy, x0, n1, mixed, o, x1, n2, g, gp, dyb, dn, dmixed, acc, turned, w, vec,
                   limit_of, grads, values, ready):
    width, hidden, count = sh.width, sh.hidden, sh.count
    panels = width // 128

    def round_stream():
        def step(at):
            dyb[pl.ds(at, 16), :] = dy[pl.ds(at, 16), :].astype(BF16)

        for_rows(count, 16, step, 2)

    def into_stream(at, size, value):
        dy[pl.ds(at, size), :] = dy[pl.ds(at, size), :] + value

    def from_dn(at, size):
        return dn[pl.ds(at, size), :]

    round_stream()
    ready("fc2", g)
    grads.weight("fc2", g, hidden, dyb, turned)
    ready("gp", gp)

    def hidden_band(band, carry):
        acc[...] = dot_nt(dyb[...], row_band(w["fc2"], panels, band))

        def step(at):
            here = pl.ds(at, 16)
            g[here, lanes(band)] = (acc[here, :] * gp[here, lanes(band)]).astype(BF16)

        for_rows(count, 16, step, 4)
        return carry

    lax.fori_loop(0, hidden // 256, hidden_band, 0)
    ready("fc1", n2)
    grads.weight("fc1", n2, width, g, turned)

    def back_through(left, name):
        def body(band, carry):
            acc[...] = dot_nt(left[...], row_band(w[name], grads.section.panels[name], band))

            def step(at):
                dn[pl.ds(at, 16), lanes(band)] = acc[pl.ds(at, 16), :]

            for_rows(count, 16, step, 4)
            return carry

        lax.fori_loop(0, width // 256, body, 0)

    back_through(g, "fc1")
    ready("x1", x1)
    values["g2"], values["b2"] = norm_backward(x1, vec("g2"), from_dn, into_stream, count, width)
    round_stream()
    ready("proj", o)
    grads.weight("proj", o, width, dyb, turned)

    def out_band(band, carry):
        acc[...] = dot_nt(dyb[...], row_band(w["proj"], panels, band))

        def step(at):
            o[pl.ds(at, 16), lanes(band)] = acc[pl.ds(at, 16), :].astype(BF16)

        for_rows(count, 16, step, 4)
        return carry

    lax.fori_loop(0, width // 256, out_band, 0)
    ready("mixed", mixed)
    attention_backward(mixed, o, dmixed, limit_of, sh.images, sh.rows, width, sh.size)
    ready("qkv", n1)
    grads.weight("qkv", n1, width, dmixed, turned)
    back_through(dmixed, "qkv")
    ready("x0", x0)
    values["g1"], values["b1"] = norm_backward(x0, vec("g1"), from_dn, into_stream, count, width)


def load_vectors(section, vec_unit, own_section, gathered, held, vec_ref, sem):
    blocks = sorted({v[2] for v in section.vectors.values()})
    copies = [
        pltpu.make_async_copy(
            gathered.at[own_section, block, pl.ds(vec_unit, VEC_UNITS)], held.at[k], sem
        )
        for k, block in enumerate(blocks)
    ]
    for copy in copies:
        copy.start()

    def finish():
        for copy in copies:
            copy.wait()
        names = {}
        for k, block in enumerate(blocks):
            rows = held[k].reshape(16 * VEC_UNITS, 128).astype(F32)
            for i, (name, (_, panels, at_block, at)) in enumerate(section.vectors.items()):
                names[name] = i
                if at_block != block:
                    continue
                for panel in range(panels):
                    vec_ref[i : i + 1, panel * 128 : panel * 128 + 128] = rows[
                        at + panel : at + panel + 1, :
                    ]
        return lambda name: vec_ref[names[name] : names[name] + 1, :]

    return finish


def load_weights(section, own_section, gathered, w, sems):
    copies = {}
    for k, (name, ref) in enumerate(w.items()):
        panels = section.panels[name]
        copies[name] = [
            pltpu.make_async_copy(
                gathered.at[own_section, block, pl.ds(unit, groups * panels)],
                ref.reshape(ref.shape[0] * panels, 16, 128).at[
                    pl.ds(group * panels, groups * panels)
                ],
                sems.at[k],
            )
            for block, unit, group, groups in section.pieces(name)
        ]
        for copy in copies[name]:
            copy.start()

    def ready(name):
        for copy in copies.get(name, ()):
            copy.wait()

    return ready


def weight_scratch(layout, names):
    shapes = dict(layout)
    return [
        pltpu.VMEM((shapes[n][0] // GROUP, shapes[n][1] // 128, GROUP, 128), BF16)
        for n in names
    ]


def picks(perm_ref, image):
    here = pl.ds(pl.multiple_of(image * ROWS_D, 16), ROWS_D)
    patch = lax.broadcasted_iota(jnp.int32, (ROWS_D, ROWS_D), 1)
    return jnp.where(perm_ref[here, :] == patch, 1.0, 0.0).astype(BF16)


W_ENC = ["patch", "qkv", "proj", "fc1", "fc2"]


def encoder_kernel(plan, sh, refs):
    section = plan.sections[0]
    (info, gathered, patches, perm, pos, pp_out, x0_out, n1_out, mixed_out, o_out, x1_out, n2_out,
     g_out, gp_out, y_out, latent_out, w_patch, w_qkv, w_proj, w_fc1, w_fc2, held, vec_ref, pp, xe,
     x0, n1, mixed, o, x1, n2, g, gp, y, latent, acc, w_sems, out_sems) = refs
    w = dict(zip(W_ENC, (w_patch, w_qkv, w_proj, w_fc1, w_fc2)))
    finish_vec = load_vectors(section, plan.vec_unit, 0, gathered, held, vec_ref, w_sems.at[5])
    ready = load_weights(section, 0, gathered, w, w_sems)
    outs = []

    targets = [(pp, pp_out), (x0, x0_out), (n1, n1_out), (mixed, mixed_out), (o, o_out),
               (x1, x1_out), (n2, n2_out), (g, g_out), (gp, gp_out), (y, y_out),
               (latent, latent_out)]

    def saved(ref):
        for k, (source, target) in enumerate(targets):
            if source is ref:
                copy = pltpu.make_async_copy(source, target, out_sems.at[k])
                copy.start()
                outs.append(copy)

    def gather(image, carry):
        chosen = picks(perm, image)
        pp[image] = dot(chosen, patches[image]).astype(BF16)
        here = pl.ds(pl.multiple_of(image * ROWS_E, 16), ROWS_E)
        xe[here, :] = pp[image, 0:ROWS_E, :]
        few = chosen[0:ROWS_E, :]
        x0[here, :] = (dot(few, pos[0]) + dot(few, pos[1])) + dot(few, pos[2])
        return carry

    lax.fori_loop(0, sh.images, gather, 0)
    saved(pp)
    vec = finish_vec()
    ready("patch")
    bias = vec("patch_b")

    def put(pair):
        part = vec_ref[0:1, lanes(pair)]

        def step(at):
            here = pl.ds(at, 16)
            x0[here, lanes(pair)] = (acc[here, :] + part) + x0[here, lanes(pair)]

        for_rows(sh.count, 16, step, 4)

    del bias
    times_columns(xe, w["patch"], D // 128, PIX, acc, put)
    saved(x0)
    block_forward(
        sh, x0, n1, mixed, o, x1, n2, g, gp, y, w, vec, lambda i: info[1 + i], acc, ready, saved
    )
    norm_forward(y, vec("gf"), vec("bf"), latent, sh.count, D)
    saved(latent)
    for copy in outs:
        copy.wait()


ANY = pl.BlockSpec(memory_space=pl.ANY)
IN_VMEM = pl.BlockSpec(memory_space=pltpu.VMEM)
IN_SMEM = pl.BlockSpec(memory_space=pltpu.SMEM)


def saved_shapes(sh):
    count, width, hidden = sh.count, sh.width, sh.hidden
    return [
        ((count, width), F32),
        ((count, width), BF16),
        ((count, 3 * width), BF16),
        ((count, width), BF16),
        ((count, width), F32),
        ((count, width), BF16),
        ((count, hidden), BF16),
        ((count, hidden), F32),
        ((count, width), F32),
    ]


def encoder(plan, sh, info, gathered, patches, perm, pos):
    saved = saved_shapes(sh)
    pp_shape = ((sh.images, ROWS_D, PIX), BF16)
    latent_shape = ((sh.count, D), BF16)
    outs = [pp_shape, *saved, latent_shape]
    holders = len({v[2] for v in plan.sections[0].vectors.values()})
    return pl.pallas_call(
        lambda *refs: encoder_kernel(plan, sh, refs),
        out_shape=[jax.ShapeDtypeStruct(*s) for s in outs],
        in_specs=[IN_SMEM, ANY, IN_VMEM, IN_VMEM, IN_VMEM],
        out_specs=[ANY] * len(outs),
        scratch_shapes=[
            *weight_scratch(ENC, W_ENC),
            pltpu.VMEM((holders, VEC_UNITS, 16, 128), BF16),
            pltpu.VMEM((8, D), F32),
            pltpu.VMEM(*pp_shape),
            pltpu.VMEM((sh.count, PIX), BF16),
            *[pltpu.VMEM(*s) for s in saved],
            pltpu.VMEM(*latent_shape),
            pltpu.VMEM((sh.count, 256), F32),
            pltpu.SemaphoreType.DMA((6,)),
            pltpu.SemaphoreType.DMA((len(outs),)),
        ],
        compiler_params=pltpu.CompilerParams(vmem_limit_bytes=VMEM_BYTES),
        name="encoder_forward",
    )(info, gathered, patches, perm, pos)


W_DEC = ["embed", "qkv", "proj", "fc1", "fc2", "head"]


def decoder_kernel(plan, sh, refs):
    section = plan.sections[1]
    (info, scale, gathered, latent_in, pp_in, perm, pos, keep_out, send_out, grad_latent, loss_out,
     w_embed, w_qkv, w_proj, w_fc1, w_fc2, w_head, held, vec_ref, pp, latent, embedded, x0, n1,
     mixed, o, x1, n2, g, gp, y, f, dn, guess, acc, acc_e, turned, turned_e, stage, vec_stage, w_sems,
     in_sems, grad_sems) = refs
    w = dict(zip(W_DEC, (w_embed, w_qkv, w_proj, w_fc1, w_fc2, w_head)))
    copy_latent = pltpu.make_async_copy(latent_in, latent, in_sems.at[0])
    copy_pp = pltpu.make_async_copy(pp_in, pp, in_sems.at[1])
    copy_latent.start()
    finish_vec = load_vectors(section, plan.vec_unit, 1, gathered, held, vec_ref, w_sems.at[6])
    ready = load_weights(section, 1, gathered, w, w_sems)
    copy_pp.start()
    images, count = sh.images, sh.count
    count_e = images * ROWS_E
    vec = finish_vec()
    copy_latent.wait()
    ready("embed")

    def put_embedded(pair):
        def step(at):
            embedded[pl.ds(at, 16), lanes(pair)] = acc_e[pl.ds(at, 16), :]

        for_rows(count_e, 16, step, 4)

    times_columns(latent, w["embed"], DD // 128, D, acc_e, put_embedded)

    def tokens(image, carry):
        chosen = picks(perm, image)
        place = (dot(chosen, pos[0]) + dot(chosen, pos[1])) + dot(chosen, pos[2])
        start = pl.multiple_of(image * ROWS_D, 16)
        kept = info[1 + image]
        token = vec_ref[0:1, :]
        few = embedded[pl.ds(pl.multiple_of(image * ROWS_E, 16), ROWS_E), :]
        rank = lax.broadcasted_iota(jnp.int32, (ROWS_E, DD), 0)
        x0[pl.ds(start, ROWS_E), :] = jnp.where(rank < kept, few, token) + place[:ROWS_E, :]
        x0[pl.ds(start + ROWS_E, ROWS_D - ROWS_E), :] = token + place[ROWS_E:, :]
        return carry

    lax.fori_loop(0, images, tokens, 0)
    block_forward(
        sh, x0, n1, mixed, o, x1, n2, g, gp, y, w, vec, lambda i: NP, acc, ready, lambda ref: None
    )
    norm_forward(y, vec("gf"), vec("bf"), f, count, DD)
    ready("head")
    copy_pp.wait()
    factor = scale[0]

    def predict_image(image, total):
        start = pl.multiple_of(image * ROWS_D, 16)
        kept = info[1 + image]
        here = pl.ds(start, ROWS_D)
        for pair in range(PIX // 256):
            guess[:, pair * 256 : pair * 256 + 256] = dot(
                f[here, :], columns(w["head"], PIX // 128, DD, pair)
            )

        def rows(i, total):
            at = pl.multiple_of(i * 16, 16)
            target, _ = norm_rows(pp[image, pl.ds(at, 16), :].astype(F32), PIX)
            off = guess[pl.ds(at, 16), :] - target
            rank = lax.broadcasted_iota(jnp.int32, (16, PIX), 0) + at
            off = jnp.where((rank >= kept) & (rank < NP), off, 0.0)
            pp[image, pl.ds(at, 16), :] = (off * factor).astype(BF16)
            return total + jnp.sum((off * off).reshape(2, 8, PIX), axis=0)

        return lax.fori_loop(0, ROWS_D // 16, rows, total)

    total = lax.fori_loop(0, images, predict_image, jnp.zeros((8, PIX), F32))
    total = jnp.sum(jnp.sum(total, axis=0, keepdims=True), axis=1, keepdims=True)
    loss_out[...] = jnp.broadcast_to(total * (1.0 / PIX), (8, 128))

    own = info[0]
    grads = Gradients(section, plan.half, own, stage, grad_sems, keep_out, send_out)
    dpred = pp.reshape(count, PIX)
    grads.weight("head", f, DD, dpred, turned)

    def final_band(band, carry):
        acc[...] = dot_nt(dpred[...], row_band(w["head"], PIX // 128, band))

        def step(at):
            dn[pl.ds(at, 16), lanes(band)] = acc[pl.ds(at, 16), :]

        for_rows(count, 16, step, 4)
        return carry

    lax.fori_loop(0, DD // 256, final_band, 0)
    values = {}

    def from_dn(at, size):
        return dn[pl.ds(at, size), :]

    def put_y(at, size, value):
        y[pl.ds(at, size), :] = value

    values["gf"], values["bf"] = norm_backward(y, vec("gf"), from_dn, put_y, count, DD)
    block_backward(
        sh, y, x0, n1, mixed, o, x1, n2, g, gp, f, dn, g.at[:, pl.ds(0, 3 * DD)], acc, turned, w, vec, lambda i: NP,
        grads, values, lambda *a: None,
    )

    def split(image, total):
        start = pl.multiple_of(image * ROWS_D, 16)
        kept = info[1 + image]

        def rows(i, total):
            at = pl.multiple_of(i * 16, 16)
            grad = y[pl.ds(start + at, 16), :]
            rank = lax.broadcasted_iota(jnp.int32, (16, DD), 0) + at
            free = jnp.where(rank >= kept, grad, 0.0)

            @pl.when(i < ROWS_E // 16)
            def _():
                taken = jnp.where(rank < kept, grad, 0.0).astype(BF16)
                n1[pl.ds(pl.multiple_of(image * ROWS_E, 16) + at, 16), :] = taken

            return total + jnp.sum(free.reshape(2, 8, DD), axis=0)

        return lax.fori_loop(0, ROWS_D // 16, rows, total)

    total = lax.fori_loop(0, images, split, jnp.zeros((8, DD), F32))
    values["mask"] = jnp.sum(total, axis=0, keepdims=True)
    placed = n1.at[pl.ds(0, count_e)]
    grads.weight("embed", latent, D, placed, turned_e)

    def latent_band(band, carry):
        acc_e[...] = dot_nt(placed[...], row_band(w["embed"], DD // 128, band))

        def step(at):
            grad_latent[pl.ds(at, 16), lanes(band)] = acc_e[pl.ds(at, 16), :].astype(BF16)

        for_rows(count_e, 16, step, 4)
        return carry

    lax.fori_loop(0, D // 256, latent_band, 0)
    grads.vectors(values, vec_stage, plan.vec_unit)


def grad_shapes(plan, section):
    blocks = plan.sections[section].blocks_used
    inner = factors(plan.dp)[1] * factors(plan.dp)[2]
    blocks = -(-blocks // inner) * inner
    return [jax.ShapeDtypeStruct((blocks, plan.half, 16, 128), F32)] * 2


def decoder(plan, sh, info, scale, gathered, latent, pp, perm, pos):
    count_e = sh.images * ROWS_E
    holders = len({v[2] for v in plan.sections[1].vectors.values()})
    saved = saved_shapes(sh)
    most = max(plan.sections[1].panels.values())
    return pl.pallas_call(
        lambda *refs: decoder_kernel(plan, sh, refs),
        out_shape=[
            *grad_shapes(plan, 1),
            jax.ShapeDtypeStruct((count_e, D), BF16),
            jax.ShapeDtypeStruct((8, 128), F32),
        ],
        in_specs=[IN_SMEM, IN_SMEM, ANY, ANY, ANY, IN_VMEM, IN_VMEM],
        out_specs=[ANY, ANY, IN_VMEM, IN_VMEM],
        scratch_shapes=[
            *weight_scratch(DEC, W_DEC),
            pltpu.VMEM((holders, VEC_UNITS, 16, 128), BF16),
            pltpu.VMEM((8, DD), F32),
            pltpu.VMEM((sh.images, ROWS_D, PIX), BF16),
            pltpu.VMEM((count_e, D), BF16),
            pltpu.VMEM((count_e, DD), F32),
            *[pltpu.VMEM(*s) for s in saved],
            pltpu.VMEM((sh.count, DD), BF16),
            pltpu.VMEM((sh.count, DD), F32),
            pltpu.VMEM((ROWS_D, PIX), F32),
            pltpu.VMEM((sh.count, 256), F32),
            pltpu.VMEM((count_e, 256), F32),
            pltpu.VMEM((256, sh.count), BF16),
            pltpu.VMEM((256, count_e), BF16),
            pltpu.VMEM((2, 16 * most, 16, 128), F32),
            pltpu.VMEM((holders, VEC_UNITS, 16, 128), F32),
            pltpu.SemaphoreType.DMA((7,)),
            pltpu.SemaphoreType.DMA((2,)),
            pltpu.SemaphoreType.DMA((3,)),
        ],
        compiler_params=pltpu.CompilerParams(vmem_limit_bytes=VMEM_BYTES),
        name="decoder_both",
    )(info, scale, gathered, latent, pp, perm, pos)


W_BACK = ["fc2", "fc1", "proj", "qkv"]


def encoder_back_kernel(plan, sh, refs):
    section = plan.sections[0]
    (info, gathered, grad_latent, pp_in, x0_in, n1_in, mixed_in, o_in, x1_in, n2_in, g_in, gp_in,
     y_in, keep_out, send_out, w_fc2, w_fc1, w_proj, w_qkv, held, vec_ref, xe, x0, n1, mixed, o, x1,
     n2, g, gp, y, dyb, dn, dmixed, acc, turned, stage, vec_stage, w_sems, in_sems,
     grad_sems) = refs
    w = dict(zip(W_BACK, (w_fc2, w_fc1, w_proj, w_qkv)))
    finish_vec = load_vectors(section, plan.vec_unit, 0, gathered, held, vec_ref, w_sems.at[4])
    loads = {}
    pairs = [(y, y_in), (g, g_in), (gp, gp_in), (n2, n2_in), (x1, x1_in), (o, o_in),
             (mixed, mixed_in), (n1, n1_in), (x0, x0_in)]
    for k, (ref, source) in enumerate(pairs):
        loads[id(ref)] = pltpu.make_async_copy(source, ref, in_sems.at[k])
        loads[id(ref)].start()
    weights_ready = load_weights(section, 0, gathered, w, w_sems)
    patch_loads = [
        pltpu.make_async_copy(
            pp_in.at[i, pl.ds(0, ROWS_E)], xe.at[pl.ds(i * ROWS_E, ROWS_E)], in_sems.at[9]
        )
        for i in range(sh.images)
    ]
    for copy in patch_loads:
        copy.start()

    def ready(name, ref):
        loads[id(ref)].wait()
        weights_ready(name)

    vec = finish_vec()
    loads[id(y)].wait()
    values = {}

    def from_latent(at, size):
        return grad_latent[pl.ds(at, size), :].astype(F32)

    def put_y(at, size, value):
        y[pl.ds(at, size), :] = value

    values["gf"], values["bf"] = norm_backward(y, vec("gf"), from_latent, put_y, sh.count, D)
    grads = Gradients(section, plan.half, info[0], stage, grad_sems, keep_out, send_out)
    block_backward(
        sh, y, x0, n1, mixed, o, x1, n2, g, gp, dyb, dn, dmixed, acc, turned, w, vec,
        lambda i: info[1 + i], grads, values, ready,
    )

    def body(i, total):
        at = pl.multiple_of(i * 16, 16)
        grad = y[pl.ds(at, 16), :]
        dyb[pl.ds(at, 16), :] = grad.astype(BF16)
        return total + jnp.sum(grad.reshape(2, 8, D), axis=0)

    total = lax.fori_loop(0, sh.count // 16, body, jnp.zeros((8, D), F32))
    values["patch_b"] = jnp.sum(total, axis=0, keepdims=True)
    for copy in patch_loads:
        copy.wait()
    grads.weight("patch", xe, PIX, dyb, turned)
    grads.vectors(values, vec_stage, plan.vec_unit)


def encoder_back(plan, sh, info, gathered, grad_latent, pp, saved):
    shapes = saved_shapes(sh)
    holders = len({v[2] for v in plan.sections[0].vectors.values()})
    most = max(plan.sections[0].panels.values())
    return pl.pallas_call(
        lambda *refs: encoder_back_kernel(plan, sh, refs),
        out_shape=grad_shapes(plan, 0),
        in_specs=[IN_SMEM, ANY, IN_VMEM, *[ANY] * 10],
        out_specs=[ANY, ANY],
        scratch_shapes=[
            *weight_scratch(ENC, W_BACK),
            pltpu.VMEM((holders, VEC_UNITS, 16, 128), BF16),
            pltpu.VMEM((8, D), F32),
            pltpu.VMEM((sh.count, PIX), BF16),
            *[pltpu.VMEM(*s) for s in shapes],
            pltpu.VMEM((sh.count, D), BF16),
            pltpu.VMEM((sh.count, D), F32),
            pltpu.VMEM((sh.count, 3 * D), BF16),
            pltpu.VMEM((sh.count, 256), F32),
            pltpu.VMEM((256, sh.count), BF16),
            pltpu.VMEM((2, 16 * most, 16, 128), F32),
            pltpu.VMEM((holders, VEC_UNITS, 16, 128), F32),
            pltpu.SemaphoreType.DMA((5,)),
            pltpu.SemaphoreType.DMA((10,)),
            pltpu.SemaphoreType.DMA((3,)),
        ],
        compiler_params=pltpu.CompilerParams(vmem_limit_bytes=VMEM_BYTES),
        name="encoder_backward",
    )(info, gathered, grad_latent, pp, *saved)


class Grid:
    def __init__(self, dp):
        self.sizes = factors(dp)
        self.dp = dp
        me = lax.axis_index("dp")
        _, b, c = self.sizes
        self.at = (me // (b * c), me // c % b, me % c)

    def shift(self, axis, by, held=None):
        a, b, c = self.sizes
        pairs = []
        for me in range(self.dp):
            at = [me // (b * c), me // c % b, me % c]
            if held is not None and at[axis] not in held:
                continue
            at[axis] += by
            if 0 <= at[axis] < self.sizes[axis]:
                pairs.append((me, (at[0] * b + at[1]) * c + at[2]))
        return pairs


def pick(value, index, axis):
    return lax.dynamic_index_in_dim(value, index, axis, keepdims=False)


def scatter_axis(grid, terms, axis, dim, targets):
    size, at = grid.sizes[axis], grid.at[axis]

    def own(target):
        target = jnp.clip(target, 0, targets - 1)
        total = pick(terms[0], target, dim)
        for term in terms[1:]:
            total = total + pick(term, target, dim)
        return total

    if size == 1:
        return [pick(term, jnp.zeros((), jnp.int32), dim) for term in terms]
    if size == 2 and targets == 2:
        got = lax.ppermute(own(1 - at), "dp", grid.shift(axis, 1) + grid.shift(axis, -1))
        return [pick(term, at, dim) for term in terms] + [got]
    up = None
    down = None
    for step in range(1, size):
        held = [z for z in range(step) if size - step + z < targets and z < size - 1]
        mine = own(size - step + at)
        if up is not None:
            mine = mine + up
        up = lax.ppermute(mine, "dp", grid.shift(axis, 1, held)) if held else None
        held = [z for z in range(1, size) if 0 <= step - 1 - (size - 1 - z) < targets]
        mine = own(step - 1 - (size - 1 - at))
        if down is not None:
            mine = mine + down
        down = lax.ppermute(mine, "dp", grid.shift(axis, -1, held)) if held else None
    last = jnp.clip(at, 0, targets - 1)
    out = [pick(term, last, dim) for term in terms]
    return out + [v for v in (up, down) if v is not None]


def scatter_sum(grid, keep, got):
    a, b, c = grid.sizes
    half = keep.shape[1]
    targets = keep.shape[0] // (b * c)
    cut = [0, -(-half // 3), -(-2 * half // 3), half]
    orders = [(2, 1, 0), (1, 0, 2), (0, 2, 1)]
    parts = []
    for part, order in enumerate(orders):
        terms = [
            v.reshape((targets, b, c) + v.shape[1:])[:, :, :, cut[part] : cut[part + 1]]
            for v in (keep, got)
        ]
        left = [0, 1, 2]
        for axis in order:
            dim = left.index(axis)
            terms = scatter_axis(grid, terms, axis, dim, (targets, b, c)[axis])
            left.remove(axis)
        total = terms[0]
        for term in terms[1:]:
            total = total + term
        parts.append(total)
    return jnp.concatenate(parts, axis=0)


def sum_everywhere(grid, value):
    value = value + lax.ppermute(value, "section", [(0, 1), (1, 0)])
    for axis, size in enumerate(grid.sizes):
        step = 1
        stride = math.prod(grid.sizes[axis + 1 :])
        while step < size:
            pairs = [
                (i, i + (step if i // stride // step % 2 == 0 else -step) * stride)
                for i in range(grid.dp)
            ]
            value = value + lax.ppermute(value, "dp", pairs)
            step *= 2
    return value


def sincos(width):
    places = np.arange(NP).astype(np.float32)[:, None]
    column = np.arange(width)
    rates = np.exp(
        -(np.float32(2.0) * (column // 2).astype(np.float32) / np.float32(width))
        * np.float32(math.log(10000.0))
    ).astype(np.float32)
    phases = (places * rates[None, :]).astype(np.float32)
    table = np.where(
        column[None, :] % 2 == 0, np.sin(phases.astype(np.float64)), np.cos(phases.astype(np.float64))
    ).astype(np.float32)
    parts = []
    left = np.zeros((ROWS_D, width), np.float32)
    left[:NP] = table
    for _ in range(3):
        high = left.astype(jnp.bfloat16)
        parts.append(high)
        left = left - high.astype(np.float32)
    return np.stack(parts)


def on_device(patches, keep, perm, master, first, second, ema):
    dp = lax.axis_size("dp")
    section = lax.axis_index("section")
    me = lax.axis_index("dp")
    shard = master.shape[1]
    plan = Plan(dp, shard // 128)
    grid = Grid(dp)
    rows = plan.shard_rows

    flat = master.reshape(rows, 128)
    following = lax.ppermute(
        flat[: plan.head_rows], "dp", [(i, i - 1) for i in range(1, dp)]
    )
    index = jnp.asarray(plan.pack_index)[section, me]
    packed = move_rows(index, [flat, following], (plan.units, 16, 128), BF16)
    gathered = lax.all_gather(packed, ("section", "dp"), axis=0, tiled=True)
    gathered = gathered.reshape(2, dp, plan.units, 16, 128)

    count = sum_everywhere(grid, jnp.sum(NP - keep).astype(F32)) * 0.5
    images = patches.shape[0] // 2
    mine = section * images
    patches = lax.dynamic_slice_in_dim(patches, mine, images, 0)
    patches = jnp.pad(patches, ((0, 0), (0, ROWS_D - NP), (0, 0)))
    order = lax.dynamic_slice_in_dim(perm, mine, images, 0)
    order = jnp.pad(order, ((0, 0), (0, ROWS_D - NP)), constant_values=ROWS_D - 1)
    order = order.reshape(images * ROWS_D, 1)
    kept = lax.dynamic_slice_in_dim(keep, mine, images, 0)
    info = jnp.concatenate([section[None].astype(jnp.int32), kept])
    scale = ((1.0 / count) * (1.0 / PIX) * 2.0).reshape(1)

    shape_e = Shape(images, ROWS_E, D, HEADS_E, FF_E)
    shape_d = Shape(images, ROWS_D, DD, HEADS_D, FF_D)
    pp, *saved, latent = encoder(
        plan, shape_e, info, gathered, patches, order, jnp.asarray(sincos(D))
    )
    keep_d, send_d, grad_latent, loss = decoder(
        plan, shape_d, info, scale, gathered, latent, pp, order, jnp.asarray(sincos(DD))
    )
    swap = [(0, 1), (1, 0)]
    sum_d = scatter_sum(grid, keep_d, lax.ppermute(send_d, "section", swap))
    keep_e, send_e = encoder_back(plan, shape_e, info, gathered, grad_latent, pp, saved)
    sum_e = scatter_sum(grid, keep_e, lax.ppermute(send_e, "section", swap))

    half_mine = jnp.where(section == 0, sum_e, sum_d)
    half_other = lax.ppermute(jnp.where(section == 0, sum_d, sum_e), "section", swap)
    block = jnp.where(
        section == 0,
        jnp.concatenate([half_mine, half_other], axis=0),
        jnp.concatenate([half_other, half_mine], axis=0),
    )
    start = jnp.asarray(plan.tail_start)[section, me]
    tail = jnp.concatenate(
        [
            lax.dynamic_slice_in_dim(block, start, plan.tail_units, 0),
            block[plan.vec_unit :],
        ],
        axis=0,
    )
    tail = lax.ppermute(tail, "dp", [(i, i + 1) for i in range(dp - 1)])
    index = jnp.asarray(plan.unpack_index)[section, me]
    shard_total = move_rows(index, [block, tail], (rows, 128), F32, zero_at=plan.zero_row)

    squares = jnp.sum(shard_total * shard_total)
    sums = sum_everywhere(grid, jnp.stack([squares, loss[0, 0]]))
    loss_sum = sums[1]
    norm = jnp.sqrt(sums[0])
    factor = jnp.minimum(1.0, clip_limit / (norm + norm_epsilon))
    clipped = (shard_total * factor).reshape(master.shape)
    new_first = beta_one * first + (1.0 - beta_one) * clipped
    new_second = beta_two * second + (1.0 - beta_two) * clipped * clipped
    first_hat = new_first / (1.0 - beta_one**STEP)
    second_hat = new_second / (1.0 - beta_two**STEP)
    new_master = master - learn_rate * (
        first_hat / (jnp.sqrt(second_hat) + adam_epsilon) + weight_decay * master
    )
    new_ema = average_keep * ema + (1.0 - average_keep) * new_master
    return (new_master, new_first, new_second, new_ema, norm, loss_sum, count)


def solution(mesh):
    return jax.shard_map(
        on_device,
        mesh=mesh,
        in_specs=(
            P("dp", None, None),
            P("dp"),
            P("dp", None),
            P("section", "dp"),
            P("section", "dp"),
            P("section", "dp"),
            P("section", "dp"),
        ),
        out_specs=(
            P("section", "dp"),
            P("section", "dp"),
            P("section", "dp"),
            P("section", "dp"),
            P(),
            P(),
            P(),
        ),
        check_vma=False,
    )
```

time: 2940 us -> 1180 us (0.40)
  waiting for transfers between devices: 1290 us -> 399 us
  local copies, waits for them, and re-layouts: 625 us -> 55.5 us
  Pallas kernels: 0 us -> 433 us
  other arithmetic: 518 us -> 126 us
  matrix products: 358 us -> 0 us
  starting transfers between devices: 10.3 us -> 129 us
  blocking collectives: 79 us -> 0 us
    unnamed x3 -> x1, waiting for transfers between devices: 787 us -> 0.02 us
    pallas_call x0 -> x5, Pallas kernels: none -> 433 us  [the longest x1 240 us: decoder(): pl.pallas_call(lambda *refs: decoder_kernel(plan, sh, refs), out_shape=[*...]
    dot_general x75 -> x0, matrix products: 339 us -> none  [the longest x12 114 us: block(): hidden = round_grad(jnp.einsum('blw,wk->blk', normed, fc_one))]
    add_any x3 -> x0, other arithmetic: 290 us -> none  [unpack(): pieces.append(flat[offset:offset + amount].reshape(shape))]
    slice x51 -> x12, local copies, waits for them, and re-layouts: 237 us -> 44.4 us  [the longest x8 41.7 us: scatter_sum(): v.reshape((targets, b, c) + v.shape[1:])[:, :, :, cut[part]:cut[part + 1]]]
    reshape x30 -> x1, local copies, waits for them, and re-layouts: 191 us -> 1.13 us  [on_device(): order = order.reshape(images * ROWS_D, 1)]
    all_gather x1, waiting for transfers between devices: 308 us -> 168 us  [on_device(): gathered = lax.all_gather(packed, ('section', 'dp'), axis=0, tiled=True)]
    ppermute x6 -> x60, starting transfers between devices: 10.2 us -> 129 us  [the longest x15 63.9 us: scatter_axis(): up = lax.ppermute(mine, 'dp', grid.shift(axis, 1, held)) if held else None]
  transfers between devices with their start and end apart: 8 -> 61, of which waited for: 5 -> 22; matrix products, arithmetic and copies ran while one was open for 32% -> 13% of each run, Pallas kernels for 0% -> 0%
where the time goes in v1:
time: 1180 us; the launch traced here: 1170 us
  Pallas kernels  433 us (37%)
  waiting for transfers between devices  399 us (34%)
  starting transfers between devices  129 us (11%)
  other arithmetic  126 us (11%)
  local copies, waits for them, and re-layouts  55.5 us (5%)
  between operations  24.6 us (2%)
    pallas_call x1, Pallas kernels, decoder(): pl.pallas_call(lambda *refs: decoder_kernel(plan, sh, refs), out_shape=[*...  240 us
    all_gather x1, waiting for transfers between devices, on_device(): gathered = lax.all_gather(packed, ('section', 'dp'), axis=0, tiled=True)  168 us
    pallas_call x1, Pallas kernels, encoder_back(): pl.pallas_call(lambda *refs: encoder_back_kernel(plan, sh, refs), out_sha...  117 us
    ppermute x15, waiting for transfers between devices, scatter_axis(): up = lax.ppermute(mine, 'dp', grid.shift(axis, 1, held)) if held else None  99.8 us
    ppermute x15, starting transfers between devices, scatter_axis(): up = lax.ppermute(mine, 'dp', grid.shift(axis, 1, held)) if held else None  63.9 us
    pallas_call x1, Pallas kernels, encoder(): pl.pallas_call(lambda *refs: encoder_kernel(plan, sh, refs), out_shape=[j...  61.8 us
    ppermute x18, waiting for transfers between devices, scatter_axis(): lax.ppermute(mine, 'dp', grid.shift(axis, -1, held))  46.4 us
    slice x8, local copies, waits for them, and re-layouts, scatter_sum(): v.reshape((targets, b, c) + v.shape[1:])[:, :, :, cut[part]:cut[part + 1]]  41.7 us
  transfers between devices with their start and end apart: 61, of which 22 were waited for; matrix products, arithmetic and copies ran while one was open for 13% of the time, Pallas kernels for 0%

profile of v1, /device:TPU:0, one launch (start us, length us, event | category | flops | bytes accessed | tf_op | source)
XLA Modules:
  0.0 1167.7 jit_solution(922142214458232147)
XLA Ops:
  10.4 18.3 %reduce.1 = f32[479616]{0:T(1024)S(1)} reduce(f32[1,479616]{1,0:T(1,128)} %param.15, f32[]{:T(128)} %constant.3568), dimensions={0}, to_apply=%param.15.reduce_sub_computation | reduce | bytes 3836932 | tf_op args[3]
  28.7 7.6 move_rows.2
  44.5 6.9 collective-permute-start.2
  52.2 4.4 collective-permute-start.3
  66.4 167.7 %all-gather.2.cloned.1.call-done = bf16[8128,16,128]{2,1,0:T(8,128)(2,1)} async-done(((bf16[254,16,128]{2,1,0:T(8,128)(2,1)}), bf16[8128,16,128]{2,1,0:T(8,128)(2,1)}) %all-gather.2.cloned.1.call-update) | async-done | bytes 33292304 | tf_op jit(solution)/shard_map/all_gather | solution.py:1178
  234.0 61.8 %encoder_forward.1 = (bf16[6,208,768]{2,1,0:T(8,128)(2,1)}, f32[672,768]{1,0:T(8,128)}, bf16[672,768]{1,0:T(8,128)(2,1)}, bf16[672,2304]{1,0:T(8,128)(2,1)}, bf1...) custom-call(s32[7]{0:T(128)} %pad_add_fusion.refs_0_, ...), custom_call_target="tpu_custom_call" | custom-call | tf_op jit(solution)/shard_map/encoder_forward/pallas_call | solution.py:742
  295.8 240.3 %decoder_both.1 = (f32[12,127,16,128]{3,2,1,0:T(8,128)}, f32[12,127,16,128]{3,2,1,0:T(8,128)}, bf16[672,768]{1,0:T(8,128)(2,1)}, f32[8,128]{1,0:T(8,128)}) custom-call(s32[7]{0:T(128)} %pad_add_fusion.refs_0_, f32[1]{0:T(128)} %bitcast.4.refs_1_, bf16[2,16,254,16,128]{4,3,2,1,0:T(8,128)(2,1)} %bitcast.370, bf16[672,768]{1,0:T(8,128)(2,1)} %get-tuple-element.24.refs_3_, ...), custom_call_target="tpu_custom_call" | custom-call | tf_op jit(solution)/shard_map/decoder_both/pallas_call | solution.py:917
  536.1 117.0 %encoder_backward.1 = (f32[16,127,16,128]{3,2,1,0:T(8,128)}, f32[16,127,16,128]{3,2,1,0:T(8,128)}) custom-call(s32[7]{0:T(128)} %pad_add_fusion.refs_0_, bf16[2,16,254,16,128]{4,3,2,1,0:T(8,128)(2,1)} %bitcast.371, bf16[672,768]{1,0:T(8,128)(2,1)} %get-tuple-element.26.refs_2_, bf16[6,208,768]{2,1,0:T(8,128)(2,1)} %get-tuple-element.25.refs_4_.refs_3_, ...), custom_call_target="tpu_custom_call" | custom-call | tf_op jit(solution)/shard_map/encoder_backward/pallas_call | solution.py:1018
  653.8 4.0 fusion.31
  657.8 38.6 %collective-permute-done.31 = f32[12,127,16,128]{3,2,1,0:T(8,128)} collective-permute-done((f32[12,127,16,128]{3,2,1,0:T(8,128)}, f32[12,127,16,128]{3,2,1,0:T(8,128)}, u32[]{:S(2)}, u32[]{:S(2)}) %collective-permute-start.31) | collective-permute-done | bytes 12484640 | tf_op jit(solution)/shard_map/ppermute | solution.py:1202
  696.4 4.0 fusion.32
  709.1 9.3 fusion.29
  721.0 4.1 slice.79
  728.3 9.4 fusion.30
  737.7 4.5 add_bitcast_fusion.1
  743.5 3.4 bitcast_add_fusion.3
  747.6 3.1 slice.72
  750.8 5.2 slice.73
  760.1 4.5 add_bitcast_fusion.7
  764.6 2.9 collective-permute-start.23
  769.7 7.3 collective-permute-done.32
  779.2 3.0 bitcast_add_fusion.8
  782.8 27.3 %collective-permute-done.40 = f32[2,42,16,128]{3,2,1,0:T(8,128)} collective-permute-done((f32[2,42,16,128]{3,2,1,0:T(8,128)}, f32[2,42,16,128]{3,2,1,0:T(8,128)}, u32[]{:S(2)}, u32[]{:S(2)}) %collective-permute-start.40) | collective-permute-done | bytes 688160 | tf_op jit(solution)/shard_map/ppermute | solution.py:1092
  811.8 3.3 fusion.6
  816.7 3.6 bitcast_add_fusion.6
  820.3 16.0 %collective-permute-done.33 = f32[3,43,16,128]{3,2,1,0:T(8,128)} collective-permute-done((f32[3,43,16,128]{3,2,1,0:T(8,128)}, f32[3,43,16,128]{3,2,1,0:T(8,128)}, u32[]{:S(2)}, u32[]{:S(2)}) %collective-permute-start.33) | collective-permute-done | bytes 1056800 | tf_op jit(solution)/shard_map/ppermute | solution.py:1083
  845.0 3.3 bitcast_add_fusion.2
  852.5 3.3 bitcast_add_fusion
  855.9 48.1 %collective-permute-done.34 = f32[43,16,128]{2,1,0:T(8,128)S(1)} collective-permute-done((f32[43,16,128]{2,1,0:T(8,128)S(1)}, f32[43,16,128]{2,1,0:T(8,128)S(1)}, u32[]{:S(2)}, u32[]{:S(2)}) %collective-permute-start.34) | collective-permute-done | bytes 352288 | tf_op jit(solution)/shard_map/ppermute | solution.py:1092
  904.0 5.2 collective-permute-start.16
  913.1 2.9 fusion.13
  917.8 3.9 bitcast_add_fusion.7
  924.9 4.5 collective-permute-start.17
  931.0 4.7 collective-permute-start.41
  937.4 3.1 collective-permute-done.8
  948.2 23.4 %collective-permute-done.9 = f32[43,16,128]{2,1,0:T(8,128)S(1)} collective-permute-done((f32[43,16,128]{2,1,0:T(8,128)S(1)}, f32[43,16,128]{2,1,0:T(8,128)S(1)}, u32[]{:S(2)}, u32[]{:S(2)}) %collective-permute-start.9) | collective-permute-done | bytes 352288 | tf_op jit(solution)/shard_map/ppermute | solution.py:1092
  973.7 4.5 collective-permute-start.10
  991.2 43.0 %collective-permute-done.38 = f32[43,16,128]{2,1,0:T(8,128)S(1)} collective-permute-done((f32[43,16,128]{2,1,0:T(8,128)S(1)}, f32[43,16,128]{2,1,0:T(8,128)S(1)}, u32[]{:S(2)}, u32[]{:S(2)}) %collective-permute-start.38) | collective-permute-done | bytes 352288 | tf_op jit(solution)/shard_map/ppermute | solution.py:1097
  1043.2 2.8 collective-permute-start.18
  1051.5 23.7 %collective-permute-start.11 = (f32[43,16,128]{2,1,0:T(8,128)S(1)}, f32[43,16,128]{2,1,0:T(8,128)S(1)}, u32[]{:S(2)}, u32[]{:S(2)}) collective-permute-start(f32[43,16,128]{2,1,0:T(8,128)S(1)} %get-tuple-element.49), channel_id=1, source_target_pairs={{0,4},{1,5},{2,6},{3,7},{4,8},{5,9},{6,10},{7,11},{8,12},{9,13},{1... | collective-permute-start | bytes 1056776 | tf_op jit(solution)/shard_map/ppermute | solution.py:1092
  1082.4 3.4 collective-permute-done.14
  1093.6 2.7 collective-permute-start.54
  1100.8 6.2 move_rows.3
  1112.0 8.5 collective-permute-start.56
  1123.4 3.2 collective-permute-start.57
  1128.1 3.5 collective-permute-done.58
  1131.6 3.5 collective-permute-done.59
  1138.6 19.6 %multiply_add_fusion = (f32[1,479616]{1,0:T(1,128)}, f32[1,479616]{1,0:T(1,128)}, f32[1,479616]{1,0:T(1,128)}, f32[1,479616]{1,0:T(1,128)}) fusion(f32[1,479616]{1,0:T(1,128)S(1)} %copy-done.12, f32[1,479616]{1,0:T(1,128)S(1)} %copy-done.11, f32[1,1,3747,128]{3,2,1,0:T(8,128)S(1)} %multiply_bitcast_fusion, f32[1,479616]{1,0:T(1,128)} %param.16, ...), kind=kLoop, calls=%fused_computation.11 | loop fusion | flops 8633088 | bytes 17266176 | tf_op jit(solution)/shard_map/add | solution.py:1238
  (229 shorter events, 138.5 us)
Async XLA Ops:
  7.2 226.8 %all-gather.2.cloned.1.call-start = ((), (), s32[]{:S(2)}) async-start(), calls=%async_computation | async-start | bytes 34332672 | tf_op jit(solution)/shard_map/all_gather | solution.py:1178
  8.2 20.5 %collective-permute-start = (f32[384,128]{1,0:T(8,128)S(1)}, f32[384,128]{1,0:T(8,128)S(1)}, u32[]{:S(2)}, u32[]{:S(2)}) collective-permute-start(f32[384,128]{1,0:T(8,128)S(1)} %bitcast.386), channel_id=1, source_target_pairs={{1,0},{2,1},{3,2},{4,3},{5,4},{6,5},{7,6},{8,7},{9,8},{10,9},{11,1... | collective-permute-start | bytes 589832 | tf_op jit(solution)/shard_map/ppermute | solution.py:1173
  653.2 75.2 %collective-permute-start.6 = (f32[16,127,16,128]{3,2,1,0:T(8,128)}, f32[16,127,16,128]{3,2,1,0:T(8,128)}, u32[]{:S(2)}, u32[]{:S(2)}) collective-permute-start(f32[16,127,16,128]{3,2,1,0:T(8,128)} %get-tuple-element.37), channel_id=1, source_target_pairs={{0,16},{16,0},{1,17},{17,1},{2,18},{18,2},{3,19},{19,3},{4,20},{20... | collective-permute-start | bytes 49938440 | tf_op jit(solution)/shard_map/ppermute | solution.py:1204
  653.5 43.0 %collective-permute-start.31 = (f32[12,127,16,128]{3,2,1,0:T(8,128)}, f32[12,127,16,128]{3,2,1,0:T(8,128)}, u32[]{:S(2)}, u32[]{:S(2)}) collective-permute-start(f32[12,127,16,128]{3,2,1,0:T(8,128)} %get-tuple-element.39), channel_id=1, source_target_pairs={{0,16},{16,0},{1,17},{17,1},{2,18},{18,2},{3,19},{19,3},{4,20},{20... | collective-permute-start | bytes 37453832 | tf_op jit(solution)/shard_map/ppermute | solution.py:1202
  702.6 40.9 %collective-permute-start.46 = (f32[2,2,42,16,128]{4,3,2,1,0:T(8,128)}, f32[2,2,42,16,128]{4,3,2,1,0:T(8,128)S(1)}, u32[]{:S(2)}, u32[]{:S(2)}) collective-permute-start(f32[2,2,42,16,128]{4,3,2,1,0:T(8,128)} %get-tuple-element.67), channel_id=1, source_target_pairs={{0,4},{1,5},{2,6},{3,7},{16,20},{17,21},{18,22},{19,23}} | collective-permute-start | bytes 4128776 | tf_op jit(solution)/shard_map/ppermute | solution.py:1092
  704.2 39.3 %collective-permute-start.48 = (f32[2,2,42,16,128]{4,3,2,1,0:T(8,128)}, f32[2,2,42,16,128]{4,3,2,1,0:T(8,128)}, u32[]{:S(2)}, u32[]{:S(2)}) collective-permute-start(f32[2,2,42,16,128]{4,3,2,1,0:T(8,128)} %get-tuple-element.68), channel_id=1, source_target_pairs={{12,8},{13,9},{14,10},{15,11},{28,24},{29,25},{30,26},{31,27}} | collective-permute-start | bytes 4128776 | tf_op jit(solution)/shard_map/ppermute | solution.py:1097
  707.6 57.0 %collective-permute-start.39 = (f32[3,2,42,16,128]{4,3,2,1,0:T(8,128)}, f32[3,2,42,16,128]{4,3,2,1,0:T(8,128)S(1)}, u32[]{:S(2)}, u32[]{:S(2)}) collective-permute-start(f32[3,2,42,16,128]{4,3,2,1,0:T(8,128)} %add_bitcast_fusion.3), channel_id=1, source_target_pairs={{0,2},{1,3},{4,6},{5,7},{8,10},{9,11},{12,14},{13,15},{2,0},{3,1},... | collective-permute-start | bytes 6193160 | tf_op jit(solution)/shard_map/ppermute | solution.py:1083
  727.8 49.2 %collective-permute-start.32 = (f32[3,2,43,16,128]{4,3,2,1,0:T(8,128)}, f32[3,2,43,16,128]{4,3,2,1,0:T(8,128)}, u32[]{:S(2)}, u32[]{:S(2)}) collective-permute-start(f32[3,2,43,16,128]{4,3,2,1,0:T(8,128)} %add_bitcast_fusion.2), channel_id=1, source_target_pairs={{0,1},{2,3},{4,5},{6,7},{8,9},{10,11},{12,13},{14,15},{1,0},{3,2},... | collective-permute-start | bytes 6340616 | tf_op jit(solution)/shard_map/ppermute | solution.py:1083
  742.2 100.9 %collective-permute-start.15 = (f32[4,2,42,16,128]{4,3,2,1,0:T(8,128)}, f32[4,2,42,16,128]{4,3,2,1,0:T(8,128)}, u32[]{:S(2)}, u32[]{:S(2)}) collective-permute-start(f32[4,2,42,16,128]{4,3,2,1,0:T(8,128)} %add_bitcast_fusion.1), channel_id=1, source_target_pairs={{0,2},{1,3},{4,6},{5,7},{8,10},{9,11},{12,14},{13,15},{2,0},{3,1},... | collective-permute-start | bytes 8257544 | tf_op jit(solution)/shard_map/ppermute | solution.py:1083
  746.9 35.3 %collective-permute-start.49 = (f32[2,2,42,16,128]{4,3,2,1,0:T(8,128)}, f32[2,2,42,16,128]{4,3,2,1,0:T(8,128)S(1)}, u32[]{:S(2)}, u32[]{:S(2)}) collective-permute-start(f32[2,2,42,16,128]{4,3,2,1,0:T(8,128)} %get-tuple-element.66), channel_id=1, source_target_pairs={{8,4},{9,5},{10,6},{11,7},{12,8},{13,9},{14,10},{15,11},{24,20},{2... | collective-permute-start | bytes 4128776 | tf_op jit(solution)/shard_map/ppermute | solution.py:1097
  759.3 91.6 %collective-permute-start.7 = (f32[4,2,43,16,128]{4,3,2,1,0:T(8,128)}, f32[4,2,43,16,128]{4,3,2,1,0:T(8,128)}, u32[]{:S(2)}, u32[]{:S(2)}) collective-permute-start(f32[4,2,43,16,128]{4,3,2,1,0:T(8,128)} %add_bitcast_fusion), channel_id=1, source_target_pairs={{0,1},{2,3},{4,5},{6,7},{8,9},{10,11},{12,13},{14,15},{1,0},{3,2},... | collective-permute-start | bytes 8454152 | tf_op jit(solution)/shard_map/ppermute | solution.py:1083
  764.6 50.5 %collective-permute-start.23 = (f32[2,2,42,16,128]{4,3,2,1,0:T(8,128)}, f32[2,2,42,16,128]{4,3,2,1,0:T(8,128)}, u32[]{:S(2)}, u32[]{:S(2)}) collective-permute-start(f32[2,2,42,16,128]{4,3,2,1,0:T(8,128)} %get-tuple-element.61), channel_id=1, source_target_pairs={{0,4},{1,5},{2,6},{3,7},{16,20},{17,21},{18,22},{19,23}} | collective-permute-start | bytes 4128776 | tf_op jit(solution)/shard_map/ppermute | solution.py:1092
  777.0 33.1 %collective-permute-start.40 = (f32[2,42,16,128]{3,2,1,0:T(8,128)}, f32[2,42,16,128]{3,2,1,0:T(8,128)}, u32[]{:S(2)}, u32[]{:S(2)}) collective-permute-start(f32[2,42,16,128]{3,2,1,0:T(8,128)} %bitcast_add_fusion.14), channel_id=1, source_target_pairs={{0,4},{1,5},{2,6},{3,7},{16,20},{17,21},{18,22},{19,23}} | collective-permute-start | bytes 2064392 | tf_op jit(solution)/shard_map/ppermute | solution.py:1092
  782.2 54.1 %collective-permute-start.33 = (f32[3,43,16,128]{3,2,1,0:T(8,128)}, f32[3,43,16,128]{3,2,1,0:T(8,128)}, u32[]{:S(2)}, u32[]{:S(2)}) collective-permute-start(f32[3,43,16,128]{3,2,1,0:T(8,128)} %bitcast_add_fusion.8), channel_id=1, source_target_pairs={{0,2},{1,3},{4,6},{5,7},{8,10},{9,11},{12,14},{13,15},{2,0},{3,1},... | collective-permute-start | bytes 3170312 | tf_op jit(solution)/shard_map/ppermute | solution.py:1083
  810.1 99.2 %collective-permute-start.26 = (f32[2,2,42,16,128]{4,3,2,1,0:T(8,128)}, f32[2,2,42,16,128]{4,3,2,1,0:T(8,128)}, u32[]{:S(2)}, u32[]{:S(2)}) collective-permute-start(f32[2,2,42,16,128]{4,3,2,1,0:T(8,128)} %get-tuple-element.62), channel_id=1, source_target_pairs={{12,8},{13,9},{14,10},{15,11},{28,24},{29,25},{30,26},{31,27}} | collective-permute-start | bytes 4128776 | tf_op jit(solution)/shard_map/ppermute | solution.py:1097
  815.1 25.3 %collective-permute-start.42 = (f32[2,42,16,128]{3,2,1,0:T(8,128)}, f32[2,42,16,128]{3,2,1,0:T(8,128)}, u32[]{:S(2)}, u32[]{:S(2)}) collective-permute-start(f32[2,42,16,128]{3,2,1,0:T(8,128)} %get-tuple-element.64), channel_id=1, source_target_pairs={{12,8},{13,9},{14,10},{15,11},{28,24},{29,25},{30,26},{31,27}} | collective-permute-start | bytes 2064392 | tf_op jit(solution)/shard_map/ppermute | solution.py:1097
  836.3 79.6 %collective-permute-start.24 = (f32[2,2,42,16,128]{4,3,2,1,0:T(8,128)}, f32[2,2,42,16,128]{4,3,2,1,0:T(8,128)}, u32[]{:S(2)}, u32[]{:S(2)}) collective-permute-start(f32[2,2,42,16,128]{4,3,2,1,0:T(8,128)} %bitcast_add_fusion.6), channel_id=1, source_target_pairs={{0,4},{1,5},{2,6},{3,7},{4,8},{5,9},{6,10},{7,11},{16,20},{17,21},... | collective-permute-start | bytes 4128776 | tf_op jit(solution)/shard_map/ppermute | solution.py:1092
  840.4 81.3 %collective-permute-start.47 = (f32[2,2,42,16,128]{4,3,2,1,0:T(8,128)}, f32[2,2,42,16,128]{4,3,2,1,0:T(8,128)S(1)}, u32[]{:S(2)}, u32[]{:S(2)}) collective-permute-start(f32[2,2,42,16,128]{4,3,2,1,0:T(8,128)} %get-tuple-element.65), channel_id=1, source_target_pairs={{0,4},{1,5},{2,6},{3,7},{4,8},{5,9},{6,10},{7,11},{16,20},{17,21},... | collective-permute-start | bytes 4128776 | tf_op jit(solution)/shard_map/ppermute | solution.py:1092
  843.1 60.9 %collective-permute-start.34 = (f32[43,16,128]{2,1,0:T(8,128)S(1)}, f32[43,16,128]{2,1,0:T(8,128)S(1)}, u32[]{:S(2)}, u32[]{:S(2)}) collective-permute-start(f32[43,16,128]{2,1,0:T(8,128)S(1)} %bitcast_add_fusion.30), channel_id=1, source_target_pairs={{0,4},{1,5},{2,6},{3,7},{16,20},{17,21},{18,22},{19,23}} | collective-permute-start | bytes 1056776 | tf_op jit(solution)/shard_map/ppermute | solution.py:1092
  850.9 80.0 %collective-permute-start.50 = (f32[2,2,42,16,128]{4,3,2,1,0:T(8,128)}, f32[2,2,42,16,128]{4,3,2,1,0:T(8,128)}, u32[]{:S(2)}, u32[]{:S(2)}) collective-permute-start(f32[2,2,42,16,128]{4,3,2,1,0:T(8,128)} %bitcast_add_fusion.2), channel_id=1, source_target_pairs={{4,0},{5,1},{6,2},{7,3},{8,4},{9,5},{10,6},{11,7},{12,8},{13,9},{1... | collective-permute-start | bytes 4128776 | tf_op jit(solution)/shard_map/ppermute | solution.py:1097
  904.0 18.4 %collective-permute-start.16 = (f32[2,42,16,128]{3,2,1,0:T(8,128)}, f32[2,42,16,128]{3,2,1,0:T(8,128)}, u32[]{:S(2)}, u32[]{:S(2)}) collective-permute-start(f32[2,42,16,128]{3,2,1,0:T(8,128)} %bitcast_add_fusion.21), channel_id=1, source_target_pairs={{0,4},{1,5},{2,6},{3,7},{16,20},{17,21},{18,22},{19,23}} | collective-permute-start | bytes 2064392 | tf_op jit(solution)/shard_map/ppermute | solution.py:1092
  909.2 31.3 %collective-permute-start.8 = (f32[4,43,16,128]{3,2,1,0:T(8,128)}, f32[4,43,16,128]{3,2,1,0:T(8,128)}, u32[]{:S(2)}, u32[]{:S(2)}) collective-permute-start(f32[4,43,16,128]{3,2,1,0:T(8,128)} %bitcast_add_fusion), channel_id=1, source_target_pairs={{0,2},{1,3},{4,6},{5,7},{8,10},{9,11},{12,14},{13,15},{2,0},{3,1},... | collective-permute-start | bytes 4227080 | tf_op jit(solution)/shard_map/ppermute | solution.py:1083
  916.0 8.9 collective-permute-start.36
  921.7 21.5 %collective-permute-start.43 = (f32[2,42,16,128]{3,2,1,0:T(8,128)}, f32[2,42,16,128]{3,2,1,0:T(8,128)S(1)}, u32[]{:S(2)}, u32[]{:S(2)}) collective-permute-start(f32[2,42,16,128]{3,2,1,0:T(8,128)} %fusion.4), channel_id=1, source_target_pairs={{8,4},{9,5},{10,6},{11,7},{12,8},{13,9},{14,10},{15,11},{24,20},{2... | collective-permute-start | bytes 2064392 | tf_op jit(solution)/shard_map/ppermute | solution.py:1097
  922.4 51.2 %collective-permute-start.27 = (f32[2,2,42,16,128]{4,3,2,1,0:T(8,128)}, f32[2,2,42,16,128]{4,3,2,1,0:T(8,128)S(1)}, u32[]{:S(2)}, u32[]{:S(2)}) collective-permute-start(f32[2,2,42,16,128]{4,3,2,1,0:T(8,128)} %get-tuple-element.60), channel_id=1, source_target_pairs={{8,4},{9,5},{10,6},{11,7},{12,8},{13,9},{14,10},{15,11},{24,20},{2... | collective-permute-start | bytes 4128776 | tf_op jit(solution)/shard_map/ppermute | solution.py:1097
  924.9 21.0 %collective-permute-start.17 = (f32[2,42,16,128]{3,2,1,0:T(8,128)S(1)}, f32[2,42,16,128]{3,2,1,0:T(8,128)S(1)}, u32[]{:S(2)}, u32[]{:S(2)}) collective-permute-start(f32[2,42,16,128]{3,2,1,0:T(8,128)S(1)} %fusion.9), channel_id=1, source_target_pairs={{0,4},{1,5},{2,6},{3,7},{4,8},{5,9},{6,10},{7,11},{16,20},{17,21},... | collective-permute-start | bytes 2064392 | tf_op jit(solution)/shard_map/ppermute | solution.py:1092
  931.0 47.5 %collective-permute-start.41 = (f32[2,42,16,128]{3,2,1,0:T(8,128)S(1)}, f32[2,42,16,128]{3,2,1,0:T(8,128)S(1)}, u32[]{:S(2)}, u32[]{:S(2)}) collective-permute-start(f32[2,42,16,128]{3,2,1,0:T(8,128)S(1)} %copy-done.18), channel_id=1, source_target_pairs={{0,4},{1,5},{2,6},{3,7},{4,8},{5,9},{6,10},{7,11},{16,20},{17,21},... | collective-permute-start | bytes 2064392 | tf_op jit(solution)/shard_map/ppermute | solution.py:1092
  940.5 39.3 %collective-permute-start.35 = (f32[43,16,128]{2,1,0:T(8,128)S(1)}, f32[43,16,128]{2,1,0:T(8,128)S(1)}, u32[]{:S(2)}, u32[]{:S(2)}) collective-permute-start(f32[43,16,128]{2,1,0:T(8,128)S(1)} %copy-done.19), channel_id=1, source_target_pairs={{0,4},{1,5},{2,6},{3,7},{4,8},{5,9},{6,10},{7,11},{16,20},{17,21},... | collective-permute-start | bytes 1056776 | tf_op jit(solution)/shard_map/ppermute | solution.py:1092
  943.2 28.5 %collective-permute-start.9 = (f32[43,16,128]{2,1,0:T(8,128)S(1)}, f32[43,16,128]{2,1,0:T(8,128)S(1)}, u32[]{:S(2)}, u32[]{:S(2)}) collective-permute-start(f32[43,16,128]{2,1,0:T(8,128)S(1)} %bitcast_add_fusion.42), channel_id=1, source_target_pairs={{0,4},{1,5},{2,6},{3,7},{16,20},{17,21},{18,22},{19,23}} | collective-permute-start | bytes 1056776 | tf_op jit(solution)/shard_map/ppermute | solution.py:1092
  945.9 36.0 %collective-permute-start.37 = (f32[43,16,128]{2,1,0:T(8,128)S(1)}, f32[43,16,128]{2,1,0:T(8,128)S(1)}, u32[]{:S(2)}, u32[]{:S(2)}) collective-permute-start(f32[43,16,128]{2,1,0:T(8,128)S(1)} %fusion.11), channel_id=1, source_target_pairs={{8,4},{9,5},{10,6},{11,7},{12,8},{13,9},{14,10},{15,11},{24,20},{2... | collective-permute-start | bytes 1056776 | tf_op jit(solution)/shard_map/ppermute | solution.py:1097
  971.6 13.0 %collective-permute-start.19 = (f32[2,42,16,128]{3,2,1,0:T(8,128)S(1)}, f32[2,42,16,128]{3,2,1,0:T(8,128)S(1)}, u32[]{:S(2)}, u32[]{:S(2)}) collective-permute-start(f32[2,42,16,128]{3,2,1,0:T(8,128)S(1)} %get-tuple-element.52), channel_id=1, source_target_pairs={{12,8},{13,9},{14,10},{15,11},{28,24},{29,25},{30,26},{31,27}} | collective-permute-start | bytes 2064392 | tf_op jit(solution)/shard_map/ppermute | solution.py:1097
  973.7 13.2 %collective-permute-start.10 = (f32[43,16,128]{2,1,0:T(8,128)S(1)}, f32[43,16,128]{2,1,0:T(8,128)S(1)}, u32[]{:S(2)}, u32[]{:S(2)}) collective-permute-start(f32[43,16,128]{2,1,0:T(8,128)S(1)} %fusion.18), channel_id=1, source_target_pairs={{0,4},{1,5},{2,6},{3,7},{4,8},{5,9},{6,10},{7,11},{16,20},{17,21},... | collective-permute-start | bytes 1056776 | tf_op jit(solution)/shard_map/ppermute | solution.py:1092
  978.5 56.4 %collective-permute-start.51 = (f32[2,42,16,128]{3,2,1,0:T(8,128)S(1)}, f32[2,42,16,128]{3,2,1,0:T(8,128)S(1)}, u32[]{:S(2)}, u32[]{:S(2)}) collective-permute-start(f32[2,42,16,128]{3,2,1,0:T(8,128)S(1)} %bitcast_add_fusion.9), channel_id=1, source_target_pairs={{0,1},{2,3},{4,5},{6,7},{8,9},{10,11},{12,13},{14,15},{1,0},{3,2},... | collective-permute-start | bytes 2064392 | tf_op jit(solution)/shard_map/ppermute | solution.py:1083
  979.9 63.3 %collective-permute-start.25 = (f32[2,2,42,16,128]{4,3,2,1,0:T(8,128)S(1)}, f32[2,2,42,16,128]{4,3,2,1,0:T(8,128)S(1)}, u32[]{:S(2)}, u32[]{:S(2)}) collective-permute-start(f32[2,2,42,16,128]{4,3,2,1,0:T(8,128)S(1)} %copy-done.17), channel_id=1, source_target_pairs={{0,4},{1,5},{2,6},{3,7},{4,8},{5,9},{6,10},{7,11},{8,12},{9,13},{1... | collective-permute-start | bytes 4128776 | tf_op jit(solution)/shard_map/ppermute | solution.py:1092
  981.9 64.1 %collective-permute-start.28 = (f32[2,2,42,16,128]{4,3,2,1,0:T(8,128)S(1)}, f32[2,2,42,16,128]{4,3,2,1,0:T(8,128)S(1)}, u32[]{:S(2)}, u32[]{:S(2)}) collective-permute-start(f32[2,2,42,16,128]{4,3,2,1,0:T(8,128)S(1)} %bitcast_add_fusion.5), channel_id=1, source_target_pairs={{4,0},{5,1},{6,2},{7,3},{8,4},{9,5},{10,6},{11,7},{12,8},{13,9},{1... | collective-permute-start | bytes 4128776 | tf_op jit(solution)/shard_map/ppermute | solution.py:1097
  984.6 53.8 %collective-permute-start.44 = (f32[2,42,16,128]{3,2,1,0:T(8,128)S(1)}, f32[2,42,16,128]{3,2,1,0:T(8,128)S(1)}, u32[]{:S(2)}, u32[]{:S(2)}) collective-permute-start(f32[2,42,16,128]{3,2,1,0:T(8,128)S(1)} %fusion.5), channel_id=1, source_target_pairs={{4,0},{5,1},{6,2},{7,3},{8,4},{9,5},{10,6},{11,7},{12,8},{13,9},{1... | collective-permute-start | bytes 2064392 | tf_op jit(solution)/shard_map/ppermute | solution.py:1097
  986.9 47.3 %collective-permute-start.38 = (f32[43,16,128]{2,1,0:T(8,128)S(1)}, f32[43,16,128]{2,1,0:T(8,128)S(1)}, u32[]{:S(2)}, u32[]{:S(2)}) collective-permute-start(f32[43,16,128]{2,1,0:T(8,128)S(1)} %fusion.12), channel_id=1, source_target_pairs={{4,0},{5,1},{6,2},{7,3},{8,4},{9,5},{10,6},{11,7},{12,8},{13,9},{1... | collective-permute-start | bytes 1056776 | tf_op jit(solution)/shard_map/ppermute | solution.py:1097
  1034.2 12.7 %collective-permute-start.20 = (f32[2,42,16,128]{3,2,1,0:T(8,128)S(1)}, f32[2,42,16,128]{3,2,1,0:T(8,128)S(1)}, u32[]{:S(2)}, u32[]{:S(2)}) collective-permute-start(f32[2,42,16,128]{3,2,1,0:T(8,128)S(1)} %fusion.7), channel_id=1, source_target_pairs={{8,4},{9,5},{10,6},{11,7},{12,8},{13,9},{14,10},{15,11},{24,20},{2... | collective-permute-start | bytes 2064392 | tf_op jit(solution)/shard_map/ppermute | solution.py:1097
  1038.4 10.4 collective-permute-start.52
  1040.3 36.1 %collective-permute-start.45 = (f32[42,16,128]{2,1,0:T(8,128)S(1)}, f32[42,16,128]{2,1,0:T(8,128)S(1)}, u32[]{:S(2)}, u32[]{:S(2)}) collective-permute-start(f32[42,16,128]{2,1,0:T(8,128)S(1)} %bitcast_add_fusion.56), channel_id=1, source_target_pairs={{0,1},{2,3},{4,5},{6,7},{8,9},{10,11},{12,13},{14,15},{1,0},{3,2},... | collective-permute-start | bytes 1032200 | tf_op jit(solution)/shard_map/ppermute | solution.py:1083
  1043.2 37.4 %collective-permute-start.18 = (f32[2,42,16,128]{3,2,1,0:T(8,128)S(1)}, f32[2,42,16,128]{3,2,1,0:T(8,128)S(1)}, u32[]{:S(2)}, u32[]{:S(2)}) collective-permute-start(f32[2,42,16,128]{3,2,1,0:T(8,128)S(1)} %get-tuple-element.51), channel_id=1, source_target_pairs={{0,4},{1,5},{2,6},{3,7},{4,8},{5,9},{6,10},{7,11},{8,12},{9,13},{1... | collective-permute-start | bytes 2064392 | tf_op jit(solution)/shard_map/ppermute | solution.py:1092
  1046.9 32.0 %collective-permute-start.29 = (f32[2,42,16,128]{3,2,1,0:T(8,128)S(1)}, f32[2,42,16,128]{3,2,1,0:T(8,128)S(1)}, u32[]{:S(2)}, u32[]{:S(2)}) collective-permute-start(f32[2,42,16,128]{3,2,1,0:T(8,128)S(1)} %bitcast_add_fusion.16), channel_id=1, source_target_pairs={{0,1},{2,3},{4,5},{6,7},{8,9},{10,11},{12,13},{14,15},{1,0},{3,2},... | collective-permute-start | bytes 2064392 | tf_op jit(solution)/shard_map/ppermute | solution.py:1083
  1048.8 31.8 %collective-permute-start.21 = (f32[2,42,16,128]{3,2,1,0:T(8,128)S(1)}, f32[2,42,16,128]{3,2,1,0:T(8,128)S(1)}, u32[]{:S(2)}, u32[]{:S(2)}) collective-permute-start(f32[2,42,16,128]{3,2,1,0:T(8,128)S(1)} %fusion.8), channel_id=1, source_target_pairs={{4,0},{5,1},{6,2},{7,3},{8,4},{9,5},{10,6},{11,7},{12,8},{13,9},{1... | collective-permute-start | bytes 2064392 | tf_op jit(solution)/shard_map/ppermute | solution.py:1097
  1051.5 30.9 %collective-permute-start.11 = (f32[43,16,128]{2,1,0:T(8,128)S(1)}, f32[43,16,128]{2,1,0:T(8,128)S(1)}, u32[]{:S(2)}, u32[]{:S(2)}) collective-permute-start(f32[43,16,128]{2,1,0:T(8,128)S(1)} %get-tuple-element.49), channel_id=1, source_target_pairs={{0,4},{1,5},{2,6},{3,7},{4,8},{5,9},{6,10},{7,11},{8,12},{9,13},{1... | collective-permute-start | bytes 1056776 | tf_op jit(solution)/shard_map/ppermute | solution.py:1092
  1076.5 9.2 collective-permute-start.14
  1079.1 8.0 collective-permute-start.30
  1081.7 7.3 collective-permute-start.22
  1112.0 10.0 collective-permute-start.56
  (45 other events, 925.9 us)
Sparse Core Ops, SparseCore 0:
  36.5 197.4 all-gather.1

commit v2 on v1

--- a/solution.py
+++ b/solution.py
@@ -1,3 +1,4 @@
+import functools
 import math
 
 import jax
@@ -35,6 +36,9 @@
 GROUP = 16
 VEC_UNITS = 2
 VMEM_BYTES = 60 * 1024 * 1024
+ANY = pl.BlockSpec(memory_space=pl.ANY)
+IN_VMEM = pl.BlockSpec(memory_space=pltpu.VMEM)
+IN_SMEM = pl.BlockSpec(memory_space=pltpu.SMEM)
 
 ENC = [
     ("patch", (PIX, D)),
@@ -107,6 +111,18 @@
                 out.append([block, unit, group, 1])
         return [tuple(p) for p in out]
 
+    def runs(self, name, cuts, first=0, count=None):
+        panels = self.panels[name]
+        out = []
+        for block, unit, group, groups in self.pieces(name, first, count):
+            at, left = (group - first) * panels, groups * panels
+            while left:
+                place = max(i for i in range(len(cuts) - 1) if cuts[i] <= unit)
+                take = min(left, cuts[place + 1] - unit)
+                out.append((block, place, unit - cuts[place], at, take))
+                unit, at, left = unit + take, at + take, left - take
+        return out
+
 
 class Plan:
     def __init__(self, dp, shard_rows):
@@ -118,8 +134,13 @@
         self.vec_unit = units
         self.units = units + VEC_UNITS
         self.half = self.units // 2
+        half = self.half
+        self.part_cuts = [0, -(-half // 3), -(-2 * half // 3), half]
+        self.cuts = self.part_cuts[:-1] + [half + c for c in self.part_cuts]
+        self.half_cuts = [0, half, self.units]
         self.head_rows = 8 * -(-max(16 * max(s.panels.values()) for s in self.sections) // 8)
         self.tail_units = max(max(s.panels.values()) for s in self.sections)
+        self.pack_base = 8 * -(-shard_rows // 8)
         self.pack_rows = shard_rows + self.head_rows
         self.pack_index = np.zeros((2, dp, self.units * 16), np.int32)
         self.tail_rows = 16 * (self.tail_units + VEC_UNITS)
@@ -137,10 +158,28 @@
                 for panel in range(panels):
                     self.place(s, block, self.vec_unit * 16 + at + panel, row + panel)
 
+    def bins(self, s):
+        if s == 0:
+            return [(0, self.dp // 2), (self.dp // 2, self.dp - self.dp // 2)]
+        used = self.sections[1].blocks_used
+        main = 1 << (used.bit_length() - 1)
+        return [(0, main), (main, max(used - main, 1))]
+
+    def tail_parts(self):
+        first, count = self.bins(1)[1]
+        section = self.sections[1]
+        most = max(section.fill[first : first + count], default=0)
+        if any(v[2] >= first for v in section.vectors.values()):
+            most = self.units
+        held = [u % self.half for u in range(most)]
+        cuts = self.part_cuts
+        return [p for p in range(3) if any(cuts[p] <= u < cuts[p + 1] for u in held)]
+
     def place(self, s, block, block_row, flat_row):
         local = flat_row - block * self.shard_rows
         assert 0 <= local < self.pack_rows
-        self.pack_index[s, block, block_row] = local
+        gap = self.pack_base - self.shard_rows if local >= self.shard_rows else 0
+        self.pack_index[s, block, block_row] = local + gap
         owner, at = divmod(flat_row, self.shard_rows)
         if owner == block:
             self.unpack_index[s, owner, at] = block_row
@@ -154,23 +193,7 @@
             self.unpack_index[s, owner, at] = self.units * 16 + source
 
 
-def factors(dp):
-    if dp == 16:
-        return (4, 2, 2)
-    if dp == 64:
-        return (4, 4, 4)
-    return (dp, 1, 1)
-
-
-def move_rows_kernel(index_ref, *refs, count, sizes, zero_at):
-    sources, out_ref, held, done = refs[: len(sizes)], refs[-3], refs[-2], refs[-1]
-    at = 0
-    for source, size in zip(sources, sizes):
-        held[pl.ds(at, size), :] = source[...].reshape(size, 128)
-        at += size
-    if zero_at is not None:
-        held[pl.ds(zero_at, 8), :] = jnp.zeros((8, 128), F32)
-
+def move_rows_in(index_ref, held, done, count):
     def eight(i, carry):
         for j in range(8):
             row = i * 8 + j
@@ -180,25 +203,146 @@
     lax.fori_loop(0, count // 8, eight, 0)
     for row in range(count // 8 * 8, count):
         done[pl.ds(row, 1), :] = held[pl.ds(index_ref[row], 1), :]
-    out_ref[...] = done[...].reshape(out_ref.shape).astype(out_ref.dtype)
-
-
-def move_rows(index, sources, out_shape, dtype, zero_at=None):
-    sizes = [math.prod(s.shape) // 128 for s in sources]
-    count = math.prod(out_shape) // 128
-    total = sum(sizes) + 8
-    import functools
-
+
+
+def pack_kernel(base, index_ref, flat, following, out_ref, held, done, sems):
+    rows, more = flat.shape[0], following.shape[0]
+    copies = [
+        pltpu.make_async_copy(flat.at[:, 0], held.at[pl.ds(0, rows)], sems.at[0]),
+        pltpu.make_async_copy(following.at[:, 0], held.at[pl.ds(base, more)], sems.at[1]),
+    ]
+    for copy in copies:
+        copy.start()
+    for copy in copies:
+        copy.wait()
+    count = done.shape[0]
+    move_rows_in(index_ref, held, done, count)
+    out_ref[...] = done[...].reshape(out_ref.shape).astype(BF16)
+
+
+def pack(plan, index, flat, following):
+    count = plan.units * 16
     return pl.pallas_call(
-        functools.partial(move_rows_kernel, count=count, sizes=sizes, zero_at=zero_at),
-        out_shape=jax.ShapeDtypeStruct(out_shape, dtype),
-        in_specs=[pl.BlockSpec(memory_space=pltpu.SMEM)]
-        + [pl.BlockSpec(memory_space=pltpu.VMEM)] * len(sources),
-        out_specs=pl.BlockSpec(memory_space=pltpu.VMEM),
-        scratch_shapes=[pltpu.VMEM((total, 128), F32), pltpu.VMEM((count, 128), F32)],
+        functools.partial(pack_kernel, plan.pack_base),
+        out_shape=jax.ShapeDtypeStruct((plan.units, 16, 128), BF16),
+        in_specs=[IN_SMEM, ANY, ANY],
+        out_specs=IN_VMEM,
+        scratch_shapes=[
+            pltpu.VMEM((plan.pack_base + plan.head_rows, 128), F32),
+            pltpu.VMEM((count, 128), F32),
+            pltpu.SemaphoreType.DMA((2,)),
+        ],
         compiler_params=pltpu.CompilerParams(vmem_limit_bytes=32 * 1024 * 1024),
-        name="move_rows",
-    )(index, *sources)
+        name="pack_rows",
+    )(index, flat, following)
+
+
+def unpack_kernel(zero_row, rows, index_ref, block, tail, out_ref, squares, held):
+    at = 0
+    for source in (block, tail):
+        size = source.shape[0] * 16
+        held[pl.ds(at, size), :] = source[...].reshape(size, 128)
+        at += size
+    held[pl.ds(zero_row, 8), :] = jnp.zeros((8, 128), F32)
+    out_ref[pl.ds(out_ref.shape[0] - 16, 16), :] = jnp.zeros((16, 128), F32)
+    move_rows_in(index_ref, held, out_ref, rows)
+
+    def body(i, total):
+        value = out_ref[pl.ds(pl.multiple_of(i * 8, 8), 8), :]
+        return total + value * value
+
+    squares[...] = lax.fori_loop(
+        0, out_ref.shape[0] // 8, body, jnp.zeros((8, 128), F32), unroll=8
+    )
+
+
+def unpack(plan, index, block, tail):
+    rows = plan.shard_rows
+    padded = 16 * -(-rows // 16)
+    return pl.pallas_call(
+        functools.partial(unpack_kernel, plan.zero_row, rows),
+        out_shape=[
+            jax.ShapeDtypeStruct((padded, 128), F32),
+            jax.ShapeDtypeStruct((8, 128), F32),
+        ],
+        in_specs=[IN_SMEM, IN_VMEM, IN_VMEM],
+        out_specs=[IN_VMEM, IN_VMEM],
+        scratch_shapes=[pltpu.VMEM((plan.zero_row + 8, 128), F32)],
+        compiler_params=pltpu.CompilerParams(vmem_limit_bytes=32 * 1024 * 1024),
+        name="unpack_rows",
+    )(index, block, tail)
+
+
+def update_kernel(rows, chunk, factor_ref, total, *refs):
+    states, outs, held, made, in_sems, out_sems = (
+        refs[:4], refs[4:8], refs[8:12], refs[12:16], refs[16], refs[17],
+    )
+    starts = list(range(0, rows, chunk))
+    sizes = [min(chunk, rows - at) for at in starts]
+    loads = [
+        [
+            pltpu.make_async_copy(
+                source.at[pl.ds(at, size), 0], ref.at[pl.ds(at, size)], in_sems.at[k, j]
+            )
+            for j, (source, ref) in enumerate(zip(states, held))
+        ]
+        for k, (at, size) in enumerate(zip(starts, sizes))
+    ]
+    for group in loads:
+        for copy in group:
+            copy.start()
+    stores = []
+    factor = factor_ref[0]
+    for k, (at, size) in enumerate(zip(starts, sizes)):
+        for copy in loads[k]:
+            copy.wait()
+
+        def body(i, carry):
+            here = pl.ds(pl.multiple_of(at + i * 16, 8), 16)
+            master, first, second, ema = (ref[here, :] for ref in held)
+            clipped = total[here, :] * factor
+            new_first = beta_one * first + (1.0 - beta_one) * clipped
+            new_second = beta_two * second + (1.0 - beta_two) * clipped * clipped
+            first_hat = new_first * (1.0 / (1.0 - beta_one**STEP))
+            second_hat = new_second * (1.0 / (1.0 - beta_two**STEP))
+            new_master = master - learn_rate * (
+                first_hat / (jnp.sqrt(second_hat) + adam_epsilon) + weight_decay * master
+            )
+            made[0][here, :] = new_master
+            made[1][here, :] = new_first
+            made[2][here, :] = new_second
+            made[3][here, :] = average_keep * ema + (1.0 - average_keep) * new_master
+            return carry
+
+        lax.fori_loop(0, -(-size // 16), body, 0, unroll=2)
+        for j in range(4):
+            copy = pltpu.make_async_copy(
+                made[j].at[pl.ds(at, size)], outs[j].at[pl.ds(at, size), 0], out_sems.at[k, j]
+            )
+            copy.start()
+            stores.append(copy)
+    for copy in stores:
+        copy.wait()
+
+
+def update(plan, factor, total, states):
+    rows = plan.shard_rows
+    chunk = 16 * -(-rows // (16 * 4))
+    padded = 16 * -(-rows // 16)
+    count = -(-rows // chunk)
+    return pl.pallas_call(
+        functools.partial(update_kernel, rows, chunk),
+        out_shape=[jax.ShapeDtypeStruct((rows, 1, 128), F32)] * 4,
+        in_specs=[IN_SMEM, IN_VMEM, *[ANY] * 4],
+        out_specs=[ANY] * 4,
+        scratch_shapes=[
+            *[pltpu.VMEM((padded, 128), F32)] * 8,
+            pltpu.SemaphoreType.DMA((count, 4)),
+            pltpu.SemaphoreType.DMA((count, 4)),
+        ],
+        compiler_params=pltpu.CompilerParams(vmem_limit_bytes=40 * 1024 * 1024),
+        name="update_states",
+    )(factor, total, *states)
 
 
 def dot(a, b):
@@ -247,6 +391,10 @@
     return pl.ds(pl.multiple_of(pair * 256, 256), 256)
 
 
+def norm_block(count):
+    return next(n for n in (224, 208, 112, 104, 16) if count % n == 0)
+
+
 def norm_rows(x, width):
     mean = jnp.sum(x, axis=1, keepdims=True) * (1.0 / width)
     centre = x - mean
@@ -255,15 +403,19 @@
     return centre * rstd, rstd
 
 
-def norm_forward(x_ref, gain, shift, out_ref, count, width, size=16):
+def norm_forward(x_ref, gain, shift, out_ref, count, width):
+    size = norm_block(count)
+
     def step(at):
         hat, _ = norm_rows(x_ref[pl.ds(at, size), :], width)
         out_ref[pl.ds(at, size), :] = (hat * gain + shift).astype(out_ref.dtype)
 
-    for_rows(count, size, step, 2)
-
-
-def norm_backward(x_ref, gain, grad_of, put, count, width, size=16):
+    for_rows(count, size, step)
+
+
+def norm_backward(x_ref, gain, grad_of, put, count, width):
+    size = norm_block(count)
+
     def body(i, carry):
         gain_sum, shift_sum = carry
         at = pl.multiple_of(i * size, size)
@@ -424,38 +576,31 @@
 
 
 class Gradients:
-    def __init__(self, section, half, own, stage, sems, keep, send):
-        self.section, self.half, self.own = section, half, own
-        self.stage, self.sems, self.keep, self.send = stage, sems, keep, send
+    def __init__(self, plan, s, own, stage, sems, targets):
+        self.plan, self.section, self.own = plan, plan.sections[s], own
+        self.bins = plan.bins(s)
+        self.stage, self.sems, self.targets = stage, sems, targets
         self.turn = 0
         self.flying = [[], []]
 
-    def pieces(self, name, first, count):
-        panels = self.section.panels[name]
-        out = []
-        for block, unit, group, groups in self.section.pieces(name, first, count):
-            start, left = unit, groups * panels
-            at = (group - first) * panels
-            while left:
-                side = 0 if start < self.half else 1
-                take = min(left, self.half - start) if side == 0 else left
-                out.append((block, side, start - side * self.half, at, take))
-                start, at, left = start + take, at + take, left - take
-        return out
-
-    def copy_out(self, source, block, side, unit, take, sem):
+    def copy_out(self, source, block, place, unit, take, sem):
+        which = max(i for i, (first, _) in enumerate(self.bins) if first <= block)
+        block = block - self.bins[which][0]
+        side, part = place // 3, place % 3
+        keep, send = (self.targets[which * 6 + i * 3 + part] for i in range(2))
+
         def to(target):
             return pltpu.make_async_copy(source, target.at[block, pl.ds(unit, take)], sem)
 
         @pl.when(self.own == side)
         def _():
-            to(self.keep).start()
+            to(keep).start()
 
         @pl.when(self.own != side)
         def _():
-            to(self.send).start()
-
-        return to(self.keep)
+            to(send).start()
+
+        return to(keep)
 
     def drain(self, slot):
         for copy in self.flying[slot]:
@@ -480,18 +625,21 @@
                 return carry
 
             lax.fori_loop(0, panels // 2, body, 0)
-            for block, side, unit, at, take in self.pieces(name, band * 16, 16):
+            for block, place, unit, at, take in self.section.runs(
+                name, self.plan.cuts, band * 16, 16
+            ):
                 self.flying[slot].append(
                     self.copy_out(
-                        stage.at[pl.ds(at, take)], block, side, unit, take, self.sems.at[slot]
+                        stage.at[pl.ds(at, take)], block, place, unit, take, self.sems.at[slot]
                     )
                 )
 
-    def vectors(self, values, scratch, vec_unit):
-        blocks = sorted({v[2] for v in self.section.vectors.values()})
+    def finish(self, values, scratch):
+        vectors = self.section.vectors
+        blocks = sorted({vectors[name][2] for name in values})
         for k, block in enumerate(blocks):
-            scratch[k] = jnp.zeros((16 * VEC_UNITS, 128), F32).reshape(VEC_UNITS, 16, 128)
-            for name, (_, panels, at_block, at) in self.section.vectors.items():
+            scratch[k] = jnp.zeros((VEC_UNITS, 16, 128), F32)
+            for name, (_, panels, at_block, at) in vectors.items():
                 if at_block != block:
                     continue
                 for panel in range(panels):
@@ -499,10 +647,10 @@
                     scratch[k, unit, row : row + 1, :] = values[name][
                         :, panel * 128 : panel * 128 + 128
                     ]
+        unit = self.plan.vec_unit - self.plan.cuts[5]
+        assert unit >= 0
         copies = [
-            self.copy_out(
-                scratch.at[k], block, 1, vec_unit - self.half, VEC_UNITS, self.sems.at[2]
-            )
+            self.copy_out(scratch.at[k], block, 5, unit, VEC_UNITS, self.sems.at[2])
             for k, block in enumerate(blocks)
         ]
         for copy in copies:
@@ -511,101 +659,112 @@
         self.drain(1)
 
 
-def block_backward(sh, dy, x0, n1, mixed, o, x1, n2, g, gp, dyb, dn, dmixed, acc, turned, w, vec,
-                   limit_of, grads, values, ready):
-    width, hidden, count = sh.width, sh.hidden, sh.count
-    panels = width // 128
-
-    def round_stream():
+class Backward:
+    def __init__(self, sh, w, vec, limit_of, grads, values, acc, turned, ready):
+        self.sh, self.w, self.vec, self.limit_of = sh, w, vec, limit_of
+        self.grads, self.values, self.acc, self.turned, self.ready = grads, values, acc, turned, ready
+        self.panels = sh.width // 128
+
+    def round_stream(self, dy, dyb):
         def step(at):
             dyb[pl.ds(at, 16), :] = dy[pl.ds(at, 16), :].astype(BF16)
 
-        for_rows(count, 16, step, 2)
-
-    def into_stream(at, size, value):
-        dy[pl.ds(at, size), :] = dy[pl.ds(at, size), :] + value
-
-    def from_dn(at, size):
-        return dn[pl.ds(at, size), :]
-
-    round_stream()
-    ready("fc2", g)
-    grads.weight("fc2", g, hidden, dyb, turned)
-    ready("gp", gp)
-
-    def hidden_band(band, carry):
-        acc[...] = dot_nt(dyb[...], row_band(w["fc2"], panels, band))
-
-        def step(at):
-            here = pl.ds(at, 16)
-            g[here, lanes(band)] = (acc[here, :] * gp[here, lanes(band)]).astype(BF16)
-
-        for_rows(count, 16, step, 4)
-        return carry
-
-    lax.fori_loop(0, hidden // 256, hidden_band, 0)
-    ready("fc1", n2)
-    grads.weight("fc1", n2, width, g, turned)
-
-    def back_through(left, name):
+        for_rows(self.sh.count, 16, step, 4)
+
+    def bands(self, left, name, count, put):
+        acc = self.acc
+        panels = self.grads.section.panels[name]
+
         def body(band, carry):
-            acc[...] = dot_nt(left[...], row_band(w[name], grads.section.panels[name], band))
+            acc[...] = dot_nt(left[...], row_band(self.w[name], panels, band))
 
             def step(at):
-                dn[pl.ds(at, 16), lanes(band)] = acc[pl.ds(at, 16), :]
-
-            for_rows(count, 16, step, 4)
+                here = pl.ds(at, 16)
+                put(here, lanes(band), acc[here, :])
+
+            for_rows(self.sh.count, 16, step, 4)
             return carry
 
-        lax.fori_loop(0, width // 256, body, 0)
-
-    back_through(g, "fc1")
-    ready("x1", x1)
-    values["g2"], values["b2"] = norm_backward(x1, vec("g2"), from_dn, into_stream, count, width)
-    round_stream()
-    ready("proj", o)
-    grads.weight("proj", o, width, dyb, turned)
-
-    def out_band(band, carry):
-        acc[...] = dot_nt(dyb[...], row_band(w["proj"], panels, band))
-
-        def step(at):
-            o[pl.ds(at, 16), lanes(band)] = acc[pl.ds(at, 16), :].astype(BF16)
-
-        for_rows(count, 16, step, 4)
-        return carry
-
-    lax.fori_loop(0, width // 256, out_band, 0)
-    ready("mixed", mixed)
-    attention_backward(mixed, o, dmixed, limit_of, sh.images, sh.rows, width, sh.size)
-    ready("qkv", n1)
-    grads.weight("qkv", n1, width, dmixed, turned)
-    back_through(dmixed, "qkv")
-    ready("x0", x0)
-    values["g1"], values["b1"] = norm_backward(x0, vec("g1"), from_dn, into_stream, count, width)
-
-
-def load_vectors(section, vec_unit, own_section, gathered, held, vec_ref, sem):
+        lax.fori_loop(0, count // 256, body, 0)
+
+    def through_norm(self, x, dn, dy, gain, shift, dn_is=None):
+        def from_dn(at, size):
+            return dn[pl.ds(at, size), :]
+
+        def into_stream(at, size, value):
+            dy[pl.ds(at, size), :] = dy[pl.ds(at, size), :] + value
+
+        self.values[gain], self.values[shift] = norm_backward(
+            x, self.vec(gain), from_dn, into_stream, self.sh.count, self.sh.width
+        )
+
+    def second_product(self, dy, dyb, g, gp):
+        self.round_stream(dy, dyb)
+        self.ready("fc2", g)
+        self.grads.weight("fc2", g, self.sh.hidden, dyb, self.turned)
+        self.ready(None, gp)
+
+        def put(here, there, value):
+            g[here, there] = (value * gp[here, there]).astype(BF16)
+
+        self.bands(dyb, "fc2", self.sh.hidden, put)
+
+    def first_product(self, dy, g, n2, x1, dn):
+        def put(here, there, value):
+            dn[here, there] = value
+
+        self.ready("fc1", n2)
+        self.grads.weight("fc1", n2, self.sh.width, g, self.turned)
+        self.bands(g, "fc1", self.sh.width, put)
+        self.ready(None, x1)
+        self.through_norm(x1, dn, dy, "g2", "b2")
+
+    def attention(self, dy, dyb, o, mixed, dmixed):
+        sh = self.sh
+        self.round_stream(dy, dyb)
+        self.ready("proj", o)
+        self.grads.weight("proj", o, sh.width, dyb, self.turned)
+
+        def put(here, there, value):
+            o[here, there] = value.astype(BF16)
+
+        self.bands(dyb, "proj", sh.width, put)
+        self.ready(None, mixed)
+        attention_backward(mixed, o, dmixed, self.limit_of, sh.images, sh.rows, sh.width, sh.size)
+
+    def mixing(self, dy, dmixed, n1, x0, dn):
+        def put(here, there, value):
+            dn[here, there] = value
+
+        self.ready("qkv", n1)
+        self.grads.weight("qkv", n1, self.sh.width, dmixed, self.turned)
+        self.bands(dmixed, "qkv", self.sh.width, put)
+        self.ready(None, x0)
+        self.through_norm(x0, dn, dy, "g1", "b1")
+
+
+def load_vectors(plan, s, gathered, held, vec_ref, sem):
+    section = plan.sections[s]
     blocks = sorted({v[2] for v in section.vectors.values()})
     copies = [
         pltpu.make_async_copy(
-            gathered.at[own_section, block, pl.ds(vec_unit, VEC_UNITS)], held.at[k], sem
+            gathered.at[1, block, pl.ds(plan.vec_unit - plan.half, VEC_UNITS)], held.at[k], sem
         )
         for k, block in enumerate(blocks)
     ]
     for copy in copies:
         copy.start()
+    names = {name: i for i, name in enumerate(section.vectors)}
 
     def finish():
         for copy in copies:
             copy.wait()
-        names = {}
         for k, block in enumerate(blocks):
             rows = held[k].reshape(16 * VEC_UNITS, 128).astype(F32)
-            for i, (name, (_, panels, at_block, at)) in enumerate(section.vectors.items()):
-                names[name] = i
+            for name, (_, panels, at_block, at) in section.vectors.items():
                 if at_block != block:
                     continue
+                i = names[name]
                 for panel in range(panels):
                     vec_ref[i : i + 1, panel * 128 : panel * 128 + 128] = rows[
                         at + panel : at + panel + 1, :
@@ -615,19 +774,17 @@
     return finish
 
 
-def load_weights(section, own_section, gathered, w, sems):
+def load_weights(plan, s, gathered, w, sems):
+    section = plan.sections[s]
     copies = {}
     for k, (name, ref) in enumerate(w.items()):
         panels = section.panels[name]
+        flat = ref.reshape(ref.shape[0] * panels, 16, 128)
         copies[name] = [
             pltpu.make_async_copy(
-                gathered.at[own_section, block, pl.ds(unit, groups * panels)],
-                ref.reshape(ref.shape[0] * panels, 16, 128).at[
-                    pl.ds(group * panels, groups * panels)
-                ],
-                sems.at[k],
+                gathered.at[side, block, pl.ds(unit, take)], flat.at[pl.ds(at, take)], sems.at[k]
             )
-            for block, unit, group, groups in section.pieces(name)
+            for block, side, unit, at, take in section.runs(name, plan.half_cuts)
         ]
         for copy in copies[name]:
             copy.start()
@@ -657,13 +814,12 @@
 
 
 def encoder_kernel(plan, sh, refs):
-    section = plan.sections[0]
     (info, gathered, patches, perm, pos, pp_out, x0_out, n1_out, mixed_out, o_out, x1_out, n2_out,
      g_out, gp_out, y_out, latent_out, w_patch, w_qkv, w_proj, w_fc1, w_fc2, held, vec_ref, pp, xe,
      x0, n1, mixed, o, x1, n2, g, gp, y, latent, acc, w_sems, out_sems) = refs
     w = dict(zip(W_ENC, (w_patch, w_qkv, w_proj, w_fc1, w_fc2)))
-    finish_vec = load_vectors(section, plan.vec_unit, 0, gathered, held, vec_ref, w_sems.at[5])
-    ready = load_weights(section, 0, gathered, w, w_sems)
+    finish_vec = load_vectors(plan, 0, gathered, held, vec_ref, w_sems.at[5])
+    ready = load_weights(plan, 0, gathered, w, w_sems)
     outs = []
 
     targets = [(pp, pp_out), (x0, x0_out), (n1, n1_out), (mixed, mixed_out), (o, o_out),
@@ -690,7 +846,6 @@
     saved(pp)
     vec = finish_vec()
     ready("patch")
-    bias = vec("patch_b")
 
     def put(pair):
         part = vec_ref[0:1, lanes(pair)]
@@ -701,7 +856,6 @@
 
         for_rows(sh.count, 16, step, 4)
 
-    del bias
     times_columns(xe, w["patch"], D // 128, PIX, acc, put)
     saved(x0)
     block_forward(
@@ -713,9 +867,10 @@
         copy.wait()
 
 
-ANY = pl.BlockSpec(memory_space=pl.ANY)
-IN_VMEM = pl.BlockSpec(memory_space=pltpu.VMEM)
-IN_SMEM = pl.BlockSpec(memory_space=pltpu.SMEM)
+def lasting(microseconds):
+    return pl.CostEstimate(
+        flops=int(microseconds * 1e9), bytes_accessed=1 << 20, transcendentals=0
+    )
 
 
 def saved_shapes(sh):
@@ -757,6 +912,7 @@
             pltpu.SemaphoreType.DMA((len(outs),)),
         ],
         compiler_params=pltpu.CompilerParams(vmem_limit_bytes=VMEM_BYTES),
+        cost_estimate=lasting(50),
         name="encoder_forward",
     )(info, gathered, patches, perm, pos)
 
@@ -765,8 +921,9 @@
 
 
 def decoder_kernel(plan, sh, refs):
-    section = plan.sections[1]
-    (info, scale, gathered, latent_in, pp_in, perm, pos, keep_out, send_out, grad_latent, loss_out,
+    info, scale, gathered, latent_in, pp_in, perm, pos = refs[:7]
+    targets, refs = refs[7:19], refs[19:]
+    (grad_latent, loss_out,
      w_embed, w_qkv, w_proj, w_fc1, w_fc2, w_head, held, vec_ref, pp, latent, embedded, x0, n1,
      mixed, o, x1, n2, g, gp, y, f, dn, guess, acc, acc_e, turned, turned_e, stage, vec_stage, w_sems,
      in_sems, grad_sems) = refs
@@ -774,8 +931,8 @@
     copy_latent = pltpu.make_async_copy(latent_in, latent, in_sems.at[0])
     copy_pp = pltpu.make_async_copy(pp_in, pp, in_sems.at[1])
     copy_latent.start()
-    finish_vec = load_vectors(section, plan.vec_unit, 1, gathered, held, vec_ref, w_sems.at[6])
-    ready = load_weights(section, 1, gathered, w, w_sems)
+    finish_vec = load_vectors(plan, 1, gathered, held, vec_ref, w_sems.at[6])
+    ready = load_weights(plan, 1, gathered, w, w_sems)
     copy_pp.start()
     images, count = sh.images, sh.count
     count_e = images * ROWS_E
@@ -836,22 +993,18 @@
     total = jnp.sum(jnp.sum(total, axis=0, keepdims=True), axis=1, keepdims=True)
     loss_out[...] = jnp.broadcast_to(total * (1.0 / PIX), (8, 128))
 
-    own = info[0]
-    grads = Gradients(section, plan.half, own, stage, grad_sems, keep_out, send_out)
+    grads = Gradients(plan, 1, info[0], stage, grad_sems, targets)
+    values = {}
+    back = Backward(
+        sh, w, vec, lambda i: NP, grads, values, acc, turned, lambda name, ref: None
+    )
     dpred = pp.reshape(count, PIX)
     grads.weight("head", f, DD, dpred, turned)
 
-    def final_band(band, carry):
-        acc[...] = dot_nt(dpred[...], row_band(w["head"], PIX // 128, band))
-
-        def step(at):
-            dn[pl.ds(at, 16), lanes(band)] = acc[pl.ds(at, 16), :]
-
-        for_rows(count, 16, step, 4)
-        return carry
-
-    lax.fori_loop(0, DD // 256, final_band, 0)
-    values = {}
+    def put_dn(here, there, value):
+        dn[here, there] = value
+
+    back.bands(dpred, "head", DD, put_dn)
 
     def from_dn(at, size):
         return dn[pl.ds(at, size), :]
@@ -860,10 +1013,11 @@
         y[pl.ds(at, size), :] = value
 
     values["gf"], values["bf"] = norm_backward(y, vec("gf"), from_dn, put_y, count, DD)
-    block_backward(
-        sh, y, x0, n1, mixed, o, x1, n2, g, gp, f, dn, g.at[:, pl.ds(0, 3 * DD)], acc, turned, w, vec, lambda i: NP,
-        grads, values, lambda *a: None,
-    )
+    back.second_product(y, f, g, gp)
+    back.first_product(y, g, n2, x1, dn)
+    dmixed = g.at[:, pl.ds(0, 3 * DD)]
+    back.attention(y, f, o, mixed, dmixed)
+    back.mixing(y, dmixed, n1, x0, dn)
 
     def split(image, total):
         start = pl.multiple_of(image * ROWS_D, 16)
@@ -899,14 +1053,17 @@
         return carry
 
     lax.fori_loop(0, D // 256, latent_band, 0)
-    grads.vectors(values, vec_stage, plan.vec_unit)
-
-
-def grad_shapes(plan, section):
-    blocks = plan.sections[section].blocks_used
-    inner = factors(plan.dp)[1] * factors(plan.dp)[2]
-    blocks = -(-blocks // inner) * inner
-    return [jax.ShapeDtypeStruct((blocks, plan.half, 16, 128), F32)] * 2
+    grads.finish(values, vec_stage)
+
+
+def grad_shapes(plan, s):
+    cuts = plan.part_cuts
+    return [
+        jax.ShapeDtypeStruct((count, cuts[part + 1] - cuts[part], 16, 128), F32)
+        for _, count in plan.bins(s)
+        for _ in range(2)
+        for part in range(3)
+    ]
 
 
 def decoder(plan, sh, info, scale, gathered, latent, pp, perm, pos):
@@ -922,7 +1079,7 @@
             jax.ShapeDtypeStruct((8, 128), F32),
         ],
         in_specs=[IN_SMEM, IN_SMEM, ANY, ANY, ANY, IN_VMEM, IN_VMEM],
-        out_specs=[ANY, ANY, IN_VMEM, IN_VMEM],
+        out_specs=[*[ANY] * 12, IN_VMEM, IN_VMEM],
         scratch_shapes=[
             *weight_scratch(DEC, W_DEC),
             pltpu.VMEM((holders, VEC_UNITS, 16, 128), BF16),
@@ -945,197 +1102,300 @@
             pltpu.SemaphoreType.DMA((3,)),
         ],
         compiler_params=pltpu.CompilerParams(vmem_limit_bytes=VMEM_BYTES),
+        cost_estimate=lasting(160),
         name="decoder_both",
     )(info, scale, gathered, latent, pp, perm, pos)
 
 
-W_BACK = ["fc2", "fc1", "proj", "qkv"]
-
-
-def encoder_back_kernel(plan, sh, refs):
-    section = plan.sections[0]
-    (info, gathered, grad_latent, pp_in, x0_in, n1_in, mixed_in, o_in, x1_in, n2_in, g_in, gp_in,
-     y_in, keep_out, send_out, w_fc2, w_fc1, w_proj, w_qkv, held, vec_ref, xe, x0, n1, mixed, o, x1,
-     n2, g, gp, y, dyb, dn, dmixed, acc, turned, stage, vec_stage, w_sems, in_sems,
-     grad_sems) = refs
-    w = dict(zip(W_BACK, (w_fc2, w_fc1, w_proj, w_qkv)))
-    finish_vec = load_vectors(section, plan.vec_unit, 0, gathered, held, vec_ref, w_sems.at[4])
-    loads = {}
-    pairs = [(y, y_in), (g, g_in), (gp, gp_in), (n2, n2_in), (x1, x1_in), (o, o_in),
-             (mixed, mixed_in), (n1, n1_in), (x0, x0_in)]
-    for k, (ref, source) in enumerate(pairs):
-        loads[id(ref)] = pltpu.make_async_copy(source, ref, in_sems.at[k])
-        loads[id(ref)].start()
-    weights_ready = load_weights(section, 0, gathered, w, w_sems)
-    patch_loads = [
-        pltpu.make_async_copy(
-            pp_in.at[i, pl.ds(0, ROWS_E)], xe.at[pl.ds(i * ROWS_E, ROWS_E)], in_sems.at[9]
+class Stage:
+    def __init__(self, plan, sh, weights, reads, temps, outs, most, cost, name, body):
+        self.plan, self.sh, self.weights, self.reads = plan, sh, weights, reads
+        self.temps, self.outs, self.most, self.cost, self.name = temps, outs, most, cost, name
+        self.body = body
+
+    def kernel(self, blocks, *refs):
+        refs = list(refs)
+
+        def take(count):
+            got = refs[:count]
+            del refs[:count]
+            return got
+
+        plan, sh = self.plan, self.sh
+        info, gathered = take(2)
+        sources = dict(zip(self.reads, take(len(self.reads))))
+        take(blocks)
+        targets = take(len(grad_shapes(plan, 0)))
+        results = dict(zip(self.outs, take(len(self.outs))))
+        w = dict(zip(self.weights, take(len(self.weights))))
+        here = dict(zip(self.reads, take(len(self.reads))))
+        temps = dict(zip(self.temps, take(len(self.temps))))
+        held, vec_ref, acc, turned, stage, vec_stage, w_sems, in_sems, grad_sems = refs
+        finish_vec = load_vectors(plan, 0, gathered, held, vec_ref, w_sems.at[len(w)])
+        loads = {}
+        for k, (name, ref) in enumerate(here.items()):
+            if name == "xe":
+                copies = [
+                    pltpu.make_async_copy(
+                        sources[name].at[i, pl.ds(0, ROWS_E)],
+                        ref.at[pl.ds(i * ROWS_E, ROWS_E)],
+                        in_sems.at[k],
+                    )
+                    for i in range(sh.images)
+                ]
+            else:
+                copies = [pltpu.make_async_copy(sources[name], ref, in_sems.at[k])]
+            for copy in copies:
+                copy.start()
+            loads[id(ref)] = copies
+        weights_ready = load_weights(plan, 0, gathered, w, w_sems)
+        vec = finish_vec()
+
+        def ready(name, ref=None):
+            for copy in loads.pop(id(ref), ()):
+                copy.wait()
+            if name is not None:
+                weights_ready(name)
+
+        values = {}
+        grads = Gradients(plan, 0, info[0], stage, grad_sems, targets)
+        back = Backward(
+            sh, w, vec, lambda i: info[1 + i], grads, values, acc, turned, ready
         )
-        for i in range(sh.images)
-    ]
-    for copy in patch_loads:
-        copy.start()
-
-    def ready(name, ref):
-        loads[id(ref)].wait()
-        weights_ready(name)
-
-    vec = finish_vec()
-    loads[id(y)].wait()
-    values = {}
+        self.body(back, {**here, **temps}, results)
+        assert not loads
+        grads.finish(values, vec_stage)
+
+    def __call__(self, info, gathered, arrays, blocks):
+        plan, sh = self.plan, self.sh
+        count, width, hidden = sh.count, sh.width, sh.hidden
+        known = {
+            "dz": ((count, width), BF16),
+            "y": ((count, width), F32),
+            "dy": ((count, width), F32),
+            "x0": ((count, width), F32),
+            "x1": ((count, width), F32),
+            "dn": ((count, width), F32),
+            "n1": ((count, width), BF16),
+            "n2": ((count, width), BF16),
+            "o": ((count, width), BF16),
+            "dyb": ((count, width), BF16),
+            "xe": ((count, PIX), BF16),
+            "mixed": ((count, 3 * width), BF16),
+            "dmixed": ((count, 3 * width), BF16),
+            "g": ((count, hidden), BF16),
+            "gp": ((count, hidden), F32),
+        }
+        holders = len({v[2] for v in plan.sections[0].vectors.values()})
+        targets = grad_shapes(plan, 0)
+        before = 2 + len(self.reads)
+        got = pl.pallas_call(
+            functools.partial(self.kernel, len(blocks)),
+            out_shape=[*targets, *[jax.ShapeDtypeStruct(*known[n]) for n in self.outs]],
+            in_specs=[IN_SMEM, *[ANY] * (1 + len(self.reads) + len(blocks))],
+            out_specs=[*[ANY] * len(targets), *[IN_VMEM] * len(self.outs)],
+            input_output_aliases={before + i: i for i in range(len(blocks))},
+            scratch_shapes=[
+                *weight_scratch(ENC, self.weights),
+                *[pltpu.VMEM(*known[n]) for n in self.reads],
+                *[pltpu.VMEM(*known[n]) for n in self.temps],
+                pltpu.VMEM((holders, VEC_UNITS, 16, 128), BF16),
+                pltpu.VMEM((8, D), F32),
+                pltpu.VMEM((count, 256), F32),
+                pltpu.VMEM((256, count), BF16),
+                pltpu.VMEM((2, 16 * self.most, 16, 128), F32),
+                pltpu.VMEM((holders, VEC_UNITS, 16, 128), F32),
+                pltpu.SemaphoreType.DMA((len(self.weights) + 1,)),
+                pltpu.SemaphoreType.DMA((len(self.reads),)),
+                pltpu.SemaphoreType.DMA((3,)),
+            ],
+            compiler_params=pltpu.CompilerParams(vmem_limit_bytes=VMEM_BYTES),
+            cost_estimate=lasting(self.cost),
+            name=self.name,
+        )(info, gathered, *[arrays[n] for n in self.reads], *blocks)
+        return got[: len(targets)], dict(zip(self.outs, got[len(targets) :]))
+
+
+def back_second(back, r, out):
+    sh = back.sh
+    back.ready(None, r["dz"])
+    back.ready(None, r["y"])
 
     def from_latent(at, size):
-        return grad_latent[pl.ds(at, size), :].astype(F32)
-
-    def put_y(at, size, value):
-        y[pl.ds(at, size), :] = value
-
-    values["gf"], values["bf"] = norm_backward(y, vec("gf"), from_latent, put_y, sh.count, D)
-    grads = Gradients(section, plan.half, info[0], stage, grad_sems, keep_out, send_out)
-    block_backward(
-        sh, y, x0, n1, mixed, o, x1, n2, g, gp, dyb, dn, dmixed, acc, turned, w, vec,
-        lambda i: info[1 + i], grads, values, ready,
+        return r["dz"][pl.ds(at, size), :].astype(F32)
+
+    def put(at, size, value):
+        out["dy"][pl.ds(at, size), :] = value
+
+    back.values["gf"], back.values["bf"] = norm_backward(
+        r["y"], back.vec("gf"), from_latent, put, sh.count, D
     )
+    back.second_product(out["dy"], r["dyb"], r["g"], r["gp"])
+
+    def step(at):
+        out["g"][pl.ds(at, 16), :] = r["g"][pl.ds(at, 16), :]
+
+    for_rows(sh.count, 16, step, 2)
+
+
+def copy_rows(count, source, target):
+    def step(at):
+        target[pl.ds(at, 16), :] = source[pl.ds(at, 16), :]
+
+    for_rows(count, 16, step, 4)
+
+
+def back_first(back, r, out):
+    back.ready(None, r["dy"])
+    back.ready(None, r["g"])
+    copy_rows(back.sh.count, r["dy"], out["dy"])
+    back.first_product(out["dy"], r["g"], r["n2"], r["x1"], r["dn"])
+
+
+def back_attention(back, r, out):
+    back.ready(None, r["dy"])
+    back.attention(r["dy"], r["dyb"], r["o"], r["mixed"], out["dmixed"])
+
+
+def back_mixing(back, r, out):
+    back.ready(None, r["dy"])
+    back.ready(None, r["dmixed"])
+    back.mixing(r["dy"], r["dmixed"], r["n1"], r["x0"], r["dn"])
 
     def body(i, total):
         at = pl.multiple_of(i * 16, 16)
-        grad = y[pl.ds(at, 16), :]
-        dyb[pl.ds(at, 16), :] = grad.astype(BF16)
+        grad = r["dy"][pl.ds(at, 16), :]
+        r["dyb"][pl.ds(at, 16), :] = grad.astype(BF16)
         return total + jnp.sum(grad.reshape(2, 8, D), axis=0)
 
-    total = lax.fori_loop(0, sh.count // 16, body, jnp.zeros((8, D), F32))
-    values["patch_b"] = jnp.sum(total, axis=0, keepdims=True)
-    for copy in patch_loads:
-        copy.wait()
-    grads.weight("patch", xe, PIX, dyb, turned)
-    grads.vectors(values, vec_stage, plan.vec_unit)
-
-
-def encoder_back(plan, sh, info, gathered, grad_latent, pp, saved):
-    shapes = saved_shapes(sh)
-    holders = len({v[2] for v in plan.sections[0].vectors.values()})
-    most = max(plan.sections[0].panels.values())
-    return pl.pallas_call(
-        lambda *refs: encoder_back_kernel(plan, sh, refs),
-        out_shape=grad_shapes(plan, 0),
-        in_specs=[IN_SMEM, ANY, IN_VMEM, *[ANY] * 10],
-        out_specs=[ANY, ANY],
-        scratch_shapes=[
-            *weight_scratch(ENC, W_BACK),
-            pltpu.VMEM((holders, VEC_UNITS, 16, 128), BF16),
-            pltpu.VMEM((8, D), F32),
-            pltpu.VMEM((sh.count, PIX), BF16),
-            *[pltpu.VMEM(*s) for s in shapes],
-            pltpu.VMEM((sh.count, D), BF16),
-            pltpu.VMEM((sh.count, D), F32),
-            pltpu.VMEM((sh.count, 3 * D), BF16),
-            pltpu.VMEM((sh.count, 256), F32),
-            pltpu.VMEM((256, sh.count), BF16),
-            pltpu.VMEM((2, 16 * most, 16, 128), F32),
-            pltpu.VMEM((holders, VEC_UNITS, 16, 128), F32),
-            pltpu.SemaphoreType.DMA((5,)),
-            pltpu.SemaphoreType.DMA((10,)),
-            pltpu.SemaphoreType.DMA((3,)),
-        ],
-        compiler_params=pltpu.CompilerParams(vmem_limit_bytes=VMEM_BYTES),
-        name="encoder_backward",
-    )(info, gathered, grad_latent, pp, *saved)
-
-
-class Grid:
-    def __init__(self, dp):
-        self.sizes = factors(dp)
-        self.dp = dp
-        me = lax.axis_index("dp")
-        _, b, c = self.sizes
-        self.at = (me // (b * c), me // c % b, me % c)
-
-    def shift(self, axis, by, held=None):
-        a, b, c = self.sizes
-        pairs = []
-        for me in range(self.dp):
-            at = [me // (b * c), me // c % b, me % c]
-            if held is not None and at[axis] not in held:
-                continue
-            at[axis] += by
-            if 0 <= at[axis] < self.sizes[axis]:
-                pairs.append((me, (at[0] * b + at[1]) * c + at[2]))
-        return pairs
+    total = lax.fori_loop(0, back.sh.count // 16, body, jnp.zeros((8, D), F32))
+    back.values["patch_b"] = jnp.sum(total, axis=0, keepdims=True)
+    back.ready(None, r["xe"])
+    back.grads.weight("patch", r["xe"], PIX, r["dyb"], back.turned)
+
+
+def encoder_back_stages(plan, sh):
+    most = {n: plan.sections[0].panels[n] for n in ("fc1", "fc2", "qkv", "proj")}
+    return [
+        Stage(plan, sh, ["fc2"], ["y", "dz", "g", "gp"], ["dyb"], ["dy", "g"], most["fc2"], 25,
+              "encoder_back_fc2", back_second),
+        Stage(plan, sh, ["fc1"], ["g", "dy", "n2", "x1"], ["dn"], ["dy"], most["fc1"], 20,
+              "encoder_back_fc1", back_first),
+        Stage(plan, sh, ["proj"], ["dy", "o", "mixed"], ["dyb"], ["dmixed"], most["proj"], 35,
+              "encoder_back_attention", back_attention),
+        Stage(plan, sh, ["qkv"], ["dy", "dmixed", "n1", "x0", "xe"], ["dn", "dyb"], [],
+              most["qkv"], 25, "encoder_back_qkv", back_mixing),
+    ]
 
 
 def pick(value, index, axis):
     return lax.dynamic_index_in_dim(value, index, axis, keepdims=False)
 
 
-def scatter_axis(grid, terms, axis, dim, targets):
-    size, at = grid.sizes[axis], grid.at[axis]
-
-    def own(target):
-        target = jnp.clip(target, 0, targets - 1)
-        total = pick(terms[0], target, dim)
-        for term in terms[1:]:
-            total = total + pick(term, target, dim)
-        return total
-
-    if size == 1:
-        return [pick(term, jnp.zeros((), jnp.int32), dim) for term in terms]
-    if size == 2 and targets == 2:
-        got = lax.ppermute(own(1 - at), "dp", grid.shift(axis, 1) + grid.shift(axis, -1))
-        return [pick(term, at, dim) for term in terms] + [got]
-    up = None
-    down = None
-    for step in range(1, size):
-        held = [z for z in range(step) if size - step + z < targets and z < size - 1]
-        mine = own(size - step + at)
-        if up is not None:
-            mine = mine + up
-        up = lax.ppermute(mine, "dp", grid.shift(axis, 1, held)) if held else None
-        held = [z for z in range(1, size) if 0 <= step - 1 - (size - 1 - z) < targets]
-        mine = own(step - 1 - (size - 1 - at))
-        if down is not None:
-            mine = mine + down
-        down = lax.ppermute(mine, "dp", grid.shift(axis, -1, held)) if held else None
-    last = jnp.clip(at, 0, targets - 1)
-    out = [pick(term, last, dim) for term in terms]
-    return out + [v for v in (up, down) if v is not None]
-
-
-def scatter_sum(grid, keep, got):
-    a, b, c = grid.sizes
-    half = keep.shape[1]
-    targets = keep.shape[0] // (b * c)
-    cut = [0, -(-half // 3), -(-2 * half // 3), half]
-    orders = [(2, 1, 0), (1, 0, 2), (0, 2, 1)]
-    parts = []
-    for part, order in enumerate(orders):
-        terms = [
-            v.reshape((targets, b, c) + v.shape[1:])[:, :, :, cut[part] : cut[part + 1]]
-            for v in (keep, got)
+def total_of(terms):
+    total = terms[0]
+    for term in terms[1:]:
+        total = total + term
+    return total
+
+
+def tie(*trees):
+    return lax.optimization_barrier(trees)
+
+
+class Flow:
+    def __init__(self, dp, keep, send, first):
+        self.dp = dp
+        self.me = lax.axis_index("dp")
+        self.keep, self.given = keep, send
+        count = keep[0].shape[0]
+        self.bits = count.bit_length() - 1
+        assert count == 1 << self.bits and dp & (dp - 1) == 0
+        self.all_bits = dp.bit_length() - 1
+        self.first = first
+        low = [b for b in range(0, self.bits, 1)]
+        if dp == 64:
+            low = [b for b in (0, 2, 4, 1, 3) if b < self.bits]
+        turn = min(3, len(low))
+        self.orders = [low[p % turn :][: turn - p % turn] + low[: p % turn] + low[turn:] for p in range(3)]
+        self.left = [list(range(self.bits - 1, -1, -1)) for _ in range(3)]
+        self.step = -1
+        self.terms = None
+
+    def done(self):
+        return self.step == self.all_bits
+
+    def payload(self):
+        if self.step < 0:
+            return list(self.given)
+        out = []
+        for part in range(3):
+            if self.step < self.bits:
+                bit = self.orders[part][self.step]
+                dim = self.left[part].index(bit)
+                other = 1 - (self.me >> bit & 1)
+                out.append(total_of([pick(t, other, dim) for t in self.terms[part]]))
+            else:
+                out.append(total_of(self.terms[part]))
+        return out
+
+    def send(self, payload):
+        if self.step < 0:
+            return [lax.ppermute(p, "section", [(0, 1), (1, 0)]) for p in payload]
+        out = []
+        for part in range(3):
+            if self.step < self.bits:
+                flip = 1 << self.orders[part][self.step]
+                pairs = [(i, i ^ flip) for i in range(self.dp)]
+            else:
+                flip = 1 << self.step
+                pairs = [(i, i ^ flip) for i in range(self.dp) if (i ^ self.first) & flip]
+            out.append(lax.ppermute(payload[part], "dp", pairs))
+        return out
+
+    def take(self, got):
+        if self.step < 0:
+            self.terms = [
+                [v.reshape((2,) * self.bits + v.shape[1:]) for v in pair]
+                for pair in zip(self.keep, got)
+            ]
+        elif self.step < self.bits:
+            for part in range(3):
+                bit = self.orders[part][self.step]
+                dim = self.left[part].index(bit)
+                mine = self.me >> bit & 1
+                self.terms[part] = [pick(t, mine, dim) for t in self.terms[part]] + [got[part]]
+                self.left[part].remove(bit)
+        else:
+            self.terms = [t + [g] for t, g in zip(self.terms, got)]
+        self.step += 1
+
+    def result(self):
+        return jnp.concatenate([total_of(t) for t in self.terms], axis=0)
+
+
+def move_on(flows, *others):
+    flows = [f for f in flows if f is not None and not f.done()]
+    payloads, others = tie([f.payload() for f in flows], others)
+    return flows, [f.send(p) for f, p in zip(flows, payloads)], others
+
+
+def arrive(flows, got):
+    for flow, values in zip(flows, got):
+        flow.take(values)
+
+
+def sum_everywhere(dp, value):
+    value = value + lax.ppermute(value, "section", [(0, 1), (1, 0)])
+    bits = dp.bit_length() - 1
+    for low in range(0, bits, 2):
+        got = [
+            lax.ppermute(value, "dp", [(i, i ^ (flip << low)) for i in range(dp)])
+            for flip in range(1, 1 << min(2, bits - low))
         ]
-        left = [0, 1, 2]
-        for axis in order:
-            dim = left.index(axis)
-            terms = scatter_axis(grid, terms, axis, dim, (targets, b, c)[axis])
-            left.remove(axis)
-        total = terms[0]
-        for term in terms[1:]:
-            total = total + term
-        parts.append(total)
-    return jnp.concatenate(parts, axis=0)
-
-
-def sum_everywhere(grid, value):
-    value = value + lax.ppermute(value, "section", [(0, 1), (1, 0)])
-    for axis, size in enumerate(grid.sizes):
-        step = 1
-        stride = math.prod(grid.sizes[axis + 1 :])
-        while step < size:
-            pairs = [
-                (i, i + (step if i // stride // step % 2 == 0 else -step) * stride)
-                for i in range(grid.dp)
-            ]
-            value = value + lax.ppermute(value, "dp", pairs)
-            step *= 2
+        value = value + got[0]
+        if len(got) == 3:
+            value = value + (got[1] + got[2])
     return value
 
 
@@ -1166,19 +1426,28 @@
     me = lax.axis_index("dp")
     shard = master.shape[1]
     plan = Plan(dp, shard // 128)
-    grid = Grid(dp)
-    rows = plan.shard_rows
-
-    flat = master.reshape(rows, 128)
+    rows, half = plan.shard_rows, plan.half
+    swap = [(0, 1), (1, 0)]
+    states = [v.reshape(rows, 1, 128) for v in (master, first, second, ema)]
+
     following = lax.ppermute(
-        flat[: plan.head_rows], "dp", [(i, i - 1) for i in range(1, dp)]
+        states[0][: plan.head_rows], "dp", [(i, i - 1) for i in range(1, dp)]
     )
     index = jnp.asarray(plan.pack_index)[section, me]
-    packed = move_rows(index, [flat, following], (plan.units, 16, 128), BF16)
-    gathered = lax.all_gather(packed, ("section", "dp"), axis=0, tiled=True)
-    gathered = gathered.reshape(2, dp, plan.units, 16, 128)
-
-    count = sum_everywhere(grid, jnp.sum(NP - keep).astype(F32)) * 0.5
+    packed = pack(plan, index, states[0], following)
+    mine = lax.dynamic_slice_in_dim(packed, section * half, half, 0)
+    given = lax.ppermute(
+        lax.dynamic_slice_in_dim(packed, (1 - section) * half, half, 0), "section", swap
+    )
+    half_e = jnp.where(section == 0, mine, given)
+    half_d = jnp.where(section == 0, given, mine)
+    gathered_e = lax.all_gather(half_e, ("section", "dp"), axis=0, tiled=True)
+    gathered_e = gathered_e.reshape(2, dp, half, 16, 128)
+    half_d, _ = tie(half_d, gathered_e[0, 0, 0])
+    gathered_d = lax.all_gather(half_d, ("section", "dp"), axis=0, tiled=True)
+    gathered_d = gathered_d.reshape(2, dp, half, 16, 128)
+
+    count = sum_everywhere(dp, jnp.sum(NP - keep).astype(F32)) * 0.5
     images = patches.shape[0] // 2
     mine = section * images
     patches = lax.dynamic_slice_in_dim(patches, mine, images, 0)
@@ -1193,16 +1462,53 @@
     shape_e = Shape(images, ROWS_E, D, HEADS_E, FF_E)
     shape_d = Shape(images, ROWS_D, DD, HEADS_D, FF_D)
     pp, *saved, latent = encoder(
-        plan, shape_e, info, gathered, patches, order, jnp.asarray(sincos(D))
+        plan, shape_e, info, gathered_e, patches, order, jnp.asarray(sincos(D))
     )
-    keep_d, send_d, grad_latent, loss = decoder(
-        plan, shape_d, info, scale, gathered, latent, pp, order, jnp.asarray(sincos(DD))
+    arrays = dict(zip(("x0", "n1", "mixed", "o", "x1", "n2", "g", "gp", "y"), saved))
+    arrays["xe"] = pp
+    *sums_d, arrays["dz"], loss = decoder(
+        plan, shape_d, info, scale, gathered_d, latent, pp, order, jnp.asarray(sincos(DD))
     )
-    swap = [(0, 1), (1, 0)]
-    sum_d = scatter_sum(grid, keep_d, lax.ppermute(send_d, "section", swap))
-    keep_e, send_e = encoder_back(plan, shape_e, info, gathered, grad_latent, pp, saved)
-    sum_e = scatter_sum(grid, keep_e, lax.ppermute(send_e, "section", swap))
-
+
+    stages = encoder_back_stages(plan, shape_e)
+    tail_parts = plan.tail_parts()
+    tail_got = [lax.ppermute(sums_d[9 + p], "section", swap) for p in tail_parts]
+    main = Flow(dp, sums_d[0:3], sums_d[3:6], 0)
+    low = high = None
+    blocks = []
+    for number, stage in enumerate(stages):
+        flows, got, (arrays, blocks) = move_on([main, high], arrays, blocks)
+        blocks, made = stage(info, gathered_e, arrays, blocks)
+        arrays = {**arrays, **made}
+        got, arrays, blocks = tie(got, arrays, blocks)
+        arrive(flows, got)
+        if number == 0:
+            tail_sum = lax.psum(
+                [sums_d[6 + p] + g for p, g in zip(tail_parts, tail_got)], "dp"
+            )
+        if number == 1:
+            high = Flow(dp, blocks[6:9], blocks[9:12], dp // 2)
+    low = Flow(dp, blocks[0:3], blocks[3:6], 0)
+    every = [main, high, low]
+    while not all(f.done() for f in every):
+        flows, got, _ = move_on(every)
+        arrive(flows, got)
+
+    cuts = plan.part_cuts
+    first_tail, tail_blocks = plan.bins(1)[1]
+    tail_at = jnp.clip(me - first_tail, 0, tail_blocks - 1)
+    tail_sum = dict(zip(tail_parts, tail_sum))
+    sum_tail = jnp.concatenate(
+        [
+            pick(tail_sum[p], tail_at, 0)
+            if p in tail_sum
+            else jnp.zeros((cuts[p + 1] - cuts[p], 16, 128), F32)
+            for p in range(3)
+        ],
+        axis=0,
+    )
+    sum_d = jnp.where(me < first_tail, main.result(), sum_tail)
+    sum_e = jnp.where(me < dp // 2, low.result(), high.result())
     half_mine = jnp.where(section == 0, sum_e, sum_d)
     half_other = lax.ppermute(jnp.where(section == 0, sum_d, sum_e), "section", swap)
     block = jnp.where(
@@ -1220,23 +1526,13 @@
     )
     tail = lax.ppermute(tail, "dp", [(i, i + 1) for i in range(dp - 1)])
     index = jnp.asarray(plan.unpack_index)[section, me]
-    shard_total = move_rows(index, [block, tail], (rows, 128), F32, zero_at=plan.zero_row)
-
-    squares = jnp.sum(shard_total * shard_total)
-    sums = sum_everywhere(grid, jnp.stack([squares, loss[0, 0]]))
-    loss_sum = sums[1]
+    total, squares = unpack(plan, index, block, tail)
+
+    sums = sum_everywhere(dp, jnp.stack([jnp.sum(squares), loss[0, 0]]))
     norm = jnp.sqrt(sums[0])
     factor = jnp.minimum(1.0, clip_limit / (norm + norm_epsilon))
-    clipped = (shard_total * factor).reshape(master.shape)
-    new_first = beta_one * first + (1.0 - beta_one) * clipped
-    new_second = beta_two * second + (1.0 - beta_two) * clipped * clipped
-    first_hat = new_first / (1.0 - beta_one**STEP)
-    second_hat = new_second / (1.0 - beta_two**STEP)
-    new_master = master - learn_rate * (
-        first_hat / (jnp.sqrt(second_hat) + adam_epsilon) + weight_decay * master
-    )
-    new_ema = average_keep * ema + (1.0 - average_keep) * new_master
-    return (new_master, new_first, new_second, new_ema, norm, loss_sum, count)
+    made = update(plan, factor.reshape(1), total, states)
+    return (*[v.reshape(1, shard) for v in made], norm, sums[1], count)
 
 
 def solution(mesh):

time: 1180 us -> 979 us (0.83)
  Pallas kernels: 433 us -> 358 us
  other arithmetic: 126 us -> 79.3 us
  waiting for transfers between devices: 399 us -> 370 us
  starting transfers between devices: 129 us -> 104 us
  local copies, waits for them, and re-layouts: 55.5 us -> 31.1 us
    pallas_call x1, Pallas kernels: 240 us -> 170 us  [decoder(): pl.pallas_call(lambda *refs: decoder_kernel(plan, sh, refs), out_shape=[*...]
    ppermute x56 -> x61, waiting for transfers between devices: 228 us -> 163 us  [the longest x36 141 us: send(): out.append(lax.ppermute(payload[part], 'dp', pairs))]
    psum x0 -> x1, waiting for transfers between devices: none -> 54.6 us  [on_device(): lax.psum([sums_d[6 + p] + g for p, g in zip(tail_parts, tail_got)], 'dp')]
    slice x11 -> x3, local copies, waits for them, and re-layouts: 44.4 us -> 2.71 us  [the longest x1 1.19 us: on_device(): sums = sum_everywhere(dp, jnp.stack([jnp.sum(squares), loss[0, 0]]))]
    add x48 -> x46, other arithmetic: 103 us -> 66.6 us  [the longest x44 66.6 us: total_of(): total = total + term]
    ppermute x56 -> x61, starting transfers between devices: 125 us -> 99.5 us  [the longest x36 69.1 us: send(): out.append(lax.ppermute(payload[part], 'dp', pairs))]
    all_gather x1 -> x2, waiting for transfers between devices: 168 us -> 148 us  [the longest x1 84 us: on_device(): gathered_e = lax.all_gather(half_e, ('section', 'dp'), axis=0, tiled=True)]
    unnamed x7 -> x0, other arithmetic: 18.4 us -> none
  transfers between devices with their start and end apart: 61 -> 68, of which waited for: 22 -> 30; matrix products, arithmetic and copies ran while one was open for 13% -> 4% of each run, Pallas kernels for 0% -> 17%
where the time goes in v2:
time: 979 us; the launch traced here: 968 us
  waiting for transfers between devices  370 us (38%)
  Pallas kernels  358 us (37%)
  starting transfers between devices  104 us (11%)
  other arithmetic  79.3 us (8%)
  local copies, waits for them, and re-layouts  31.1 us (3%)
  between operations  25 us (3%)
    pallas_call x1, Pallas kernels, decoder(): pl.pallas_call(lambda *refs: decoder_kernel(plan, sh, refs), out_shape=[*...  170 us
    ppermute x36, waiting for transfers between devices, send(): out.append(lax.ppermute(payload[part], 'dp', pairs))  141 us
    pallas_call x4, Pallas kernels, __call__(): pl.pallas_call(functools.partial(self.kernel, len(blocks)), out_shape=[*t...  113 us
    all_gather x1, waiting for transfers between devices, on_device(): gathered_e = lax.all_gather(half_e, ('section', 'dp'), axis=0, tiled=True)  84 us
    ppermute x36, starting transfers between devices, send(): out.append(lax.ppermute(payload[part], 'dp', pairs))  69.1 us
    add x44, other arithmetic, total_of(): total = total + term  66.6 us
    all_gather x1, waiting for transfers between devices, on_device(): gathered_d = lax.all_gather(half_d, ('section', 'dp'), axis=0, tiled=True)  63.8 us
    psum x1, waiting for transfers between devices, on_device(): lax.psum([sums_d[6 + p] + g for p, g in zip(tail_parts, tail_got)], 'dp')  54.6 us
  transfers between devices with their start and end apart: 68, of which 30 were waited for; matrix products, arithmetic and copies ran while one was open for 4% of the time, Pallas kernels for 17%

profile of v2, /device:TPU:0, one launch (start us, length us, event | category | flops | bytes accessed | tf_op | source)
XLA Modules:
  0.0 967.8 jit_solution(15171511056666983007)
XLA Ops:
  10.4 7.5 collective-permute-done.7.following
  19.4 6.8 pack_rows.1
  38.0 5.9 collective-permute-start.3
  50.6 4.6 collective-permute-start.6
  56.5 2.5 collective-permute-start.4
  62.0 84.0 %all-gather.5.cloned.1.call-done = bf16[4064,16,128]{2,1,0:T(8,128)(2,1)} async-done(((bf16[127,16,128]{2,1,0:T(8,128)(2,1)}), bf16[4064,16,128]{2,1,0:T(8,128)(2,1)}) %all-gather.5.cloned.1.call-update) | async-done | bytes 16646160 | tf_op jit(solution)/shard_map/all_gather | solution.py:1444
  146.0 52.6 %encoder_forward.1 = (bf16[6,208,768]{2,1,0:T(8,128)(2,1)}, f32[672,768]{1,0:T(8,128)}, bf16[672,768]{1,0:T(8,128)(2,1)}, bf16[672,2304]{1,0:T(8,128)(2,1)}, bf1...) custom-call(s32[7]{0:T(128)} %pad_add_fusion.refs_0_, ...), custom_call_target="tpu_custom_call" | custom-call | flops 49999998976 | bytes 1048576 | tf_op jit(solution)/shard_map/encoder_forward/pallas_call | solution.py:897
  198.6 63.8 %all-gather.3.cloned.1.call-done = bf16[4064,16,128]{2,1,0:T(8,128)(2,1)} async-done(((bf16[127,16,128]{2,1,0:T(8,128)(2,1)}), bf16[4064,16,128]{2,1,0:T(8,128)(2,1)}) %all-gather.3.cloned.1.call-update) | async-done | bytes 16646160 | tf_op jit(solution)/shard_map/all_gather | solution.py:1447
  262.4 169.7 %decoder_both.1 = (f32[8,43,16,128]{3,2,1,0:T(8,128)}, f32[8,42,16,128]{3,2,1,0:T(8,128)}, f32[8,42,16,128]{3,2,1,0:T(8,128)}, f32[8,43,16,128]{3,2,1,0:T(8,128)...) custom-call(s32[7]{0:T(128)} %pad_add_fusion.refs_0_, ...), custom_call_target="tpu_custom_call" | custom-call | flops 160000000000 | bytes 1048576 | tf_op jit(solution)/shard_map/decoder_both/pallas_call | solution.py:1074
  432.9 30.9 %encoder_back_fc2.1 = (f32[8,43,16,128]{3,2,1,0:T(8,128)}, f32[8,42,16,128]{3,2,1,0:T(8,128)}, f32[8,42,16,128]{3,2,1,0:T(8,128)}, f32[8,43,16,128]{3,2,1,0:T(8,...) custom-call(s32[7]{0:T(128)} %pad_add_fusion.refs_0_, ...), custom_call_target="tpu_custom_call" | custom-call | flops 24999999488 | bytes 1048576 | tf_op jit(solution)/shard_map/encoder_back_fc2/pallas_call | solution.py:1192
  465.4 3.2 add_bitcast_fusion.8
  468.6 2.7 add_bitcast_fusion.7
  471.4 2.7 add_bitcast_fusion.2
  476.5 23.9 %encoder_back_fc1.1 = (f32[8,43,16,128]{3,2,1,0:T(8,128)}, f32[8,42,16,128]{3,2,1,0:T(8,128)}, f32[8,42,16,128]{3,2,1,0:T(8,128)}, f32[8,43,16,128]{3,2,1,0:T(8,...) custom-call(s32[7]{0:T(128)} %pad_add_fusion.refs_0_, ...), custom_call_target="tpu_custom_call", output_to_operand_aliasing={{0}: (6, {}), {1}: (7, {}), {2}: (8, {}), {3}: (9, {}), {4}... | custom-call | flops 20000000000 | bytes 1048576 | tf_op jit(solution)/shard_map/encoder_back_fc1/pallas_call | solution.py:1192
  500.4 6.4 collective-permute-done.13
  508.8 2.5 bitcast_add_fusion.2
  511.3 3.6 bitcast_add_fusion.7
  523.5 4.6 collective-permute-done.19
  528.7 35.3 %encoder_back_attention.1 = (f32[8,43,16,128]{3,2,1,0:T(8,128)}, f32[8,42,16,128]{3,2,1,0:T(8,128)}, f32[8,42,16,128]{3,2,1,0:T(8,128)}, f32[8,43,16,128]{3,2,1,...) custom-call(s32[7]{0:T(128)} %pad_add_fusion.refs_0_, ...), custom_call_target="tpu_custom_call", output_to_operand_aliasing={{0}: (5, {}), {1}: (6, {}), {2}: (7, {}), {3}: (8, {}), {4}... | custom-call | flops 35000000512 | bytes 1048576 | tf_op jit(solution)/shard_map/encoder_back_attention/pallas_call | solution.py:1192
  569.8 2.6 add_bitcast_fusion.6
  572.4 2.6 add_bitcast_fusion.5
  575.0 2.7 add_bitcast_fusion.1
  583.1 4.5 collective-permute-done.22
  589.0 22.6 %encoder_back_qkv.1 = (f32[8,43,16,128]{3,2,1,0:T(8,128)}, f32[8,42,16,128]{3,2,1,0:T(8,128)}, f32[8,42,16,128]{3,2,1,0:T(8,128)}, f32[8,43,16,128]{3,2,1,0:T(8,...) custom-call(s32[7]{0:T(128)} %pad_add_fusion.refs_0_, ...), custom_call_target="tpu_custom_call", output_to_operand_aliasing={{0}: (7, {}), {1}: (8, {}), {2}: (9, {}), {3}: (10, {}), {4... | custom-call | flops 24999999488 | bytes 1048576 | tf_op jit(solution)/shard_map/encoder_back_qkv/pallas_call | solution.py:1192
  611.7 6.8 collective-permute-done.25
  619.7 2.4 fusion.7
  622.1 2.4 fusion.8
  634.7 14.6 %collective-permute-done.29 = f32[2,42,16,128]{3,2,1,0:T(8,128)S(1)} collective-permute-done((f32[2,42,16,128]{3,2,1,0:T(8,128)S(1)}, f32[2,42,16,128]{3,2,1,0:T(8,128)S(1)}, u32[]{:S(2)}, u32[]{:S(2)}) %collective-permute-start.29) | collective-permute-done | bytes 688160 | tf_op jit(solution)/shard_map/ppermute | solution.py:1353
  653.2 13.5 %collective-permute-done.28 = f32[2,43,16,128]{3,2,1,0:T(8,128)S(1)} collective-permute-done((f32[2,43,16,128]{3,2,1,0:T(8,128)S(1)}, f32[2,43,16,128]{3,2,1,0:T(8,128)S(1)}, u32[]{:S(2)}, u32[]{:S(2)}) %collective-permute-start.28) | collective-permute-done | bytes 704544 | tf_op jit(solution)/shard_map/ppermute | solution.py:1353
  668.3 3.6 copy-done.19
  677.9 35.8 %collective-permute-done.35 = f32[42,16,128]{2,1,0:T(8,128)S(1)} collective-permute-done((f32[42,16,128]{2,1,0:T(8,128)S(1)}, f32[42,16,128]{2,1,0:T(8,128)S(1)}, u32[]{:S(2)}, u32[]{:S(2)}) %collective-permute-start.35) | collective-permute-done | bytes 344096 | tf_op jit(solution)/shard_map/ppermute | solution.py:1353
  718.0 3.1 collective-permute-done.34
  726.0 10.6 %collective-permute-done.40 = f32[2,42,16,128]{3,2,1,0:T(8,128)S(1)} collective-permute-done((f32[2,42,16,128]{3,2,1,0:T(8,128)S(1)}, f32[2,42,16,128]{3,2,1,0:T(8,128)S(1)}, u32[]{:S(2)}, u32[]{:S(2)}) %collective-permute-start.40) | collective-permute-done | bytes 688160 | tf_op jit(solution)/shard_map/ppermute | solution.py:1353
  750.5 5.5 collective-permute-start.49
  758.1 24.1 %collective-permute-start.48 = (f32[43,16,128]{2,1,0:T(8,128)S(1)}, f32[43,16,128]{2,1,0:T(8,128)}, u32[]{:S(2)}, u32[]{:S(2)}) collective-permute-start(f32[43,16,128]{2,1,0:T(8,128)S(1)} %fusion.1), channel_id=1, source_target_pairs={{0,8},{1,9},{2,10},{3,11},{4,12},{5,13},{6,14},{7,15},{16,24},{17,... | collective-permute-start | bytes 1056776 | tf_op jit(solution)/shard_map/ppermute | solution.py:1353
  784.9 26.0 %collective-permute-done.53 = f32[42,16,128]{2,1,0:T(8,128)S(1)} collective-permute-done((f32[42,16,128]{2,1,0:T(8,128)}, f32[42,16,128]{2,1,0:T(8,128)S(1)}, u32[]{:S(2)}, u32[]{:S(2)}) %collective-permute-start.53) | collective-permute-done | bytes 344096 | tf_op jit(solution)/shard_map/ppermute | solution.py:1353
  810.8 2.2 collective-permute-start.50
  813.1 5.5 collective-permute-done.51
  829.2 4.4 collective-permute-done.46
  834.7 6.2 collective-permute-done.47
  843.1 54.6 %all-reduce.5.cloned.1.call-done = (f32[42,16,128]{2,1,0:T(8,128)}, f32[43,16,128]{2,1,0:T(8,128)}) async-done(((f32[42,16,128]{2,1,0:T(8,128)}, f32[43,16,128]{2,1,0:T(8,128)}), (f32[42,16,128]{2,1,0:T(8,128)}, f32[43,16,128]{2,1,0:T(8,128)})) %all-reduce.5.cloned.1.call-update) | async-done | bytes 696336 | tf_op jit(solution)/shard_map/psum | solution.py:1486
  897.7 2.4 broadcast_select_fusion
  905.9 3.4 collective-permute-start.57
  911.4 3.0 collective-permute-done.57.tail
  914.4 6.5 unpack_rows.1
  926.6 2.7 collective-permute-start.61
  934.1 2.7 collective-permute-start.64
  948.7 9.9 %update_states.1 = (f32[3747,1,128]{2,1,0:T(1,128)}, f32[3747,1,128]{2,1,0:T(1,128)}, f32[3747,1,128]{2,1,0:T(1,128)}, f32[3747,1,128]{2,1,0:T(1,128)}) custom-call(f32[1]{0:T(128)} %bitcast.112.factor_ref, f32[3760,128]{1,0:T(8,128)S(1)} %copy-done.5, f32[3747,1,128]{2,1,0:T(1,128)S(1)} %bitcast.260, f32[3747,1,128]{2,1,0:T(1,128)S(1)} %bitcast.261, ...), custom_call_target="tpu_custom_call" | custom-call | tf_op jit(solution)/shard_map/update_states/pallas_call | solution.py:333
  (274 shorter events, 143.0 us)
Async XLA Ops:
  7.2 138.8 %all-gather.5.cloned.1.call-start = ((), (), s32[]{:S(2)}) async-start(), calls=%async_computation.1 | async-start | bytes 17166336 | tf_op jit(solution)/shard_map/all_gather | solution.py:1444
  29.3 233.1 %all-gather.3.cloned.1.call-start = ((), (), s32[]{:S(2)}) async-start(), calls=%async_computation | async-start | bytes 17166336 | tf_op jit(solution)/shard_map/all_gather | solution.py:1447
  30.1 867.6 %all-reduce.5.cloned.1.call-start = ((), (), s32[]{:S(2)}) async-start(), calls=%async_computation.2 | async-start | bytes 1392640 | tf_op jit(solution)/shard_map/psum | solution.py:1486
  38.0 11.4 %collective-permute-start.3 = (f32[]{:T(128)}, f32[]{:T(128)}, u32[]{:S(2)}, u32[]{:S(2)}) collective-permute-start(f32[]{:T(128)} %add.1239), channel_id=1, source_target_pairs={{0,3},{1,2},{2,1},{3,0},{4,7},{5,6},{6,5},{7,4},{8,11},{9,10},{10,... | collective-permute-start | bytes 20 | tf_op jit(solution)/shard_map/ppermute | solution.py:1393
  432.1 31.7 %collective-permute-start.9 = (f32[8,43,16,128]{3,2,1,0:T(8,128)}, f32[8,43,16,128]{3,2,1,0:T(8,128)S(1)}, u32[]{:S(2)}, u32[]{:S(2)}) collective-permute-start(f32[8,43,16,128]{3,2,1,0:T(8,128)} %get-tuple-element.290), channel_id=1, source_target_pairs={{0,16},{16,0},{1,17},{17,1},{2,18},{18,2},{3,19},{19,3},{4,20},{20... | collective-permute-start | bytes 8454152 | tf_op jit(solution)/shard_map/ppermute | solution.py:1344
  432.4 31.4 %collective-permute-start.10 = (f32[8,42,16,128]{3,2,1,0:T(8,128)}, f32[8,42,16,128]{3,2,1,0:T(8,128)}, u32[]{:S(2)}, u32[]{:S(2)}) collective-permute-start(f32[8,42,16,128]{3,2,1,0:T(8,128)} %get-tuple-element.291), channel_id=1, source_target_pairs={{0,16},{16,0},{1,17},{17,1},{2,18},{18,2},{3,19},{19,3},{4,20},{20... | collective-permute-start | bytes 8257544 | tf_op jit(solution)/shard_map/ppermute | solution.py:1344
  432.7 31.1 %collective-permute-start.11 = (f32[8,42,16,128]{3,2,1,0:T(8,128)}, f32[8,42,16,128]{3,2,1,0:T(8,128)}, u32[]{:S(2)}, u32[]{:S(2)}) collective-permute-start(f32[8,42,16,128]{3,2,1,0:T(8,128)} %get-tuple-element.292), channel_id=1, source_target_pairs={{0,16},{16,0},{1,17},{17,1},{2,18},{18,2},{3,19},{19,3},{4,20},{20... | collective-permute-start | bytes 8257544 | tf_op jit(solution)/shard_map/ppermute | solution.py:1344
  474.1 32.7 %collective-permute-start.13 = (f32[2,2,42,16,128]{4,3,2,1,0:T(8,128)}, f32[2,2,42,16,128]{4,3,2,1,0:T(8,128)}, u32[]{:S(2)}, u32[]{:S(2)}) collective-permute-start(f32[2,2,42,16,128]{4,3,2,1,0:T(8,128)} %add_bitcast_fusion.8), channel_id=1, source_target_pairs={{0,2},{1,3},{2,0},{3,1},{4,6},{5,7},{6,4},{7,5},{8,10},{9,11},{10,... | collective-permute-start | bytes 4128776 | tf_op jit(solution)/shard_map/ppermute | solution.py:1353
  475.6 32.4 %collective-permute-start.14 = (f32[2,2,42,16,128]{4,3,2,1,0:T(8,128)}, f32[2,2,42,16,128]{4,3,2,1,0:T(8,128)}, u32[]{:S(2)}, u32[]{:S(2)}) collective-permute-start(f32[2,2,42,16,128]{4,3,2,1,0:T(8,128)} %add_bitcast_fusion.7), channel_id=1, source_target_pairs={{0,4},{1,5},{2,6},{3,7},{4,0},{5,1},{6,2},{7,3},{8,12},{9,13},{10,... | collective-permute-start | bytes 4128776 | tf_op jit(solution)/shard_map/ppermute | solution.py:1353
  476.0 32.8 %collective-permute-start.12 = (f32[2,2,43,16,128]{4,3,2,1,0:T(8,128)}, f32[2,2,43,16,128]{4,3,2,1,0:T(8,128)}, u32[]{:S(2)}, u32[]{:S(2)}) collective-permute-start(f32[2,2,43,16,128]{4,3,2,1,0:T(8,128)} %add_bitcast_fusion.2), channel_id=1, source_target_pairs={{0,1},{1,0},{2,3},{3,2},{4,5},{5,4},{6,7},{7,6},{8,9},{9,8},{10,11... | collective-permute-start | bytes 4227080 | tf_op jit(solution)/shard_map/ppermute | solution.py:1353
  514.9 13.8 %collective-permute-start.18 = (f32[8,43,16,128]{3,2,1,0:T(8,128)S(1)}, f32[8,43,16,128]{3,2,1,0:T(8,128)}, u32[]{:S(2)}, u32[]{:S(2)}) collective-permute-start(f32[8,43,16,128]{3,2,1,0:T(8,128)S(1)} %copy-done.41), channel_id=1, source_target_pairs={{0,16},{16,0},{1,17},{17,1},{2,18},{18,2},{3,19},{19,3},{4,20},{20... | collective-permute-start | bytes 8454152 | tf_op jit(solution)/shard_map/ppermute | solution.py:1344
  514.9 13.2 %collective-permute-start.19 = (f32[8,42,16,128]{3,2,1,0:T(8,128)S(1)}, f32[8,42,16,128]{3,2,1,0:T(8,128)}, u32[]{:S(2)}, u32[]{:S(2)}) collective-permute-start(f32[8,42,16,128]{3,2,1,0:T(8,128)S(1)} %copy-done.44), channel_id=1, source_target_pairs={{0,16},{16,0},{1,17},{17,1},{2,18},{18,2},{3,19},{19,3},{4,20},{20... | collective-permute-start | bytes 8257544 | tf_op jit(solution)/shard_map/ppermute | solution.py:1344
  515.4 13.2 %collective-permute-start.20 = (f32[8,42,16,128]{3,2,1,0:T(8,128)}, f32[8,42,16,128]{3,2,1,0:T(8,128)}, u32[]{:S(2)}, u32[]{:S(2)}) collective-permute-start(f32[8,42,16,128]{3,2,1,0:T(8,128)} %get-tuple-element.422.refs_16_), channel_id=1, source_target_pairs={{0,16},{16,0},{1,17},{17,1},{2,18},{18,2},{3,19},{19,3},{4,20},{20... | collective-permute-start | bytes 8257544 | tf_op jit(solution)/shard_map/ppermute | solution.py:1344
  515.5 48.4 %collective-permute-start.16 = (f32[2,42,16,128]{3,2,1,0:T(8,128)}, f32[2,42,16,128]{3,2,1,0:T(8,128)}, u32[]{:S(2)}, u32[]{:S(2)}) collective-permute-start(f32[2,42,16,128]{3,2,1,0:T(8,128)} %get-tuple-element.403), channel_id=1, source_target_pairs={{0,4},{1,5},{2,6},{3,7},{4,0},{5,1},{6,2},{7,3},{8,12},{9,13},{10,... | collective-permute-start | bytes 2064392 | tf_op jit(solution)/shard_map/ppermute | solution.py:1353
  517.1 46.8 %collective-permute-start.17 = (f32[2,42,16,128]{3,2,1,0:T(8,128)}, f32[2,42,16,128]{3,2,1,0:T(8,128)}, u32[]{:S(2)}, u32[]{:S(2)}) collective-permute-start(f32[2,42,16,128]{3,2,1,0:T(8,128)} %get-tuple-element.404), channel_id=1, source_target_pairs={{0,1},{1,0},{2,3},{3,2},{4,5},{5,4},{6,7},{7,6},{8,9},{9,8},{10,11... | collective-permute-start | bytes 2064392 | tf_op jit(solution)/shard_map/ppermute | solution.py:1353
  528.1 35.9 %collective-permute-start.15 = (f32[2,43,16,128]{3,2,1,0:T(8,128)}, f32[2,43,16,128]{3,2,1,0:T(8,128)S(1)}, u32[]{:S(2)}, u32[]{:S(2)}) collective-permute-start(f32[2,43,16,128]{3,2,1,0:T(8,128)} %bitcast_add_fusion.2), channel_id=1, source_target_pairs={{0,2},{1,3},{2,0},{3,1},{4,6},{5,7},{6,4},{7,5},{8,10},{9,11},{10,... | collective-permute-start | bytes 2113544 | tf_op jit(solution)/shard_map/ppermute | solution.py:1353
  579.1 32.6 %collective-permute-start.23 = (f32[42,16,128]{2,1,0:T(8,128)}, f32[42,16,128]{2,1,0:T(8,128)}, u32[]{:S(2)}, u32[]{:S(2)}) collective-permute-start(f32[42,16,128]{2,1,0:T(8,128)} %bitcast_add_fusion.41), channel_id=1, source_target_pairs={{0,2},{1,3},{2,0},{3,1},{4,6},{5,7},{6,4},{7,5},{8,10},{9,11},{10,... | collective-permute-start | bytes 1032200 | tf_op jit(solution)/shard_map/ppermute | solution.py:1353
  579.7 32.0 %collective-permute-start.21 = (f32[43,16,128]{2,1,0:T(8,128)}, f32[43,16,128]{2,1,0:T(8,128)S(1)}, u32[]{:S(2)}, u32[]{:S(2)}) collective-permute-start(f32[43,16,128]{2,1,0:T(8,128)} %bitcast_add_fusion.19), channel_id=1, source_target_pairs={{0,4},{1,5},{2,6},{3,7},{4,0},{5,1},{6,2},{7,3},{8,12},{9,13},{10,... | collective-permute-start | bytes 1056776 | tf_op jit(solution)/shard_map/ppermute | solution.py:1353
  581.3 37.1 %collective-permute-start.25 = (f32[2,2,42,16,128]{4,3,2,1,0:T(8,128)}, f32[2,2,42,16,128]{4,3,2,1,0:T(8,128)}, u32[]{:S(2)}, u32[]{:S(2)}) collective-permute-start(f32[2,2,42,16,128]{4,3,2,1,0:T(8,128)} %add_bitcast_fusion.6), channel_id=1, source_target_pairs={{0,2},{1,3},{2,0},{3,1},{4,6},{5,7},{6,4},{7,5},{8,10},{9,11},{10,... | collective-permute-start | bytes 4128776 | tf_op jit(solution)/shard_map/ppermute | solution.py:1353
  582.7 36.2 %collective-permute-start.26 = (f32[2,2,42,16,128]{4,3,2,1,0:T(8,128)}, f32[2,2,42,16,128]{4,3,2,1,0:T(8,128)}, u32[]{:S(2)}, u32[]{:S(2)}) collective-permute-start(f32[2,2,42,16,128]{4,3,2,1,0:T(8,128)} %add_bitcast_fusion.5), channel_id=1, source_target_pairs={{0,4},{1,5},{2,6},{3,7},{4,0},{5,1},{6,2},{7,3},{8,12},{9,13},{10,... | collective-permute-start | bytes 4128776 | tf_op jit(solution)/shard_map/ppermute | solution.py:1353
  587.6 32.1 %collective-permute-start.24 = (f32[2,2,43,16,128]{4,3,2,1,0:T(8,128)}, f32[2,2,43,16,128]{4,3,2,1,0:T(8,128)}, u32[]{:S(2)}, u32[]{:S(2)}) collective-permute-start(f32[2,2,43,16,128]{4,3,2,1,0:T(8,128)} %add_bitcast_fusion.1), channel_id=1, source_target_pairs={{0,1},{1,0},{2,3},{3,2},{4,5},{5,4},{6,7},{7,6},{8,9},{9,8},{10,11... | collective-permute-start | bytes 4227080 | tf_op jit(solution)/shard_map/ppermute | solution.py:1353
  630.9 37.0 %collective-permute-start.31 = (f32[8,42,16,128]{3,2,1,0:T(8,128)S(1)}, f32[8,42,16,128]{3,2,1,0:T(8,128)S(1)}, u32[]{:S(2)}, u32[]{:S(2)}) collective-permute-start(f32[8,42,16,128]{3,2,1,0:T(8,128)S(1)} %copy-done.42), channel_id=1, source_target_pairs={{0,16},{16,0},{1,17},{17,1},{2,18},{18,2},{3,19},{19,3},{4,20},{20... | collective-permute-start | bytes 8257544 | tf_op jit(solution)/shard_map/ppermute | solution.py:1344
  631.0 37.1 %collective-permute-start.32 = (f32[8,42,16,128]{3,2,1,0:T(8,128)S(1)}, f32[8,42,16,128]{3,2,1,0:T(8,128)S(1)}, u32[]{:S(2)}, u32[]{:S(2)}) collective-permute-start(f32[8,42,16,128]{3,2,1,0:T(8,128)S(1)} %copy-done.43), channel_id=1, source_target_pairs={{0,16},{16,0},{1,17},{17,1},{2,18},{18,2},{3,19},{19,3},{4,20},{20... | collective-permute-start | bytes 8257544 | tf_op jit(solution)/shard_map/ppermute | solution.py:1344
  631.5 36.9 %collective-permute-start.27 = (f32[8,43,16,128]{3,2,1,0:T(8,128)S(1)}, f32[8,43,16,128]{3,2,1,0:T(8,128)S(1)}, u32[]{:S(2)}, u32[]{:S(2)}) collective-permute-start(f32[8,43,16,128]{3,2,1,0:T(8,128)S(1)} %copy-done.40), channel_id=1, source_target_pairs={{0,16},{16,0},{1,17},{17,1},{2,18},{18,2},{3,19},{19,3},{4,20},{20... | collective-permute-start | bytes 8454152 | tf_op jit(solution)/shard_map/ppermute | solution.py:1344
  631.5 17.8 %collective-permute-start.29 = (f32[2,42,16,128]{3,2,1,0:T(8,128)S(1)}, f32[2,42,16,128]{3,2,1,0:T(8,128)S(1)}, u32[]{:S(2)}, u32[]{:S(2)}) collective-permute-start(f32[2,42,16,128]{3,2,1,0:T(8,128)S(1)} %bitcast_add_fusion.6), channel_id=1, source_target_pairs={{0,4},{1,5},{2,6},{3,7},{4,0},{5,1},{6,2},{7,3},{8,12},{9,13},{10,... | collective-permute-start | bytes 2064392 | tf_op jit(solution)/shard_map/ppermute | solution.py:1353
  633.2 18.8 %collective-permute-start.30 = (f32[2,42,16,128]{3,2,1,0:T(8,128)S(1)}, f32[2,42,16,128]{3,2,1,0:T(8,128)S(1)}, u32[]{:S(2)}, u32[]{:S(2)}) collective-permute-start(f32[2,42,16,128]{3,2,1,0:T(8,128)S(1)} %bitcast_add_fusion.5), channel_id=1, source_target_pairs={{0,1},{1,0},{2,3},{3,2},{4,5},{5,4},{6,7},{7,6},{8,9},{9,8},{10,11... | collective-permute-start | bytes 2064392 | tf_op jit(solution)/shard_map/ppermute | solution.py:1353
  649.3 17.3 %collective-permute-start.28 = (f32[2,43,16,128]{3,2,1,0:T(8,128)S(1)}, f32[2,43,16,128]{3,2,1,0:T(8,128)S(1)}, u32[]{:S(2)}, u32[]{:S(2)}) collective-permute-start(f32[2,43,16,128]{3,2,1,0:T(8,128)S(1)} %bitcast_add_fusion.1), channel_id=1, source_target_pairs={{0,2},{1,3},{2,0},{3,1},{4,6},{5,7},{6,4},{7,5},{8,10},{9,11},{10,... | collective-permute-start | bytes 2113544 | tf_op jit(solution)/shard_map/ppermute | solution.py:1353
  672.2 50.1 %collective-permute-start.37 = (f32[2,2,42,16,128]{4,3,2,1,0:T(8,128)S(1)}, f32[2,2,42,16,128]{4,3,2,1,0:T(8,128)S(1)}, u32[]{:S(2)}, u32[]{:S(2)}) collective-permute-start(f32[2,2,42,16,128]{4,3,2,1,0:T(8,128)S(1)} %add_bitcast_fusion.4), channel_id=1, source_target_pairs={{0,2},{1,3},{2,0},{3,1},{4,6},{5,7},{6,4},{7,5},{8,10},{9,11},{10,... | collective-permute-start | bytes 4128776 | tf_op jit(solution)/shard_map/ppermute | solution.py:1353
  673.7 48.8 %collective-permute-start.38 = (f32[2,2,42,16,128]{4,3,2,1,0:T(8,128)S(1)}, f32[2,2,42,16,128]{4,3,2,1,0:T(8,128)S(1)}, u32[]{:S(2)}, u32[]{:S(2)}) collective-permute-start(f32[2,2,42,16,128]{4,3,2,1,0:T(8,128)S(1)} %add_bitcast_fusion.3), channel_id=1, source_target_pairs={{0,4},{1,5},{2,6},{3,7},{4,0},{5,1},{6,2},{7,3},{8,12},{9,13},{10,... | collective-permute-start | bytes 4128776 | tf_op jit(solution)/shard_map/ppermute | solution.py:1353
  675.3 47.3 %collective-permute-start.33 = (f32[2,2,43,16,128]{4,3,2,1,0:T(8,128)S(1)}, f32[2,2,43,16,128]{4,3,2,1,0:T(8,128)S(1)}, u32[]{:S(2)}, u32[]{:S(2)}) collective-permute-start(f32[2,2,43,16,128]{4,3,2,1,0:T(8,128)S(1)} %add_bitcast_fusion), channel_id=1, source_target_pairs={{0,1},{1,0},{2,3},{3,2},{4,5},{5,4},{6,7},{7,6},{8,9},{9,8},{10,11... | collective-permute-start | bytes 4227080 | tf_op jit(solution)/shard_map/ppermute | solution.py:1353
  676.0 37.6 %collective-permute-start.35 = (f32[42,16,128]{2,1,0:T(8,128)S(1)}, f32[42,16,128]{2,1,0:T(8,128)S(1)}, u32[]{:S(2)}, u32[]{:S(2)}) collective-permute-start(f32[42,16,128]{2,1,0:T(8,128)S(1)} %bitcast_add_fusion.35), channel_id=1, source_target_pairs={{0,1},{1,0},{2,3},{3,2},{4,5},{5,4},{6,7},{7,6},{8,9},{9,8},{10,11... | collective-permute-start | bytes 1032200 | tf_op jit(solution)/shard_map/ppermute | solution.py:1353
  677.4 38.7 %collective-permute-start.36 = (f32[42,16,128]{2,1,0:T(8,128)S(1)}, f32[42,16,128]{2,1,0:T(8,128)S(1)}, u32[]{:S(2)}, u32[]{:S(2)}) collective-permute-start(f32[42,16,128]{2,1,0:T(8,128)S(1)} %bitcast_add_fusion.33), channel_id=1, source_target_pairs={{0,2},{1,3},{2,0},{3,1},{4,6},{5,7},{6,4},{7,5},{8,10},{9,11},{10,... | collective-permute-start | bytes 1032200 | tf_op jit(solution)/shard_map/ppermute | solution.py:1353
  722.8 13.8 %collective-permute-start.40 = (f32[2,42,16,128]{3,2,1,0:T(8,128)S(1)}, f32[2,42,16,128]{3,2,1,0:T(8,128)S(1)}, u32[]{:S(2)}, u32[]{:S(2)}) collective-permute-start(f32[2,42,16,128]{3,2,1,0:T(8,128)S(1)} %bitcast_add_fusion.4), channel_id=1, source_target_pairs={{0,4},{1,5},{2,6},{3,7},{4,0},{5,1},{6,2},{7,3},{8,12},{9,13},{10,... | collective-permute-start | bytes 2064392 | tf_op jit(solution)/shard_map/ppermute | solution.py:1353
  723.3 14.2 %collective-permute-start.41 = (f32[2,42,16,128]{3,2,1,0:T(8,128)S(1)}, f32[2,42,16,128]{3,2,1,0:T(8,128)S(1)}, u32[]{:S(2)}, u32[]{:S(2)}) collective-permute-start(f32[2,42,16,128]{3,2,1,0:T(8,128)S(1)} %bitcast_add_fusion.3), channel_id=1, source_target_pairs={{0,1},{1,0},{2,3},{3,2},{4,5},{5,4},{6,7},{7,6},{8,9},{9,8},{10,11... | collective-permute-start | bytes 2064392 | tf_op jit(solution)/shard_map/ppermute | solution.py:1353
  724.1 14.4 %collective-permute-start.39 = (f32[2,43,16,128]{3,2,1,0:T(8,128)S(1)}, f32[2,43,16,128]{3,2,1,0:T(8,128)S(1)}, u32[]{:S(2)}, u32[]{:S(2)}) collective-permute-start(f32[2,43,16,128]{3,2,1,0:T(8,128)S(1)} %bitcast_add_fusion), channel_id=1, source_target_pairs={{0,2},{1,3},{2,0},{3,1},{4,6},{5,7},{6,4},{7,5},{8,10},{9,11},{10,... | collective-permute-start | bytes 2113544 | tf_op jit(solution)/shard_map/ppermute | solution.py:1353
  725.5 13.9 %collective-permute-start.55 = (f32[1,42,16,128]{3,2,1,0:T(8,128)S(1)}, f32[1,42,16,128]{3,2,1,0:T(8,128)S(1)}, u32[]{:S(2)}, u32[]{:S(2)}) collective-permute-start(f32[1,42,16,128]{3,2,1,0:T(8,128)S(1)} %copy-done.46), channel_id=1, source_target_pairs={{0,16},{16,0},{1,17},{17,1},{2,18},{18,2},{3,19},{19,3},{4,20},{20... | collective-permute-start | bytes 1032200 | tf_op jit(solution)/shard_map/ppermute | solution.py:1475
  725.5 16.0 %collective-permute-start.54 = (f32[1,43,16,128]{3,2,1,0:T(8,128)S(1)}, f32[1,43,16,128]{3,2,1,0:T(8,128)S(1)}, u32[]{:S(2)}, u32[]{:S(2)}) collective-permute-start(f32[1,43,16,128]{3,2,1,0:T(8,128)S(1)} %copy-done.45), channel_id=1, source_target_pairs={{0,16},{16,0},{1,17},{17,1},{2,18},{18,2},{3,19},{19,3},{4,20},{20... | collective-permute-start | bytes 1056776 | tf_op jit(solution)/shard_map/ppermute | solution.py:1475
  740.1 10.3 %collective-permute-start.44 = (f32[42,16,128]{2,1,0:T(8,128)}, f32[42,16,128]{2,1,0:T(8,128)}, u32[]{:S(2)}, u32[]{:S(2)}) collective-permute-start(f32[42,16,128]{2,1,0:T(8,128)} %bitcast_add_fusion.25), channel_id=1, source_target_pairs={{0,2},{1,3},{2,0},{3,1},{4,6},{5,7},{6,4},{7,5},{8,10},{9,11},{10,... | collective-permute-start | bytes 1032200 | tf_op jit(solution)/shard_map/ppermute | solution.py:1353
  742.4 41.2 %collective-permute-start.52 = (f32[42,16,128]{2,1,0:T(8,128)}, f32[42,16,128]{2,1,0:T(8,128)S(1)}, u32[]{:S(2)}, u32[]{:S(2)}) collective-permute-start(f32[42,16,128]{2,1,0:T(8,128)} %fusion.8), channel_id=1, source_target_pairs={{8,0},{9,1},{10,2},{11,3},{12,4},{13,5},{14,6},{15,7},{24,16},{25,... | collective-permute-start | bytes 1032200 | tf_op jit(solution)/shard_map/ppermute | solution.py:1353
  743.8 67.0 %collective-permute-start.53 = (f32[42,16,128]{2,1,0:T(8,128)}, f32[42,16,128]{2,1,0:T(8,128)S(1)}, u32[]{:S(2)}, u32[]{:S(2)}) collective-permute-start(f32[42,16,128]{2,1,0:T(8,128)} %fusion.7), channel_id=1, source_target_pairs={{8,0},{9,1},{10,2},{11,3},{12,4},{13,5},{14,6},{15,7},{24,16},{25,... | collective-permute-start | bytes 1032200 | tf_op jit(solution)/shard_map/ppermute | solution.py:1353
  745.1 73.4 %collective-permute-start.51 = (f32[43,16,128]{2,1,0:T(8,128)S(1)}, f32[43,16,128]{2,1,0:T(8,128)S(1)}, u32[]{:S(2)}, u32[]{:S(2)}) collective-permute-start(f32[43,16,128]{2,1,0:T(8,128)S(1)} %fusion.2), channel_id=1, source_target_pairs={{8,0},{9,1},{10,2},{11,3},{12,4},{13,5},{14,6},{15,7},{24,16},{25,... | collective-permute-start | bytes 1056776 | tf_op jit(solution)/shard_map/ppermute | solution.py:1353
  746.4 11.7 %collective-permute-start.42 = (f32[43,16,128]{2,1,0:T(8,128)S(1)}, f32[43,16,128]{2,1,0:T(8,128)S(1)}, u32[]{:S(2)}, u32[]{:S(2)}) collective-permute-start(f32[43,16,128]{2,1,0:T(8,128)S(1)} %bitcast_add_fusion.9), channel_id=1, source_target_pairs={{0,4},{1,5},{2,6},{3,7},{4,0},{5,1},{6,2},{7,3},{8,12},{9,13},{10,... | collective-permute-start | bytes 1056776 | tf_op jit(solution)/shard_map/ppermute | solution.py:1353
  750.5 70.1 %collective-permute-start.49 = (f32[42,16,128]{2,1,0:T(8,128)}, f32[42,16,128]{2,1,0:T(8,128)S(1)}, u32[]{:S(2)}, u32[]{:S(2)}) collective-permute-start(f32[42,16,128]{2,1,0:T(8,128)} %fusion.6), channel_id=1, source_target_pairs={{0,8},{1,9},{2,10},{3,11},{4,12},{5,13},{6,14},{7,15},{16,24},{17,... | collective-permute-start | bytes 1032200 | tf_op jit(solution)/shard_map/ppermute | solution.py:1353
  758.1 70.0 %collective-permute-start.48 = (f32[43,16,128]{2,1,0:T(8,128)S(1)}, f32[43,16,128]{2,1,0:T(8,128)}, u32[]{:S(2)}, u32[]{:S(2)}) collective-permute-start(f32[43,16,128]{2,1,0:T(8,128)S(1)} %fusion.1), channel_id=1, source_target_pairs={{0,8},{1,9},{2,10},{3,11},{4,12},{5,13},{6,14},{7,15},{16,24},{17,... | collective-permute-start | bytes 1056776 | tf_op jit(solution)/shard_map/ppermute | solution.py:1353
  783.6 58.5 %collective-permute-start.45 = (f32[43,16,128]{2,1,0:T(8,128)S(1)}, f32[43,16,128]{2,1,0:T(8,128)}, u32[]{:S(2)}, u32[]{:S(2)}) collective-permute-start(f32[43,16,128]{2,1,0:T(8,128)S(1)} %fusion), channel_id=1, source_target_pairs={{8,0},{9,1},{10,2},{11,3},{12,4},{13,5},{14,6},{15,7},{24,16},{25,... | collective-permute-start | bytes 1056776 | tf_op jit(solution)/shard_map/ppermute | solution.py:1353
  810.8 16.3 %collective-permute-start.50 = (f32[42,16,128]{2,1,0:T(8,128)S(1)}, f32[42,16,128]{2,1,0:T(8,128)}, u32[]{:S(2)}, u32[]{:S(2)}) collective-permute-start(f32[42,16,128]{2,1,0:T(8,128)S(1)} %copy-done.27), channel_id=1, source_target_pairs={{0,8},{1,9},{2,10},{3,11},{4,12},{5,13},{6,14},{7,15},{16,24},{17,... | collective-permute-start | bytes 1032200 | tf_op jit(solution)/shard_map/ppermute | solution.py:1353
  819.3 14.3 %collective-permute-start.46 = (f32[42,16,128]{2,1,0:T(8,128)}, f32[42,16,128]{2,1,0:T(8,128)}, u32[]{:S(2)}, u32[]{:S(2)}) collective-permute-start(f32[42,16,128]{2,1,0:T(8,128)} %fusion.4), channel_id=1, source_target_pairs={{8,0},{9,1},{10,2},{11,3},{12,4},{13,5},{14,6},{15,7},{24,16},{25,... | collective-permute-start | bytes 1032200 | tf_op jit(solution)/shard_map/ppermute | solution.py:1353
  821.3 19.5 %collective-permute-start.47 = (f32[42,16,128]{2,1,0:T(8,128)}, f32[42,16,128]{2,1,0:T(8,128)}, u32[]{:S(2)}, u32[]{:S(2)}) collective-permute-start(f32[42,16,128]{2,1,0:T(8,128)} %fusion.3), channel_id=1, source_target_pairs={{8,0},{9,1},{10,2},{11,3},{12,4},{13,5},{14,6},{15,7},{24,16},{25,... | collective-permute-start | bytes 1032200 | tf_op jit(solution)/shard_map/ppermute | solution.py:1353
  (68 other events, 817.7 us)
Sparse Core Ops, SparseCore 0:
  29.4 116.5 all-gather.4
  148.9 113.5 all-gather.2
  742.5 155.1 all-reduce.4

commit v3 on v2

--- a/solution.py
+++ b/solution.py
@@ -135,8 +135,8 @@
         self.units = units + VEC_UNITS
         self.half = self.units // 2
         half = self.half
+        self.quarter = -(-half // 2)
         self.part_cuts = [0, -(-half // 3), -(-2 * half // 3), half]
-        self.cuts = self.part_cuts[:-1] + [half + c for c in self.part_cuts]
         self.half_cuts = [0, half, self.units]
         self.head_rows = 8 * -(-max(16 * max(s.panels.values()) for s in self.sections) // 8)
         self.tail_units = max(max(s.panels.values()) for s in self.sections)
@@ -165,15 +165,15 @@
         main = 1 << (used.bit_length() - 1)
         return [(0, main), (main, max(used - main, 1))]
 
-    def tail_parts(self):
+    def tail_used(self):
         first, count = self.bins(1)[1]
         section = self.sections[1]
-        most = max(section.fill[first : first + count], default=0)
-        if any(v[2] >= first for v in section.vectors.values()):
-            most = self.units
-        held = [u % self.half for u in range(most)]
-        cuts = self.part_cuts
-        return [p for p in range(3) if any(cuts[p] <= u < cuts[p + 1] for u in held)]
+        assert count == 1 and all(v[2] < first for v in section.vectors.values())
+        used = section.fill[first]
+        return min(used, self.half), max(used - self.half, 0)
+
+    def bin_units(self, s):
+        return [self.half, self.half if s == 0 else max(self.tail_used())]
 
     def place(self, s, block, block_row, flat_row):
         local = flat_row - block * self.shard_rows
@@ -237,7 +237,7 @@
     )(index, flat, following)
 
 
-def unpack_kernel(zero_row, rows, index_ref, block, tail, out_ref, squares, held):
+def unpack_kernel(zero_row, rows, index_ref, block, tail, out_ref, held):
     at = 0
     for source in (block, tail):
         size = source.shape[0] * 16
@@ -247,26 +247,15 @@
     out_ref[pl.ds(out_ref.shape[0] - 16, 16), :] = jnp.zeros((16, 128), F32)
     move_rows_in(index_ref, held, out_ref, rows)
 
-    def body(i, total):
-        value = out_ref[pl.ds(pl.multiple_of(i * 8, 8), 8), :]
-        return total + value * value
-
-    squares[...] = lax.fori_loop(
-        0, out_ref.shape[0] // 8, body, jnp.zeros((8, 128), F32), unroll=8
-    )
-
 
 def unpack(plan, index, block, tail):
     rows = plan.shard_rows
     padded = 16 * -(-rows // 16)
     return pl.pallas_call(
         functools.partial(unpack_kernel, plan.zero_row, rows),
-        out_shape=[
-            jax.ShapeDtypeStruct((padded, 128), F32),
-            jax.ShapeDtypeStruct((8, 128), F32),
-        ],
+        out_shape=jax.ShapeDtypeStruct((padded, 128), F32),
         in_specs=[IN_SMEM, IN_VMEM, IN_VMEM],
-        out_specs=[IN_VMEM, IN_VMEM],
+        out_specs=IN_VMEM,
         scratch_shapes=[pltpu.VMEM((plan.zero_row + 8, 128), F32)],
         compiler_params=pltpu.CompilerParams(vmem_limit_bytes=32 * 1024 * 1024),
         name="unpack_rows",
@@ -340,7 +329,7 @@
             pltpu.SemaphoreType.DMA((count, 4)),
             pltpu.SemaphoreType.DMA((count, 4)),
         ],
-        compiler_params=pltpu.CompilerParams(vmem_limit_bytes=40 * 1024 * 1024),
+        compiler_params=pltpu.CompilerParams(vmem_limit_bytes=VMEM_BYTES),
         name="update_states",
     )(factor, total, *states)
 
@@ -355,6 +344,13 @@
 
 def dot_tn(a, b):
     return lax.dot_general(a, b, (((0,), (0,)), ((), ())), preferred_element_type=F32)
+
+
+def total_of(terms):
+    total = terms[0]
+    for term in terms[1:]:
+        total = total + term
+    return total
 
 
 def for_rows(count, size, step, unroll=1):
@@ -378,13 +374,29 @@
     return jnp.concatenate(parts, axis=1)
 
 
-def times_columns(left, weight, panels, depth, acc, finish):
+def row_chunks(count):
+    size = next(n for n in (208, 224, 112, 104, 16) if count % n == 0)
+    return [slice(at, at + size) for at in range(0, count, size)]
+
+
+def times_columns(left, weight, panels, depth, finish):
     def body(pair, carry):
-        acc[...] = dot(left[...], columns(weight, panels, depth, pair))
-        finish(pair)
+        right = columns(weight, panels, depth, pair)
+        for here in row_chunks(left.shape[0]):
+            finish(pair, here, dot(left[here, :], right))
         return carry
 
     lax.fori_loop(0, panels // 2, body, 0)
+
+
+def times_bands(left, weight, panels, count, finish):
+    def body(band, carry):
+        right = row_band(weight, panels, band)
+        for here in row_chunks(left.shape[0]):
+            finish(here, lanes(band), dot_nt(left[here, :], right))
+        return carry
+
+    lax.fori_loop(0, count // 256, body, 0)
 
 
 def lanes(pair):
@@ -442,6 +454,14 @@
     ]
 
 
+def softmax_columns(scores, limit):
+    key = lax.broadcasted_iota(jnp.int32, scores.shape, 0)
+    scores = jnp.where(key < limit, scores, -1e30)
+    top = jnp.max(scores, axis=0, keepdims=True)
+    raised = jnp.exp(scores - top)
+    return raised * (1.0 / jnp.sum(raised, axis=0, keepdims=True))
+
+
 def softmax_rows(scores, limit):
     key = lax.broadcasted_iota(jnp.int32, scores.shape, 1)
     scores = jnp.where(key < limit, scores, -1e30)
@@ -463,14 +483,12 @@
 
         query, keys, values = part(0), part(1), part(2)
         limit = limit_of(image)
-        total = jnp.zeros((rows, 128), F32)
-        for mask in masks:
-            probs = softmax_rows(dot_nt(query * mask, keys), limit).astype(BF16)
-            total = total + dot(probs, values * mask)
+        probs = [softmax_rows(dot_nt(query * mask, keys), limit).astype(BF16) for mask in masks]
+        total = total_of([dot(p, values) * m.astype(F32) for p, m in zip(probs, masks)])
         out[here, pl.ds(pl.multiple_of(panel * 128, 128), 128)] = total.astype(BF16)
         return carry
 
-    lax.fori_loop(0, images * panels, body, 0)
+    lax.fori_loop(0, images * panels, body, 0, unroll=4)
 
 
 def attention_backward(mixed, grad_out, grad_mixed, limit_of, images, rows, width, size):
@@ -486,25 +504,27 @@
 
         query, keys, values = (mixed[here, place(third)] for third in range(3))
         grad = grad_out[here, place(0)]
+        turned = keys.T
         limit = limit_of(image)
         zero = jnp.zeros((rows, 128), F32)
-        grad_query, grad_keys, grad_values = zero, zero, zero
-        for mask in masks:
+        grad_query, grad_keys, grad_values = [], zero, zero
+        for h, mask in enumerate(masks):
             masked_query = query * mask
             masked_grad = grad * mask
-            probs = softmax_rows(dot_nt(masked_query, keys), limit)
-            grad_probs = dot_nt(masked_grad, values)
-            inner = jnp.sum(probs * grad_probs, axis=1, keepdims=True)
+            probs = softmax_columns(dot_nt(keys, masked_query), limit)
+            grad_probs = dot_nt(values, masked_grad)
+            inner = jnp.sum(probs * grad_probs, axis=0, keepdims=True)
             grad_scores = (probs * (grad_probs - inner)).astype(BF16)
-            grad_values = grad_values + dot_tn(probs.astype(BF16), masked_grad)
-            grad_query = grad_query + dot(grad_scores, keys * mask)
-            grad_keys = grad_keys + dot_tn(grad_scores, masked_query)
-        grad_mixed[here, place(0)] = (grad_query * (1.0 / math.sqrt(size))).astype(BF16)
+            grad_values = grad_values + dot(probs.astype(BF16), masked_grad)
+            grad_keys = grad_keys + dot(grad_scores, masked_query)
+            grad_query.append(dot(turned[h * size : h * size + size, :], grad_scores))
+        grad_query = jnp.concatenate(grad_query, axis=0) * (1.0 / math.sqrt(size))
+        grad_mixed[here, place(0)] = grad_query.astype(BF16).T
         grad_mixed[here, place(1)] = grad_keys.astype(BF16)
         grad_mixed[here, place(2)] = grad_values.astype(BF16)
         return carry
 
-    lax.fori_loop(0, images * panels, body, 0)
+    lax.fori_loop(0, images * panels, body, 0, unroll=2)
 
 
 def gelu_parts(value):
@@ -521,57 +541,45 @@
         self.count = images * rows
 
 
-def block_forward(sh, x0, n1, mixed, o, x1, n2, g, gp, y, w, vec, limit_of, acc, ready, saved):
+def block_forward(sh, x0, n1, mixed, o, x1, n2, g, gp, y, w, vec, limit_of, ready, saved):
     width, hidden, count = sh.width, sh.hidden, sh.count
     panels = width // 128
     norm_forward(x0, vec("g1"), vec("b1"), n1, count, width)
     saved(n1)
     ready("qkv")
 
-    def put_mixed(pair):
+    def put_mixed(pair, here, value):
         scale = jnp.where(pair < panels // 2, 1.0 / math.sqrt(sh.size), 1.0)
-
-        def step(at):
-            mixed[pl.ds(at, 16), lanes(pair)] = (acc[pl.ds(at, 16), :] * scale).astype(BF16)
-
-        for_rows(count, 16, step, 4)
-
-    times_columns(n1, w["qkv"], 3 * panels, width, acc, put_mixed)
+        mixed[here, lanes(pair)] = (value * scale).astype(BF16)
+
+    times_columns(n1, w["qkv"], 3 * panels, width, put_mixed)
     saved(mixed)
     attention_forward(mixed, o, limit_of, sh.images, sh.rows, width, sh.size)
     saved(o)
     ready("proj")
 
     def put_sum(base, out):
-        def finish(pair):
-            def step(at):
-                here = pl.ds(at, 16)
-                out[here, lanes(pair)] = base[here, lanes(pair)] + acc[here, :]
-
-            for_rows(count, 16, step, 4)
+        def finish(pair, here, value):
+            out[here, lanes(pair)] = base[here, lanes(pair)] + value
 
         return finish
 
-    times_columns(o, w["proj"], panels, width, acc, put_sum(x0, x1))
+    times_columns(o, w["proj"], panels, width, put_sum(x0, x1))
     saved(x1)
     norm_forward(x1, vec("g2"), vec("b2"), n2, count, width)
     saved(n2)
     ready("fc1")
 
-    def put_hidden(pair):
-        def step(at):
-            here = pl.ds(at, 16)
-            value, slope = gelu_parts(acc[here, :])
-            g[here, lanes(pair)] = value.astype(BF16)
-            gp[here, lanes(pair)] = slope
-
-        for_rows(count, 16, step, 2)
-
-    times_columns(n2, w["fc1"], hidden // 128, width, acc, put_hidden)
+    def put_hidden(pair, here, value):
+        value, slope = gelu_parts(value)
+        g[here, lanes(pair)] = value.astype(BF16)
+        gp[here, lanes(pair)] = slope
+
+    times_columns(n2, w["fc1"], hidden // 128, width, put_hidden)
     saved(g)
     saved(gp)
     ready("fc2")
-    times_columns(g, w["fc2"], panels, hidden, acc, put_sum(x1, y))
+    times_columns(g, w["fc2"], panels, hidden, put_sum(x1, y))
     saved(y)
 
 
@@ -583,11 +591,10 @@
         self.turn = 0
         self.flying = [[], []]
 
-    def copy_out(self, source, block, place, unit, take, sem):
+    def copy_out(self, source, block, side, unit, take, sem):
         which = max(i for i, (first, _) in enumerate(self.bins) if first <= block)
         block = block - self.bins[which][0]
-        side, part = place // 3, place % 3
-        keep, send = (self.targets[which * 6 + i * 3 + part] for i in range(2))
+        keep, send = self.targets[2 * which], self.targets[2 * which + 1]
 
         def to(target):
             return pltpu.make_async_copy(source, target.at[block, pl.ds(unit, take)], sem)
@@ -625,12 +632,12 @@
                 return carry
 
             lax.fori_loop(0, panels // 2, body, 0)
-            for block, place, unit, at, take in self.section.runs(
-                name, self.plan.cuts, band * 16, 16
+            for block, side, unit, at, take in self.section.runs(
+                name, self.plan.half_cuts, band * 16, 16
             ):
                 self.flying[slot].append(
                     self.copy_out(
-                        stage.at[pl.ds(at, take)], block, place, unit, take, self.sems.at[slot]
+                        stage.at[pl.ds(at, take)], block, side, unit, take, self.sems.at[slot]
                     )
                 )
 
@@ -647,10 +654,9 @@
                     scratch[k, unit, row : row + 1, :] = values[name][
                         :, panel * 128 : panel * 128 + 128
                     ]
-        unit = self.plan.vec_unit - self.plan.cuts[5]
-        assert unit >= 0
+        unit = self.plan.vec_unit - self.plan.half
         copies = [
-            self.copy_out(scratch.at[k], block, 5, unit, VEC_UNITS, self.sems.at[2])
+            self.copy_out(scratch.at[k], block, 1, unit, VEC_UNITS, self.sems.at[2])
             for k, block in enumerate(blocks)
         ]
         for copy in copies:
@@ -660,9 +666,9 @@
 
 
 class Backward:
-    def __init__(self, sh, w, vec, limit_of, grads, values, acc, turned, ready):
+    def __init__(self, sh, w, vec, limit_of, grads, values, turned, ready):
         self.sh, self.w, self.vec, self.limit_of = sh, w, vec, limit_of
-        self.grads, self.values, self.acc, self.turned, self.ready = grads, values, acc, turned, ready
+        self.grads, self.values, self.turned, self.ready = grads, values, turned, ready
         self.panels = sh.width // 128
 
     def round_stream(self, dy, dyb):
@@ -672,20 +678,7 @@
         for_rows(self.sh.count, 16, step, 4)
 
     def bands(self, left, name, count, put):
-        acc = self.acc
-        panels = self.grads.section.panels[name]
-
-        def body(band, carry):
-            acc[...] = dot_nt(left[...], row_band(self.w[name], panels, band))
-
-            def step(at):
-                here = pl.ds(at, 16)
-                put(here, lanes(band), acc[here, :])
-
-            for_rows(self.sh.count, 16, step, 4)
-            return carry
-
-        lax.fori_loop(0, count // 256, body, 0)
+        times_bands(left, self.w[name], self.grads.section.panels[name], count, put)
 
     def through_norm(self, x, dn, dy, gain, shift, dn_is=None):
         def from_dn(at, size):
@@ -743,14 +736,33 @@
         self.through_norm(x0, dn, dy, "g1", "b1")
 
 
+def held_at(plan, s, gathered, block, side, unit, take):
+    if s == 0:
+        return [(gathered[0].at[side, block, pl.ds(unit, take)], 0, take)]
+    if block == plan.bins(1)[1][0]:
+        return [(gathered[1].at[side, pl.ds(unit, take)], 0, take)]
+    out = []
+    quarter = plan.quarter
+    if unit < quarter:
+        few = min(take, quarter - unit)
+        out.append((gathered[0].at[side, 2 * block, pl.ds(unit, few)], 0, few))
+    if unit + take > quarter:
+        skip = max(quarter - unit, 0)
+        few = take - skip
+        source = gathered[0].at[side, 2 * block + 1, pl.ds(unit + skip - quarter, few)]
+        out.append((source, skip, few))
+    return out
+
+
 def load_vectors(plan, s, gathered, held, vec_ref, sem):
     section = plan.sections[s]
     blocks = sorted({v[2] for v in section.vectors.values()})
     copies = [
-        pltpu.make_async_copy(
-            gathered.at[1, block, pl.ds(plan.vec_unit - plan.half, VEC_UNITS)], held.at[k], sem
+        pltpu.make_async_copy(source, held.at[k, pl.ds(skip, few)], sem)
+        for k, block in enumerate(blocks)
+        for source, skip, few in held_at(
+            plan, s, gathered, block, 1, plan.vec_unit - plan.half, VEC_UNITS
         )
-        for k, block in enumerate(blocks)
     ]
     for copy in copies:
         copy.start()
@@ -781,10 +793,9 @@
         panels = section.panels[name]
         flat = ref.reshape(ref.shape[0] * panels, 16, 128)
         copies[name] = [
-            pltpu.make_async_copy(
-                gathered.at[side, block, pl.ds(unit, take)], flat.at[pl.ds(at, take)], sems.at[k]
-            )
+            pltpu.make_async_copy(source, flat.at[pl.ds(at + skip, few)], sems.at[k])
             for block, side, unit, at, take in section.runs(name, plan.half_cuts)
+            for source, skip, few in held_at(plan, s, gathered, block, side, unit, take)
         ]
         for copy in copies[name]:
             copy.start()
@@ -816,10 +827,10 @@
 def encoder_kernel(plan, sh, refs):
     (info, gathered, patches, perm, pos, pp_out, x0_out, n1_out, mixed_out, o_out, x1_out, n2_out,
      g_out, gp_out, y_out, latent_out, w_patch, w_qkv, w_proj, w_fc1, w_fc2, held, vec_ref, pp, xe,
-     x0, n1, mixed, o, x1, n2, g, gp, y, latent, acc, w_sems, out_sems) = refs
+     x0, n1, mixed, o, x1, n2, g, gp, y, latent, w_sems, out_sems) = refs
     w = dict(zip(W_ENC, (w_patch, w_qkv, w_proj, w_fc1, w_fc2)))
-    finish_vec = load_vectors(plan, 0, gathered, held, vec_ref, w_sems.at[5])
-    ready = load_weights(plan, 0, gathered, w, w_sems)
+    finish_vec = load_vectors(plan, 0, [gathered], held, vec_ref, w_sems.at[5])
+    ready = load_weights(plan, 0, [gathered], w, w_sems)
     outs = []
 
     targets = [(pp, pp_out), (x0, x0_out), (n1, n1_out), (mixed, mixed_out), (o, o_out),
@@ -847,19 +858,14 @@
     vec = finish_vec()
     ready("patch")
 
-    def put(pair):
+    def put(pair, here, value):
         part = vec_ref[0:1, lanes(pair)]
-
-        def step(at):
-            here = pl.ds(at, 16)
-            x0[here, lanes(pair)] = (acc[here, :] + part) + x0[here, lanes(pair)]
-
-        for_rows(sh.count, 16, step, 4)
-
-    times_columns(xe, w["patch"], D // 128, PIX, acc, put)
+        x0[here, lanes(pair)] = (value + part) + x0[here, lanes(pair)]
+
+    times_columns(xe, w["patch"], D // 128, PIX, put)
     saved(x0)
     block_forward(
-        sh, x0, n1, mixed, o, x1, n2, g, gp, y, w, vec, lambda i: info[1 + i], acc, ready, saved
+        sh, x0, n1, mixed, o, x1, n2, g, gp, y, w, vec, lambda i: info[1 + i], ready, saved
     )
     norm_forward(y, vec("gf"), vec("bf"), latent, sh.count, D)
     saved(latent)
@@ -907,7 +913,6 @@
             pltpu.VMEM((sh.count, PIX), BF16),
             *[pltpu.VMEM(*s) for s in saved],
             pltpu.VMEM(*latent_shape),
-            pltpu.VMEM((sh.count, 256), F32),
             pltpu.SemaphoreType.DMA((6,)),
             pltpu.SemaphoreType.DMA((len(outs),)),
         ],
@@ -921,11 +926,12 @@
 
 
 def decoder_kernel(plan, sh, refs):
-    info, scale, gathered, latent_in, pp_in, perm, pos = refs[:7]
-    targets, refs = refs[7:19], refs[19:]
+    info, scale, gathered, gathered_tail, latent_in, pp_in, perm, pos = refs[:8]
+    gathered = [gathered, gathered_tail]
+    targets, refs = refs[8:12], refs[12:]
     (grad_latent, loss_out,
      w_embed, w_qkv, w_proj, w_fc1, w_fc2, w_head, held, vec_ref, pp, latent, embedded, x0, n1,
-     mixed, o, x1, n2, g, gp, y, f, dn, guess, acc, acc_e, turned, turned_e, stage, vec_stage, w_sems,
+     mixed, o, x1, n2, g, gp, y, f, dn, guess, turned, turned_e, stage, vec_stage, w_sems,
      in_sems, grad_sems) = refs
     w = dict(zip(W_DEC, (w_embed, w_qkv, w_proj, w_fc1, w_fc2, w_head)))
     copy_latent = pltpu.make_async_copy(latent_in, latent, in_sems.at[0])
@@ -940,13 +946,10 @@
     copy_latent.wait()
     ready("embed")
 
-    def put_embedded(pair):
-        def step(at):
-            embedded[pl.ds(at, 16), lanes(pair)] = acc_e[pl.ds(at, 16), :]
-
-        for_rows(count_e, 16, step, 4)
-
-    times_columns(latent, w["embed"], DD // 128, D, acc_e, put_embedded)
+    def put_embedded(pair, here, value):
+        embedded[here, lanes(pair)] = value
+
+    times_columns(latent, w["embed"], DD // 128, D, put_embedded)
 
     def tokens(image, carry):
         chosen = picks(perm, image)
@@ -962,7 +965,7 @@
 
     lax.fori_loop(0, images, tokens, 0)
     block_forward(
-        sh, x0, n1, mixed, o, x1, n2, g, gp, y, w, vec, lambda i: NP, acc, ready, lambda ref: None
+        sh, x0, n1, mixed, o, x1, n2, g, gp, y, w, vec, lambda i: NP, ready, lambda ref: None
     )
     norm_forward(y, vec("gf"), vec("bf"), f, count, DD)
     ready("head")
@@ -996,7 +999,7 @@
     grads = Gradients(plan, 1, info[0], stage, grad_sems, targets)
     values = {}
     back = Backward(
-        sh, w, vec, lambda i: NP, grads, values, acc, turned, lambda name, ref: None
+        sh, w, vec, lambda i: NP, grads, values, turned, lambda name, ref: None
     )
     dpred = pp.reshape(count, PIX)
     grads.weight("head", f, DD, dpred, turned)
@@ -1043,26 +1046,18 @@
     placed = n1.at[pl.ds(0, count_e)]
     grads.weight("embed", latent, D, placed, turned_e)
 
-    def latent_band(band, carry):
-        acc_e[...] = dot_nt(placed[...], row_band(w["embed"], DD // 128, band))
-
-        def step(at):
-            grad_latent[pl.ds(at, 16), lanes(band)] = acc_e[pl.ds(at, 16), :].astype(BF16)
-
-        for_rows(count_e, 16, step, 4)
-        return carry
-
-    lax.fori_loop(0, D // 256, latent_band, 0)
+    def put_latent(here, there, value):
+        grad_latent[here, there] = value.astype(BF16)
+
+    times_bands(placed, w["embed"], DD // 128, D, put_latent)
     grads.finish(values, vec_stage)
 
 
 def grad_shapes(plan, s):
-    cuts = plan.part_cuts
     return [
-        jax.ShapeDtypeStruct((count, cuts[part + 1] - cuts[part], 16, 128), F32)
-        for _, count in plan.bins(s)
+        jax.ShapeDtypeStruct((count, units, 16, 128), F32)
+        for (_, count), units in zip(plan.bins(s), plan.bin_units(s))
         for _ in range(2)
-        for part in range(3)
     ]
 
 
@@ -1078,8 +1073,8 @@
             jax.ShapeDtypeStruct((count_e, D), BF16),
             jax.ShapeDtypeStruct((8, 128), F32),
         ],
-        in_specs=[IN_SMEM, IN_SMEM, ANY, ANY, ANY, IN_VMEM, IN_VMEM],
-        out_specs=[*[ANY] * 12, IN_VMEM, IN_VMEM],
+        in_specs=[IN_SMEM, IN_SMEM, ANY, ANY, ANY, ANY, IN_VMEM, IN_VMEM],
+        out_specs=[*[ANY] * 4, IN_VMEM, IN_VMEM],
         scratch_shapes=[
             *weight_scratch(DEC, W_DEC),
             pltpu.VMEM((holders, VEC_UNITS, 16, 128), BF16),
@@ -1091,8 +1086,6 @@
             pltpu.VMEM((sh.count, DD), BF16),
             pltpu.VMEM((sh.count, DD), F32),
             pltpu.VMEM((ROWS_D, PIX), F32),
-            pltpu.VMEM((sh.count, 256), F32),
-            pltpu.VMEM((count_e, 256), F32),
             pltpu.VMEM((256, sh.count), BF16),
             pltpu.VMEM((256, count_e), BF16),
             pltpu.VMEM((2, 16 * most, 16, 128), F32),
@@ -1104,14 +1097,15 @@
         compiler_params=pltpu.CompilerParams(vmem_limit_bytes=VMEM_BYTES),
         cost_estimate=lasting(160),
         name="decoder_both",
-    )(info, scale, gathered, latent, pp, perm, pos)
+    )(info, scale, *gathered, latent, pp, perm, pos)
 
 
 class Stage:
-    def __init__(self, plan, sh, weights, reads, temps, outs, most, cost, name, body):
+    def __init__(self, plan, sh, weights, reads, temps, outs, most, cost, name, body, bins=2):
         self.plan, self.sh, self.weights, self.reads = plan, sh, weights, reads
         self.temps, self.outs, self.most, self.cost, self.name = temps, outs, most, cost, name
         self.body = body
+        self.bins = bins
 
     def kernel(self, blocks, *refs):
         refs = list(refs)
@@ -1125,13 +1119,13 @@
         info, gathered = take(2)
         sources = dict(zip(self.reads, take(len(self.reads))))
         take(blocks)
-        targets = take(len(grad_shapes(plan, 0)))
+        targets = take(2 * self.bins)
         results = dict(zip(self.outs, take(len(self.outs))))
         w = dict(zip(self.weights, take(len(self.weights))))
         here = dict(zip(self.reads, take(len(self.reads))))
         temps = dict(zip(self.temps, take(len(self.temps))))
-        held, vec_ref, acc, turned, stage, vec_stage, w_sems, in_sems, grad_sems = refs
-        finish_vec = load_vectors(plan, 0, gathered, held, vec_ref, w_sems.at[len(w)])
+        held, vec_ref, turned, stage, vec_stage, w_sems, in_sems, grad_sems = refs
+        finish_vec = load_vectors(plan, 0, [gathered], held, vec_ref, w_sems.at[len(w)])
         loads = {}
         for k, (name, ref) in enumerate(here.items()):
             if name == "xe":
@@ -1148,7 +1142,7 @@
             for copy in copies:
                 copy.start()
             loads[id(ref)] = copies
-        weights_ready = load_weights(plan, 0, gathered, w, w_sems)
+        weights_ready = load_weights(plan, 0, [gathered], w, w_sems)
         vec = finish_vec()
 
         def ready(name, ref=None):
@@ -1160,7 +1154,7 @@
         values = {}
         grads = Gradients(plan, 0, info[0], stage, grad_sems, targets)
         back = Backward(
-            sh, w, vec, lambda i: info[1 + i], grads, values, acc, turned, ready
+            sh, w, vec, lambda i: info[1 + i], grads, values, turned, ready
         )
         self.body(back, {**here, **temps}, results)
         assert not loads
@@ -1187,7 +1181,7 @@
             "gp": ((count, hidden), F32),
         }
         holders = len({v[2] for v in plan.sections[0].vectors.values()})
-        targets = grad_shapes(plan, 0)
+        targets = grad_shapes(plan, 0)[: 2 * self.bins]
         before = 2 + len(self.reads)
         got = pl.pallas_call(
             functools.partial(self.kernel, len(blocks)),
@@ -1201,7 +1195,6 @@
                 *[pltpu.VMEM(*known[n]) for n in self.temps],
                 pltpu.VMEM((holders, VEC_UNITS, 16, 128), BF16),
                 pltpu.VMEM((8, D), F32),
-                pltpu.VMEM((count, 256), F32),
                 pltpu.VMEM((256, count), BF16),
                 pltpu.VMEM((2, 16 * self.most, 16, 128), F32),
                 pltpu.VMEM((holders, VEC_UNITS, 16, 128), F32),
@@ -1282,9 +1275,9 @@
         Stage(plan, sh, ["fc1"], ["g", "dy", "n2", "x1"], ["dn"], ["dy"], most["fc1"], 20,
               "encoder_back_fc1", back_first),
         Stage(plan, sh, ["proj"], ["dy", "o", "mixed"], ["dyb"], ["dmixed"], most["proj"], 35,
-              "encoder_back_attention", back_attention),
+              "encoder_back_attention", back_attention, 1),
         Stage(plan, sh, ["qkv"], ["dy", "dmixed", "n1", "x0", "xe"], ["dn", "dyb"], [],
-              most["qkv"], 25, "encoder_back_qkv", back_mixing),
+              most["qkv"], 25, "encoder_back_qkv", back_mixing, 1),
     ]
 
 
@@ -1292,33 +1285,49 @@
     return lax.dynamic_index_in_dim(value, index, axis, keepdims=False)
 
 
-def total_of(terms):
-    total = terms[0]
-    for term in terms[1:]:
-        total = total + term
-    return total
-
-
 def tie(*trees):
     return lax.optimization_barrier(trees)
 
 
+class Term:
+    def __init__(self, base, bits, first, last, fixed=()):
+        self.base, self.bits, self.first, self.last = base, bits, first, last
+        self.fixed = dict(fixed)
+
+    def at(self, bit, index):
+        return Term(self.base, self.bits, self.first, self.last, {**self.fixed, bit: index})
+
+    def value(self):
+        zero = jnp.zeros((), jnp.int32)
+        starts = [self.fixed.get(b, zero).astype(jnp.int32) for b in self.bits]
+        sizes = [1 if b in self.fixed else 2 for b in self.bits]
+        left = [n for n in sizes if n == 2]
+        starts += [jnp.full((), self.first, jnp.int32), zero, zero]
+        count = self.last - self.first
+        out = lax.dynamic_slice(self.base, starts, [*sizes, count, 16, 128])
+        return out.reshape(*left, count, 16, 128)
+
+
+def sum_of(terms):
+    return total_of([term.value() for term in terms])
+
+
 class Flow:
-    def __init__(self, dp, keep, send, first):
+    def __init__(self, dp, keep, send, first, parts=3):
         self.dp = dp
         self.me = lax.axis_index("dp")
         self.keep, self.given = keep, send
-        count = keep[0].shape[0]
+        count, units = keep.shape[:2]
         self.bits = count.bit_length() - 1
         assert count == 1 << self.bits and dp & (dp - 1) == 0
         self.all_bits = dp.bit_length() - 1
         self.first = first
-        low = [b for b in range(0, self.bits, 1)]
+        low = list(range(self.bits))
         if dp == 64:
             low = [b for b in (0, 2, 4, 1, 3) if b < self.bits]
-        turn = min(3, len(low))
-        self.orders = [low[p % turn :][: turn - p % turn] + low[: p % turn] + low[turn:] for p in range(3)]
-        self.left = [list(range(self.bits - 1, -1, -1)) for _ in range(3)]
+        turn = max(min(3, len(low)), 1)
+        self.cuts = [units * p // parts for p in range(parts + 1)]
+        self.orders = [low[p % turn : turn] + low[: p % turn] + low[turn:] for p in range(parts)]
         self.step = -1
         self.terms = None
 
@@ -1327,51 +1336,52 @@
 
     def payload(self):
         if self.step < 0:
-            return list(self.given)
+            return [self.given]
+        if self.step >= self.bits:
+            return [self.result()]
         out = []
-        for part in range(3):
-            if self.step < self.bits:
-                bit = self.orders[part][self.step]
-                dim = self.left[part].index(bit)
-                other = 1 - (self.me >> bit & 1)
-                out.append(total_of([pick(t, other, dim) for t in self.terms[part]]))
-            else:
-                out.append(total_of(self.terms[part]))
+        for terms, order in zip(self.terms, self.orders):
+            bit = order[self.step]
+            other = 1 - (self.me >> bit & 1)
+            out.append(sum_of([t.at(bit, other) for t in terms]))
         return out
 
     def send(self, payload):
         if self.step < 0:
-            return [lax.ppermute(p, "section", [(0, 1), (1, 0)]) for p in payload]
+            return [lax.ppermute(payload[0], "section", [(0, 1), (1, 0)])]
+        if self.step >= self.bits:
+            flip = 1 << self.step
+            pairs = [(i, i ^ flip) for i in range(self.dp) if (i ^ self.first) & flip]
+            return [lax.ppermute(payload[0], "dp", pairs)]
         out = []
-        for part in range(3):
-            if self.step < self.bits:
-                flip = 1 << self.orders[part][self.step]
-                pairs = [(i, i ^ flip) for i in range(self.dp)]
-            else:
-                flip = 1 << self.step
-                pairs = [(i, i ^ flip) for i in range(self.dp) if (i ^ self.first) & flip]
-            out.append(lax.ppermute(payload[part], "dp", pairs))
+        for value, order in zip(payload, self.orders):
+            flip = 1 << order[self.step]
+            out.append(lax.ppermute(value, "dp", [(i, i ^ flip) for i in range(self.dp)]))
         return out
 
     def take(self, got):
+        ranges = list(zip(self.cuts[:-1], self.cuts[1:]))
         if self.step < 0:
+            bits = list(range(self.bits - 1, -1, -1))
+            shape = (2,) * self.bits + self.keep.shape[1:]
             self.terms = [
-                [v.reshape((2,) * self.bits + v.shape[1:]) for v in pair]
-                for pair in zip(self.keep, got)
+                [Term(v.reshape(shape), bits, *r) for v in (self.keep, got[0])] for r in ranges
             ]
         elif self.step < self.bits:
-            for part in range(3):
-                bit = self.orders[part][self.step]
-                dim = self.left[part].index(bit)
+            for k, (order, value) in enumerate(zip(self.orders, got)):
+                bit = order[self.step]
                 mine = self.me >> bit & 1
-                self.terms[part] = [pick(t, mine, dim) for t in self.terms[part]] + [got[part]]
-                self.left[part].remove(bit)
+                gone = order[: self.step + 1]
+                bits = [b for b in range(self.bits - 1, -1, -1) if b not in gone]
+                self.terms[k] = [t.at(bit, mine) for t in self.terms[k]]
+                self.terms[k].append(Term(value, bits, 0, value.shape[-3]))
         else:
-            self.terms = [t + [g] for t, g in zip(self.terms, got)]
+            for k, r in enumerate(ranges):
+                self.terms[k].append(Term(got[0], [], *r))
         self.step += 1
 
     def result(self):
-        return jnp.concatenate([total_of(t) for t in self.terms], axis=0)
+        return jnp.concatenate([sum_of(t) for t in self.terms], axis=0)
 
 
 def move_on(flows, *others):
@@ -1397,6 +1407,49 @@
         if len(got) == 3:
             value = value + (got[1] + got[2])
     return value
+
+
+def squares_of(plan, s, value, section, me):
+    section_plan = plan.sections[s]
+    vectors = np.zeros((plan.dp,), np.int32)
+    for _, panels, block, at in section_plan.vectors.values():
+        vectors[block] = max(vectors[block], at + panels)
+    filled = jnp.asarray(np.asarray(section_plan.fill, np.int32) * 16)[me]
+    vectors = jnp.asarray(vectors)[me]
+    shape = value.shape
+    row = lax.broadcasted_iota(jnp.int32, shape, 0) * 16 + lax.broadcasted_iota(jnp.int32, shape, 1)
+    row = row + section * (plan.half * 16)
+    extra = row - plan.vec_unit * 16
+    valid = (row < filled) | ((extra >= 0) & (extra < vectors))
+    return jnp.sum(jnp.where(valid, value * value, 0.0))
+
+
+def gather_decoder(plan, half_d, section, me, after):
+    dp, quarter = plan.dp, plan.quarter
+    first = plan.bins(1)[1][0]
+    assert 2 * first == dp
+    used = max(plan.tail_used())
+    spread = jnp.pad(half_d, ((0, 2 * quarter - plan.half), (0, 0), (0, 0)))
+    spread = total_of(
+        [
+            lax.ppermute(
+                spread[i * quarter : (i + 1) * quarter],
+                "dp",
+                [(b, 2 * b + i) for b in range(first)],
+            )
+            for i in range(2)
+        ]
+    )
+    rest = jnp.where(me == first, half_d[:used], jnp.zeros((), BF16))
+    holders = [first]
+    for bit in reversed(range(dp.bit_length() - 1)):
+        rest = rest + lax.ppermute(rest, "dp", [(i, i ^ 1 << bit) for i in holders])
+        holders = holders + [i ^ 1 << bit for i in holders]
+    other = lax.ppermute(rest, "section", [(0, 1), (1, 0)])
+    rest = jnp.where(section == 0, jnp.stack([rest, other]), jnp.stack([other, rest]))
+    spread, _ = tie(spread, after[0, 0, 0])
+    gathered = lax.all_gather(spread, ("section", "dp"), axis=0, tiled=True)
+    return gathered.reshape(2, dp, quarter, 16, 128), rest
 
 
 def sincos(width):
@@ -1443,9 +1496,7 @@
     half_d = jnp.where(section == 0, given, mine)
     gathered_e = lax.all_gather(half_e, ("section", "dp"), axis=0, tiled=True)
     gathered_e = gathered_e.reshape(2, dp, half, 16, 128)
-    half_d, _ = tie(half_d, gathered_e[0, 0, 0])
-    gathered_d = lax.all_gather(half_d, ("section", "dp"), axis=0, tiled=True)
-    gathered_d = gathered_d.reshape(2, dp, half, 16, 128)
+    gathered_d = gather_decoder(plan, half_d, section, me, gathered_e)
 
     count = sum_everywhere(dp, jnp.sum(NP - keep).astype(F32)) * 0.5
     images = patches.shape[0] // 2
@@ -1471,44 +1522,37 @@
     )
 
     stages = encoder_back_stages(plan, shape_e)
-    tail_parts = plan.tail_parts()
-    tail_got = [lax.ppermute(sums_d[9 + p], "section", swap) for p in tail_parts]
-    main = Flow(dp, sums_d[0:3], sums_d[3:6], 0)
+    first_tail = plan.bins(1)[1][0]
+    main = Flow(dp, sums_d[0], sums_d[1], 0)
+    rest = Flow(dp, sums_d[2], sums_d[3], first_tail, 1)
+    flows, got, _ = move_on([main])
+    got, arrays = tie(got, arrays)
+    arrive(flows, got)
     low = high = None
     blocks = []
     for number, stage in enumerate(stages):
-        flows, got, (arrays, blocks) = move_on([main, high], arrays, blocks)
+        flows, got, (arrays, blocks) = move_on([main, rest, high], arrays, blocks)
         blocks, made = stage(info, gathered_e, arrays, blocks)
         arrays = {**arrays, **made}
         got, arrays, blocks = tie(got, arrays, blocks)
         arrive(flows, got)
-        if number == 0:
-            tail_sum = lax.psum(
-                [sums_d[6 + p] + g for p, g in zip(tail_parts, tail_got)], "dp"
-            )
         if number == 1:
-            high = Flow(dp, blocks[6:9], blocks[9:12], dp // 2)
-    low = Flow(dp, blocks[0:3], blocks[3:6], 0)
-    every = [main, high, low]
+            high = Flow(dp, blocks[2], blocks[3], dp // 2)
+            blocks = blocks[:2]
+    low = Flow(dp, blocks[0], blocks[1], 0)
+    every = [main, rest, high, low]
     while not all(f.done() for f in every):
         flows, got, _ = move_on(every)
         arrive(flows, got)
 
-    cuts = plan.part_cuts
-    first_tail, tail_blocks = plan.bins(1)[1]
-    tail_at = jnp.clip(me - first_tail, 0, tail_blocks - 1)
-    tail_sum = dict(zip(tail_parts, tail_sum))
-    sum_tail = jnp.concatenate(
-        [
-            pick(tail_sum[p], tail_at, 0)
-            if p in tail_sum
-            else jnp.zeros((cuts[p + 1] - cuts[p], 16, 128), F32)
-            for p in range(3)
-        ],
-        axis=0,
-    )
+    sum_tail = rest.result()
+    sum_tail = jnp.pad(sum_tail, ((0, half - sum_tail.shape[0]), (0, 0), (0, 0)))
     sum_d = jnp.where(me < first_tail, main.result(), sum_tail)
     sum_e = jnp.where(me < dp // 2, low.result(), high.result())
+    squares = [
+        squares_of(plan, s, v, section, me) for s, v in enumerate((sum_e, sum_d))
+    ]
+    sums = sum_everywhere(dp, jnp.stack([squares[0] + squares[1], loss[0, 0]]))
     half_mine = jnp.where(section == 0, sum_e, sum_d)
     half_other = lax.ppermute(jnp.where(section == 0, sum_d, sum_e), "section", swap)
     block = jnp.where(
@@ -1526,9 +1570,7 @@
     )
     tail = lax.ppermute(tail, "dp", [(i, i + 1) for i in range(dp - 1)])
     index = jnp.asarray(plan.unpack_index)[section, me]
-    total, squares = unpack(plan, index, block, tail)
-
-    sums = sum_everywhere(dp, jnp.stack([jnp.sum(squares), loss[0, 0]]))
+    total = unpack(plan, index, block, tail)
     norm = jnp.sqrt(sums[0])
     factor = jnp.minimum(1.0, clip_limit / (norm + norm_epsilon))
     made = update(plan, factor.reshape(1), total, states)

time: 979 us -> 812 us (0.83)
  waiting for transfers between devices: 370 us -> 289 us
  Pallas kernels: 358 us -> 310 us
  local copies, waits for them, and re-layouts: 31.1 us -> 15.6 us
  other arithmetic: 79.3 us -> 66.8 us
    psum x1 -> x0, waiting for transfers between devices: 54.6 us -> none  [on_device(): lax.psum([sums_d[6 + p] + g for p, g in zip(tail_parts, tail_got)], 'dp')]
    ppermute x47 -> x45, waiting for transfers between devices: 145 us -> 196 us  [the longest x27 75.8 us: send(): lax.ppermute(value, 'dp', [(i, i ^ flip) for i in range(self.dp)])]
    all_gather x1, waiting for transfers between devices: 84 us -> 34.1 us  [on_device(): gathered_e = lax.all_gather(half_e, ('section', 'dp'), axis=0, tiled=True)]
    pallas_call x1, Pallas kernels: 170 us -> 141 us  [decoder(): pl.pallas_call(lambda *refs: decoder_kernel(plan, sh, refs), out_shape=[*...]
    all_gather x1, waiting for transfers between devices: 63.8 us -> 39.4 us  [gather_decoder(): gathered = lax.all_gather(spread, ('section', 'dp'), axis=0, tiled=True)]
    unnamed x99 -> x40, local copies, waits for them, and re-layouts: 21.6 us -> 3.79 us
    ppermute x47 -> x45, starting transfers between devices: 71.6 us -> 57.2 us  [the longest x27 28.9 us: send(): lax.ppermute(value, 'dp', [(i, i ^ flip) for i in range(self.dp)])]
    add x44 -> x39, other arithmetic: 66.6 us -> 53.1 us  [total_of(): total = total + term]
  transfers between devices with their start and end apart: 68 -> 65, of which waited for: 30 -> 29; matrix products, arithmetic and copies ran while one was open for 4% -> 4% of each run, Pallas kernels for 17% -> 18%
where the time goes in v3:
time: 812 us; the launch traced here: 806 us
  Pallas kernels  310 us (38%)
  waiting for transfers between devices  289 us (36%)
  starting transfers between devices  99.2 us (12%)
  other arithmetic  66.8 us (8%)
  between operations  26.1 us (3%)
  local copies, waits for them, and re-layouts  15.6 us (2%)
    pallas_call x1, Pallas kernels, decoder(): pl.pallas_call(lambda *refs: decoder_kernel(plan, sh, refs), out_shape=[*...  141 us
    pallas_call x4, Pallas kernels, __call__(): pl.pallas_call(functools.partial(self.kernel, len(blocks)), out_shape=[*t...  108 us
    ppermute x27, waiting for transfers between devices, send(): lax.ppermute(value, 'dp', [(i, i ^ flip) for i in range(self.dp)])  75.8 us
    ppermute x7, waiting for transfers between devices, send(): return [lax.ppermute(payload[0], 'dp', pairs)]  65.9 us
    add x39, other arithmetic, total_of(): total = total + term  53.1 us
    all_gather x1, waiting for transfers between devices, gather_decoder(): gathered = lax.all_gather(spread, ('section', 'dp'), axis=0, tiled=True)  39.4 us
    pallas_call x1, Pallas kernels, encoder(): pl.pallas_call(lambda *refs: encoder_kernel(plan, sh, refs), out_shape=[j...  39.4 us
    ppermute x4, waiting for transfers between devices, gather_decoder(): rest = rest + lax.ppermute(rest, 'dp', [(i, i ^ 1 << bit) for i in holders])  36.1 us
  transfers between devices with their start and end apart: 65, of which 29 were waited for; matrix products, arithmetic and copies ran while one was open for 4% of the time, Pallas kernels for 18%

profile of v3, /device:TPU:0, one launch (start us, length us, event | category | flops | bytes accessed | tf_op | source)
XLA Modules:
  0.0 805.9 jit_solution(852948108947690459)
XLA Ops:
  10.4 7.5 collective-permute-done.7.following
  19.4 6.8 pack_rows.1
  29.2 4.6 collective-permute-start.10
  34.5 5.1 collective-permute-done.10
  41.7 24.9 %collective-permute-done.11 = bf16[48,16,128]{2,1,0:T(8,128)(2,1)S(1)} collective-permute-done((bf16[48,16,128]{2,1,0:T(8,128)(2,1)S(1)}, bf16[48,16,128]{2,1,0:T(8,128)(2,1)S(1)}, u32[]{:S(2)}, u32[]{:S(2)}) %collective-permute-start.11) | collective-permute-done | bytes 196640 | tf_op jit(solution)/shard_map/ppermute | solution.py:1446
  68.0 8.1 %collective-permute-done.12 = bf16[48,16,128]{2,1,0:T(8,128)(2,1)S(1)} collective-permute-done((bf16[48,16,128]{2,1,0:T(8,128)(2,1)S(1)}, bf16[48,16,128]{2,1,0:T(8,128)(2,1)S(1)}, u32[]{:S(2)}, u32[]{:S(2)}) %collective-permute-start.12) | collective-permute-done | bytes 196640 | tf_op jit(solution)/shard_map/ppermute | solution.py:1446
  77.4 3.2 collective-permute-done.13
  90.3 3.8 collective-permute-start.2
  94.1 2.4 collective-permute-start.3
  101.8 5.5 collective-permute-start.5
  107.3 3.8 collective-permute-start.6
  117.2 34.1 %all-gather.5.cloned.1.call-done = bf16[4064,16,128]{2,1,0:T(8,128)(2,1)} async-done(((bf16[127,16,128]{2,1,0:T(8,128)(2,1)}), bf16[4064,16,128]{2,1,0:T(8,128)(2,1)}) %all-gather.5.cloned.1.call-update) | async-done | bytes 16646160 | tf_op jit(solution)/shard_map/all_gather | solution.py:1497
  151.3 39.4 %encoder_forward.1 = (bf16[6,208,768]{2,1,0:T(8,128)(2,1)}, f32[672,768]{1,0:T(8,128)}, bf16[672,768]{1,0:T(8,128)(2,1)}, bf16[672,2304]{1,0:T(8,128)(2,1)}, bf1...) custom-call(s32[7]{0:T(128)} %pad_add_fusion.refs_0_, ...), custom_call_target="tpu_custom_call" | custom-call | flops 49999998976 | bytes 1048576 | tf_op jit(solution)/shard_map/encoder_forward/pallas_call | solution.py:903
  190.7 39.4 %all-gather.3.cloned.1.call-done = bf16[2048,16,128]{2,1,0:T(8,128)(2,1)} async-done(((bf16[64,16,128]{2,1,0:T(8,128)(2,1)}), bf16[2048,16,128]{2,1,0:T(8,128)(2,1)}) %all-gather.3.cloned.1.call-update) | async-done | bytes 8388624 | tf_op jit(solution)/shard_map/all_gather | solution.py:1451
  230.1 141.3 %decoder_both.1 = (f32[8,127,16,128]{3,2,1,0:T(8,128)}, f32[8,127,16,128]{3,2,1,0:T(8,128)}, f32[1,48,16,128]{3,2,1,0:T(8,128)}, f32[1,48,16,128]{3,2,1,0:T(8,12...) custom-call(s32[7]{0:T(128)} %pad_add_fusion.refs_0_, f32[1]{0:T(128)} %bitcast.3.refs_1_, ...), custom_call_target="tpu_custom_call" | custom-call | flops 160000000000 | bytes 1048576 | tf_op jit(solution)/shard_map/decoder_both/pallas_call | solution.py:1069
  371.7 13.1 %collective-permute-done.16 = f32[8,127,16,128]{3,2,1,0:T(8,128)} collective-permute-done((f32[8,127,16,128]{3,2,1,0:T(8,128)}, f32[8,127,16,128]{3,2,1,0:T(8,128)}, u32[]{:S(2)}, u32[]{:S(2)}) %collective-permute-start.16) | collective-permute-done | bytes 8323104 | tf_op jit(solution)/shard_map/ppermute | solution.py:1351
  384.8 3.0 add_bitcast_fusion.2
  387.9 3.0 add_bitcast_fusion.7
  390.9 3.1 add_bitcast_fusion.8
  397.5 29.5 %encoder_back_fc2.1 = (f32[8,127,16,128]{3,2,1,0:T(8,128)}, f32[8,127,16,128]{3,2,1,0:T(8,128)}, f32[8,127,16,128]{3,2,1,0:T(8,128)}, f32[8,127,16,128]{3,2,1,0:...) custom-call(s32[7]{0:T(128)} %pad_add_fusion.refs_0_, bf16[2,16,127,16,128]{4,3,2,1,0:T(8,128)(2,1)} %bitcast.296, ...), custom_call_target="tpu_custom_call" | custom-call | flops 24999999488 | bytes 1048576 | tf_op jit(solution)/shard_map/encoder_back_fc2/pallas_call | solution.py:1186
  431.6 3.3 bitcast_add_fusion.7
  438.9 24.4 %encoder_back_fc1.1 = (f32[8,127,16,128]{3,2,1,0:T(8,128)}, f32[8,127,16,128]{3,2,1,0:T(8,128)}, f32[8,127,16,128]{3,2,1,0:T(8,128)}, f32[8,127,16,128]{3,2,1,0:T(8,128)}, f32[672,768]{1,0:T(8,128)}) custom-call(s32[7]{0:T(128)} %pad_add_fusion.refs_0_, ...), custom_call_target="tpu_custom_call", output_to_operand_aliasing={{0}: (6, {}), {1}: (7, {}), {2}: (8, {}), {3}: (9, {})} | custom-call | flops 20000000000 | bytes 1048576 | tf_op jit(solution)/shard_map/encoder_back_fc1/pallas_call | solution.py:1186
  465.7 2.7 bitcast_add_fusion.39
  469.6 2.7 collective-permute-start.27
  473.9 3.4 collective-permute-start.26
  477.2 31.7 %encoder_back_attention.1 = (f32[8,127,16,128]{3,2,1,0:T(8,128)}, f32[8,127,16,128]{3,2,1,0:T(8,128)}, bf16[672,2304]{1,0:T(8,128)(2,1)}) custom-call(s32[7]{0:T(128)} %pad_add_fusion.refs_0_, bf16[2,16,127,16,128]{4,3,2,1,0:T(8,128)(2,1)} %bitcast.298, f32[672,768]{1,0:T(8,128)} %get-tuple-element.317.refs_2_, ...), custom_call_target="tpu_custom_call", output_to_operand_aliasing={{0}: (5, {}), {1}: (6, {})} | custom-call | flops 35000000512 | bytes 1048576 | tf_op jit(solution)/shard_map/encoder_back_attention/pallas_call | solution.py:1186
  509.0 3.2 add_bitcast_fusion.1
  512.2 3.0 add_bitcast_fusion.5
  515.2 3.0 add_bitcast_fusion.6
  526.0 22.5 %encoder_back_qkv.1 = (f32[8,127,16,128]{3,2,1,0:T(8,128)}, f32[8,127,16,128]{3,2,1,0:T(8,128)}) custom-call(s32[7]{0:T(128)} %pad_add_fusion.refs_0_, bf16[2,16,127,16,128]{4,3,2,1,0:T(8,128)(2,1)} %bitcast.299, f32[672,768]{1,0:T(8,128)} %get-tuple-element.317.refs_2_, ...), custom_call_target="tpu_custom_call", output_to_operand_aliasing={{0}: (7, {}), {1}: (8, {})} | custom-call | flops 24999999488 | bytes 1048576 | tf_op jit(solution)/shard_map/encoder_back_qkv/pallas_call | solution.py:1186
  548.6 37.5 %collective-permute-done.31 = f32[48,16,128]{2,1,0:T(8,128)} collective-permute-done((f32[48,16,128]{2,1,0:T(8,128)S(1)}, f32[48,16,128]{2,1,0:T(8,128)}, u32[]{:S(2)}, u32[]{:S(2)}) %collective-permute-start.31) | collective-permute-done | bytes 393248 | tf_op jit(solution)/shard_map/ppermute | solution.py:1355
  589.6 2.6 bitcast_add_fusion.5
  593.0 17.1 %collective-permute-done.36 = f32[2,42,16,128]{3,2,1,0:T(8,128)S(1)} collective-permute-done((f32[2,42,16,128]{3,2,1,0:T(8,128)S(1)}, f32[2,42,16,128]{3,2,1,0:T(8,128)S(1)}, u32[]{:S(2)}, u32[]{:S(2)}) %collective-permute-start.36) | collective-permute-done | bytes 688160 | tf_op jit(solution)/shard_map/ppermute | solution.py:1359
  619.6 35.2 %collective-permute-done.40 = f32[42,16,128]{2,1,0:T(8,128)S(1)} collective-permute-done((f32[42,16,128]{2,1,0:T(8,128)S(1)}, f32[42,16,128]{2,1,0:T(8,128)S(1)}, u32[]{:S(2)}, u32[]{:S(2)}) %collective-permute-start.40) | collective-permute-done | bytes 344096 | tf_op jit(solution)/shard_map/ppermute | solution.py:1359
  657.2 5.7 collective-permute-done.42
  668.6 11.4 %collective-permute-done.45 = f32[2,42,16,128]{3,2,1,0:T(8,128)S(1)} collective-permute-done((f32[2,42,16,128]{3,2,1,0:T(8,128)S(1)}, f32[2,42,16,128]{3,2,1,0:T(8,128)S(1)}, u32[]{:S(2)}, u32[]{:S(2)}) %collective-permute-start.45) | collective-permute-done | bytes 688160 | tf_op jit(solution)/shard_map/ppermute | solution.py:1359
  686.3 3.8 collective-permute-start.52
  690.2 2.6 collective-permute-done.48
  698.1 6.6 collective-permute-start.53
  706.9 11.1 %collective-permute-done.53 = f32[48,16,128]{2,1,0:T(8,128)S(1)} collective-permute-done((f32[48,16,128]{2,1,0:T(8,128)S(1)}, f32[48,16,128]{2,1,0:T(8,128)S(1)}, u32[]{:S(2)}, u32[]{:S(2)}) %collective-permute-start.53) | collective-permute-done | bytes 393248 | tf_op jit(solution)/shard_map/ppermute | solution.py:1355
  720.3 17.3 %collective-permute-done.51 = f32[127,16,128]{2,1,0:T(8,128)} collective-permute-done((f32[127,16,128]{2,1,0:T(8,128)}, f32[127,16,128]{2,1,0:T(8,128)}, u32[]{:S(2)}, u32[]{:S(2)}) %collective-permute-start.51) | collective-permute-done | bytes 1040416 | tf_op jit(solution)/shard_map/ppermute | solution.py:1355
  740.1 4.1 select_reduce_fusion
  757.2 2.5 collective-permute-done.57
  759.8 9.5 %collective-permute-start.58 = (f32[2]{0:T(128)S(1)}, f32[2]{0:T(128)S(1)}, u32[]{:S(2)}, u32[]{:S(2)}) collective-permute-start(f32[2]{0:T(128)S(1)} %add_add_fusion.2), channel_id=1, source_target_pairs={{0,4},{1,5},{2,6},{3,7},{4,0},{5,1},{6,2},{7,3},{8,12},{9,13},{10,... | collective-permute-start | bytes 32 | tf_op jit(solution)/shard_map/ppermute | solution.py:1403
  769.3 3.4 collective-permute-start.59
  774.5 3.4 collective-permute-start.62
  781.3 5.9 unpack_rows.1.total
  788.4 8.2 %update_states.1 = (f32[3747,1,128]{2,1,0:T(1,128)}, f32[3747,1,128]{2,1,0:T(1,128)}, f32[3747,1,128]{2,1,0:T(1,128)}, f32[3747,1,128]{2,1,0:T(1,128)}) custom-call(f32[1]{0:T(128)} %bitcast.104.factor_ref, f32[3760,128]{1,0:T(8,128)} %copy-done.3, f32[3747,1,128]{2,1,0:T(1,128)} %bitcast.251, f32[3747,1,128]{2,1,0:T(1,128)} %bitcast.290, ...), custom_call_target="tpu_custom_call" | custom-call | tf_op jit(solution)/shard_map/update_states/pallas_call | solution.py:322
  (213 shorter events, 110.6 us)
Async XLA Ops:
  7.2 144.1 %all-gather.5.cloned.1.call-start = ((), (), s32[]{:S(2)}) async-start(), calls=%async_computation.1 | async-start | bytes 17166336 | tf_op jit(solution)/shard_map/all_gather | solution.py:1497
  8.2 9.7 %collective-permute-start.7 = (f32[384,1,128]{2,1,0:T(1,128)S(1)}, f32[384,1,128]{2,1,0:T(1,128)S(1)}, u32[]{:S(2)}, u32[]{:S(2)}) collective-permute-start(f32[384,1,128]{2,1,0:T(1,128)S(1)} %slice_bitcast_fusion), channel_id=1, source_target_pairs={{1,0},{2,1},{3,2},{4,3},{5,4},{6,5},{7,6},{8,7},{9,8},{10,9},{11,1... | collective-permute-start | bytes 589832 | tf_op jit(solution)/shard_map/ppermute | solution.py:1486
  29.1 201.0 %all-gather.3.cloned.1.call-start = ((), (), s32[]{:S(2)}) async-start(), calls=%async_computation | async-start | bytes 8650752 | tf_op jit(solution)/shard_map/all_gather | solution.py:1451
  29.2 10.4 %collective-permute-start.10 = (bf16[64,16,128]{2,1,0:T(8,128)(2,1)S(1)}, bf16[64,16,128]{2,1,0:T(8,128)(2,1)S(1)}, u32[]{:S(2)}, u32[]{:S(2)}) collective-permute-start(bf16[64,16,128]{2,1,0:T(8,128)(2,1)S(1)} %get-tuple-element.386), channel_id=1, source_target_pairs={{0,1},{1,3},{2,5},{3,7},{4,9},{5,11},{6,13},{7,15},{16,17},{17,19}... | collective-permute-start | bytes 786440 | tf_op jit(solution)/shard_map/ppermute | solution.py:1435
  40.4 26.2 %collective-permute-start.11 = (bf16[48,16,128]{2,1,0:T(8,128)(2,1)S(1)}, bf16[48,16,128]{2,1,0:T(8,128)(2,1)S(1)}, u32[]{:S(2)}, u32[]{:S(2)}) collective-permute-start(bf16[48,16,128]{2,1,0:T(8,128)(2,1)S(1)} %slice_select_fusion), channel_id=1, source_target_pairs={{8,0},{24,16}} | collective-permute-start | bytes 589832 | tf_op jit(solution)/shard_map/ppermute | solution.py:1446
  66.6 9.4 %collective-permute-start.12 = (bf16[48,16,128]{2,1,0:T(8,128)(2,1)S(1)}, bf16[48,16,128]{2,1,0:T(8,128)(2,1)S(1)}, u32[]{:S(2)}, u32[]{:S(2)}) collective-permute-start(bf16[48,16,128]{2,1,0:T(8,128)(2,1)S(1)} %fusion.22), channel_id=1, source_target_pairs={{8,12},{0,4},{24,28},{16,20}} | collective-permute-start | bytes 589832 | tf_op jit(solution)/shard_map/ppermute | solution.py:1446
  85.5 30.9 %collective-permute-start.15 = (bf16[48,16,128]{2,1,0:T(8,128)(2,1)S(1)}, bf16[48,16,128]{2,1,0:T(8,128)(2,1)S(1)}, u32[]{:S(2)}, u32[]{:S(2)}) collective-permute-start(bf16[48,16,128]{2,1,0:T(8,128)(2,1)S(1)} %add.422), channel_id=1, source_target_pairs={{0,16},{16,0},{1,17},{17,1},{2,18},{18,2},{3,19},{19,3},{4,20},{20... | collective-permute-start | bytes 589832 | tf_op jit(solution)/shard_map/ppermute | solution.py:1448
  90.3 10.3 %collective-permute-start.2 = (f32[]{:T(128)}, f32[]{:T(128)}, u32[]{:S(2)}, u32[]{:S(2)}) collective-permute-start(f32[]{:T(128)} %add.408), channel_id=1, source_target_pairs={{0,2},{1,3},{2,0},{3,1},{4,6},{5,7},{6,4},{7,5},{8,10},{9,11},{10,... | collective-permute-start | bytes 20 | tf_op jit(solution)/shard_map/ppermute | solution.py:1403
  101.8 13.4 %collective-permute-start.5 = (f32[]{:T(128)}, f32[]{:T(128)}, u32[]{:S(2)}, u32[]{:S(2)}) collective-permute-start(f32[]{:T(128)} %add.411), channel_id=1, source_target_pairs={{0,8},{1,9},{2,10},{3,11},{4,12},{5,13},{6,14},{7,15},{8,0},{9,1},... | collective-permute-start | bytes 20 | tf_op jit(solution)/shard_map/ppermute | solution.py:1403
  371.4 13.5 %collective-permute-start.16 = (f32[8,127,16,128]{3,2,1,0:T(8,128)}, f32[8,127,16,128]{3,2,1,0:T(8,128)}, u32[]{:S(2)}, u32[]{:S(2)}) collective-permute-start(f32[8,127,16,128]{3,2,1,0:T(8,128)} %get-tuple-element.184), channel_id=1, source_target_pairs={{0,16},{16,0},{1,17},{17,1},{2,18},{18,2},{3,19},{19,3},{4,20},{20... | collective-permute-start | bytes 24969224 | tf_op jit(solution)/shard_map/ppermute | solution.py:1351
  394.0 35.1 %collective-permute-start.19 = (f32[2,2,43,16,128]{4,3,2,1,0:T(8,128)}, f32[2,2,43,16,128]{4,3,2,1,0:T(8,128)S(1)}, u32[]{:S(2)}, u32[]{:S(2)}) collective-permute-start(f32[2,2,43,16,128]{4,3,2,1,0:T(8,128)} %add_bitcast_fusion.2), channel_id=1, source_target_pairs={{0,4},{1,5},{2,6},{3,7},{4,0},{5,1},{6,2},{7,3},{8,12},{9,13},{10,... | collective-permute-start | bytes 4227080 | tf_op jit(solution)/shard_map/ppermute | solution.py:1359
  395.5 32.3 %collective-permute-start.17 = (f32[2,2,42,16,128]{4,3,2,1,0:T(8,128)}, f32[2,2,42,16,128]{4,3,2,1,0:T(8,128)S(1)}, u32[]{:S(2)}, u32[]{:S(2)}) collective-permute-start(f32[2,2,42,16,128]{4,3,2,1,0:T(8,128)} %add_bitcast_fusion.8), channel_id=1, source_target_pairs={{0,1},{1,0},{2,3},{3,2},{4,5},{5,4},{6,7},{7,6},{8,9},{9,8},{10,11... | collective-permute-start | bytes 4128776 | tf_op jit(solution)/shard_map/ppermute | solution.py:1359
  396.9 32.1 %collective-permute-start.18 = (f32[2,2,42,16,128]{4,3,2,1,0:T(8,128)}, f32[2,2,42,16,128]{4,3,2,1,0:T(8,128)}, u32[]{:S(2)}, u32[]{:S(2)}) collective-permute-start(f32[2,2,42,16,128]{4,3,2,1,0:T(8,128)} %add_bitcast_fusion.7), channel_id=1, source_target_pairs={{0,2},{1,3},{2,0},{3,1},{4,6},{5,7},{6,4},{7,5},{8,10},{9,11},{10,... | collective-permute-start | bytes 4128776 | tf_op jit(solution)/shard_map/ppermute | solution.py:1359
  397.5 29.5 %collective-permute-start.20 = (f32[1,48,16,128]{3,2,1,0:T(8,128)S(1)}, f32[1,48,16,128]{3,2,1,0:T(8,128)S(1)}, u32[]{:S(2)}, u32[]{:S(2)}) collective-permute-start(f32[1,48,16,128]{3,2,1,0:T(8,128)S(1)} %copy-done.14), channel_id=1, source_target_pairs={{0,16},{16,0},{1,17},{17,1},{2,18},{18,2},{3,19},{19,3},{4,20},{20... | collective-permute-start | bytes 1179656 | tf_op jit(solution)/shard_map/ppermute | solution.py:1351
  434.9 28.4 %collective-permute-start.23 = (f32[2,43,16,128]{3,2,1,0:T(8,128)S(1)}, f32[2,43,16,128]{3,2,1,0:T(8,128)}, u32[]{:S(2)}, u32[]{:S(2)}) collective-permute-start(f32[2,43,16,128]{3,2,1,0:T(8,128)S(1)} %bitcast_add_fusion.2), channel_id=1, source_target_pairs={{0,1},{1,0},{2,3},{3,2},{4,5},{5,4},{6,7},{7,6},{8,9},{9,8},{10,11... | collective-permute-start | bytes 2113544 | tf_op jit(solution)/shard_map/ppermute | solution.py:1359
  435.6 27.7 %collective-permute-start.21 = (f32[2,42,16,128]{3,2,1,0:T(8,128)}, f32[2,42,16,128]{3,2,1,0:T(8,128)}, u32[]{:S(2)}, u32[]{:S(2)}) collective-permute-start(f32[2,42,16,128]{3,2,1,0:T(8,128)} %get-tuple-element.247), channel_id=1, source_target_pairs={{0,2},{1,3},{2,0},{3,1},{4,6},{5,7},{6,4},{7,5},{8,10},{9,11},{10,... | collective-permute-start | bytes 2064392 | tf_op jit(solution)/shard_map/ppermute | solution.py:1359
  437.1 26.2 %collective-permute-start.22 = (f32[2,42,16,128]{3,2,1,0:T(8,128)}, f32[2,42,16,128]{3,2,1,0:T(8,128)}, u32[]{:S(2)}, u32[]{:S(2)}) collective-permute-start(f32[2,42,16,128]{3,2,1,0:T(8,128)} %get-tuple-element.248), channel_id=1, source_target_pairs={{0,4},{1,5},{2,6},{3,7},{4,0},{5,1},{6,2},{7,3},{8,12},{9,13},{10,... | collective-permute-start | bytes 2064392 | tf_op jit(solution)/shard_map/ppermute | solution.py:1359
  437.6 25.7 %collective-permute-start.24 = (f32[48,16,128]{2,1,0:T(8,128)S(1)}, f32[48,16,128]{2,1,0:T(8,128)}, u32[]{:S(2)}, u32[]{:S(2)}) collective-permute-start(f32[48,16,128]{2,1,0:T(8,128)S(1)} %add_bitcast_fusion.9), channel_id=1, source_target_pairs={{1,0},{3,2},{5,4},{7,6},{9,8},{11,10},{13,12},{15,14},{17,16},{19,... | collective-permute-start | bytes 1179656 | tf_op jit(solution)/shard_map/ppermute | solution.py:1355
  468.3 40.6 %collective-permute-start.29 = (f32[8,127,16,128]{3,2,1,0:T(8,128)}, f32[8,127,16,128]{3,2,1,0:T(8,128)}, u32[]{:S(2)}, u32[]{:S(2)}) collective-permute-start(f32[8,127,16,128]{3,2,1,0:T(8,128)} %get-tuple-element.286), channel_id=1, source_target_pairs={{0,16},{16,0},{1,17},{17,1},{2,18},{18,2},{3,19},{19,3},{4,20},{20... | collective-permute-start | bytes 24969224 | tf_op jit(solution)/shard_map/ppermute | solution.py:1351
  468.3 40.6 %collective-permute-start.28 = (f32[48,16,128]{2,1,0:T(8,128)S(1)}, f32[48,16,128]{2,1,0:T(8,128)S(1)}, u32[]{:S(2)}, u32[]{:S(2)}) collective-permute-start(f32[48,16,128]{2,1,0:T(8,128)S(1)} %add.462), channel_id=1, source_target_pairs={{2,0},{3,1},{6,4},{7,5},{10,8},{11,9},{14,12},{15,13},{18,16},{19,... | collective-permute-start | bytes 1179656 | tf_op jit(solution)/shard_map/ppermute | solution.py:1355
  469.6 39.3 %collective-permute-start.27 = (f32[43,16,128]{2,1,0:T(8,128)S(1)}, f32[43,16,128]{2,1,0:T(8,128)}, u32[]{:S(2)}, u32[]{:S(2)}) collective-permute-start(f32[43,16,128]{2,1,0:T(8,128)S(1)} %bitcast_add_fusion.19), channel_id=1, source_target_pairs={{0,2},{1,3},{2,0},{3,1},{4,6},{5,7},{6,4},{7,5},{8,10},{9,11},{10,... | collective-permute-start | bytes 1056776 | tf_op jit(solution)/shard_map/ppermute | solution.py:1359
  472.4 36.6 %collective-permute-start.25 = (f32[42,16,128]{2,1,0:T(8,128)}, f32[42,16,128]{2,1,0:T(8,128)}, u32[]{:S(2)}, u32[]{:S(2)}) collective-permute-start(f32[42,16,128]{2,1,0:T(8,128)} %get-tuple-element.282), channel_id=1, source_target_pairs={{0,4},{1,5},{2,6},{3,7},{4,0},{5,1},{6,2},{7,3},{8,12},{9,13},{10,... | collective-permute-start | bytes 1032200 | tf_op jit(solution)/shard_map/ppermute | solution.py:1359
  473.9 35.1 %collective-permute-start.26 = (f32[42,16,128]{2,1,0:T(8,128)}, f32[42,16,128]{2,1,0:T(8,128)}, u32[]{:S(2)}, u32[]{:S(2)}) collective-permute-start(f32[42,16,128]{2,1,0:T(8,128)} %get-tuple-element.283), channel_id=1, source_target_pairs={{0,1},{1,0},{2,3},{3,2},{4,5},{5,4},{6,7},{7,6},{8,9},{9,8},{10,11... | collective-permute-start | bytes 1032200 | tf_op jit(solution)/shard_map/ppermute | solution.py:1359
  522.9 63.2 %collective-permute-start.34 = (f32[2,2,43,16,128]{4,3,2,1,0:T(8,128)}, f32[2,2,43,16,128]{4,3,2,1,0:T(8,128)S(1)}, u32[]{:S(2)}, u32[]{:S(2)}) collective-permute-start(f32[2,2,43,16,128]{4,3,2,1,0:T(8,128)} %add_bitcast_fusion.1), channel_id=1, source_target_pairs={{0,4},{1,5},{2,6},{3,7},{4,0},{5,1},{6,2},{7,3},{8,12},{9,13},{10,... | collective-permute-start | bytes 4227080 | tf_op jit(solution)/shard_map/ppermute | solution.py:1359
  523.4 62.7 %collective-permute-start.32 = (f32[2,2,42,16,128]{4,3,2,1,0:T(8,128)}, f32[2,2,42,16,128]{4,3,2,1,0:T(8,128)}, u32[]{:S(2)}, u32[]{:S(2)}) collective-permute-start(f32[2,2,42,16,128]{4,3,2,1,0:T(8,128)} %add_bitcast_fusion.6), channel_id=1, source_target_pairs={{0,1},{1,0},{2,3},{3,2},{4,5},{5,4},{6,7},{7,6},{8,9},{9,8},{10,11... | collective-permute-start | bytes 4128776 | tf_op jit(solution)/shard_map/ppermute | solution.py:1359
  523.4 62.7 %collective-permute-start.33 = (f32[2,2,42,16,128]{4,3,2,1,0:T(8,128)}, f32[2,2,42,16,128]{4,3,2,1,0:T(8,128)}, u32[]{:S(2)}, u32[]{:S(2)}) collective-permute-start(f32[2,2,42,16,128]{4,3,2,1,0:T(8,128)} %add_bitcast_fusion.5), channel_id=1, source_target_pairs={{0,2},{1,3},{2,0},{3,1},{4,6},{5,7},{6,4},{7,5},{8,10},{9,11},{10,... | collective-permute-start | bytes 4128776 | tf_op jit(solution)/shard_map/ppermute | solution.py:1359
  523.4 62.6 %collective-permute-start.30 = (f32[127,16,128]{2,1,0:T(8,128)}, f32[127,16,128]{2,1,0:T(8,128)S(1)}, u32[]{:S(2)}, u32[]{:S(2)}) collective-permute-start(f32[127,16,128]{2,1,0:T(8,128)} %pad_maximum_fusion), channel_id=1, source_target_pairs={{8,0},{9,1},{10,2},{11,3},{12,4},{13,5},{14,6},{15,7},{24,16},{25,... | collective-permute-start | bytes 3121160 | tf_op jit(solution)/shard_map/ppermute | solution.py:1355
  524.7 61.3 %collective-permute-start.31 = (f32[48,16,128]{2,1,0:T(8,128)S(1)}, f32[48,16,128]{2,1,0:T(8,128)}, u32[]{:S(2)}, u32[]{:S(2)}) collective-permute-start(f32[48,16,128]{2,1,0:T(8,128)S(1)} %add.474), channel_id=1, source_target_pairs={{4,0},{5,1},{6,2},{7,3},{12,8},{13,9},{14,10},{15,11},{20,16},{21,... | collective-permute-start | bytes 1179656 | tf_op jit(solution)/shard_map/ppermute | solution.py:1355
  592.1 21.0 %collective-permute-start.35 = (f32[8,127,16,128]{3,2,1,0:T(8,128)}, f32[8,127,16,128]{3,2,1,0:T(8,128)S(1)}, u32[]{:S(2)}, u32[]{:S(2)}) collective-permute-start(f32[8,127,16,128]{3,2,1,0:T(8,128)} %get-tuple-element.331), channel_id=1, source_target_pairs={{0,16},{16,0},{1,17},{17,1},{2,18},{18,2},{3,19},{19,3},{4,20},{20... | collective-permute-start | bytes 24969224 | tf_op jit(solution)/shard_map/ppermute | solution.py:1351
  592.2 17.9 %collective-permute-start.36 = (f32[2,42,16,128]{3,2,1,0:T(8,128)S(1)}, f32[2,42,16,128]{3,2,1,0:T(8,128)S(1)}, u32[]{:S(2)}, u32[]{:S(2)}) collective-permute-start(f32[2,42,16,128]{3,2,1,0:T(8,128)S(1)} %get-tuple-element.332), channel_id=1, source_target_pairs={{0,2},{1,3},{2,0},{3,1},{4,6},{5,7},{6,4},{7,5},{8,10},{9,11},{10,... | collective-permute-start | bytes 2064392 | tf_op jit(solution)/shard_map/ppermute | solution.py:1359
  592.7 17.5 %collective-permute-start.37 = (f32[2,42,16,128]{3,2,1,0:T(8,128)S(1)}, f32[2,42,16,128]{3,2,1,0:T(8,128)S(1)}, u32[]{:S(2)}, u32[]{:S(2)}) collective-permute-start(f32[2,42,16,128]{3,2,1,0:T(8,128)S(1)} %get-tuple-element.333), channel_id=1, source_target_pairs={{0,4},{1,5},{2,6},{3,7},{4,0},{5,1},{6,2},{7,3},{8,12},{9,13},{10,... | collective-permute-start | bytes 2064392 | tf_op jit(solution)/shard_map/ppermute | solution.py:1359
  592.7 19.2 %collective-permute-start.38 = (f32[2,43,16,128]{3,2,1,0:T(8,128)S(1)}, f32[2,43,16,128]{3,2,1,0:T(8,128)S(1)}, u32[]{:S(2)}, u32[]{:S(2)}) collective-permute-start(f32[2,43,16,128]{3,2,1,0:T(8,128)S(1)} %bitcast_add_fusion.1), channel_id=1, source_target_pairs={{0,1},{1,0},{2,3},{3,2},{4,5},{5,4},{6,7},{7,6},{8,9},{9,8},{10,11... | collective-permute-start | bytes 2113544 | tf_op jit(solution)/shard_map/ppermute | solution.py:1359
  613.7 51.5 %collective-permute-start.39 = (f32[2,2,42,16,128]{4,3,2,1,0:T(8,128)S(1)}, f32[2,2,42,16,128]{4,3,2,1,0:T(8,128)S(1)}, u32[]{:S(2)}, u32[]{:S(2)}) collective-permute-start(f32[2,2,42,16,128]{4,3,2,1,0:T(8,128)S(1)} %add_bitcast_fusion.4), channel_id=1, source_target_pairs={{0,1},{1,0},{2,3},{3,2},{4,5},{5,4},{6,7},{7,6},{8,9},{9,8},{10,11... | collective-permute-start | bytes 4128776 | tf_op jit(solution)/shard_map/ppermute | solution.py:1359
  614.1 51.1 %collective-permute-start.43 = (f32[2,2,42,16,128]{4,3,2,1,0:T(8,128)S(1)}, f32[2,2,42,16,128]{4,3,2,1,0:T(8,128)S(1)}, u32[]{:S(2)}, u32[]{:S(2)}) collective-permute-start(f32[2,2,42,16,128]{4,3,2,1,0:T(8,128)S(1)} %add_bitcast_fusion.3), channel_id=1, source_target_pairs={{0,2},{1,3},{2,0},{3,1},{4,6},{5,7},{6,4},{7,5},{8,10},{9,11},{10,... | collective-permute-start | bytes 4128776 | tf_op jit(solution)/shard_map/ppermute | solution.py:1359
  615.8 49.7 %collective-permute-start.44 = (f32[2,2,43,16,128]{4,3,2,1,0:T(8,128)S(1)}, f32[2,2,43,16,128]{4,3,2,1,0:T(8,128)S(1)}, u32[]{:S(2)}, u32[]{:S(2)}) collective-permute-start(f32[2,2,43,16,128]{4,3,2,1,0:T(8,128)S(1)} %add_bitcast_fusion), channel_id=1, source_target_pairs={{0,4},{1,5},{2,6},{3,7},{4,0},{5,1},{6,2},{7,3},{8,12},{9,13},{10,... | collective-permute-start | bytes 4227080 | tf_op jit(solution)/shard_map/ppermute | solution.py:1359
  616.1 38.7 %collective-permute-start.40 = (f32[42,16,128]{2,1,0:T(8,128)S(1)}, f32[42,16,128]{2,1,0:T(8,128)S(1)}, u32[]{:S(2)}, u32[]{:S(2)}) collective-permute-start(f32[42,16,128]{2,1,0:T(8,128)S(1)} %get-tuple-element.336), channel_id=1, source_target_pairs={{0,4},{1,5},{2,6},{3,7},{4,0},{5,1},{6,2},{7,3},{8,12},{9,13},{10,... | collective-permute-start | bytes 1032200 | tf_op jit(solution)/shard_map/ppermute | solution.py:1359
  617.8 37.5 %collective-permute-start.41 = (f32[42,16,128]{2,1,0:T(8,128)S(1)}, f32[42,16,128]{2,1,0:T(8,128)S(1)}, u32[]{:S(2)}, u32[]{:S(2)}) collective-permute-start(f32[42,16,128]{2,1,0:T(8,128)S(1)} %get-tuple-element.337), channel_id=1, source_target_pairs={{0,1},{1,0},{2,3},{3,2},{4,5},{5,4},{6,7},{7,6},{8,9},{9,8},{10,11... | collective-permute-start | bytes 1032200 | tf_op jit(solution)/shard_map/ppermute | solution.py:1359
  665.7 14.4 %collective-permute-start.45 = (f32[2,42,16,128]{3,2,1,0:T(8,128)S(1)}, f32[2,42,16,128]{3,2,1,0:T(8,128)S(1)}, u32[]{:S(2)}, u32[]{:S(2)}) collective-permute-start(f32[2,42,16,128]{3,2,1,0:T(8,128)S(1)} %get-tuple-element.341), channel_id=1, source_target_pairs={{0,2},{1,3},{2,0},{3,1},{4,6},{5,7},{6,4},{7,5},{8,10},{9,11},{10,... | collective-permute-start | bytes 2064392 | tf_op jit(solution)/shard_map/ppermute | solution.py:1359
  666.5 15.1 %collective-permute-start.46 = (f32[2,42,16,128]{3,2,1,0:T(8,128)S(1)}, f32[2,42,16,128]{3,2,1,0:T(8,128)S(1)}, u32[]{:S(2)}, u32[]{:S(2)}) collective-permute-start(f32[2,42,16,128]{3,2,1,0:T(8,128)S(1)} %get-tuple-element.342), channel_id=1, source_target_pairs={{0,4},{1,5},{2,6},{3,7},{4,0},{5,1},{6,2},{7,3},{8,12},{9,13},{10,... | collective-permute-start | bytes 2064392 | tf_op jit(solution)/shard_map/ppermute | solution.py:1359
  667.0 14.8 %collective-permute-start.47 = (f32[2,43,16,128]{3,2,1,0:T(8,128)S(1)}, f32[2,43,16,128]{3,2,1,0:T(8,128)S(1)}, u32[]{:S(2)}, u32[]{:S(2)}) collective-permute-start(f32[2,43,16,128]{3,2,1,0:T(8,128)S(1)} %bitcast_add_fusion), channel_id=1, source_target_pairs={{0,1},{1,0},{2,3},{3,2},{4,5},{5,4},{6,7},{7,6},{8,9},{9,8},{10,11... | collective-permute-start | bytes 2113544 | tf_op jit(solution)/shard_map/ppermute | solution.py:1359
  681.9 10.8 %collective-permute-start.48 = (f32[42,16,128]{2,1,0:T(8,128)S(1)}, f32[42,16,128]{2,1,0:T(8,128)S(1)}, u32[]{:S(2)}, u32[]{:S(2)}) collective-permute-start(f32[42,16,128]{2,1,0:T(8,128)S(1)} %get-tuple-element.344), channel_id=1, source_target_pairs={{0,4},{1,5},{2,6},{3,7},{4,0},{5,1},{6,2},{7,3},{8,12},{9,13},{10,... | collective-permute-start | bytes 1032200 | tf_op jit(solution)/shard_map/ppermute | solution.py:1359
  684.2 8.5 %collective-permute-start.49 = (f32[42,16,128]{2,1,0:T(8,128)S(1)}, f32[42,16,128]{2,1,0:T(8,128)S(1)}, u32[]{:S(2)}, u32[]{:S(2)}) collective-permute-start(f32[42,16,128]{2,1,0:T(8,128)S(1)} %get-tuple-element.345), channel_id=1, source_target_pairs={{0,1},{1,0},{2,3},{3,2},{4,5},{5,4},{6,7},{7,6},{8,9},{9,8},{10,11... | collective-permute-start | bytes 1032200 | tf_op jit(solution)/shard_map/ppermute | solution.py:1359
  686.3 31.7 %collective-permute-start.52 = (f32[127,16,128]{2,1,0:T(8,128)}, f32[127,16,128]{2,1,0:T(8,128)}, u32[]{:S(2)}, u32[]{:S(2)}) collective-permute-start(f32[127,16,128]{2,1,0:T(8,128)} %pad_maximum_fusion.1), channel_id=1, source_target_pairs={{0,8},{1,9},{2,10},{3,11},{4,12},{5,13},{6,14},{7,15},{16,24},{17,... | collective-permute-start | bytes 3121160 | tf_op jit(solution)/shard_map/ppermute | solution.py:1355
  694.4 43.2 %collective-permute-start.51 = (f32[127,16,128]{2,1,0:T(8,128)}, f32[127,16,128]{2,1,0:T(8,128)}, u32[]{:S(2)}, u32[]{:S(2)}) collective-permute-start(f32[127,16,128]{2,1,0:T(8,128)} %pad_maximum_fusion.2), channel_id=1, source_target_pairs={{8,0},{9,1},{10,2},{11,3},{12,4},{13,5},{14,6},{15,7},{24,16},{25,... | collective-permute-start | bytes 3121160 | tf_op jit(solution)/shard_map/ppermute | solution.py:1355
  698.1 19.9 %collective-permute-start.53 = (f32[48,16,128]{2,1,0:T(8,128)S(1)}, f32[48,16,128]{2,1,0:T(8,128)S(1)}, u32[]{:S(2)}, u32[]{:S(2)}) collective-permute-start(f32[48,16,128]{2,1,0:T(8,128)S(1)} %add.481), channel_id=1, source_target_pairs={{0,8},{1,9},{2,10},{3,11},{4,12},{5,13},{6,14},{7,15},{16,24},{17,... | collective-permute-start | bytes 1179656 | tf_op jit(solution)/shard_map/ppermute | solution.py:1355
  744.1 28.6 %collective-permute-start.61 = (f32[127,16,128]{2,1,0:T(8,128)S(1)}, f32[127,16,128]{2,1,0:T(8,128)}, u32[]{:S(2)}, u32[]{:S(2)}) collective-permute-start(f32[127,16,128]{2,1,0:T(8,128)S(1)} %get-tuple-element.377), channel_id=1, source_target_pairs={{0,16},{16,0},{1,17},{17,1},{2,18},{18,2},{3,19},{19,3},{4,20},{20... | collective-permute-start | bytes 3121160 | tf_op jit(solution)/shard_map/ppermute | solution.py:1557
  759.8 18.2 %collective-permute-start.58 = (f32[2]{0:T(128)S(1)}, f32[2]{0:T(128)S(1)}, u32[]{:S(2)}, u32[]{:S(2)}) collective-permute-start(f32[2]{0:T(128)S(1)} %add_add_fusion.2), channel_id=1, source_target_pairs={{0,4},{1,5},{2,6},{3,7},{4,0},{5,1},{6,2},{7,3},{8,12},{9,13},{10,... | collective-permute-start | bytes 32 | tf_op jit(solution)/shard_map/ppermute | solution.py:1403
  769.3 8.7 %collective-permute-start.59 = (f32[2]{0:T(128)S(1)}, f32[2]{0:T(128)S(1)}, u32[]{:S(2)}, u32[]{:S(2)}) collective-permute-start(f32[2]{0:T(128)S(1)} %add_add_fusion.2), channel_id=1, source_target_pairs={{0,8},{1,9},{2,10},{3,11},{4,12},{5,13},{6,14},{7,15},{8,0},{9,1},... | collective-permute-start | bytes 32 | tf_op jit(solution)/shard_map/ppermute | solution.py:1403
  (37 other events, 345.8 us)
Sparse Core Ops, SparseCore 0:
  29.2 122.0 all-gather.4
  154.2 75.8 all-gather.2

commit v4 on v3

--- a/solution.py
+++ b/solution.py
@@ -36,6 +36,7 @@
 GROUP = 16
 VEC_UNITS = 2
 VMEM_BYTES = 60 * 1024 * 1024
+COST = 2e8
 ANY = pl.BlockSpec(memory_space=pl.ANY)
 IN_VMEM = pl.BlockSpec(memory_space=pltpu.VMEM)
 IN_SMEM = pl.BlockSpec(memory_space=pltpu.SMEM)
@@ -361,12 +362,9 @@
     lax.fori_loop(0, count // size, body, 0, unroll=unroll)
 
 
-def columns(weight, panels, depth, pair):
-    halves = [
-        weight[:, 2 * pair + i].reshape(depth, 128)
-        for i in range(2)
-    ]
-    return jnp.concatenate(halves, axis=1)
+def columns(weight, depth, first, count):
+    parts = [weight[:, first + i].reshape(depth, 128) for i in range(count)]
+    return jnp.concatenate(parts, axis=1)
 
 
 def row_band(weight, panels, band):
@@ -379,20 +377,29 @@
     return [slice(at, at + size) for at in range(0, count, size)]
 
 
+def wide_chunks(count):
+    size = next(n for n in (416, 336, 112, 104, 16) if count % n == 0)
+    return [slice(at, at + size) for at in range(0, count, size)]
+
+
 def times_columns(left, weight, panels, depth, finish):
-    def body(pair, carry):
-        right = columns(weight, panels, depth, pair)
+    group = 4 if panels % 4 == 0 else 2
+
+    def body(index, carry):
+        right = columns(weight, depth, group * index, group)
+        width = group * 128
+        there = pl.ds(pl.multiple_of(index * width, width), width)
         for here in row_chunks(left.shape[0]):
-            finish(pair, here, dot(left[here, :], right))
+            finish(index * width, here, there, dot(left[here, :], right))
         return carry
 
-    lax.fori_loop(0, panels // 2, body, 0)
+    lax.fori_loop(0, panels // group, body, 0)
 
 
 def times_bands(left, weight, panels, count, finish):
     def body(band, carry):
         right = row_band(weight, panels, band)
-        for here in row_chunks(left.shape[0]):
+        for here in wide_chunks(left.shape[0]):
             finish(here, lanes(band), dot_nt(left[here, :], right))
         return carry
 
@@ -488,7 +495,7 @@
         out[here, pl.ds(pl.multiple_of(panel * 128, 128), 128)] = total.astype(BF16)
         return carry
 
-    lax.fori_loop(0, images * panels, body, 0, unroll=4)
+    lax.fori_loop(0, images * panels, body, 0, unroll=6)
 
 
 def attention_backward(mixed, grad_out, grad_mixed, limit_of, images, rows, width, size):
@@ -524,7 +531,7 @@
         grad_mixed[here, place(2)] = grad_values.astype(BF16)
         return carry
 
-    lax.fori_loop(0, images * panels, body, 0, unroll=2)
+    lax.fori_loop(0, images * panels, body, 0, unroll=3)
 
 
 def gelu_parts(value):
@@ -548,9 +555,9 @@
     saved(n1)
     ready("qkv")
 
-    def put_mixed(pair, here, value):
-        scale = jnp.where(pair < panels // 2, 1.0 / math.sqrt(sh.size), 1.0)
-        mixed[here, lanes(pair)] = (value * scale).astype(BF16)
+    def put_mixed(start, here, there, value):
+        scale = jnp.where(start < width, 1.0 / math.sqrt(sh.size), 1.0)
+        mixed[here, there] = (value * scale).astype(BF16)
 
     times_columns(n1, w["qkv"], 3 * panels, width, put_mixed)
     saved(mixed)
@@ -559,8 +566,8 @@
     ready("proj")
 
     def put_sum(base, out):
-        def finish(pair, here, value):
-            out[here, lanes(pair)] = base[here, lanes(pair)] + value
+        def finish(_, here, there, value):
+            out[here, there] = base[here, there] + value
 
         return finish
 
@@ -570,10 +577,10 @@
     saved(n2)
     ready("fc1")
 
-    def put_hidden(pair, here, value):
+    def put_hidden(_, here, there, value):
         value, slope = gelu_parts(value)
-        g[here, lanes(pair)] = value.astype(BF16)
-        gp[here, lanes(pair)] = slope
+        g[here, there] = value.astype(BF16)
+        gp[here, there] = slope
 
     times_columns(n2, w["fc1"], hidden // 128, width, put_hidden)
     saved(g)
@@ -712,18 +719,22 @@
         self.ready(None, x1)
         self.through_norm(x1, dn, dy, "g2", "b2")
 
-    def attention(self, dy, dyb, o, mixed, dmixed):
+    def projection(self, dy, dyb, o, grad):
         sh = self.sh
         self.round_stream(dy, dyb)
         self.ready("proj", o)
         self.grads.weight("proj", o, sh.width, dyb, self.turned)
 
         def put(here, there, value):
-            o[here, there] = value.astype(BF16)
+            grad[here, there] = value.astype(BF16)
 
         self.bands(dyb, "proj", sh.width, put)
+
+    def attention(self, grad, mixed, dmixed):
+        sh = self.sh
+        self.ready(None, grad)
         self.ready(None, mixed)
-        attention_backward(mixed, o, dmixed, self.limit_of, sh.images, sh.rows, sh.width, sh.size)
+        attention_backward(mixed, grad, dmixed, self.limit_of, sh.images, sh.rows, sh.width, sh.size)
 
     def mixing(self, dy, dmixed, n1, x0, dn):
         def put(here, there, value):
@@ -858,9 +869,8 @@
     vec = finish_vec()
     ready("patch")
 
-    def put(pair, here, value):
-        part = vec_ref[0:1, lanes(pair)]
-        x0[here, lanes(pair)] = (value + part) + x0[here, lanes(pair)]
+    def put(_, here, there, value):
+        x0[here, there] = (value + vec_ref[0:1, there]) + x0[here, there]
 
     times_columns(xe, w["patch"], D // 128, PIX, put)
     saved(x0)
@@ -875,7 +885,7 @@
 
 def lasting(microseconds):
     return pl.CostEstimate(
-        flops=int(microseconds * 1e9), bytes_accessed=1 << 20, transcendentals=0
+        flops=int(microseconds * COST), bytes_accessed=1 << 20, transcendentals=0
     )
 
 
@@ -946,8 +956,8 @@
     copy_latent.wait()
     ready("embed")
 
-    def put_embedded(pair, here, value):
-        embedded[here, lanes(pair)] = value
+    def put_embedded(_, here, there, value):
+        embedded[here, there] = value
 
     times_columns(latent, w["embed"], DD // 128, D, put_embedded)
 
@@ -978,7 +988,7 @@
         here = pl.ds(start, ROWS_D)
         for pair in range(PIX // 256):
             guess[:, pair * 256 : pair * 256 + 256] = dot(
-                f[here, :], columns(w["head"], PIX // 128, DD, pair)
+                f[here, :], columns(w["head"], DD, 2 * pair, 2)
             )
 
         def rows(i, total):
@@ -1019,7 +1029,8 @@
     back.second_product(y, f, g, gp)
     back.first_product(y, g, n2, x1, dn)
     dmixed = g.at[:, pl.ds(0, 3 * DD)]
-    back.attention(y, f, o, mixed, dmixed)
+    back.projection(y, f, o, o)
+    back.attention(o, mixed, dmixed)
     back.mixing(y, dmixed, n1, x0, dn)
 
     def split(image, total):
@@ -1174,6 +1185,7 @@
             "n2": ((count, width), BF16),
             "o": ((count, width), BF16),
             "dyb": ((count, width), BF16),
+            "do": ((count, width), BF16),
             "xe": ((count, PIX), BF16),
             "mixed": ((count, 3 * width), BF16),
             "dmixed": ((count, 3 * width), BF16),
@@ -1245,9 +1257,13 @@
     back.first_product(out["dy"], r["g"], r["n2"], r["x1"], r["dn"])
 
 
+def back_projection(back, r, out):
+    back.ready(None, r["dy"])
+    back.projection(r["dy"], r["dyb"], r["o"], out["do"])
+
+
 def back_attention(back, r, out):
-    back.ready(None, r["dy"])
-    back.attention(r["dy"], r["dyb"], r["o"], r["mixed"], out["dmixed"])
+    back.attention(r["do"], r["mixed"], out["dmixed"])
 
 
 def back_mixing(back, r, out):
@@ -1274,8 +1290,10 @@
               "encoder_back_fc2", back_second),
         Stage(plan, sh, ["fc1"], ["g", "dy", "n2", "x1"], ["dn"], ["dy"], most["fc1"], 20,
               "encoder_back_fc1", back_first),
-        Stage(plan, sh, ["proj"], ["dy", "o", "mixed"], ["dyb"], ["dmixed"], most["proj"], 35,
-              "encoder_back_attention", back_attention, 1),
+        Stage(plan, sh, ["proj"], ["dy", "o"], ["dyb"], ["do"], most["proj"], 10,
+              "encoder_back_proj", back_projection, 1),
+        Stage(plan, sh, [], ["do", "mixed"], [], ["dmixed"], 1, 25,
+              "encoder_back_attention", back_attention, 0),
         Stage(plan, sh, ["qkv"], ["dy", "dmixed", "n1", "x0", "xe"], ["dn", "dyb"], [],
               most["qkv"], 25, "encoder_back_qkv", back_mixing, 1),
     ]
@@ -1333,6 +1351,9 @@
 
     def done(self):
         return self.step == self.all_bits
+
+    def last(self):
+        return self.step == self.all_bits - 1
 
     def payload(self):
         if self.step < 0:
@@ -1525,17 +1546,24 @@
     first_tail = plan.bins(1)[1][0]
     main = Flow(dp, sums_d[0], sums_d[1], 0)
     rest = Flow(dp, sums_d[2], sums_d[3], first_tail, 1)
-    flows, got, _ = move_on([main])
+    flows, got, _ = move_on([main, rest])
     got, arrays = tie(got, arrays)
     arrive(flows, got)
     low = high = None
     blocks = []
+    late = []
     for number, stage in enumerate(stages):
         flows, got, (arrays, blocks) = move_on([main, rest, high], arrays, blocks)
-        blocks, made = stage(info, gathered_e, arrays, blocks)
+        if stage.bins:
+            blocks, made = stage(info, gathered_e, arrays, blocks)
+        else:
+            _, made = stage(info, gathered_e, arrays, [])
         arrays = {**arrays, **made}
-        got, arrays, blocks = tie(got, arrays, blocks)
-        arrive(flows, got)
+        kept = [g for f, g in zip(flows, got) if not f.last()]
+        kept, late, arrays, blocks = tie(kept, late, arrays, blocks)
+        late = [g for f, g in zip(flows, got) if f.last()]
+        kept = iter(kept)
+        arrive(flows, [g if f.last() else next(kept) for f, g in zip(flows, got)])
         if number == 1:
             high = Flow(dp, blocks[2], blocks[3], dp // 2)
             blocks = blocks[:2]

time: 812 us -> 785 us (0.967)
  starting transfers between devices: 99.2 us -> 88 us
  Pallas kernels: 310 us -> 300 us
  waiting for transfers between devices: 289 us -> 280 us
    ppermute x7, waiting for transfers between devices: 65.9 us -> 44.6 us  [send(): return [lax.ppermute(payload[0], 'dp', pairs)]]
    ppermute x27, waiting for transfers between devices: 75.8 us -> 86.5 us  [send(): lax.ppermute(value, 'dp', [(i, i ^ flip) for i in range(self.dp)])]
    ppermute x12, starting transfers between devices: 35.6 us -> 27.1 us  [sum_everywhere(): lax.ppermute(value, 'dp', [(i, i ^ flip << low) for i in range(dp)])]
    pallas_call x4 -> x5, Pallas kernels: 108 us -> 107 us  [__call__(): pl.pallas_call(functools.partial(self.kernel, len(blocks)), out_shape=[*t...]
  transfers between devices with their start and end apart: 65 -> 65, of which waited for: 29 -> 33; matrix products, arithmetic and copies ran while one was open for 4% -> 5% of each run, Pallas kernels for 18% -> 19%
where the time goes in v4:
time: 785 us; the launch traced here: 779 us
  Pallas kernels  300 us (38%)
  waiting for transfers between devices  280 us (36%)
  starting transfers between devices  88 us (11%)
  other arithmetic  69.3 us (9%)
  between operations  26.1 us (3%)
  local copies, waits for them, and re-layouts  16.5 us (2%)
    pallas_call x1, Pallas kernels, decoder(): pl.pallas_call(lambda *refs: decoder_kernel(plan, sh, refs), out_shape=[*...  135 us
    pallas_call x5, Pallas kernels, __call__(): pl.pallas_call(functools.partial(self.kernel, len(blocks)), out_shape=[*t...  107 us
    ppermute x27, waiting for transfers between devices, send(): lax.ppermute(value, 'dp', [(i, i ^ flip) for i in range(self.dp)])  86.5 us
    add x39, other arithmetic, total_of(): total = total + term  55.2 us
    ppermute x7, waiting for transfers between devices, send(): return [lax.ppermute(payload[0], 'dp', pairs)]  44.6 us
    all_gather x1, waiting for transfers between devices, gather_decoder(): gathered = lax.all_gather(spread, ('section', 'dp'), axis=0, tiled=True)  41 us
    pallas_call x1, Pallas kernels, encoder(): pl.pallas_call(lambda *refs: encoder_kernel(plan, sh, refs), out_shape=[j...  37.8 us
    ppermute x4, waiting for transfers between devices, gather_decoder(): rest = rest + lax.ppermute(rest, 'dp', [(i, i ^ 1 << bit) for i in holders])  36.1 us
  transfers between devices with their start and end apart: 65, of which 33 were waited for; matrix products, arithmetic and copies ran while one was open for 5% of the time, Pallas kernels for 19%

profile of v4, /device:TPU:0, one launch (start us, length us, event | category | flops | bytes accessed | tf_op | source)
XLA Modules:
  0.0 779.5 jit_solution(11432253772359391067)
XLA Ops:
  10.4 7.5 collective-permute-done.7.following
  19.4 6.8 pack_rows.1
  29.2 4.6 collective-permute-start.10
  34.5 5.1 collective-permute-done.10
  41.7 24.9 %collective-permute-done.11 = bf16[48,16,128]{2,1,0:T(8,128)(2,1)S(1)} collective-permute-done((bf16[48,16,128]{2,1,0:T(8,128)(2,1)S(1)}, bf16[48,16,128]{2,1,0:T(8,128)(2,1)S(1)}, u32[]{:S(2)}, u32[]{:S(2)}) %collective-permute-start.11) | collective-permute-done | bytes 196640 | tf_op jit(solution)/shard_map/ppermute | solution.py:1467
  67.9 8.1 %collective-permute-done.12 = bf16[48,16,128]{2,1,0:T(8,128)(2,1)S(1)} collective-permute-done((bf16[48,16,128]{2,1,0:T(8,128)(2,1)S(1)}, bf16[48,16,128]{2,1,0:T(8,128)(2,1)S(1)}, u32[]{:S(2)}, u32[]{:S(2)}) %collective-permute-start.12) | collective-permute-done | bytes 196640 | tf_op jit(solution)/shard_map/ppermute | solution.py:1467
  77.4 3.2 collective-permute-done.13
  90.3 3.8 collective-permute-start.2
  101.8 5.5 collective-permute-start.5
  107.3 3.8 collective-permute-start.6
  117.2 34.1 %all-gather.5.cloned.1.call-done = bf16[4064,16,128]{2,1,0:T(8,128)(2,1)} async-done(((bf16[127,16,128]{2,1,0:T(8,128)(2,1)}), bf16[4064,16,128]{2,1,0:T(8,128)(2,1)}) %all-gather.5.cloned.1.call-update) | async-done | bytes 16646160 | tf_op jit(solution)/shard_map/all_gather | solution.py:1518
  151.4 37.8 %encoder_forward.1 = (bf16[6,208,768]{2,1,0:T(8,128)(2,1)}, f32[672,768]{1,0:T(8,128)}, bf16[672,768]{1,0:T(8,128)(2,1)}, bf16[672,2304]{1,0:T(8,128)(2,1)}, bf1...) custom-call(s32[7]{0:T(128)} %pad_add_fusion.refs_0_, ...), custom_call_target="tpu_custom_call" | custom-call | flops 10000000000 | bytes 1048576 | tf_op jit(solution)/shard_map/encoder_forward/pallas_call | solution.py:913
  189.2 41.0 %all-gather.3.cloned.1.call-done = bf16[2048,16,128]{2,1,0:T(8,128)(2,1)} async-done(((bf16[64,16,128]{2,1,0:T(8,128)(2,1)}), bf16[2048,16,128]{2,1,0:T(8,128)(2,1)}) %all-gather.3.cloned.1.call-update) | async-done | bytes 8388624 | tf_op jit(solution)/shard_map/all_gather | solution.py:1472
  230.2 134.6 %decoder_both.1 = (f32[8,127,16,128]{3,2,1,0:T(8,128)}, f32[8,127,16,128]{3,2,1,0:T(8,128)}, f32[1,48,16,128]{3,2,1,0:T(8,128)}, f32[1,48,16,128]{3,2,1,0:T(8,12...) custom-call(s32[7]{0:T(128)} %pad_add_fusion.refs_0_, f32[1]{0:T(128)} %bitcast.3.refs_1_, ...), custom_call_target="tpu_custom_call" | custom-call | flops 32000000000 | bytes 1048576 | tf_op jit(solution)/shard_map/decoder_both/pallas_call | solution.py:1080
  365.4 4.6 collective-permute-done.17
  370.0 8.8 %collective-permute-done.16 = f32[8,127,16,128]{3,2,1,0:T(8,128)} collective-permute-done((f32[8,127,16,128]{3,2,1,0:T(8,128)}, f32[8,127,16,128]{3,2,1,0:T(8,128)}, u32[]{:S(2)}, u32[]{:S(2)}) %collective-permute-start.16) | collective-permute-done | bytes 8323104 | tf_op jit(solution)/shard_map/ppermute | solution.py:1372
  378.8 3.0 add_bitcast_fusion.2
  381.9 3.0 add_bitcast_fusion.7
  384.9 3.1 add_bitcast_fusion.8
  392.9 28.2 %encoder_back_fc2.1 = (f32[8,127,16,128]{3,2,1,0:T(8,128)}, f32[8,127,16,128]{3,2,1,0:T(8,128)}, f32[8,127,16,128]{3,2,1,0:T(8,128)}, f32[8,127,16,128]{3,2,1,0:...) custom-call(s32[7]{0:T(128)} %pad_add_fusion.refs_0_, bf16[2,16,127,16,128]{4,3,2,1,0:T(8,128)(2,1)} %bitcast.255, ...), custom_call_target="tpu_custom_call" | custom-call | flops 5000000000 | bytes 1048576 | tf_op jit(solution)/shard_map/encoder_back_fc2/pallas_call | solution.py:1198
  421.2 9.1 %collective-permute-done.21 = f32[48,16,128]{2,1,0:T(8,128)S(1)} collective-permute-done((f32[48,16,128]{2,1,0:T(8,128)S(1)}, f32[48,16,128]{2,1,0:T(8,128)S(1)}, u32[]{:S(2)}, u32[]{:S(2)}) %collective-permute-start.21) | collective-permute-done | bytes 393248 | tf_op jit(solution)/shard_map/ppermute | solution.py:1376
  431.8 3.5 bitcast_add_fusion.7
  438.6 23.3 %encoder_back_fc1.1 = (f32[8,127,16,128]{3,2,1,0:T(8,128)}, f32[8,127,16,128]{3,2,1,0:T(8,128)}, f32[8,127,16,128]{3,2,1,0:T(8,128)}, f32[8,127,16,128]{3,2,1,0:T(8,128)}, f32[672,768]{1,0:T(8,128)}) custom-call(s32[7]{0:T(128)} %pad_add_fusion.refs_0_, ...), custom_call_target="tpu_custom_call", output_to_operand_aliasing={{0}: (6, {}), {1}: (7, {}), {2}: (8, {}), {3}: (9, {})} | custom-call | flops 4000000000 | bytes 1048576 | tf_op jit(solution)/shard_map/encoder_back_fc1/pallas_call | solution.py:1198
  465.0 2.7 bitcast_add_fusion.41
  469.0 2.8 collective-permute-start.28
  476.4 8.2 %encoder_back_proj.1 = (f32[8,127,16,128]{3,2,1,0:T(8,128)}, f32[8,127,16,128]{3,2,1,0:T(8,128)}, bf16[672,768]{1,0:T(8,128)(2,1)}) custom-call(s32[7]{0:T(128)} %pad_add_fusion.refs_0_, bf16[2,16,127,16,128]{4,3,2,1,0:T(8,128)(2,1)} %bitcast.257, f32[672,768]{1,0:T(8,128)} %get-tuple-element.361.refs_2_, ...), custom_call_target="tpu_custom_call", output_to_operand_aliasing={{0}: (4, {}), {1}: (5, {})} | custom-call | flops 2000000000 | bytes 1048576 | tf_op jit(solution)/shard_map/encoder_back_proj/pallas_call | solution.py:1198
  484.7 4.0 collective-permute-done.26
  488.7 3.2 add_bitcast_fusion.1
  491.8 3.0 add_bitcast_fusion.5
  494.8 3.1 add_bitcast_fusion.6
  504.4 2.7 collective-permute-start.32
  508.4 25.1 %encoder_back_attention.1.refs_3_ = bf16[672,2304]{1,0:T(8,128)(2,1)} custom-call(s32[7]{0:T(128)} %pad_add_fusion.refs_0_, bf16[2,16,127,16,128]{4,3,2,1,0:T(8,128)(2,1)} %bitcast.258, bf16[672,768]{1,0:T(8,128)(2,1)} %get-tuple-element.337.refs_2_, bf16[672,2304]{1,0:T(8,128)(2,1)} %get-tuple-element.338.refs_3_), custom_call_target="tpu_custom_call" | custom-call | flops 5000000000 | bytes 1048576 | tf_op jit(solution)/shard_map/encoder_back_attention/pallas_call | solution.py:1198
  537.2 20.2 %collective-permute-done.33 = f32[2,2,43,16,128]{4,3,2,1,0:T(8,128)S(1)} collective-permute-done((f32[2,2,43,16,128]{4,3,2,1,0:T(8,128)}, f32[2,2,43,16,128]{4,3,2,1,0:T(8,128)S(1)}, u32[]{:S(2)}, u32[]{:S(2)}) %collective-permute-start.33) | collective-permute-done | bytes 1409056 | tf_op jit(solution)/shard_map/ppermute | solution.py:1380
  557.4 2.8 bitcast_add_fusion.1
  560.2 3.3 bitcast_add_fusion.5
  565.6 2.7 collective-permute-start.34
  569.6 21.9 %encoder_back_qkv.1 = (f32[8,127,16,128]{3,2,1,0:T(8,128)}, f32[8,127,16,128]{3,2,1,0:T(8,128)}) custom-call(s32[7]{0:T(128)} %pad_add_fusion.refs_0_, bf16[2,16,127,16,128]{4,3,2,1,0:T(8,128)(2,1)} %bitcast.259, f32[672,768]{1,0:T(8,128)} %get-tuple-element.361.refs_2_, ...), custom_call_target="tpu_custom_call", output_to_operand_aliasing={{0}: (7, {}), {1}: (8, {})} | custom-call | flops 5000000000 | bytes 1048576 | tf_op jit(solution)/shard_map/encoder_back_qkv/pallas_call | solution.py:1198
  597.1 8.6 %collective-permute-done.40 = f32[42,16,128]{2,1,0:T(8,128)S(1)} collective-permute-done((f32[42,16,128]{2,1,0:T(8,128)S(1)}, f32[42,16,128]{2,1,0:T(8,128)S(1)}, u32[]{:S(2)}, u32[]{:S(2)}) %collective-permute-start.40) | collective-permute-done | bytes 344096 | tf_op jit(solution)/shard_map/ppermute | solution.py:1380
  613.3 30.9 %collective-permute-done.43 = f32[2,2,42,16,128]{4,3,2,1,0:T(8,128)S(1)} collective-permute-done((f32[2,2,42,16,128]{4,3,2,1,0:T(8,128)S(1)}, f32[2,2,42,16,128]{4,3,2,1,0:T(8,128)S(1)}, u32[]{:S(2)}, u32[]{:S(2)}) %collective-permute-start.43) | collective-permute-done | bytes 1376288 | tf_op jit(solution)/shard_map/ppermute | solution.py:1380
  649.2 12.0 %collective-permute-done.46 = f32[2,42,16,128]{3,2,1,0:T(8,128)S(1)} collective-permute-done((f32[2,42,16,128]{3,2,1,0:T(8,128)S(1)}, f32[2,42,16,128]{3,2,1,0:T(8,128)S(1)}, u32[]{:S(2)}, u32[]{:S(2)}) %collective-permute-start.46) | collective-permute-done | bytes 688160 | tf_op jit(solution)/shard_map/ppermute | solution.py:1380
  666.3 3.6 collective-permute-start.53
  669.9 3.3 collective-permute-done.49
  681.8 9.5 %collective-permute-done.53 = f32[127,16,128]{2,1,0:T(8,128)} collective-permute-done((f32[127,16,128]{2,1,0:T(8,128)}, f32[127,16,128]{2,1,0:T(8,128)}, u32[]{:S(2)}, u32[]{:S(2)}) %collective-permute-start.53) | collective-permute-done | bytes 1040416 | tf_op jit(solution)/shard_map/ppermute | solution.py:1376
  693.5 26.0 %collective-permute-done.52 = f32[127,16,128]{2,1,0:T(8,128)} collective-permute-done((f32[127,16,128]{2,1,0:T(8,128)}, f32[127,16,128]{2,1,0:T(8,128)}, u32[]{:S(2)}, u32[]{:S(2)}) %collective-permute-start.52) | collective-permute-done | bytes 1040416 | tf_op jit(solution)/shard_map/ppermute | solution.py:1376
  722.0 4.3 select_reduce_fusion
  741.7 4.3 collective-permute-start.60
  754.8 5.9 unpack_rows.1.total
  761.9 8.2 %update_states.1 = (f32[3747,1,128]{2,1,0:T(1,128)}, f32[3747,1,128]{2,1,0:T(1,128)}, f32[3747,1,128]{2,1,0:T(1,128)}, f32[3747,1,128]{2,1,0:T(1,128)}) custom-call(f32[1]{0:T(128)} %bitcast.104.factor_ref, f32[3760,128]{1,0:T(8,128)} %copy-done.3, f32[3747,1,128]{2,1,0:T(1,128)} %bitcast.251, f32[3747,1,128]{2,1,0:T(1,128)} %bitcast.296, ...), custom_call_target="tpu_custom_call" | custom-call | tf_op jit(solution)/shard_map/update_states/pallas_call | solution.py:323
  (214 shorter events, 123.7 us)
Async XLA Ops:
  7.2 144.2 %all-gather.5.cloned.1.call-start = ((), (), s32[]{:S(2)}) async-start(), calls=%async_computation.1 | async-start | bytes 17166336 | tf_op jit(solution)/shard_map/all_gather | solution.py:1518
  8.2 9.7 %collective-permute-start.7 = (f32[384,1,128]{2,1,0:T(1,128)S(1)}, f32[384,1,128]{2,1,0:T(1,128)S(1)}, u32[]{:S(2)}, u32[]{:S(2)}) collective-permute-start(f32[384,1,128]{2,1,0:T(1,128)S(1)} %slice_bitcast_fusion), channel_id=1, source_target_pairs={{1,0},{2,1},{3,2},{4,3},{5,4},{6,5},{7,6},{8,7},{9,8},{10,9},{11,1... | collective-permute-start | bytes 589832 | tf_op jit(solution)/shard_map/ppermute | solution.py:1507
  29.1 201.1 %all-gather.3.cloned.1.call-start = ((), (), s32[]{:S(2)}) async-start(), calls=%async_computation | async-start | bytes 8650752 | tf_op jit(solution)/shard_map/all_gather | solution.py:1472
  29.2 10.4 %collective-permute-start.10 = (bf16[64,16,128]{2,1,0:T(8,128)(2,1)S(1)}, bf16[64,16,128]{2,1,0:T(8,128)(2,1)S(1)}, u32[]{:S(2)}, u32[]{:S(2)}) collective-permute-start(bf16[64,16,128]{2,1,0:T(8,128)(2,1)S(1)} %get-tuple-element.424), channel_id=1, source_target_pairs={{0,1},{1,3},{2,5},{3,7},{4,9},{5,11},{6,13},{7,15},{16,17},{17,19}... | collective-permute-start | bytes 786440 | tf_op jit(solution)/shard_map/ppermute | solution.py:1456
  40.4 26.2 %collective-permute-start.11 = (bf16[48,16,128]{2,1,0:T(8,128)(2,1)S(1)}, bf16[48,16,128]{2,1,0:T(8,128)(2,1)S(1)}, u32[]{:S(2)}, u32[]{:S(2)}) collective-permute-start(bf16[48,16,128]{2,1,0:T(8,128)(2,1)S(1)} %slice_select_fusion), channel_id=1, source_target_pairs={{8,0},{24,16}} | collective-permute-start | bytes 589832 | tf_op jit(solution)/shard_map/ppermute | solution.py:1467
  66.6 9.4 %collective-permute-start.12 = (bf16[48,16,128]{2,1,0:T(8,128)(2,1)S(1)}, bf16[48,16,128]{2,1,0:T(8,128)(2,1)S(1)}, u32[]{:S(2)}, u32[]{:S(2)}) collective-permute-start(bf16[48,16,128]{2,1,0:T(8,128)(2,1)S(1)} %fusion.22), channel_id=1, source_target_pairs={{8,12},{0,4},{24,28},{16,20}} | collective-permute-start | bytes 589832 | tf_op jit(solution)/shard_map/ppermute | solution.py:1467
  85.5 30.9 %collective-permute-start.15 = (bf16[48,16,128]{2,1,0:T(8,128)(2,1)S(1)}, bf16[48,16,128]{2,1,0:T(8,128)(2,1)S(1)}, u32[]{:S(2)}, u32[]{:S(2)}) collective-permute-start(bf16[48,16,128]{2,1,0:T(8,128)(2,1)S(1)} %add.422), channel_id=1, source_target_pairs={{0,16},{16,0},{1,17},{17,1},{2,18},{18,2},{3,19},{19,3},{4,20},{20... | collective-permute-start | bytes 589832 | tf_op jit(solution)/shard_map/ppermute | solution.py:1469
  90.3 10.3 %collective-permute-start.2 = (f32[]{:T(128)}, f32[]{:T(128)}, u32[]{:S(2)}, u32[]{:S(2)}) collective-permute-start(f32[]{:T(128)} %add.408), channel_id=1, source_target_pairs={{0,2},{1,3},{2,0},{3,1},{4,6},{5,7},{6,4},{7,5},{8,10},{9,11},{10,... | collective-permute-start | bytes 20 | tf_op jit(solution)/shard_map/ppermute | solution.py:1424
  101.8 13.5 %collective-permute-start.5 = (f32[]{:T(128)}, f32[]{:T(128)}, u32[]{:S(2)}, u32[]{:S(2)}) collective-permute-start(f32[]{:T(128)} %add.411), channel_id=1, source_target_pairs={{0,8},{1,9},{2,10},{3,11},{4,12},{5,13},{6,14},{7,15},{8,0},{9,1},... | collective-permute-start | bytes 20 | tf_op jit(solution)/shard_map/ppermute | solution.py:1424
  364.8 14.0 %collective-permute-start.16 = (f32[8,127,16,128]{3,2,1,0:T(8,128)}, f32[8,127,16,128]{3,2,1,0:T(8,128)}, u32[]{:S(2)}, u32[]{:S(2)}) collective-permute-start(f32[8,127,16,128]{3,2,1,0:T(8,128)} %get-tuple-element.205), channel_id=1, source_target_pairs={{0,16},{16,0},{1,17},{17,1},{2,18},{18,2},{3,19},{19,3},{4,20},{20... | collective-permute-start | bytes 24969224 | tf_op jit(solution)/shard_map/ppermute | solution.py:1372
  388.0 42.3 %collective-permute-start.20 = (f32[2,2,43,16,128]{4,3,2,1,0:T(8,128)}, f32[2,2,43,16,128]{4,3,2,1,0:T(8,128)S(1)}, u32[]{:S(2)}, u32[]{:S(2)}) collective-permute-start(f32[2,2,43,16,128]{4,3,2,1,0:T(8,128)} %add_bitcast_fusion.2), channel_id=1, source_target_pairs={{0,4},{1,5},{2,6},{3,7},{4,0},{5,1},{6,2},{7,3},{8,12},{9,13},{10,... | collective-permute-start | bytes 4227080 | tf_op jit(solution)/shard_map/ppermute | solution.py:1380
  389.6 40.6 %collective-permute-start.18 = (f32[2,2,42,16,128]{4,3,2,1,0:T(8,128)}, f32[2,2,42,16,128]{4,3,2,1,0:T(8,128)}, u32[]{:S(2)}, u32[]{:S(2)}) collective-permute-start(f32[2,2,42,16,128]{4,3,2,1,0:T(8,128)} %add_bitcast_fusion.8), channel_id=1, source_target_pairs={{0,1},{1,0},{2,3},{3,2},{4,5},{5,4},{6,7},{7,6},{8,9},{9,8},{10,11... | collective-permute-start | bytes 4128776 | tf_op jit(solution)/shard_map/ppermute | solution.py:1380
  391.0 39.2 %collective-permute-start.19 = (f32[2,2,42,16,128]{4,3,2,1,0:T(8,128)}, f32[2,2,42,16,128]{4,3,2,1,0:T(8,128)}, u32[]{:S(2)}, u32[]{:S(2)}) collective-permute-start(f32[2,2,42,16,128]{4,3,2,1,0:T(8,128)} %add_bitcast_fusion.7), channel_id=1, source_target_pairs={{0,2},{1,3},{2,0},{3,1},{4,6},{5,7},{6,4},{7,5},{8,10},{9,11},{10,... | collective-permute-start | bytes 4128776 | tf_op jit(solution)/shard_map/ppermute | solution.py:1380
  391.6 38.6 %collective-permute-start.21 = (f32[48,16,128]{2,1,0:T(8,128)S(1)}, f32[48,16,128]{2,1,0:T(8,128)S(1)}, u32[]{:S(2)}, u32[]{:S(2)}) collective-permute-start(f32[48,16,128]{2,1,0:T(8,128)S(1)} %add_bitcast_fusion.9), channel_id=1, source_target_pairs={{1,0},{3,2},{5,4},{7,6},{9,8},{11,10},{13,12},{15,14},{17,16},{19,... | collective-permute-start | bytes 1179656 | tf_op jit(solution)/shard_map/ppermute | solution.py:1376
  435.3 26.7 %collective-permute-start.24 = (f32[2,43,16,128]{3,2,1,0:T(8,128)S(1)}, f32[2,43,16,128]{3,2,1,0:T(8,128)S(1)}, u32[]{:S(2)}, u32[]{:S(2)}) collective-permute-start(f32[2,43,16,128]{3,2,1,0:T(8,128)S(1)} %bitcast_add_fusion.2), channel_id=1, source_target_pairs={{0,1},{1,0},{2,3},{3,2},{4,5},{5,4},{6,7},{7,6},{8,9},{9,8},{10,11... | collective-permute-start | bytes 2113544 | tf_op jit(solution)/shard_map/ppermute | solution.py:1380
  435.3 26.7 %collective-permute-start.22 = (f32[2,42,16,128]{3,2,1,0:T(8,128)}, f32[2,42,16,128]{3,2,1,0:T(8,128)}, u32[]{:S(2)}, u32[]{:S(2)}) collective-permute-start(f32[2,42,16,128]{3,2,1,0:T(8,128)} %get-tuple-element.269), channel_id=1, source_target_pairs={{0,2},{1,3},{2,0},{3,1},{4,6},{5,7},{6,4},{7,5},{8,10},{9,11},{10,... | collective-permute-start | bytes 2064392 | tf_op jit(solution)/shard_map/ppermute | solution.py:1380
  436.8 25.2 %collective-permute-start.23 = (f32[2,42,16,128]{3,2,1,0:T(8,128)}, f32[2,42,16,128]{3,2,1,0:T(8,128)}, u32[]{:S(2)}, u32[]{:S(2)}) collective-permute-start(f32[2,42,16,128]{3,2,1,0:T(8,128)} %get-tuple-element.270), channel_id=1, source_target_pairs={{0,4},{1,5},{2,6},{3,7},{4,0},{5,1},{6,2},{7,3},{8,12},{9,13},{10,... | collective-permute-start | bytes 2064392 | tf_op jit(solution)/shard_map/ppermute | solution.py:1380
  437.3 24.6 %collective-permute-start.25 = (f32[48,16,128]{2,1,0:T(8,128)S(1)}, f32[48,16,128]{2,1,0:T(8,128)S(1)}, u32[]{:S(2)}, u32[]{:S(2)}) collective-permute-start(f32[48,16,128]{2,1,0:T(8,128)S(1)} %add.446), channel_id=1, source_target_pairs={{2,0},{3,1},{6,4},{7,5},{10,8},{11,9},{14,12},{15,13},{18,16},{19,... | collective-permute-start | bytes 1179656 | tf_op jit(solution)/shard_map/ppermute | solution.py:1376
  467.7 20.9 %collective-permute-start.30 = (f32[8,127,16,128]{3,2,1,0:T(8,128)}, f32[8,127,16,128]{3,2,1,0:T(8,128)}, u32[]{:S(2)}, u32[]{:S(2)}) collective-permute-start(f32[8,127,16,128]{3,2,1,0:T(8,128)} %get-tuple-element.309), channel_id=1, source_target_pairs={{0,16},{16,0},{1,17},{17,1},{2,18},{18,2},{3,19},{19,3},{4,20},{20... | collective-permute-start | bytes 24969224 | tf_op jit(solution)/shard_map/ppermute | solution.py:1372
  467.7 20.9 %collective-permute-start.29 = (f32[48,16,128]{2,1,0:T(8,128)S(1)}, f32[48,16,128]{2,1,0:T(8,128)S(1)}, u32[]{:S(2)}, u32[]{:S(2)}) collective-permute-start(f32[48,16,128]{2,1,0:T(8,128)S(1)} %add.459), channel_id=1, source_target_pairs={{4,0},{5,1},{6,2},{7,3},{12,8},{13,9},{14,10},{15,11},{20,16},{21,... | collective-permute-start | bytes 1179656 | tf_op jit(solution)/shard_map/ppermute | solution.py:1376
  469.0 19.6 %collective-permute-start.28 = (f32[43,16,128]{2,1,0:T(8,128)S(1)}, f32[43,16,128]{2,1,0:T(8,128)S(1)}, u32[]{:S(2)}, u32[]{:S(2)}) collective-permute-start(f32[43,16,128]{2,1,0:T(8,128)S(1)} %bitcast_add_fusion.19), channel_id=1, source_target_pairs={{0,2},{1,3},{2,0},{3,1},{4,6},{5,7},{6,4},{7,5},{8,10},{9,11},{10,... | collective-permute-start | bytes 1056776 | tf_op jit(solution)/shard_map/ppermute | solution.py:1380
  471.8 16.8 %collective-permute-start.26 = (f32[42,16,128]{2,1,0:T(8,128)}, f32[42,16,128]{2,1,0:T(8,128)}, u32[]{:S(2)}, u32[]{:S(2)}) collective-permute-start(f32[42,16,128]{2,1,0:T(8,128)} %get-tuple-element.305), channel_id=1, source_target_pairs={{0,4},{1,5},{2,6},{3,7},{4,0},{5,1},{6,2},{7,3},{8,12},{9,13},{10,... | collective-permute-start | bytes 1032200 | tf_op jit(solution)/shard_map/ppermute | solution.py:1380
  474.5 14.2 %collective-permute-start.27 = (f32[42,16,128]{2,1,0:T(8,128)}, f32[42,16,128]{2,1,0:T(8,128)}, u32[]{:S(2)}, u32[]{:S(2)}) collective-permute-start(f32[42,16,128]{2,1,0:T(8,128)} %get-tuple-element.306), channel_id=1, source_target_pairs={{0,1},{1,0},{2,3},{3,2},{4,5},{5,4},{6,7},{7,6},{8,9},{9,8},{10,11... | collective-permute-start | bytes 1032200 | tf_op jit(solution)/shard_map/ppermute | solution.py:1380
  502.4 55.0 %collective-permute-start.33 = (f32[2,2,43,16,128]{4,3,2,1,0:T(8,128)}, f32[2,2,43,16,128]{4,3,2,1,0:T(8,128)S(1)}, u32[]{:S(2)}, u32[]{:S(2)}) collective-permute-start(f32[2,2,43,16,128]{4,3,2,1,0:T(8,128)} %add_bitcast_fusion.1), channel_id=1, source_target_pairs={{0,4},{1,5},{2,6},{3,7},{4,0},{5,1},{6,2},{7,3},{8,12},{9,13},{10,... | collective-permute-start | bytes 4227080 | tf_op jit(solution)/shard_map/ppermute | solution.py:1380
  502.4 32.4 %collective-permute-start.31 = (f32[2,2,42,16,128]{4,3,2,1,0:T(8,128)}, f32[2,2,42,16,128]{4,3,2,1,0:T(8,128)}, u32[]{:S(2)}, u32[]{:S(2)}) collective-permute-start(f32[2,2,42,16,128]{4,3,2,1,0:T(8,128)} %add_bitcast_fusion.6), channel_id=1, source_target_pairs={{0,1},{1,0},{2,3},{3,2},{4,5},{5,4},{6,7},{7,6},{8,9},{9,8},{10,11... | collective-permute-start | bytes 4128776 | tf_op jit(solution)/shard_map/ppermute | solution.py:1380
  504.4 32.8 %collective-permute-start.32 = (f32[2,2,42,16,128]{4,3,2,1,0:T(8,128)}, f32[2,2,42,16,128]{4,3,2,1,0:T(8,128)}, u32[]{:S(2)}, u32[]{:S(2)}) collective-permute-start(f32[2,2,42,16,128]{4,3,2,1,0:T(8,128)} %add_bitcast_fusion.5), channel_id=1, source_target_pairs={{0,2},{1,3},{2,0},{3,1},{4,6},{5,7},{6,4},{7,5},{8,10},{9,11},{10,... | collective-permute-start | bytes 4128776 | tf_op jit(solution)/shard_map/ppermute | solution.py:1380
  507.1 84.4 %collective-permute-start.37 = (f32[127,16,128]{2,1,0:T(8,128)}, f32[127,16,128]{2,1,0:T(8,128)}, u32[]{:S(2)}, u32[]{:S(2)}) collective-permute-start(f32[127,16,128]{2,1,0:T(8,128)} %pad_maximum_fusion), channel_id=1, source_target_pairs={{8,0},{9,1},{10,2},{11,3},{12,4},{13,5},{14,6},{15,7},{24,16},{25,... | collective-permute-start | bytes 3121160 | tf_op jit(solution)/shard_map/ppermute | solution.py:1376
  563.5 28.0 %collective-permute-start.36 = (f32[2,43,16,128]{3,2,1,0:T(8,128)}, f32[2,43,16,128]{3,2,1,0:T(8,128)}, u32[]{:S(2)}, u32[]{:S(2)}) collective-permute-start(f32[2,43,16,128]{3,2,1,0:T(8,128)} %bitcast_add_fusion.1), channel_id=1, source_target_pairs={{0,1},{1,0},{2,3},{3,2},{4,5},{5,4},{6,7},{7,6},{8,9},{9,8},{10,11... | collective-permute-start | bytes 2113544 | tf_op jit(solution)/shard_map/ppermute | solution.py:1380
  565.6 25.9 %collective-permute-start.34 = (f32[2,42,16,128]{3,2,1,0:T(8,128)}, f32[2,42,16,128]{3,2,1,0:T(8,128)}, u32[]{:S(2)}, u32[]{:S(2)}) collective-permute-start(f32[2,42,16,128]{3,2,1,0:T(8,128)} %get-tuple-element.355), channel_id=1, source_target_pairs={{0,2},{1,3},{2,0},{3,1},{4,6},{5,7},{6,4},{7,5},{8,10},{9,11},{10,... | collective-permute-start | bytes 2064392 | tf_op jit(solution)/shard_map/ppermute | solution.py:1380
  568.3 23.3 %collective-permute-start.35 = (f32[2,42,16,128]{3,2,1,0:T(8,128)S(1)}, f32[2,42,16,128]{3,2,1,0:T(8,128)}, u32[]{:S(2)}, u32[]{:S(2)}) collective-permute-start(f32[2,42,16,128]{3,2,1,0:T(8,128)S(1)} %get-tuple-element.356), channel_id=1, source_target_pairs={{0,4},{1,5},{2,6},{3,7},{4,0},{5,1},{6,2},{7,3},{8,12},{9,13},{10,... | collective-permute-start | bytes 2064392 | tf_op jit(solution)/shard_map/ppermute | solution.py:1380
  568.3 23.2 %collective-permute-start.38 = (f32[48,16,128]{2,1,0:T(8,128)S(1)}, f32[48,16,128]{2,1,0:T(8,128)S(1)}, u32[]{:S(2)}, u32[]{:S(2)}) collective-permute-start(f32[48,16,128]{2,1,0:T(8,128)S(1)} %add.477), channel_id=1, source_target_pairs={{0,8},{1,9},{2,10},{3,11},{4,12},{5,13},{6,14},{7,15},{16,24},{17,... | collective-permute-start | bytes 1179656 | tf_op jit(solution)/shard_map/ppermute | solution.py:1376
  594.9 17.2 %collective-permute-start.39 = (f32[8,127,16,128]{3,2,1,0:T(8,128)}, f32[8,127,16,128]{3,2,1,0:T(8,128)S(1)}, u32[]{:S(2)}, u32[]{:S(2)}) collective-permute-start(f32[8,127,16,128]{3,2,1,0:T(8,128)} %get-tuple-element.374), channel_id=1, source_target_pairs={{0,16},{16,0},{1,17},{17,1},{2,18},{18,2},{3,19},{19,3},{4,20},{20... | collective-permute-start | bytes 24969224 | tf_op jit(solution)/shard_map/ppermute | solution.py:1372
  595.0 10.7 %collective-permute-start.40 = (f32[42,16,128]{2,1,0:T(8,128)S(1)}, f32[42,16,128]{2,1,0:T(8,128)S(1)}, u32[]{:S(2)}, u32[]{:S(2)}) collective-permute-start(f32[42,16,128]{2,1,0:T(8,128)S(1)} %get-tuple-element.375), channel_id=1, source_target_pairs={{0,4},{1,5},{2,6},{3,7},{4,0},{5,1},{6,2},{7,3},{8,12},{9,13},{10,... | collective-permute-start | bytes 1032200 | tf_op jit(solution)/shard_map/ppermute | solution.py:1380
  597.1 10.1 %collective-permute-start.41 = (f32[42,16,128]{2,1,0:T(8,128)S(1)}, f32[42,16,128]{2,1,0:T(8,128)S(1)}, u32[]{:S(2)}, u32[]{:S(2)}) collective-permute-start(f32[42,16,128]{2,1,0:T(8,128)S(1)} %get-tuple-element.376), channel_id=1, source_target_pairs={{0,1},{1,0},{2,3},{3,2},{4,5},{5,4},{6,7},{7,6},{8,9},{9,8},{10,11... | collective-permute-start | bytes 1032200 | tf_op jit(solution)/shard_map/ppermute | solution.py:1380
  597.1 12.3 %collective-permute-start.42 = (f32[43,16,128]{2,1,0:T(8,128)S(1)}, f32[43,16,128]{2,1,0:T(8,128)S(1)}, u32[]{:S(2)}, u32[]{:S(2)}) collective-permute-start(f32[43,16,128]{2,1,0:T(8,128)S(1)} %bitcast_add_fusion.15), channel_id=1, source_target_pairs={{0,2},{1,3},{2,0},{3,1},{4,6},{5,7},{6,4},{7,5},{8,10},{9,11},{10,... | collective-permute-start | bytes 1056776 | tf_op jit(solution)/shard_map/ppermute | solution.py:1380
  612.7 31.5 %collective-permute-start.43 = (f32[2,2,42,16,128]{4,3,2,1,0:T(8,128)S(1)}, f32[2,2,42,16,128]{4,3,2,1,0:T(8,128)S(1)}, u32[]{:S(2)}, u32[]{:S(2)}) collective-permute-start(f32[2,2,42,16,128]{4,3,2,1,0:T(8,128)S(1)} %add_bitcast_fusion.4), channel_id=1, source_target_pairs={{0,1},{1,0},{2,3},{3,2},{4,5},{5,4},{6,7},{7,6},{8,9},{9,8},{10,11... | collective-permute-start | bytes 4128776 | tf_op jit(solution)/shard_map/ppermute | solution.py:1380
  613.1 31.5 %collective-permute-start.44 = (f32[2,2,42,16,128]{4,3,2,1,0:T(8,128)S(1)}, f32[2,2,42,16,128]{4,3,2,1,0:T(8,128)S(1)}, u32[]{:S(2)}, u32[]{:S(2)}) collective-permute-start(f32[2,2,42,16,128]{4,3,2,1,0:T(8,128)S(1)} %add_bitcast_fusion.3), channel_id=1, source_target_pairs={{0,2},{1,3},{2,0},{3,1},{4,6},{5,7},{6,4},{7,5},{8,10},{9,11},{10,... | collective-permute-start | bytes 4128776 | tf_op jit(solution)/shard_map/ppermute | solution.py:1380
  613.1 32.2 %collective-permute-start.45 = (f32[2,2,43,16,128]{4,3,2,1,0:T(8,128)S(1)}, f32[2,2,43,16,128]{4,3,2,1,0:T(8,128)S(1)}, u32[]{:S(2)}, u32[]{:S(2)}) collective-permute-start(f32[2,2,43,16,128]{4,3,2,1,0:T(8,128)S(1)} %add_bitcast_fusion), channel_id=1, source_target_pairs={{0,4},{1,5},{2,6},{3,7},{4,0},{5,1},{6,2},{7,3},{8,12},{9,13},{10,... | collective-permute-start | bytes 4227080 | tf_op jit(solution)/shard_map/ppermute | solution.py:1380
  645.4 15.9 %collective-permute-start.46 = (f32[2,42,16,128]{3,2,1,0:T(8,128)S(1)}, f32[2,42,16,128]{3,2,1,0:T(8,128)S(1)}, u32[]{:S(2)}, u32[]{:S(2)}) collective-permute-start(f32[2,42,16,128]{3,2,1,0:T(8,128)S(1)} %get-tuple-element.381), channel_id=1, source_target_pairs={{0,2},{1,3},{2,0},{3,1},{4,6},{5,7},{6,4},{7,5},{8,10},{9,11},{10,... | collective-permute-start | bytes 2064392 | tf_op jit(solution)/shard_map/ppermute | solution.py:1380
  647.2 15.2 %collective-permute-start.47 = (f32[2,42,16,128]{3,2,1,0:T(8,128)S(1)}, f32[2,42,16,128]{3,2,1,0:T(8,128)S(1)}, u32[]{:S(2)}, u32[]{:S(2)}) collective-permute-start(f32[2,42,16,128]{3,2,1,0:T(8,128)S(1)} %get-tuple-element.382), channel_id=1, source_target_pairs={{0,4},{1,5},{2,6},{3,7},{4,0},{5,1},{6,2},{7,3},{8,12},{9,13},{10,... | collective-permute-start | bytes 2064392 | tf_op jit(solution)/shard_map/ppermute | solution.py:1380
  647.6 15.4 %collective-permute-start.48 = (f32[2,43,16,128]{3,2,1,0:T(8,128)S(1)}, f32[2,43,16,128]{3,2,1,0:T(8,128)S(1)}, u32[]{:S(2)}, u32[]{:S(2)}) collective-permute-start(f32[2,43,16,128]{3,2,1,0:T(8,128)S(1)} %bitcast_add_fusion), channel_id=1, source_target_pairs={{0,1},{1,0},{2,3},{3,2},{4,5},{5,4},{6,7},{7,6},{8,9},{9,8},{10,11... | collective-permute-start | bytes 2113544 | tf_op jit(solution)/shard_map/ppermute | solution.py:1380
  663.1 10.1 %collective-permute-start.49 = (f32[42,16,128]{2,1,0:T(8,128)S(1)}, f32[42,16,128]{2,1,0:T(8,128)S(1)}, u32[]{:S(2)}, u32[]{:S(2)}) collective-permute-start(f32[42,16,128]{2,1,0:T(8,128)S(1)} %get-tuple-element.384), channel_id=1, source_target_pairs={{0,4},{1,5},{2,6},{3,7},{4,0},{5,1},{6,2},{7,3},{8,12},{9,13},{10,... | collective-permute-start | bytes 1032200 | tf_op jit(solution)/shard_map/ppermute | solution.py:1380
  666.3 24.9 %collective-permute-start.53 = (f32[127,16,128]{2,1,0:T(8,128)}, f32[127,16,128]{2,1,0:T(8,128)}, u32[]{:S(2)}, u32[]{:S(2)}) collective-permute-start(f32[127,16,128]{2,1,0:T(8,128)} %pad_maximum_fusion.1), channel_id=1, source_target_pairs={{0,8},{1,9},{2,10},{3,11},{4,12},{5,13},{6,14},{7,15},{16,24},{17,... | collective-permute-start | bytes 3121160 | tf_op jit(solution)/shard_map/ppermute | solution.py:1376
  674.7 44.8 %collective-permute-start.52 = (f32[127,16,128]{2,1,0:T(8,128)}, f32[127,16,128]{2,1,0:T(8,128)}, u32[]{:S(2)}, u32[]{:S(2)}) collective-permute-start(f32[127,16,128]{2,1,0:T(8,128)} %pad_maximum_fusion.2), channel_id=1, source_target_pairs={{8,0},{9,1},{10,2},{11,3},{12,4},{13,5},{14,6},{15,7},{24,16},{25,... | collective-permute-start | bytes 3121160 | tf_op jit(solution)/shard_map/ppermute | solution.py:1376
  726.3 19.7 %collective-permute-start.61 = (f32[127,16,128]{2,1,0:T(8,128)S(1)}, f32[127,16,128]{2,1,0:T(8,128)S(1)}, u32[]{:S(2)}, u32[]{:S(2)}) collective-permute-start(f32[127,16,128]{2,1,0:T(8,128)S(1)} %get-tuple-element.415), channel_id=1, source_target_pairs={{0,16},{16,0},{1,17},{17,1},{2,18},{18,2},{3,19},{19,3},{4,20},{20... | collective-permute-start | bytes 3121160 | tf_op jit(solution)/shard_map/ppermute | solution.py:1585
  741.6 9.9 %collective-permute-start.58 = (f32[2]{0:T(128)S(1)}, f32[2]{0:T(128)S(1)}, u32[]{:S(2)}, u32[]{:S(2)}) collective-permute-start(f32[2]{0:T(128)S(1)} %add_add_fusion.2), channel_id=1, source_target_pairs={{0,4},{1,5},{2,6},{3,7},{4,0},{5,1},{6,2},{7,3},{8,12},{9,13},{10,... | collective-permute-start | bytes 32 | tf_op jit(solution)/shard_map/ppermute | solution.py:1424
  741.6 9.9 %collective-permute-start.59 = (f32[2]{0:T(128)S(1)}, f32[2]{0:T(128)S(1)}, u32[]{:S(2)}, u32[]{:S(2)}) collective-permute-start(f32[2]{0:T(128)S(1)} %add_add_fusion.2), channel_id=1, source_target_pairs={{0,8},{1,9},{2,10},{3,11},{4,12},{5,13},{6,14},{7,15},{8,0},{9,1},... | collective-permute-start | bytes 32 | tf_op jit(solution)/shard_map/ppermute | solution.py:1424
  741.7 9.8 %collective-permute-start.60 = (f32[2]{0:T(128)S(1)}, f32[2]{0:T(128)S(1)}, u32[]{:S(2)}, u32[]{:S(2)}) collective-permute-start(f32[2]{0:T(128)S(1)} %add_add_fusion.2), channel_id=1, source_target_pairs={{0,12},{1,13},{2,14},{3,15},{4,8},{5,9},{6,10},{7,11},{8,4},{9,5},... | collective-permute-start | bytes 32 | tf_op jit(solution)/shard_map/ppermute | solution.py:1424
  (37 other events, 336.5 us)
Sparse Core Ops, SparseCore 0:
  29.2 122.0 all-gather.4
  154.2 75.8 all-gather.2

commit v5 on v4

--- a/solution.py
+++ b/solution.py
@@ -259,6 +259,7 @@
         out_specs=IN_VMEM,
         scratch_shapes=[pltpu.VMEM((plan.zero_row + 8, 128), F32)],
         compiler_params=pltpu.CompilerParams(vmem_limit_bytes=32 * 1024 * 1024),
+        cost_estimate=lasting(6),
         name="unpack_rows",
     )(index, block, tail)
 
@@ -991,16 +992,12 @@
                 f[here, :], columns(w["head"], DD, 2 * pair, 2)
             )
 
-        def rows(i, total):
-            at = pl.multiple_of(i * 16, 16)
-            target, _ = norm_rows(pp[image, pl.ds(at, 16), :].astype(F32), PIX)
-            off = guess[pl.ds(at, 16), :] - target
-            rank = lax.broadcasted_iota(jnp.int32, (16, PIX), 0) + at
-            off = jnp.where((rank >= kept) & (rank < NP), off, 0.0)
-            pp[image, pl.ds(at, 16), :] = (off * factor).astype(BF16)
-            return total + jnp.sum((off * off).reshape(2, 8, PIX), axis=0)
-
-        return lax.fori_loop(0, ROWS_D // 16, rows, total)
+        target, _ = norm_rows(pp[image].astype(F32), PIX)
+        off = guess[...] - target
+        rank = lax.broadcasted_iota(jnp.int32, (ROWS_D, 1), 0)
+        off = jnp.where((rank >= kept) & (rank < NP), off, 0.0)
+        pp[image] = (off * factor).astype(BF16)
+        return total + jnp.sum((off * off).reshape(ROWS_D // 8, 8, PIX), axis=0)
 
     total = lax.fori_loop(0, images, predict_image, jnp.zeros((8, PIX), F32))
     total = jnp.sum(jnp.sum(total, axis=0, keepdims=True), axis=1, keepdims=True)
@@ -1037,20 +1034,13 @@
         start = pl.multiple_of(image * ROWS_D, 16)
         kept = info[1 + image]
 
-        def rows(i, total):
-            at = pl.multiple_of(i * 16, 16)
-            grad = y[pl.ds(start + at, 16), :]
-            rank = lax.broadcasted_iota(jnp.int32, (16, DD), 0) + at
-            free = jnp.where(rank >= kept, grad, 0.0)
-
-            @pl.when(i < ROWS_E // 16)
-            def _():
-                taken = jnp.where(rank < kept, grad, 0.0).astype(BF16)
-                n1[pl.ds(pl.multiple_of(image * ROWS_E, 16) + at, 16), :] = taken
-
-            return total + jnp.sum(free.reshape(2, 8, DD), axis=0)
-
-        return lax.fori_loop(0, ROWS_D // 16, rows, total)
+        grad = y[pl.ds(start, ROWS_D), :]
+        rank = lax.broadcasted_iota(jnp.int32, (ROWS_D, 1), 0)
+        few = pl.ds(pl.multiple_of(image * ROWS_E, 16), ROWS_E)
+        taken = jnp.where(rank[:ROWS_E] < kept, grad[:ROWS_E], 0.0)
+        n1[few, :] = taken.astype(BF16)
+        free = jnp.where(rank >= kept, grad, 0.0)
+        return total + jnp.sum(free.reshape(ROWS_D // 8, 8, DD), axis=0)
 
     total = lax.fori_loop(0, images, split, jnp.zeros((8, DD), F32))
     values["mask"] = jnp.sum(total, axis=0, keepdims=True)
@@ -1167,6 +1157,7 @@
         back = Backward(
             sh, w, vec, lambda i: info[1 + i], grads, values, turned, ready
         )
+        back.out_sem = in_sems.at[len(self.reads)]
         self.body(back, {**here, **temps}, results)
         assert not loads
         grads.finish(values, vec_stage)
@@ -1199,7 +1190,7 @@
             functools.partial(self.kernel, len(blocks)),
             out_shape=[*targets, *[jax.ShapeDtypeStruct(*known[n]) for n in self.outs]],
             in_specs=[IN_SMEM, *[ANY] * (1 + len(self.reads) + len(blocks))],
-            out_specs=[*[ANY] * len(targets), *[IN_VMEM] * len(self.outs)],
+            out_specs=[*[ANY] * len(targets), *[ANY if n == "g" else IN_VMEM for n in self.outs]],
             input_output_aliases={before + i: i for i in range(len(blocks))},
             scratch_shapes=[
                 *weight_scratch(ENC, self.weights),
@@ -1211,7 +1202,7 @@
                 pltpu.VMEM((2, 16 * self.most, 16, 128), F32),
                 pltpu.VMEM((holders, VEC_UNITS, 16, 128), F32),
                 pltpu.SemaphoreType.DMA((len(self.weights) + 1,)),
-                pltpu.SemaphoreType.DMA((len(self.reads),)),
+                pltpu.SemaphoreType.DMA((len(self.reads) + 1,)),
                 pltpu.SemaphoreType.DMA((3,)),
             ],
             compiler_params=pltpu.CompilerParams(vmem_limit_bytes=VMEM_BYTES),
@@ -1236,11 +1227,11 @@
         r["y"], back.vec("gf"), from_latent, put, sh.count, D
     )
     back.second_product(out["dy"], r["dyb"], r["g"], r["gp"])
-
-    def step(at):
-        out["g"][pl.ds(at, 16), :] = r["g"][pl.ds(at, 16), :]
-
-    for_rows(sh.count, 16, step, 2)
+    copy = pltpu.make_async_copy(r["g"], out["g"], back.out_sem)
+    copy.start()
+    back.grads.drain(0)
+    back.grads.drain(1)
+    copy.wait()
 
 
 def copy_rows(count, source, target):
@@ -1331,7 +1322,8 @@
 
 
 class Flow:
-    def __init__(self, dp, keep, send, first, parts=3):
+    def __init__(self, dp, keep, send, first, shares=(1, 1, 1)):
+        parts = len(shares)
         self.dp = dp
         self.me = lax.axis_index("dp")
         self.keep, self.given = keep, send
@@ -1344,7 +1336,7 @@
         if dp == 64:
             low = [b for b in (0, 2, 4, 1, 3) if b < self.bits]
         turn = max(min(3, len(low)), 1)
-        self.cuts = [units * p // parts for p in range(parts + 1)]
+        self.cuts = [units * sum(shares[:p]) // sum(shares) for p in range(parts + 1)]
         self.orders = [low[p % turn : turn] + low[: p % turn] + low[turn:] for p in range(parts)]
         self.step = -1
         self.terms = None
@@ -1416,17 +1408,26 @@
         flow.take(values)
 
 
+def sum_in_chip(value):
+    return value + lax.ppermute(value, "section", [(0, 1), (1, 0)])
+
+
+def sum_over_dp(dp, value, low):
+    bits = dp.bit_length() - 1
+    got = [
+        lax.ppermute(value, "dp", [(i, i ^ (flip << low)) for i in range(dp)])
+        for flip in range(1, 1 << min(2, bits - low))
+    ]
+    value = value + got[0]
+    if len(got) == 3:
+        value = value + (got[1] + got[2])
+    return value
+
+
 def sum_everywhere(dp, value):
-    value = value + lax.ppermute(value, "section", [(0, 1), (1, 0)])
-    bits = dp.bit_length() - 1
-    for low in range(0, bits, 2):
-        got = [
-            lax.ppermute(value, "dp", [(i, i ^ (flip << low)) for i in range(dp)])
-            for flip in range(1, 1 << min(2, bits - low))
-        ]
-        value = value + got[0]
-        if len(got) == 3:
-            value = value + (got[1] + got[2])
+    value = sum_in_chip(value)
+    for low in range(0, dp.bit_length() - 1, 2):
+        value = sum_over_dp(dp, value, low)
     return value
 
 
@@ -1545,7 +1546,7 @@
     stages = encoder_back_stages(plan, shape_e)
     first_tail = plan.bins(1)[1][0]
     main = Flow(dp, sums_d[0], sums_d[1], 0)
-    rest = Flow(dp, sums_d[2], sums_d[3], first_tail, 1)
+    rest = Flow(dp, sums_d[2], sums_d[3], first_tail, (1,))
     flows, got, _ = move_on([main, rest])
     got, arrays = tie(got, arrays)
     arrive(flows, got)
@@ -1565,7 +1566,7 @@
         kept = iter(kept)
         arrive(flows, [g if f.last() else next(kept) for f, g in zip(flows, got)])
         if number == 1:
-            high = Flow(dp, blocks[2], blocks[3], dp // 2)
+            high = Flow(dp, blocks[2], blocks[3], dp // 2, (4, 4, 2))
             blocks = blocks[:2]
     low = Flow(dp, blocks[0], blocks[1], 0)
     every = [main, rest, high, low]
@@ -1580,9 +1581,11 @@
     squares = [
         squares_of(plan, s, v, section, me) for s, v in enumerate((sum_e, sum_d))
     ]
-    sums = sum_everywhere(dp, jnp.stack([squares[0] + squares[1], loss[0, 0]]))
     half_mine = jnp.where(section == 0, sum_e, sum_d)
     half_other = lax.ppermute(jnp.where(section == 0, sum_d, sum_e), "section", swap)
+    sums = sum_in_chip(jnp.stack([squares[0] + squares[1], loss[0, 0]]))
+    sums, half_other = tie(sums, half_other)
+    sums = sum_over_dp(dp, sums, 0)
     block = jnp.where(
         section == 0,
         jnp.concatenate([half_mine, half_other], axis=0),
@@ -1596,7 +1599,10 @@
         ],
         axis=0,
     )
+    sums, tail = tie(sums, tail)
     tail = lax.ppermute(tail, "dp", [(i, i + 1) for i in range(dp - 1)])
+    for low in range(2, dp.bit_length() - 1, 2):
+        sums = sum_over_dp(dp, sums, low)
     index = jnp.asarray(plan.unpack_index)[section, me]
     total = unpack(plan, index, block, tail)
     norm = jnp.sqrt(sums[0])

time: 785 us -> 758 us (0.966)
  waiting for transfers between devices: 280 us -> 263 us
  Pallas kernels: 300 us -> 286 us
    ppermute x27, waiting for transfers between devices: 86.5 us -> 66.5 us  [send(): lax.ppermute(value, 'dp', [(i, i ^ flip) for i in range(self.dp)])]
    pallas_call x1, Pallas kernels: 135 us -> 120 us  [decoder(): pl.pallas_call(lambda *refs: decoder_kernel(plan, sh, refs), out_shape=[*...]
    add x39 -> x43, other arithmetic: 55.2 us -> 56.9 us  [total_of(): total = total + term]
  transfers between devices with their start and end apart: 65 -> 65, of which waited for: 33 -> 30; matrix products, arithmetic and copies ran while one was open for 5% -> 5% of each run, Pallas kernels for 19% -> 19%
where the time goes in v5:
time: 758 us; the launch traced here: 753 us
  Pallas kernels  286 us (38%)
  waiting for transfers between devices  263 us (35%)
  starting transfers between devices  90.7 us (12%)
  other arithmetic  70.7 us (9%)
  between operations  26.3 us (3%)
  local copies, waits for them, and re-layouts  16.2 us (2%)
    pallas_call x1, Pallas kernels, decoder(): pl.pallas_call(lambda *refs: decoder_kernel(plan, sh, refs), out_shape=[*...  120 us
    pallas_call x5, Pallas kernels, __call__(): pl.pallas_call(functools.partial(self.kernel, len(blocks)), out_shape=[*t...  107 us
    ppermute x27, waiting for transfers between devices, send(): lax.ppermute(value, 'dp', [(i, i ^ flip) for i in range(self.dp)])  66.5 us
    add x43, other arithmetic, total_of(): total = total + term  56.9 us
    ppermute x7, waiting for transfers between devices, send(): return [lax.ppermute(payload[0], 'dp', pairs)]  50.4 us
    all_gather x1, waiting for transfers between devices, gather_decoder(): gathered = lax.all_gather(spread, ('section', 'dp'), axis=0, tiled=True)  41.4 us
    pallas_call x1, Pallas kernels, encoder(): pl.pallas_call(lambda *refs: encoder_kernel(plan, sh, refs), out_shape=[j...  37.8 us
    ppermute x4, waiting for transfers between devices, gather_decoder(): rest = rest + lax.ppermute(rest, 'dp', [(i, i ^ 1 << bit) for i in holders])  36.1 us
  transfers between devices with their start and end apart: 65, of which 30 were waited for; matrix products, arithmetic and copies ran while one was open for 5% of the time, Pallas kernels for 19%

profile of v5, /device:TPU:0, one launch (start us, length us, event | category | flops | bytes accessed | tf_op | source)
XLA Modules:
  0.0 753.2 jit_solution(1001827562380939687)
XLA Ops:
  10.4 7.5 collective-permute-done.7.following
  19.4 6.8 pack_rows.1
  29.2 4.6 collective-permute-start.10
  34.5 5.1 collective-permute-done.10
  41.7 24.9 %collective-permute-done.11 = bf16[48,16,128]{2,1,0:T(8,128)(2,1)S(1)} collective-permute-done((bf16[48,16,128]{2,1,0:T(8,128)(2,1)S(1)}, bf16[48,16,128]{2,1,0:T(8,128)(2,1)S(1)}, u32[]{:S(2)}, u32[]{:S(2)}) %collective-permute-start.11) | collective-permute-done | bytes 196640 | tf_op jit(solution)/shard_map/ppermute | solution.py:1468
  67.9 8.1 %collective-permute-done.12 = bf16[48,16,128]{2,1,0:T(8,128)(2,1)S(1)} collective-permute-done((bf16[48,16,128]{2,1,0:T(8,128)(2,1)S(1)}, bf16[48,16,128]{2,1,0:T(8,128)(2,1)S(1)}, u32[]{:S(2)}, u32[]{:S(2)}) %collective-permute-start.12) | collective-permute-done | bytes 196640 | tf_op jit(solution)/shard_map/ppermute | solution.py:1468
  77.4 3.2 collective-permute-done.13
  90.3 3.9 collective-permute-start.2
  94.2 2.3 collective-permute-start.3
  101.9 5.5 collective-permute-start.5
  107.4 3.8 collective-permute-start.6
  117.4 34.0 %all-gather.5.cloned.1.call-done = bf16[4064,16,128]{2,1,0:T(8,128)(2,1)} async-done(((bf16[127,16,128]{2,1,0:T(8,128)(2,1)}), bf16[4064,16,128]{2,1,0:T(8,128)(2,1)}) %all-gather.5.cloned.1.call-update) | async-done | bytes 16646160 | tf_op jit(solution)/shard_map/all_gather | solution.py:1519
  151.3 37.8 %encoder_forward.1 = (bf16[6,208,768]{2,1,0:T(8,128)(2,1)}, f32[672,768]{1,0:T(8,128)}, bf16[672,768]{1,0:T(8,128)(2,1)}, bf16[672,2304]{1,0:T(8,128)(2,1)}, bf1...) custom-call(s32[7]{0:T(128)} %pad_add_fusion.refs_0_, ...), custom_call_target="tpu_custom_call" | custom-call | flops 10000000000 | bytes 1048576 | tf_op jit(solution)/shard_map/encoder_forward/pallas_call | solution.py:914
  189.2 41.4 %all-gather.3.cloned.1.call-done = bf16[2048,16,128]{2,1,0:T(8,128)(2,1)} async-done(((bf16[64,16,128]{2,1,0:T(8,128)(2,1)}), bf16[2048,16,128]{2,1,0:T(8,128)(2,1)}) %all-gather.3.cloned.1.call-update) | async-done | bytes 8388624 | tf_op jit(solution)/shard_map/all_gather | solution.py:1473
  230.6 120.0 %decoder_both.1 = (f32[8,127,16,128]{3,2,1,0:T(8,128)}, f32[8,127,16,128]{3,2,1,0:T(8,128)}, f32[1,48,16,128]{3,2,1,0:T(8,128)}, f32[1,48,16,128]{3,2,1,0:T(8,12...) custom-call(s32[7]{0:T(128)} %pad_add_fusion.refs_0_, f32[1]{0:T(128)} %bitcast.3.refs_1_, ...), custom_call_target="tpu_custom_call" | custom-call | flops 32000000000 | bytes 1048576 | tf_op jit(solution)/shard_map/decoder_both/pallas_call | solution.py:1070
  351.1 4.6 collective-permute-done.17
  355.7 8.9 %collective-permute-done.16 = f32[8,127,16,128]{3,2,1,0:T(8,128)} collective-permute-done((f32[8,127,16,128]{3,2,1,0:T(8,128)}, f32[8,127,16,128]{3,2,1,0:T(8,128)}, u32[]{:S(2)}, u32[]{:S(2)}) %collective-permute-start.16) | collective-permute-done | bytes 8323104 | tf_op jit(solution)/shard_map/ppermute | solution.py:1364
  366.6 3.0 add_bitcast_fusion.6
  369.6 3.1 add_bitcast_fusion.7
  377.6 28.7 %encoder_back_fc2.1 = (f32[8,127,16,128]{3,2,1,0:T(8,128)}, f32[8,127,16,128]{3,2,1,0:T(8,128)}, f32[8,127,16,128]{3,2,1,0:T(8,128)}, f32[8,127,16,128]{3,2,1,0:...) custom-call(s32[7]{0:T(128)} %pad_add_fusion.refs_0_, bf16[2,16,127,16,128]{4,3,2,1,0:T(8,128)(2,1)} %bitcast.255, ...), custom_call_target="tpu_custom_call" | custom-call | flops 5000000000 | bytes 1048576 | tf_op jit(solution)/shard_map/encoder_back_fc2/pallas_call | solution.py:1189
  406.3 8.7 %collective-permute-done.21 = f32[48,16,128]{2,1,0:T(8,128)S(1)} collective-permute-done((f32[48,16,128]{2,1,0:T(8,128)S(1)}, f32[48,16,128]{2,1,0:T(8,128)S(1)}, u32[]{:S(2)}, u32[]{:S(2)}) %collective-permute-start.21) | collective-permute-done | bytes 393248 | tf_op jit(solution)/shard_map/ppermute | solution.py:1368
  418.3 3.5 bitcast_add_fusion.6
  425.1 23.4 %encoder_back_fc1.1 = (f32[8,127,16,128]{3,2,1,0:T(8,128)}, f32[8,127,16,128]{3,2,1,0:T(8,128)}, f32[8,127,16,128]{3,2,1,0:T(8,128)}, f32[8,127,16,128]{3,2,1,0:T(8,128)}, f32[672,768]{1,0:T(8,128)}) custom-call(s32[7]{0:T(128)} %pad_add_fusion.refs_0_, ...), custom_call_target="tpu_custom_call", output_to_operand_aliasing={{0}: (6, {}), {1}: (7, {}), {2}: (8, {}), {3}: (9, {})} | custom-call | flops 4000000000 | bytes 1048576 | tf_op jit(solution)/shard_map/encoder_back_fc1/pallas_call | solution.py:1189
  453.8 2.7 collective-permute-start.28
  456.5 2.7 collective-permute-start.26
  461.2 8.2 %encoder_back_proj.1 = (f32[8,127,16,128]{3,2,1,0:T(8,128)}, f32[8,127,16,128]{3,2,1,0:T(8,128)}, bf16[672,768]{1,0:T(8,128)(2,1)}) custom-call(s32[7]{0:T(128)} %pad_add_fusion.refs_0_, bf16[2,16,127,16,128]{4,3,2,1,0:T(8,128)(2,1)} %bitcast.257, f32[672,768]{1,0:T(8,128)} %get-tuple-element.365.refs_2_, ...), custom_call_target="tpu_custom_call", output_to_operand_aliasing={{0}: (4, {}), {1}: (5, {})} | custom-call | flops 2000000000 | bytes 1048576 | tf_op jit(solution)/shard_map/encoder_back_proj/pallas_call | solution.py:1189
  469.5 3.8 collective-permute-done.26
  473.3 2.5 add_bitcast_fusion.8
  475.8 3.3 add_bitcast_fusion
  479.2 3.3 add_bitcast_fusion.1
  486.8 2.7 collective-permute-start.32
  492.9 25.1 %encoder_back_attention.1.refs_3_ = bf16[672,2304]{1,0:T(8,128)(2,1)} custom-call(s32[7]{0:T(128)} %pad_add_fusion.refs_0_, bf16[2,16,127,16,128]{4,3,2,1,0:T(8,128)(2,1)} %bitcast.258, bf16[672,768]{1,0:T(8,128)(2,1)} %get-tuple-element.341.refs_2_, bf16[672,2304]{1,0:T(8,128)(2,1)} %get-tuple-element.342.refs_3_), custom_call_target="tpu_custom_call" | custom-call | flops 5000000000 | bytes 1048576 | tf_op jit(solution)/shard_map/encoder_back_attention/pallas_call | solution.py:1189
  518.0 10.7 %collective-permute-done.33 = f32[2,2,26,16,128]{4,3,2,1,0:T(8,128)} collective-permute-done((f32[2,2,26,16,128]{4,3,2,1,0:T(8,128)}, f32[2,2,26,16,128]{4,3,2,1,0:T(8,128)}, u32[]{:S(2)}, u32[]{:S(2)}) %collective-permute-start.33) | collective-permute-done | bytes 852000 | tf_op jit(solution)/shard_map/ppermute | solution.py:1372
  528.8 3.3 bitcast_add_fusion.1
  534.2 2.5 bitcast_add_fusion
  536.9 3.3 collective-permute-start.38
  542.3 21.9 %encoder_back_qkv.1 = (f32[8,127,16,128]{3,2,1,0:T(8,128)}, f32[8,127,16,128]{3,2,1,0:T(8,128)}) custom-call(s32[7]{0:T(128)} %pad_add_fusion.refs_0_, bf16[2,16,127,16,128]{4,3,2,1,0:T(8,128)(2,1)} %bitcast.259, f32[672,768]{1,0:T(8,128)} %get-tuple-element.365.refs_2_, ...), custom_call_target="tpu_custom_call", output_to_operand_aliasing={{0}: (7, {}), {1}: (8, {})} | custom-call | flops 5000000000 | bytes 1048576 | tf_op jit(solution)/shard_map/encoder_back_qkv/pallas_call | solution.py:1189
  572.0 4.2 collective-permute-done.42
  577.5 4.0 collective-permute-done.40
  589.0 29.0 %collective-permute-done.43 = f32[2,2,42,16,128]{4,3,2,1,0:T(8,128)S(1)} collective-permute-done((f32[2,2,42,16,128]{4,3,2,1,0:T(8,128)S(1)}, f32[2,2,42,16,128]{4,3,2,1,0:T(8,128)S(1)}, u32[]{:S(2)}, u32[]{:S(2)}) %collective-permute-start.43) | collective-permute-done | bytes 1376288 | tf_op jit(solution)/shard_map/ppermute | solution.py:1372
  623.9 11.2 %collective-permute-done.46 = f32[2,42,16,128]{3,2,1,0:T(8,128)S(1)} collective-permute-done((f32[2,42,16,128]{3,2,1,0:T(8,128)S(1)}, f32[2,42,16,128]{3,2,1,0:T(8,128)S(1)}, u32[]{:S(2)}, u32[]{:S(2)}) %collective-permute-start.46) | collective-permute-done | bytes 688160 | tf_op jit(solution)/shard_map/ppermute | solution.py:1372
  655.4 11.2 %collective-permute-done.53 = f32[127,16,128]{2,1,0:T(8,128)S(1)} collective-permute-done((f32[127,16,128]{2,1,0:T(8,128)}, f32[127,16,128]{2,1,0:T(8,128)S(1)}, u32[]{:S(2)}, u32[]{:S(2)}) %collective-permute-start.53) | collective-permute-done | bytes 1040416 | tf_op jit(solution)/shard_map/ppermute | solution.py:1368
  666.8 30.5 %collective-permute-done.52 = f32[127,16,128]{2,1,0:T(8,128)S(1)} collective-permute-done((f32[127,16,128]{2,1,0:T(8,128)S(1)}, f32[127,16,128]{2,1,0:T(8,128)S(1)}, u32[]{:S(2)}, u32[]{:S(2)}) %collective-permute-start.52) | collective-permute-done | bytes 1040416 | tf_op jit(solution)/shard_map/ppermute | solution.py:1368
  697.7 5.1 select_reduce_fusion
  717.9 4.3 collective-permute-start.61
  722.2 3.0 collective-permute-start.62
  728.6 5.9 unpack_rows.1.total
  735.7 8.2 %update_states.1 = (f32[3747,1,128]{2,1,0:T(1,128)}, f32[3747,1,128]{2,1,0:T(1,128)}, f32[3747,1,128]{2,1,0:T(1,128)}, f32[3747,1,128]{2,1,0:T(1,128)}) custom-call(f32[1]{0:T(128)} %bitcast.105.factor_ref, f32[3760,128]{1,0:T(8,128)} %copy-done.3, f32[3747,1,128]{2,1,0:T(1,128)} %bitcast.251, f32[3747,1,128]{2,1,0:T(1,128)} %bitcast.299, ...), custom_call_target="tpu_custom_call" | custom-call | tf_op jit(solution)/shard_map/update_states/pallas_call | solution.py:324
  (226 shorter events, 121.7 us)
Async XLA Ops:
  7.2 144.1 %all-gather.5.cloned.1.call-start = ((), (), s32[]{:S(2)}) async-start(), calls=%async_computation.1 | async-start | bytes 17166336 | tf_op jit(solution)/shard_map/all_gather | solution.py:1519
  8.2 9.7 %collective-permute-start.7 = (f32[384,1,128]{2,1,0:T(1,128)S(1)}, f32[384,1,128]{2,1,0:T(1,128)S(1)}, u32[]{:S(2)}, u32[]{:S(2)}) collective-permute-start(f32[384,1,128]{2,1,0:T(1,128)S(1)} %slice_bitcast_fusion), channel_id=1, source_target_pairs={{1,0},{2,1},{3,2},{4,3},{5,4},{6,5},{7,6},{8,7},{9,8},{10,9},{11,1... | collective-permute-start | bytes 589832 | tf_op jit(solution)/shard_map/ppermute | solution.py:1508
  29.1 201.5 %all-gather.3.cloned.1.call-start = ((), (), s32[]{:S(2)}) async-start(), calls=%async_computation | async-start | bytes 8650752 | tf_op jit(solution)/shard_map/all_gather | solution.py:1473
  29.2 10.4 %collective-permute-start.10 = (bf16[64,16,128]{2,1,0:T(8,128)(2,1)S(1)}, bf16[64,16,128]{2,1,0:T(8,128)(2,1)S(1)}, u32[]{:S(2)}, u32[]{:S(2)}) collective-permute-start(bf16[64,16,128]{2,1,0:T(8,128)(2,1)S(1)} %get-tuple-element.424), channel_id=1, source_target_pairs={{0,1},{1,3},{2,5},{3,7},{4,9},{5,11},{6,13},{7,15},{16,17},{17,19}... | collective-permute-start | bytes 786440 | tf_op jit(solution)/shard_map/ppermute | solution.py:1457
  40.4 26.2 %collective-permute-start.11 = (bf16[48,16,128]{2,1,0:T(8,128)(2,1)S(1)}, bf16[48,16,128]{2,1,0:T(8,128)(2,1)S(1)}, u32[]{:S(2)}, u32[]{:S(2)}) collective-permute-start(bf16[48,16,128]{2,1,0:T(8,128)(2,1)S(1)} %slice_select_fusion), channel_id=1, source_target_pairs={{8,0},{24,16}} | collective-permute-start | bytes 589832 | tf_op jit(solution)/shard_map/ppermute | solution.py:1468
  66.6 9.4 %collective-permute-start.12 = (bf16[48,16,128]{2,1,0:T(8,128)(2,1)S(1)}, bf16[48,16,128]{2,1,0:T(8,128)(2,1)S(1)}, u32[]{:S(2)}, u32[]{:S(2)}) collective-permute-start(bf16[48,16,128]{2,1,0:T(8,128)(2,1)S(1)} %fusion.22), channel_id=1, source_target_pairs={{8,12},{0,4},{24,28},{16,20}} | collective-permute-start | bytes 589832 | tf_op jit(solution)/shard_map/ppermute | solution.py:1468
  85.5 31.0 %collective-permute-start.15 = (bf16[48,16,128]{2,1,0:T(8,128)(2,1)S(1)}, bf16[48,16,128]{2,1,0:T(8,128)(2,1)S(1)}, u32[]{:S(2)}, u32[]{:S(2)}) collective-permute-start(bf16[48,16,128]{2,1,0:T(8,128)(2,1)S(1)} %add.422), channel_id=1, source_target_pairs={{0,16},{16,0},{1,17},{17,1},{2,18},{18,2},{3,19},{19,3},{4,20},{20... | collective-permute-start | bytes 589832 | tf_op jit(solution)/shard_map/ppermute | solution.py:1470
  90.3 10.3 %collective-permute-start.2 = (f32[]{:T(128)}, f32[]{:T(128)}, u32[]{:S(2)}, u32[]{:S(2)}) collective-permute-start(f32[]{:T(128)} %add.408), channel_id=1, source_target_pairs={{0,2},{1,3},{2,0},{3,1},{4,6},{5,7},{6,4},{7,5},{8,10},{9,11},{10,... | collective-permute-start | bytes 20 | tf_op jit(solution)/shard_map/ppermute | solution.py:1418
  101.9 13.4 %collective-permute-start.5 = (f32[]{:T(128)}, f32[]{:T(128)}, u32[]{:S(2)}, u32[]{:S(2)}) collective-permute-start(f32[]{:T(128)} %add.411), channel_id=1, source_target_pairs={{0,8},{1,9},{2,10},{3,11},{4,12},{5,13},{6,14},{7,15},{8,0},{9,1},... | collective-permute-start | bytes 20 | tf_op jit(solution)/shard_map/ppermute | solution.py:1418
  107.4 8.0 %collective-permute-start.6 = (f32[]{:T(128)}, f32[]{:T(128)}, u32[]{:S(2)}, u32[]{:S(2)}) collective-permute-start(f32[]{:T(128)} %add.411), channel_id=1, source_target_pairs={{0,12},{1,13},{2,14},{3,15},{4,8},{5,9},{6,10},{7,11},{8,4},{9,5},... | collective-permute-start | bytes 20 | tf_op jit(solution)/shard_map/ppermute | solution.py:1418
  350.6 14.0 %collective-permute-start.16 = (f32[8,127,16,128]{3,2,1,0:T(8,128)}, f32[8,127,16,128]{3,2,1,0:T(8,128)}, u32[]{:S(2)}, u32[]{:S(2)}) collective-permute-start(f32[8,127,16,128]{3,2,1,0:T(8,128)} %get-tuple-element.209), channel_id=1, source_target_pairs={{0,16},{16,0},{1,17},{17,1},{2,18},{18,2},{3,19},{19,3},{4,20},{20... | collective-permute-start | bytes 24969224 | tf_op jit(solution)/shard_map/ppermute | solution.py:1364
  372.7 42.3 %collective-permute-start.20 = (f32[2,2,43,16,128]{4,3,2,1,0:T(8,128)S(1)}, f32[2,2,43,16,128]{4,3,2,1,0:T(8,128)S(1)}, u32[]{:S(2)}, u32[]{:S(2)}) collective-permute-start(f32[2,2,43,16,128]{4,3,2,1,0:T(8,128)S(1)} %add_bitcast_fusion.3), channel_id=1, source_target_pairs={{0,4},{1,5},{2,6},{3,7},{4,0},{5,1},{6,2},{7,3},{8,12},{9,13},{10,... | collective-permute-start | bytes 4227080 | tf_op jit(solution)/shard_map/ppermute | solution.py:1372
  374.3 40.7 %collective-permute-start.18 = (f32[2,2,42,16,128]{4,3,2,1,0:T(8,128)}, f32[2,2,42,16,128]{4,3,2,1,0:T(8,128)}, u32[]{:S(2)}, u32[]{:S(2)}) collective-permute-start(f32[2,2,42,16,128]{4,3,2,1,0:T(8,128)} %add_bitcast_fusion.7), channel_id=1, source_target_pairs={{0,1},{1,0},{2,3},{3,2},{4,5},{5,4},{6,7},{7,6},{8,9},{9,8},{10,11... | collective-permute-start | bytes 4128776 | tf_op jit(solution)/shard_map/ppermute | solution.py:1372
  375.7 39.3 %collective-permute-start.19 = (f32[2,2,42,16,128]{4,3,2,1,0:T(8,128)}, f32[2,2,42,16,128]{4,3,2,1,0:T(8,128)}, u32[]{:S(2)}, u32[]{:S(2)}) collective-permute-start(f32[2,2,42,16,128]{4,3,2,1,0:T(8,128)} %add_bitcast_fusion.6), channel_id=1, source_target_pairs={{0,2},{1,3},{2,0},{3,1},{4,6},{5,7},{6,4},{7,5},{8,10},{9,11},{10,... | collective-permute-start | bytes 4128776 | tf_op jit(solution)/shard_map/ppermute | solution.py:1372
  376.3 38.7 %collective-permute-start.21 = (f32[48,16,128]{2,1,0:T(8,128)S(1)}, f32[48,16,128]{2,1,0:T(8,128)S(1)}, u32[]{:S(2)}, u32[]{:S(2)}) collective-permute-start(f32[48,16,128]{2,1,0:T(8,128)S(1)} %add_bitcast_fusion.9), channel_id=1, source_target_pairs={{1,0},{3,2},{5,4},{7,6},{9,8},{11,10},{13,12},{15,14},{17,16},{19,... | collective-permute-start | bytes 1179656 | tf_op jit(solution)/shard_map/ppermute | solution.py:1368
  421.8 26.7 %collective-permute-start.24 = (f32[2,43,16,128]{3,2,1,0:T(8,128)S(1)}, f32[2,43,16,128]{3,2,1,0:T(8,128)S(1)}, u32[]{:S(2)}, u32[]{:S(2)}) collective-permute-start(f32[2,43,16,128]{3,2,1,0:T(8,128)S(1)} %bitcast_add_fusion.3), channel_id=1, source_target_pairs={{0,1},{1,0},{2,3},{3,2},{4,5},{5,4},{6,7},{7,6},{8,9},{9,8},{10,11... | collective-permute-start | bytes 2113544 | tf_op jit(solution)/shard_map/ppermute | solution.py:1372
  421.8 26.7 %collective-permute-start.22 = (f32[2,42,16,128]{3,2,1,0:T(8,128)}, f32[2,42,16,128]{3,2,1,0:T(8,128)}, u32[]{:S(2)}, u32[]{:S(2)}) collective-permute-start(f32[2,42,16,128]{3,2,1,0:T(8,128)} %get-tuple-element.273), channel_id=1, source_target_pairs={{0,2},{1,3},{2,0},{3,1},{4,6},{5,7},{6,4},{7,5},{8,10},{9,11},{10,... | collective-permute-start | bytes 2064392 | tf_op jit(solution)/shard_map/ppermute | solution.py:1372
  423.3 25.2 %collective-permute-start.23 = (f32[2,42,16,128]{3,2,1,0:T(8,128)}, f32[2,42,16,128]{3,2,1,0:T(8,128)}, u32[]{:S(2)}, u32[]{:S(2)}) collective-permute-start(f32[2,42,16,128]{3,2,1,0:T(8,128)} %get-tuple-element.274), channel_id=1, source_target_pairs={{0,4},{1,5},{2,6},{3,7},{4,0},{5,1},{6,2},{7,3},{8,12},{9,13},{10,... | collective-permute-start | bytes 2064392 | tf_op jit(solution)/shard_map/ppermute | solution.py:1372
  423.8 24.7 %collective-permute-start.25 = (f32[48,16,128]{2,1,0:T(8,128)S(1)}, f32[48,16,128]{2,1,0:T(8,128)S(1)}, u32[]{:S(2)}, u32[]{:S(2)}) collective-permute-start(f32[48,16,128]{2,1,0:T(8,128)S(1)} %add.446), channel_id=1, source_target_pairs={{2,0},{3,1},{6,4},{7,5},{10,8},{11,9},{14,12},{15,13},{18,16},{19,... | collective-permute-start | bytes 1179656 | tf_op jit(solution)/shard_map/ppermute | solution.py:1368
  452.4 20.9 %collective-permute-start.30 = (f32[8,127,16,128]{3,2,1,0:T(8,128)}, f32[8,127,16,128]{3,2,1,0:T(8,128)}, u32[]{:S(2)}, u32[]{:S(2)}) collective-permute-start(f32[8,127,16,128]{3,2,1,0:T(8,128)} %get-tuple-element.313), channel_id=1, source_target_pairs={{0,16},{16,0},{1,17},{17,1},{2,18},{18,2},{3,19},{19,3},{4,20},{20... | collective-permute-start | bytes 24969224 | tf_op jit(solution)/shard_map/ppermute | solution.py:1364
  452.5 20.8 %collective-permute-start.29 = (f32[48,16,128]{2,1,0:T(8,128)S(1)}, f32[48,16,128]{2,1,0:T(8,128)S(1)}, u32[]{:S(2)}, u32[]{:S(2)}) collective-permute-start(f32[48,16,128]{2,1,0:T(8,128)S(1)} %add.459), channel_id=1, source_target_pairs={{4,0},{5,1},{6,2},{7,3},{12,8},{13,9},{14,10},{15,11},{20,16},{21,... | collective-permute-start | bytes 1179656 | tf_op jit(solution)/shard_map/ppermute | solution.py:1368
  453.8 19.5 %collective-permute-start.28 = (f32[43,16,128]{2,1,0:T(8,128)}, f32[43,16,128]{2,1,0:T(8,128)S(1)}, u32[]{:S(2)}, u32[]{:S(2)}) collective-permute-start(f32[43,16,128]{2,1,0:T(8,128)} %bitcast_add_fusion.23), channel_id=1, source_target_pairs={{0,2},{1,3},{2,0},{3,1},{4,6},{5,7},{6,4},{7,5},{8,10},{9,11},{10,... | collective-permute-start | bytes 1056776 | tf_op jit(solution)/shard_map/ppermute | solution.py:1372
  456.5 16.8 %collective-permute-start.26 = (f32[42,16,128]{2,1,0:T(8,128)S(1)}, f32[42,16,128]{2,1,0:T(8,128)S(1)}, u32[]{:S(2)}, u32[]{:S(2)}) collective-permute-start(f32[42,16,128]{2,1,0:T(8,128)S(1)} %get-tuple-element.309), channel_id=1, source_target_pairs={{0,4},{1,5},{2,6},{3,7},{4,0},{5,1},{6,2},{7,3},{8,12},{9,13},{10,... | collective-permute-start | bytes 1032200 | tf_op jit(solution)/shard_map/ppermute | solution.py:1372
  459.2 14.1 %collective-permute-start.27 = (f32[42,16,128]{2,1,0:T(8,128)S(1)}, f32[42,16,128]{2,1,0:T(8,128)S(1)}, u32[]{:S(2)}, u32[]{:S(2)}) collective-permute-start(f32[42,16,128]{2,1,0:T(8,128)S(1)} %get-tuple-element.310), channel_id=1, source_target_pairs={{0,1},{1,0},{2,3},{3,2},{4,5},{5,4},{6,7},{7,6},{8,9},{9,8},{10,11... | collective-permute-start | bytes 1032200 | tf_op jit(solution)/shard_map/ppermute | solution.py:1372
  486.8 41.9 %collective-permute-start.32 = (f32[2,2,51,16,128]{4,3,2,1,0:T(8,128)}, f32[2,2,51,16,128]{4,3,2,1,0:T(8,128)S(1)}, u32[]{:S(2)}, u32[]{:S(2)}) collective-permute-start(f32[2,2,51,16,128]{4,3,2,1,0:T(8,128)} %add_bitcast_fusion), channel_id=1, source_target_pairs={{0,2},{1,3},{2,0},{3,1},{4,6},{5,7},{6,4},{7,5},{8,10},{9,11},{10,... | collective-permute-start | bytes 5013512 | tf_op jit(solution)/shard_map/ppermute | solution.py:1372
  489.5 39.2 %collective-permute-start.31 = (f32[2,2,50,16,128]{4,3,2,1,0:T(8,128)}, f32[2,2,50,16,128]{4,3,2,1,0:T(8,128)}, u32[]{:S(2)}, u32[]{:S(2)}) collective-permute-start(f32[2,2,50,16,128]{4,3,2,1,0:T(8,128)} %add_bitcast_fusion.1), channel_id=1, source_target_pairs={{0,1},{1,0},{2,3},{3,2},{4,5},{5,4},{6,7},{7,6},{8,9},{9,8},{10,11... | collective-permute-start | bytes 4915208 | tf_op jit(solution)/shard_map/ppermute | solution.py:1372
  491.6 37.2 %collective-permute-start.33 = (f32[2,2,26,16,128]{4,3,2,1,0:T(8,128)}, f32[2,2,26,16,128]{4,3,2,1,0:T(8,128)}, u32[]{:S(2)}, u32[]{:S(2)}) collective-permute-start(f32[2,2,26,16,128]{4,3,2,1,0:T(8,128)} %add_bitcast_fusion.8), channel_id=1, source_target_pairs={{0,4},{1,5},{2,6},{3,7},{4,0},{5,1},{6,2},{7,3},{8,12},{9,13},{10,... | collective-permute-start | bytes 2555912 | tf_op jit(solution)/shard_map/ppermute | solution.py:1372
  491.6 72.7 %collective-permute-start.37 = (f32[127,16,128]{2,1,0:T(8,128)}, f32[127,16,128]{2,1,0:T(8,128)}, u32[]{:S(2)}, u32[]{:S(2)}) collective-permute-start(f32[127,16,128]{2,1,0:T(8,128)} %pad_maximum_fusion), channel_id=1, source_target_pairs={{8,0},{9,1},{10,2},{11,3},{12,4},{13,5},{14,6},{15,7},{24,16},{25,... | collective-permute-start | bytes 3121160 | tf_op jit(solution)/shard_map/ppermute | solution.py:1368
  536.6 27.6 %collective-permute-start.35 = (f32[2,51,16,128]{3,2,1,0:T(8,128)}, f32[2,51,16,128]{3,2,1,0:T(8,128)}, u32[]{:S(2)}, u32[]{:S(2)}) collective-permute-start(f32[2,51,16,128]{3,2,1,0:T(8,128)} %bitcast_add_fusion), channel_id=1, source_target_pairs={{0,4},{1,5},{2,6},{3,7},{4,0},{5,1},{6,2},{7,3},{8,12},{9,13},{10,... | collective-permute-start | bytes 2506760 | tf_op jit(solution)/shard_map/ppermute | solution.py:1372
  536.6 27.6 %collective-permute-start.34 = (f32[2,50,16,128]{3,2,1,0:T(8,128)}, f32[2,50,16,128]{3,2,1,0:T(8,128)}, u32[]{:S(2)}, u32[]{:S(2)}) collective-permute-start(f32[2,50,16,128]{3,2,1,0:T(8,128)} %bitcast_add_fusion.1), channel_id=1, source_target_pairs={{0,2},{1,3},{2,0},{3,1},{4,6},{5,7},{6,4},{7,5},{8,10},{9,11},{10,... | collective-permute-start | bytes 2457608 | tf_op jit(solution)/shard_map/ppermute | solution.py:1372
  536.9 27.3 %collective-permute-start.38 = (f32[48,16,128]{2,1,0:T(8,128)S(1)}, f32[48,16,128]{2,1,0:T(8,128)}, u32[]{:S(2)}, u32[]{:S(2)}) collective-permute-start(f32[48,16,128]{2,1,0:T(8,128)S(1)} %add.477), channel_id=1, source_target_pairs={{0,8},{1,9},{2,10},{3,11},{4,12},{5,13},{6,14},{7,15},{16,24},{17,... | collective-permute-start | bytes 1179656 | tf_op jit(solution)/shard_map/ppermute | solution.py:1368
  540.3 24.0 %collective-permute-start.36 = (f32[2,26,16,128]{3,2,1,0:T(8,128)}, f32[2,26,16,128]{3,2,1,0:T(8,128)S(1)}, u32[]{:S(2)}, u32[]{:S(2)}) collective-permute-start(f32[2,26,16,128]{3,2,1,0:T(8,128)} %bitcast_add_fusion.8), channel_id=1, source_target_pairs={{0,1},{1,0},{2,3},{3,2},{4,5},{5,4},{6,7},{7,6},{8,9},{9,8},{10,11... | collective-permute-start | bytes 1277960 | tf_op jit(solution)/shard_map/ppermute | solution.py:1372
  568.4 17.3 %collective-permute-start.39 = (f32[8,127,16,128]{3,2,1,0:T(8,128)}, f32[8,127,16,128]{3,2,1,0:T(8,128)S(1)}, u32[]{:S(2)}, u32[]{:S(2)}) collective-permute-start(f32[8,127,16,128]{3,2,1,0:T(8,128)} %get-tuple-element.378), channel_id=1, source_target_pairs={{0,16},{16,0},{1,17},{17,1},{2,18},{18,2},{3,19},{19,3},{4,20},{20... | collective-permute-start | bytes 24969224 | tf_op jit(solution)/shard_map/ppermute | solution.py:1364
  568.5 7.7 %collective-permute-start.42 = (f32[26,16,128]{2,1,0:T(8,128)S(1)}, f32[26,16,128]{2,1,0:T(8,128)S(1)}, u32[]{:S(2)}, u32[]{:S(2)}) collective-permute-start(f32[26,16,128]{2,1,0:T(8,128)S(1)} %bitcast_add_fusion.43), channel_id=1, source_target_pairs={{0,2},{1,3},{2,0},{3,1},{4,6},{5,7},{6,4},{7,5},{8,10},{9,11},{10,... | collective-permute-start | bytes 638984 | tf_op jit(solution)/shard_map/ppermute | solution.py:1372
  569.7 11.8 %collective-permute-start.40 = (f32[50,16,128]{2,1,0:T(8,128)S(1)}, f32[50,16,128]{2,1,0:T(8,128)S(1)}, u32[]{:S(2)}, u32[]{:S(2)}) collective-permute-start(f32[50,16,128]{2,1,0:T(8,128)S(1)} %bitcast_add_fusion.15), channel_id=1, source_target_pairs={{0,4},{1,5},{2,6},{3,7},{4,0},{5,1},{6,2},{7,3},{8,12},{9,13},{10,... | collective-permute-start | bytes 1228808 | tf_op jit(solution)/shard_map/ppermute | solution.py:1372
  571.7 11.4 %collective-permute-start.41 = (f32[51,16,128]{2,1,0:T(8,128)S(1)}, f32[51,16,128]{2,1,0:T(8,128)S(1)}, u32[]{:S(2)}, u32[]{:S(2)}) collective-permute-start(f32[51,16,128]{2,1,0:T(8,128)S(1)} %bitcast_add_fusion.11), channel_id=1, source_target_pairs={{0,1},{1,0},{2,3},{3,2},{4,5},{5,4},{6,7},{7,6},{8,9},{9,8},{10,11... | collective-permute-start | bytes 1253384 | tf_op jit(solution)/shard_map/ppermute | solution.py:1372
  586.3 31.7 %collective-permute-start.43 = (f32[2,2,42,16,128]{4,3,2,1,0:T(8,128)S(1)}, f32[2,2,42,16,128]{4,3,2,1,0:T(8,128)S(1)}, u32[]{:S(2)}, u32[]{:S(2)}) collective-permute-start(f32[2,2,42,16,128]{4,3,2,1,0:T(8,128)S(1)} %add_bitcast_fusion.5), channel_id=1, source_target_pairs={{0,1},{1,0},{2,3},{3,2},{4,5},{5,4},{6,7},{7,6},{8,9},{9,8},{10,11... | collective-permute-start | bytes 4128776 | tf_op jit(solution)/shard_map/ppermute | solution.py:1372
  586.7 31.4 %collective-permute-start.44 = (f32[2,2,42,16,128]{4,3,2,1,0:T(8,128)S(1)}, f32[2,2,42,16,128]{4,3,2,1,0:T(8,128)S(1)}, u32[]{:S(2)}, u32[]{:S(2)}) collective-permute-start(f32[2,2,42,16,128]{4,3,2,1,0:T(8,128)S(1)} %add_bitcast_fusion.4), channel_id=1, source_target_pairs={{0,2},{1,3},{2,0},{3,1},{4,6},{5,7},{6,4},{7,5},{8,10},{9,11},{10,... | collective-permute-start | bytes 4128776 | tf_op jit(solution)/shard_map/ppermute | solution.py:1372
  587.5 31.9 %collective-permute-start.45 = (f32[2,2,43,16,128]{4,3,2,1,0:T(8,128)S(1)}, f32[2,2,43,16,128]{4,3,2,1,0:T(8,128)S(1)}, u32[]{:S(2)}, u32[]{:S(2)}) collective-permute-start(f32[2,2,43,16,128]{4,3,2,1,0:T(8,128)S(1)} %add_bitcast_fusion.2), channel_id=1, source_target_pairs={{0,4},{1,5},{2,6},{3,7},{4,0},{5,1},{6,2},{7,3},{8,12},{9,13},{10,... | collective-permute-start | bytes 4227080 | tf_op jit(solution)/shard_map/ppermute | solution.py:1372
  619.6 15.5 %collective-permute-start.46 = (f32[2,42,16,128]{3,2,1,0:T(8,128)S(1)}, f32[2,42,16,128]{3,2,1,0:T(8,128)S(1)}, u32[]{:S(2)}, u32[]{:S(2)}) collective-permute-start(f32[2,42,16,128]{3,2,1,0:T(8,128)S(1)} %get-tuple-element.385), channel_id=1, source_target_pairs={{0,2},{1,3},{2,0},{3,1},{4,6},{5,7},{6,4},{7,5},{8,10},{9,11},{10,... | collective-permute-start | bytes 2064392 | tf_op jit(solution)/shard_map/ppermute | solution.py:1372
  620.8 15.2 %collective-permute-start.47 = (f32[2,42,16,128]{3,2,1,0:T(8,128)S(1)}, f32[2,42,16,128]{3,2,1,0:T(8,128)S(1)}, u32[]{:S(2)}, u32[]{:S(2)}) collective-permute-start(f32[2,42,16,128]{3,2,1,0:T(8,128)S(1)} %get-tuple-element.386), channel_id=1, source_target_pairs={{0,4},{1,5},{2,6},{3,7},{4,0},{5,1},{6,2},{7,3},{8,12},{9,13},{10,... | collective-permute-start | bytes 2064392 | tf_op jit(solution)/shard_map/ppermute | solution.py:1372
  622.2 15.1 %collective-permute-start.48 = (f32[2,43,16,128]{3,2,1,0:T(8,128)S(1)}, f32[2,43,16,128]{3,2,1,0:T(8,128)S(1)}, u32[]{:S(2)}, u32[]{:S(2)}) collective-permute-start(f32[2,43,16,128]{3,2,1,0:T(8,128)S(1)} %bitcast_add_fusion.2), channel_id=1, source_target_pairs={{0,1},{1,0},{2,3},{3,2},{4,5},{5,4},{6,7},{7,6},{8,9},{9,8},{10,11... | collective-permute-start | bytes 2113544 | tf_op jit(solution)/shard_map/ppermute | solution.py:1372
  638.2 9.1 %collective-permute-start.49 = (f32[42,16,128]{2,1,0:T(8,128)}, f32[42,16,128]{2,1,0:T(8,128)}, u32[]{:S(2)}, u32[]{:S(2)}) collective-permute-start(f32[42,16,128]{2,1,0:T(8,128)} %get-tuple-element.388), channel_id=1, source_target_pairs={{0,4},{1,5},{2,6},{3,7},{4,0},{5,1},{6,2},{7,3},{8,12},{9,13},{10,... | collective-permute-start | bytes 1032200 | tf_op jit(solution)/shard_map/ppermute | solution.py:1372
  639.2 8.0 %collective-permute-start.50 = (f32[42,16,128]{2,1,0:T(8,128)}, f32[42,16,128]{2,1,0:T(8,128)}, u32[]{:S(2)}, u32[]{:S(2)}) collective-permute-start(f32[42,16,128]{2,1,0:T(8,128)} %get-tuple-element.389), channel_id=1, source_target_pairs={{0,1},{1,0},{2,3},{3,2},{4,5},{5,4},{6,7},{7,6},{8,9},{9,8},{10,11... | collective-permute-start | bytes 1032200 | tf_op jit(solution)/shard_map/ppermute | solution.py:1372
  645.1 21.5 %collective-permute-start.53 = (f32[127,16,128]{2,1,0:T(8,128)}, f32[127,16,128]{2,1,0:T(8,128)S(1)}, u32[]{:S(2)}, u32[]{:S(2)}) collective-permute-start(f32[127,16,128]{2,1,0:T(8,128)} %pad_maximum_fusion.1), channel_id=1, source_target_pairs={{0,8},{1,9},{2,10},{3,11},{4,12},{5,13},{6,14},{7,15},{16,24},{17,... | collective-permute-start | bytes 3121160 | tf_op jit(solution)/shard_map/ppermute | solution.py:1368
  651.9 45.3 %collective-permute-start.52 = (f32[127,16,128]{2,1,0:T(8,128)S(1)}, f32[127,16,128]{2,1,0:T(8,128)S(1)}, u32[]{:S(2)}, u32[]{:S(2)}) collective-permute-start(f32[127,16,128]{2,1,0:T(8,128)S(1)} %pad_maximum_fusion.2), channel_id=1, source_target_pairs={{8,0},{9,1},{10,2},{11,3},{12,4},{13,5},{14,6},{15,7},{24,16},{25,... | collective-permute-start | bytes 3121160 | tf_op jit(solution)/shard_map/ppermute | solution.py:1368
  702.8 8.8 %collective-permute-start.55 = (f32[127,16,128]{2,1,0:T(8,128)}, f32[127,16,128]{2,1,0:T(8,128)S(1)}, u32[]{:S(2)}, u32[]{:S(2)}) collective-permute-start(f32[127,16,128]{2,1,0:T(8,128)} %get-tuple-element.417), channel_id=1, source_target_pairs={{0,16},{16,0},{1,17},{17,1},{2,18},{18,2},{3,19},{19,3},{4,20},{20... | collective-permute-start | bytes 3121160 | tf_op jit(solution)/shard_map/ppermute | solution.py:1585
  717.8 7.4 collective-permute-start.60
  (41 other events, 523.6 us)
Sparse Core Ops, SparseCore 0:
  29.2 122.0 all-gather.4
  154.8 75.7 all-gather.2

commit v6 on v5

--- a/solution.py
+++ b/solution.py
@@ -412,7 +412,7 @@
 
 
 def norm_block(count):
-    return next(n for n in (224, 208, 112, 104, 16) if count % n == 0)
+    return next(n for n in (416, 336, 112, 104, 16) if count % n == 0)
 
 
 def norm_rows(x, width):
@@ -1554,25 +1554,30 @@
     blocks = []
     late = []
     for number, stage in enumerate(stages):
-        flows, got, (arrays, blocks) = move_on([main, rest, high], arrays, blocks)
+        few = None if number in (0, 3) else rest
+        flows, got, (arrays, blocks) = move_on([main, few, high], arrays, blocks)
         if stage.bins:
             blocks, made = stage(info, gathered_e, arrays, blocks)
         else:
             _, made = stage(info, gathered_e, arrays, [])
         arrays = {**arrays, **made}
-        kept = [g for f, g in zip(flows, got) if not f.last()]
+        long = [f is main and f.last() for f in flows]
+        kept = [g for g, is_long in zip(got, long) if not is_long]
         kept, late, arrays, blocks = tie(kept, late, arrays, blocks)
-        late = [g for f, g in zip(flows, got) if f.last()]
+        late = [g for g, is_long in zip(got, long) if is_long]
         kept = iter(kept)
-        arrive(flows, [g if f.last() else next(kept) for f, g in zip(flows, got)])
+        arrive(flows, [g if is_long else next(kept) for g, is_long in zip(got, long)])
         if number == 1:
             high = Flow(dp, blocks[2], blocks[3], dp // 2, (4, 4, 2))
             blocks = blocks[:2]
     low = Flow(dp, blocks[0], blocks[1], 0)
     every = [main, rest, high, low]
-    while not all(f.done() for f in every):
-        flows, got, _ = move_on(every)
+    before = ()
+    for turn in range(1 + max(f.all_bits - f.step for f in every)):
+        flows, got, _ = move_on(every, before if turn == 1 else ())
+        before = got
         arrive(flows, got)
+    assert all(f.done() for f in every)
 
     sum_tail = rest.result()
     sum_tail = jnp.pad(sum_tail, ((0, half - sum_tail.shape[0]), (0, 0), (0, 0)))

time: 758 us -> 756 us (level)
  transfers between devices with their start and end apart: 65 -> 65, of which waited for: 30 -> 31; matrix products, arithmetic and copies ran while one was open for 5% -> 5% of each run, Pallas kernels for 19% -> 19%
where the time goes in v6:
time: 756 us; the launch traced here: 751 us
  Pallas kernels  284 us (38%)
  waiting for transfers between devices  259 us (34%)
  starting transfers between devices  93.9 us (12%)
  other arithmetic  70.7 us (9%)
  between operations  26.7 us (4%)
  local copies, waits for them, and re-layouts  16.6 us (2%)
    pallas_call x1, Pallas kernels, decoder(): pl.pallas_call(lambda *refs: decoder_kernel(plan, sh, refs), out_shape=[*...  118 us
    pallas_call x5, Pallas kernels, __call__(): pl.pallas_call(functools.partial(self.kernel, len(blocks)), out_shape=[*t...  108 us
    ppermute x27, waiting for transfers between devices, send(): lax.ppermute(value, 'dp', [(i, i ^ flip) for i in range(self.dp)])  64.5 us
    add x43, other arithmetic, total_of(): total = total + term  56.8 us
    ppermute x7, waiting for transfers between devices, send(): return [lax.ppermute(payload[0], 'dp', pairs)]  49.5 us
    all_gather x1, waiting for transfers between devices, gather_decoder(): gathered = lax.all_gather(spread, ('section', 'dp'), axis=0, tiled=True)  40.7 us
    pallas_call x1, Pallas kernels, encoder(): pl.pallas_call(lambda *refs: encoder_kernel(plan, sh, refs), out_shape=[j...  38 us
    ppermute x4, waiting for transfers between devices, gather_decoder(): rest = rest + lax.ppermute(rest, 'dp', [(i, i ^ 1 << bit) for i in holders])  36.1 us
  transfers between devices with their start and end apart: 65, of which 31 were waited for; matrix products, arithmetic and copies ran while one was open for 5% of the time, Pallas kernels for 19%

profile of v6, /device:TPU:0, one launch (start us, length us, event | category | flops | bytes accessed | tf_op | source)
XLA Modules:
  0.0 751.3 jit_solution(16903182091847695116)
XLA Ops:
  10.4 7.5 collective-permute-done.7.following
  19.4 6.8 pack_rows.1
  29.2 4.6 collective-permute-start.10
  34.5 5.1 collective-permute-done.10
  41.8 24.9 %collective-permute-done.11 = bf16[48,16,128]{2,1,0:T(8,128)(2,1)S(1)} collective-permute-done((bf16[48,16,128]{2,1,0:T(8,128)(2,1)S(1)}, bf16[48,16,128]{2,1,0:T(8,128)(2,1)S(1)}, u32[]{:S(2)}, u32[]{:S(2)}) %collective-permute-start.11) | collective-permute-done | bytes 196640 | tf_op jit(solution)/shard_map/ppermute | solution.py:1468
  68.0 8.1 %collective-permute-done.12 = bf16[48,16,128]{2,1,0:T(8,128)(2,1)S(1)} collective-permute-done((bf16[48,16,128]{2,1,0:T(8,128)(2,1)S(1)}, bf16[48,16,128]{2,1,0:T(8,128)(2,1)S(1)}, u32[]{:S(2)}, u32[]{:S(2)}) %collective-permute-start.12) | collective-permute-done | bytes 196640 | tf_op jit(solution)/shard_map/ppermute | solution.py:1468
  77.4 3.2 collective-permute-done.13
  90.3 3.9 collective-permute-start.2
  102.1 5.5 collective-permute-start.5
  107.6 3.8 collective-permute-start.6
  117.8 33.3 %all-gather.5.cloned.1.call-done = bf16[4064,16,128]{2,1,0:T(8,128)(2,1)} async-done(((bf16[127,16,128]{2,1,0:T(8,128)(2,1)}), bf16[4064,16,128]{2,1,0:T(8,128)(2,1)}) %all-gather.5.cloned.1.call-update) | async-done | bytes 16646160 | tf_op jit(solution)/shard_map/all_gather | solution.py:1519
  151.1 38.0 %encoder_forward.1 = (bf16[6,208,768]{2,1,0:T(8,128)(2,1)}, f32[672,768]{1,0:T(8,128)}, bf16[672,768]{1,0:T(8,128)(2,1)}, bf16[672,2304]{1,0:T(8,128)(2,1)}, bf1...) custom-call(s32[7]{0:T(128)} %pad_add_fusion.refs_0_, ...), custom_call_target="tpu_custom_call" | custom-call | flops 10000000000 | bytes 1048576 | tf_op jit(solution)/shard_map/encoder_forward/pallas_call | solution.py:914
  189.1 40.7 %all-gather.3.cloned.1.call-done = bf16[2048,16,128]{2,1,0:T(8,128)(2,1)} async-done(((bf16[64,16,128]{2,1,0:T(8,128)(2,1)}), bf16[2048,16,128]{2,1,0:T(8,128)(2,1)}) %all-gather.3.cloned.1.call-update) | async-done | bytes 8388624 | tf_op jit(solution)/shard_map/all_gather | solution.py:1473
  229.8 117.9 %decoder_both.1 = (f32[8,127,16,128]{3,2,1,0:T(8,128)}, f32[8,127,16,128]{3,2,1,0:T(8,128)}, f32[1,48,16,128]{3,2,1,0:T(8,128)}, f32[1,48,16,128]{3,2,1,0:T(8,12...) custom-call(s32[7]{0:T(128)} %pad_add_fusion.refs_0_, f32[1]{0:T(128)} %bitcast.3.refs_1_, ...), custom_call_target="tpu_custom_call" | custom-call | flops 32000000000 | bytes 1048576 | tf_op jit(solution)/shard_map/decoder_both/pallas_call | solution.py:1070
  348.3 5.2 collective-permute-done.17
  353.5 8.2 %collective-permute-done.16 = f32[8,127,16,128]{3,2,1,0:T(8,128)} collective-permute-done((f32[8,127,16,128]{3,2,1,0:T(8,128)}, f32[8,127,16,128]{3,2,1,0:T(8,128)}, u32[]{:S(2)}, u32[]{:S(2)}) %collective-permute-start.16) | collective-permute-done | bytes 8323104 | tf_op jit(solution)/shard_map/ppermute | solution.py:1364
  363.7 3.0 add_bitcast_fusion.6
  366.7 3.1 add_bitcast_fusion.7
  374.4 29.1 %encoder_back_fc2.1 = (f32[8,127,16,128]{3,2,1,0:T(8,128)}, f32[8,127,16,128]{3,2,1,0:T(8,128)}, f32[8,127,16,128]{3,2,1,0:T(8,128)}, f32[8,127,16,128]{3,2,1,0:...) custom-call(s32[7]{0:T(128)} %pad_add_fusion.refs_0_, bf16[2,16,127,16,128]{4,3,2,1,0:T(8,128)(2,1)} %bitcast.255, ...), custom_call_target="tpu_custom_call" | custom-call | flops 5000000000 | bytes 1048576 | tf_op jit(solution)/shard_map/encoder_back_fc2/pallas_call | solution.py:1189
  406.3 3.5 bitcast_add_fusion.6
  413.6 23.4 %encoder_back_fc1.1 = (f32[8,127,16,128]{3,2,1,0:T(8,128)}, f32[8,127,16,128]{3,2,1,0:T(8,128)}, f32[8,127,16,128]{3,2,1,0:T(8,128)}, f32[8,127,16,128]{3,2,1,0:T(8,128)}, f32[672,768]{1,0:T(8,128)}) custom-call(s32[7]{0:T(128)} %pad_add_fusion.refs_0_, ...), custom_call_target="tpu_custom_call", output_to_operand_aliasing={{0}: (6, {}), {1}: (7, {}), {2}: (8, {}), {3}: (9, {})} | custom-call | flops 4000000000 | bytes 1048576 | tf_op jit(solution)/shard_map/encoder_back_fc1/pallas_call | solution.py:1189
  442.5 2.7 collective-permute-start.27
  446.7 2.7 collective-permute-start.26
  449.4 8.2 %encoder_back_proj.1 = (f32[8,127,16,128]{3,2,1,0:T(8,128)}, f32[8,127,16,128]{3,2,1,0:T(8,128)}, bf16[672,768]{1,0:T(8,128)(2,1)}) custom-call(s32[7]{0:T(128)} %pad_add_fusion.refs_0_, bf16[2,16,127,16,128]{4,3,2,1,0:T(8,128)(2,1)} %bitcast.257, f32[672,768]{1,0:T(8,128)} %get-tuple-element.363.refs_2_, ...), custom_call_target="tpu_custom_call", output_to_operand_aliasing={{0}: (4, {}), {1}: (5, {})} | custom-call | flops 2000000000 | bytes 1048576 | tf_op jit(solution)/shard_map/encoder_back_proj/pallas_call | solution.py:1189
  457.7 4.4 collective-permute-done.27
  462.1 2.5 add_bitcast_fusion.8
  464.6 3.3 add_bitcast_fusion
  467.9 3.4 add_bitcast_fusion.1
  475.7 2.7 collective-permute-start.30
  481.3 25.0 %encoder_back_attention.1.refs_3_ = bf16[672,2304]{1,0:T(8,128)(2,1)} custom-call(s32[7]{0:T(128)} %pad_add_fusion.refs_0_, bf16[2,16,127,16,128]{4,3,2,1,0:T(8,128)(2,1)} %bitcast.258, bf16[672,768]{1,0:T(8,128)(2,1)} %get-tuple-element.339.refs_2_, bf16[672,2304]{1,0:T(8,128)(2,1)} %get-tuple-element.340.refs_3_), custom_call_target="tpu_custom_call" | custom-call | flops 5000000000 | bytes 1048576 | tf_op jit(solution)/shard_map/encoder_back_attention/pallas_call | solution.py:1189
  506.2 8.2 %collective-permute-done.32 = f32[2,2,26,16,128]{4,3,2,1,0:T(8,128)S(1)} collective-permute-done((f32[2,2,26,16,128]{4,3,2,1,0:T(8,128)}, f32[2,2,26,16,128]{4,3,2,1,0:T(8,128)S(1)}, u32[]{:S(2)}, u32[]{:S(2)}) %collective-permute-start.32) | collective-permute-done | bytes 852000 | tf_op jit(solution)/shard_map/ppermute | solution.py:1372
  514.5 2.7 bitcast_add_fusion.1
  519.2 2.7 bitcast_add_fusion
  528.1 22.0 %encoder_back_qkv.1 = (f32[8,127,16,128]{3,2,1,0:T(8,128)}, f32[8,127,16,128]{3,2,1,0:T(8,128)}) custom-call(s32[7]{0:T(128)} %pad_add_fusion.refs_0_, bf16[2,16,127,16,128]{4,3,2,1,0:T(8,128)(2,1)} %bitcast.259, f32[672,768]{1,0:T(8,128)} %get-tuple-element.363.refs_2_, ...), custom_call_target="tpu_custom_call", output_to_operand_aliasing={{0}: (7, {}), {1}: (8, {})} | custom-call | flops 5000000000 | bytes 1048576 | tf_op jit(solution)/shard_map/encoder_back_qkv/pallas_call | solution.py:1189
  550.1 5.7 collective-permute-done.33
  564.7 4.3 collective-permute-done.41
  570.3 4.4 collective-permute-done.39
  582.4 3.3 collective-permute-start.45
  585.7 27.1 %collective-permute-done.43 = f32[2,2,42,16,128]{4,3,2,1,0:T(8,128)S(1)} collective-permute-done((f32[2,2,42,16,128]{4,3,2,1,0:T(8,128)S(1)}, f32[2,2,42,16,128]{4,3,2,1,0:T(8,128)S(1)}, u32[]{:S(2)}, u32[]{:S(2)}) %collective-permute-start.43) | collective-permute-done | bytes 1376288 | tf_op jit(solution)/shard_map/ppermute | solution.py:1372
  620.0 10.7 %collective-permute-done.46 = f32[2,42,16,128]{3,2,1,0:T(8,128)S(1)} collective-permute-done((f32[2,42,16,128]{3,2,1,0:T(8,128)S(1)}, f32[2,42,16,128]{3,2,1,0:T(8,128)S(1)}, u32[]{:S(2)}, u32[]{:S(2)}) %collective-permute-start.46) | collective-permute-done | bytes 688160 | tf_op jit(solution)/shard_map/ppermute | solution.py:1372
  640.1 5.3 collective-permute-start.53
  652.8 11.5 %collective-permute-done.53 = f32[127,16,128]{2,1,0:T(8,128)S(1)} collective-permute-done((f32[127,16,128]{2,1,0:T(8,128)}, f32[127,16,128]{2,1,0:T(8,128)S(1)}, u32[]{:S(2)}, u32[]{:S(2)}) %collective-permute-start.53) | collective-permute-done | bytes 1040416 | tf_op jit(solution)/shard_map/ppermute | solution.py:1368
  664.4 30.6 %collective-permute-done.52 = f32[127,16,128]{2,1,0:T(8,128)S(1)} collective-permute-done((f32[127,16,128]{2,1,0:T(8,128)S(1)}, f32[127,16,128]{2,1,0:T(8,128)S(1)}, u32[]{:S(2)}, u32[]{:S(2)}) %collective-permute-start.52) | collective-permute-done | bytes 1040416 | tf_op jit(solution)/shard_map/ppermute | solution.py:1368
  695.5 5.1 select_reduce_fusion
  715.6 4.3 collective-permute-start.61
  719.9 3.4 collective-permute-start.62
  726.7 5.9 unpack_rows.1.total
  733.8 8.2 %update_states.1 = (f32[3747,1,128]{2,1,0:T(1,128)}, f32[3747,1,128]{2,1,0:T(1,128)}, f32[3747,1,128]{2,1,0:T(1,128)}, f32[3747,1,128]{2,1,0:T(1,128)}) custom-call(f32[1]{0:T(128)} %bitcast.105.factor_ref, f32[3760,128]{1,0:T(8,128)} %copy-done.3, f32[3747,1,128]{2,1,0:T(1,128)} %bitcast.251, f32[3747,1,128]{2,1,0:T(1,128)} %bitcast.299, ...), custom_call_target="tpu_custom_call" | custom-call | tf_op jit(solution)/shard_map/update_states/pallas_call | solution.py:324
  (234 shorter events, 125.7 us)
Async XLA Ops:
  7.2 143.9 %all-gather.5.cloned.1.call-start = ((), (), s32[]{:S(2)}) async-start(), calls=%async_computation.1 | async-start | bytes 17166336 | tf_op jit(solution)/shard_map/all_gather | solution.py:1519
  8.2 9.7 %collective-permute-start.7 = (f32[384,1,128]{2,1,0:T(1,128)S(1)}, f32[384,1,128]{2,1,0:T(1,128)S(1)}, u32[]{:S(2)}, u32[]{:S(2)}) collective-permute-start(f32[384,1,128]{2,1,0:T(1,128)S(1)} %slice_bitcast_fusion), channel_id=1, source_target_pairs={{1,0},{2,1},{3,2},{4,3},{5,4},{6,5},{7,6},{8,7},{9,8},{10,9},{11,1... | collective-permute-start | bytes 589832 | tf_op jit(solution)/shard_map/ppermute | solution.py:1508
  29.1 200.7 %all-gather.3.cloned.1.call-start = ((), (), s32[]{:S(2)}) async-start(), calls=%async_computation | async-start | bytes 8650752 | tf_op jit(solution)/shard_map/all_gather | solution.py:1473
  29.2 10.4 %collective-permute-start.10 = (bf16[64,16,128]{2,1,0:T(8,128)(2,1)S(1)}, bf16[64,16,128]{2,1,0:T(8,128)(2,1)S(1)}, u32[]{:S(2)}, u32[]{:S(2)}) collective-permute-start(bf16[64,16,128]{2,1,0:T(8,128)(2,1)S(1)} %get-tuple-element.424), channel_id=1, source_target_pairs={{0,1},{1,3},{2,5},{3,7},{4,9},{5,11},{6,13},{7,15},{16,17},{17,19}... | collective-permute-start | bytes 786440 | tf_op jit(solution)/shard_map/ppermute | solution.py:1457
  40.5 26.2 %collective-permute-start.11 = (bf16[48,16,128]{2,1,0:T(8,128)(2,1)S(1)}, bf16[48,16,128]{2,1,0:T(8,128)(2,1)S(1)}, u32[]{:S(2)}, u32[]{:S(2)}) collective-permute-start(bf16[48,16,128]{2,1,0:T(8,128)(2,1)S(1)} %slice_select_fusion), channel_id=1, source_target_pairs={{8,0},{24,16}} | collective-permute-start | bytes 589832 | tf_op jit(solution)/shard_map/ppermute | solution.py:1468
  66.7 9.4 %collective-permute-start.12 = (bf16[48,16,128]{2,1,0:T(8,128)(2,1)S(1)}, bf16[48,16,128]{2,1,0:T(8,128)(2,1)S(1)}, u32[]{:S(2)}, u32[]{:S(2)}) collective-permute-start(bf16[48,16,128]{2,1,0:T(8,128)(2,1)S(1)} %fusion.22), channel_id=1, source_target_pairs={{8,12},{0,4},{24,28},{16,20}} | collective-permute-start | bytes 589832 | tf_op jit(solution)/shard_map/ppermute | solution.py:1468
  85.5 31.5 %collective-permute-start.15 = (bf16[48,16,128]{2,1,0:T(8,128)(2,1)S(1)}, bf16[48,16,128]{2,1,0:T(8,128)(2,1)S(1)}, u32[]{:S(2)}, u32[]{:S(2)}) collective-permute-start(bf16[48,16,128]{2,1,0:T(8,128)(2,1)S(1)} %add.422), channel_id=1, source_target_pairs={{0,16},{16,0},{1,17},{17,1},{2,18},{18,2},{3,19},{19,3},{4,20},{20... | collective-permute-start | bytes 589832 | tf_op jit(solution)/shard_map/ppermute | solution.py:1470
  90.3 10.5 %collective-permute-start.2 = (f32[]{:T(128)}, f32[]{:T(128)}, u32[]{:S(2)}, u32[]{:S(2)}) collective-permute-start(f32[]{:T(128)} %add.408), channel_id=1, source_target_pairs={{0,2},{1,3},{2,0},{3,1},{4,6},{5,7},{6,4},{7,5},{8,10},{9,11},{10,... | collective-permute-start | bytes 20 | tf_op jit(solution)/shard_map/ppermute | solution.py:1418
  102.1 13.5 %collective-permute-start.5 = (f32[]{:T(128)}, f32[]{:T(128)}, u32[]{:S(2)}, u32[]{:S(2)}) collective-permute-start(f32[]{:T(128)} %add.411), channel_id=1, source_target_pairs={{0,8},{1,9},{2,10},{3,11},{4,12},{5,13},{6,14},{7,15},{8,0},{9,1},... | collective-permute-start | bytes 20 | tf_op jit(solution)/shard_map/ppermute | solution.py:1418
  107.6 8.0 %collective-permute-start.6 = (f32[]{:T(128)}, f32[]{:T(128)}, u32[]{:S(2)}, u32[]{:S(2)}) collective-permute-start(f32[]{:T(128)} %add.411), channel_id=1, source_target_pairs={{0,12},{1,13},{2,14},{3,15},{4,8},{5,9},{6,10},{7,11},{8,4},{9,5},... | collective-permute-start | bytes 20 | tf_op jit(solution)/shard_map/ppermute | solution.py:1418
  347.7 14.0 %collective-permute-start.16 = (f32[8,127,16,128]{3,2,1,0:T(8,128)}, f32[8,127,16,128]{3,2,1,0:T(8,128)}, u32[]{:S(2)}, u32[]{:S(2)}) collective-permute-start(f32[8,127,16,128]{3,2,1,0:T(8,128)} %get-tuple-element.209), channel_id=1, source_target_pairs={{0,16},{16,0},{1,17},{17,1},{2,18},{18,2},{3,19},{19,3},{4,20},{20... | collective-permute-start | bytes 24969224 | tf_op jit(solution)/shard_map/ppermute | solution.py:1364
  369.8 35.0 %collective-permute-start.20 = (f32[2,2,43,16,128]{4,3,2,1,0:T(8,128)S(1)}, f32[2,2,43,16,128]{4,3,2,1,0:T(8,128)S(1)}, u32[]{:S(2)}, u32[]{:S(2)}) collective-permute-start(f32[2,2,43,16,128]{4,3,2,1,0:T(8,128)S(1)} %add_bitcast_fusion.3), channel_id=1, source_target_pairs={{0,4},{1,5},{2,6},{3,7},{4,0},{5,1},{6,2},{7,3},{8,12},{9,13},{10,... | collective-permute-start | bytes 4227080 | tf_op jit(solution)/shard_map/ppermute | solution.py:1372
  371.3 32.3 %collective-permute-start.18 = (f32[2,2,42,16,128]{4,3,2,1,0:T(8,128)}, f32[2,2,42,16,128]{4,3,2,1,0:T(8,128)}, u32[]{:S(2)}, u32[]{:S(2)}) collective-permute-start(f32[2,2,42,16,128]{4,3,2,1,0:T(8,128)} %add_bitcast_fusion.7), channel_id=1, source_target_pairs={{0,1},{1,0},{2,3},{3,2},{4,5},{5,4},{6,7},{7,6},{8,9},{9,8},{10,11... | collective-permute-start | bytes 4128776 | tf_op jit(solution)/shard_map/ppermute | solution.py:1372
  372.7 32.0 %collective-permute-start.19 = (f32[2,2,42,16,128]{4,3,2,1,0:T(8,128)}, f32[2,2,42,16,128]{4,3,2,1,0:T(8,128)}, u32[]{:S(2)}, u32[]{:S(2)}) collective-permute-start(f32[2,2,42,16,128]{4,3,2,1,0:T(8,128)} %add_bitcast_fusion.6), channel_id=1, source_target_pairs={{0,2},{1,3},{2,0},{3,1},{4,6},{5,7},{6,4},{7,5},{8,10},{9,11},{10,... | collective-permute-start | bytes 4128776 | tf_op jit(solution)/shard_map/ppermute | solution.py:1372
  409.8 27.2 %collective-permute-start.23 = (f32[2,43,16,128]{3,2,1,0:T(8,128)S(1)}, f32[2,43,16,128]{3,2,1,0:T(8,128)S(1)}, u32[]{:S(2)}, u32[]{:S(2)}) collective-permute-start(f32[2,43,16,128]{3,2,1,0:T(8,128)S(1)} %bitcast_add_fusion.3), channel_id=1, source_target_pairs={{0,1},{1,0},{2,3},{3,2},{4,5},{5,4},{6,7},{7,6},{8,9},{9,8},{10,11... | collective-permute-start | bytes 2113544 | tf_op jit(solution)/shard_map/ppermute | solution.py:1372
  410.3 26.7 %collective-permute-start.21 = (f32[2,42,16,128]{3,2,1,0:T(8,128)}, f32[2,42,16,128]{3,2,1,0:T(8,128)}, u32[]{:S(2)}, u32[]{:S(2)}) collective-permute-start(f32[2,42,16,128]{3,2,1,0:T(8,128)} %get-tuple-element.271), channel_id=1, source_target_pairs={{0,2},{1,3},{2,0},{3,1},{4,6},{5,7},{6,4},{7,5},{8,10},{9,11},{10,... | collective-permute-start | bytes 2064392 | tf_op jit(solution)/shard_map/ppermute | solution.py:1372
  411.8 25.2 %collective-permute-start.22 = (f32[2,42,16,128]{3,2,1,0:T(8,128)}, f32[2,42,16,128]{3,2,1,0:T(8,128)}, u32[]{:S(2)}, u32[]{:S(2)}) collective-permute-start(f32[2,42,16,128]{3,2,1,0:T(8,128)} %get-tuple-element.272), channel_id=1, source_target_pairs={{0,4},{1,5},{2,6},{3,7},{4,0},{5,1},{6,2},{7,3},{8,12},{9,13},{10,... | collective-permute-start | bytes 2064392 | tf_op jit(solution)/shard_map/ppermute | solution.py:1372
  412.3 24.7 %collective-permute-start.24 = (f32[48,16,128]{2,1,0:T(8,128)S(1)}, f32[48,16,128]{2,1,0:T(8,128)S(1)}, u32[]{:S(2)}, u32[]{:S(2)}) collective-permute-start(f32[48,16,128]{2,1,0:T(8,128)S(1)} %add_bitcast_fusion.9), channel_id=1, source_target_pairs={{1,0},{3,2},{5,4},{7,6},{9,8},{11,10},{13,12},{15,14},{17,16},{19,... | collective-permute-start | bytes 1179656 | tf_op jit(solution)/shard_map/ppermute | solution.py:1368
  441.1 21.0 %collective-permute-start.29 = (f32[8,127,16,128]{3,2,1,0:T(8,128)}, f32[8,127,16,128]{3,2,1,0:T(8,128)}, u32[]{:S(2)}, u32[]{:S(2)}) collective-permute-start(f32[8,127,16,128]{3,2,1,0:T(8,128)} %get-tuple-element.310), channel_id=1, source_target_pairs={{0,16},{16,0},{1,17},{17,1},{2,18},{18,2},{3,19},{19,3},{4,20},{20... | collective-permute-start | bytes 24969224 | tf_op jit(solution)/shard_map/ppermute | solution.py:1364
  441.2 20.9 %collective-permute-start.28 = (f32[48,16,128]{2,1,0:T(8,128)S(1)}, f32[48,16,128]{2,1,0:T(8,128)S(1)}, u32[]{:S(2)}, u32[]{:S(2)}) collective-permute-start(f32[48,16,128]{2,1,0:T(8,128)S(1)} %add.446), channel_id=1, source_target_pairs={{2,0},{3,1},{6,4},{7,5},{10,8},{11,9},{14,12},{15,13},{18,16},{19,... | collective-permute-start | bytes 1179656 | tf_op jit(solution)/shard_map/ppermute | solution.py:1368
  442.5 19.6 %collective-permute-start.27 = (f32[43,16,128]{2,1,0:T(8,128)S(1)}, f32[43,16,128]{2,1,0:T(8,128)S(1)}, u32[]{:S(2)}, u32[]{:S(2)}) collective-permute-start(f32[43,16,128]{2,1,0:T(8,128)S(1)} %bitcast_add_fusion.23), channel_id=1, source_target_pairs={{0,2},{1,3},{2,0},{3,1},{4,6},{5,7},{6,4},{7,5},{8,10},{9,11},{10,... | collective-permute-start | bytes 1056776 | tf_op jit(solution)/shard_map/ppermute | solution.py:1372
  445.2 12.5 %collective-permute-start.25 = (f32[42,16,128]{2,1,0:T(8,128)S(1)}, f32[42,16,128]{2,1,0:T(8,128)}, u32[]{:S(2)}, u32[]{:S(2)}) collective-permute-start(f32[42,16,128]{2,1,0:T(8,128)S(1)} %get-tuple-element.306), channel_id=1, source_target_pairs={{0,4},{1,5},{2,6},{3,7},{4,0},{5,1},{6,2},{7,3},{8,12},{9,13},{10,... | collective-permute-start | bytes 1032200 | tf_op jit(solution)/shard_map/ppermute | solution.py:1372
  446.7 11.0 %collective-permute-start.26 = (f32[42,16,128]{2,1,0:T(8,128)S(1)}, f32[42,16,128]{2,1,0:T(8,128)}, u32[]{:S(2)}, u32[]{:S(2)}) collective-permute-start(f32[42,16,128]{2,1,0:T(8,128)S(1)} %get-tuple-element.307), channel_id=1, source_target_pairs={{0,1},{1,0},{2,3},{3,2},{4,5},{5,4},{6,7},{7,6},{8,9},{9,8},{10,11... | collective-permute-start | bytes 1032200 | tf_op jit(solution)/shard_map/ppermute | solution.py:1372
  475.7 38.8 %collective-permute-start.31 = (f32[2,2,51,16,128]{4,3,2,1,0:T(8,128)}, f32[2,2,51,16,128]{4,3,2,1,0:T(8,128)}, u32[]{:S(2)}, u32[]{:S(2)}) collective-permute-start(f32[2,2,51,16,128]{4,3,2,1,0:T(8,128)} %add_bitcast_fusion), channel_id=1, source_target_pairs={{0,2},{1,3},{2,0},{3,1},{4,6},{5,7},{6,4},{7,5},{8,10},{9,11},{10,... | collective-permute-start | bytes 5013512 | tf_op jit(solution)/shard_map/ppermute | solution.py:1372
  475.7 38.8 %collective-permute-start.30 = (f32[2,2,50,16,128]{4,3,2,1,0:T(8,128)}, f32[2,2,50,16,128]{4,3,2,1,0:T(8,128)}, u32[]{:S(2)}, u32[]{:S(2)}) collective-permute-start(f32[2,2,50,16,128]{4,3,2,1,0:T(8,128)} %add_bitcast_fusion.1), channel_id=1, source_target_pairs={{0,1},{1,0},{2,3},{3,2},{4,5},{5,4},{6,7},{7,6},{8,9},{9,8},{10,11... | collective-permute-start | bytes 4915208 | tf_op jit(solution)/shard_map/ppermute | solution.py:1372
  478.4 36.1 %collective-permute-start.32 = (f32[2,2,26,16,128]{4,3,2,1,0:T(8,128)}, f32[2,2,26,16,128]{4,3,2,1,0:T(8,128)S(1)}, u32[]{:S(2)}, u32[]{:S(2)}) collective-permute-start(f32[2,2,26,16,128]{4,3,2,1,0:T(8,128)} %add_bitcast_fusion.8), channel_id=1, source_target_pairs={{0,4},{1,5},{2,6},{3,7},{4,0},{5,1},{6,2},{7,3},{8,12},{9,13},{10,... | collective-permute-start | bytes 2555912 | tf_op jit(solution)/shard_map/ppermute | solution.py:1372
  480.0 70.1 %collective-permute-start.37 = (f32[127,16,128]{2,1,0:T(8,128)}, f32[127,16,128]{2,1,0:T(8,128)}, u32[]{:S(2)}, u32[]{:S(2)}) collective-permute-start(f32[127,16,128]{2,1,0:T(8,128)} %pad_maximum_fusion), channel_id=1, source_target_pairs={{8,0},{9,1},{10,2},{11,3},{12,4},{13,5},{14,6},{15,7},{24,16},{25,... | collective-permute-start | bytes 3121160 | tf_op jit(solution)/shard_map/ppermute | solution.py:1368
  521.9 33.9 %collective-permute-start.35 = (f32[2,51,16,128]{3,2,1,0:T(8,128)}, f32[2,51,16,128]{3,2,1,0:T(8,128)S(1)}, u32[]{:S(2)}, u32[]{:S(2)}) collective-permute-start(f32[2,51,16,128]{3,2,1,0:T(8,128)} %bitcast_add_fusion), channel_id=1, source_target_pairs={{0,4},{1,5},{2,6},{3,7},{4,0},{5,1},{6,2},{7,3},{8,12},{9,13},{10,... | collective-permute-start | bytes 2506760 | tf_op jit(solution)/shard_map/ppermute | solution.py:1372
  523.3 32.5 %collective-permute-start.34 = (f32[2,50,16,128]{3,2,1,0:T(8,128)}, f32[2,50,16,128]{3,2,1,0:T(8,128)}, u32[]{:S(2)}, u32[]{:S(2)}) collective-permute-start(f32[2,50,16,128]{3,2,1,0:T(8,128)} %bitcast_add_fusion.1), channel_id=1, source_target_pairs={{0,2},{1,3},{2,0},{3,1},{4,6},{5,7},{6,4},{7,5},{8,10},{9,11},{10,... | collective-permute-start | bytes 2457608 | tf_op jit(solution)/shard_map/ppermute | solution.py:1372
  525.1 30.8 %collective-permute-start.36 = (f32[2,26,16,128]{3,2,1,0:T(8,128)}, f32[2,26,16,128]{3,2,1,0:T(8,128)S(1)}, u32[]{:S(2)}, u32[]{:S(2)}) collective-permute-start(f32[2,26,16,128]{3,2,1,0:T(8,128)} %bitcast_add_fusion.8), channel_id=1, source_target_pairs={{0,1},{1,0},{2,3},{3,2},{4,5},{5,4},{6,7},{7,6},{8,9},{9,8},{10,11... | collective-permute-start | bytes 1277960 | tf_op jit(solution)/shard_map/ppermute | solution.py:1372
  526.8 29.0 %collective-permute-start.33 = (f32[48,16,128]{2,1,0:T(8,128)S(1)}, f32[48,16,128]{2,1,0:T(8,128)}, u32[]{:S(2)}, u32[]{:S(2)}) collective-permute-start(f32[48,16,128]{2,1,0:T(8,128)S(1)} %add.459), channel_id=1, source_target_pairs={{4,0},{5,1},{6,2},{7,3},{12,8},{13,9},{14,10},{15,11},{20,16},{21,... | collective-permute-start | bytes 1179656 | tf_op jit(solution)/shard_map/ppermute | solution.py:1368
  561.3 17.4 %collective-permute-start.38 = (f32[8,127,16,128]{3,2,1,0:T(8,128)}, f32[8,127,16,128]{3,2,1,0:T(8,128)S(1)}, u32[]{:S(2)}, u32[]{:S(2)}) collective-permute-start(f32[8,127,16,128]{3,2,1,0:T(8,128)} %get-tuple-element.377), channel_id=1, source_target_pairs={{0,16},{16,0},{1,17},{17,1},{2,18},{18,2},{3,19},{19,3},{4,20},{20... | collective-permute-start | bytes 24969224 | tf_op jit(solution)/shard_map/ppermute | solution.py:1364
  563.2 11.5 %collective-permute-start.39 = (f32[50,16,128]{2,1,0:T(8,128)S(1)}, f32[50,16,128]{2,1,0:T(8,128)S(1)}, u32[]{:S(2)}, u32[]{:S(2)}) collective-permute-start(f32[50,16,128]{2,1,0:T(8,128)S(1)} %bitcast_add_fusion.15), channel_id=1, source_target_pairs={{0,4},{1,5},{2,6},{3,7},{4,0},{5,1},{6,2},{7,3},{8,12},{9,13},{10,... | collective-permute-start | bytes 1228808 | tf_op jit(solution)/shard_map/ppermute | solution.py:1372
  563.2 13.0 %collective-permute-start.40 = (f32[51,16,128]{2,1,0:T(8,128)S(1)}, f32[51,16,128]{2,1,0:T(8,128)S(1)}, u32[]{:S(2)}, u32[]{:S(2)}) collective-permute-start(f32[51,16,128]{2,1,0:T(8,128)S(1)} %bitcast_add_fusion.11), channel_id=1, source_target_pairs={{0,1},{1,0},{2,3},{3,2},{4,5},{5,4},{6,7},{7,6},{8,9},{9,8},{10,11... | collective-permute-start | bytes 1253384 | tf_op jit(solution)/shard_map/ppermute | solution.py:1372
  563.4 17.6 %collective-permute-start.42 = (f32[48,16,128]{2,1,0:T(8,128)S(1)}, f32[48,16,128]{2,1,0:T(8,128)S(1)}, u32[]{:S(2)}, u32[]{:S(2)}) collective-permute-start(f32[48,16,128]{2,1,0:T(8,128)S(1)} %add.490), channel_id=1, source_target_pairs={{0,8},{1,9},{2,10},{3,11},{4,12},{5,13},{6,14},{7,15},{16,24},{17,... | collective-permute-start | bytes 1179656 | tf_op jit(solution)/shard_map/ppermute | solution.py:1368
  581.0 31.7 %collective-permute-start.43 = (f32[2,2,42,16,128]{4,3,2,1,0:T(8,128)S(1)}, f32[2,2,42,16,128]{4,3,2,1,0:T(8,128)S(1)}, u32[]{:S(2)}, u32[]{:S(2)}) collective-permute-start(f32[2,2,42,16,128]{4,3,2,1,0:T(8,128)S(1)} %add_bitcast_fusion.5), channel_id=1, source_target_pairs={{0,1},{1,0},{2,3},{3,2},{4,5},{5,4},{6,7},{7,6},{8,9},{9,8},{10,11... | collective-permute-start | bytes 4128776 | tf_op jit(solution)/shard_map/ppermute | solution.py:1372
  582.1 31.4 %collective-permute-start.44 = (f32[2,2,42,16,128]{4,3,2,1,0:T(8,128)S(1)}, f32[2,2,42,16,128]{4,3,2,1,0:T(8,128)S(1)}, u32[]{:S(2)}, u32[]{:S(2)}) collective-permute-start(f32[2,2,42,16,128]{4,3,2,1,0:T(8,128)S(1)} %add_bitcast_fusion.4), channel_id=1, source_target_pairs={{0,2},{1,3},{2,0},{3,1},{4,6},{5,7},{6,4},{7,5},{8,10},{9,11},{10,... | collective-permute-start | bytes 4128776 | tf_op jit(solution)/shard_map/ppermute | solution.py:1372
  582.4 32.9 %collective-permute-start.45 = (f32[2,2,43,16,128]{4,3,2,1,0:T(8,128)S(1)}, f32[2,2,43,16,128]{4,3,2,1,0:T(8,128)S(1)}, u32[]{:S(2)}, u32[]{:S(2)}) collective-permute-start(f32[2,2,43,16,128]{4,3,2,1,0:T(8,128)S(1)} %add_bitcast_fusion.2), channel_id=1, source_target_pairs={{0,4},{1,5},{2,6},{3,7},{4,0},{5,1},{6,2},{7,3},{8,12},{9,13},{10,... | collective-permute-start | bytes 4227080 | tf_op jit(solution)/shard_map/ppermute | solution.py:1372
  615.4 15.3 %collective-permute-start.46 = (f32[2,42,16,128]{3,2,1,0:T(8,128)S(1)}, f32[2,42,16,128]{3,2,1,0:T(8,128)S(1)}, u32[]{:S(2)}, u32[]{:S(2)}) collective-permute-start(f32[2,42,16,128]{3,2,1,0:T(8,128)S(1)} %get-tuple-element.385), channel_id=1, source_target_pairs={{0,2},{1,3},{2,0},{3,1},{4,6},{5,7},{6,4},{7,5},{8,10},{9,11},{10,... | collective-permute-start | bytes 2064392 | tf_op jit(solution)/shard_map/ppermute | solution.py:1372
  617.2 14.9 %collective-permute-start.47 = (f32[2,42,16,128]{3,2,1,0:T(8,128)S(1)}, f32[2,42,16,128]{3,2,1,0:T(8,128)S(1)}, u32[]{:S(2)}, u32[]{:S(2)}) collective-permute-start(f32[2,42,16,128]{3,2,1,0:T(8,128)S(1)} %get-tuple-element.386), channel_id=1, source_target_pairs={{0,4},{1,5},{2,6},{3,7},{4,0},{5,1},{6,2},{7,3},{8,12},{9,13},{10,... | collective-permute-start | bytes 2064392 | tf_op jit(solution)/shard_map/ppermute | solution.py:1372
  619.0 14.7 %collective-permute-start.48 = (f32[2,43,16,128]{3,2,1,0:T(8,128)S(1)}, f32[2,43,16,128]{3,2,1,0:T(8,128)S(1)}, u32[]{:S(2)}, u32[]{:S(2)}) collective-permute-start(f32[2,43,16,128]{3,2,1,0:T(8,128)S(1)} %bitcast_add_fusion.2), channel_id=1, source_target_pairs={{0,1},{1,0},{2,3},{3,2},{4,5},{5,4},{6,7},{7,6},{8,9},{9,8},{10,11... | collective-permute-start | bytes 2113544 | tf_op jit(solution)/shard_map/ppermute | solution.py:1372
  634.7 10.8 %collective-permute-start.49 = (f32[42,16,128]{2,1,0:T(8,128)}, f32[42,16,128]{2,1,0:T(8,128)}, u32[]{:S(2)}, u32[]{:S(2)}) collective-permute-start(f32[42,16,128]{2,1,0:T(8,128)} %get-tuple-element.388), channel_id=1, source_target_pairs={{0,4},{1,5},{2,6},{3,7},{4,0},{5,1},{6,2},{7,3},{8,12},{9,13},{10,... | collective-permute-start | bytes 1032200 | tf_op jit(solution)/shard_map/ppermute | solution.py:1372
  635.9 9.6 %collective-permute-start.50 = (f32[42,16,128]{2,1,0:T(8,128)}, f32[42,16,128]{2,1,0:T(8,128)}, u32[]{:S(2)}, u32[]{:S(2)}) collective-permute-start(f32[42,16,128]{2,1,0:T(8,128)} %get-tuple-element.389), channel_id=1, source_target_pairs={{0,1},{1,0},{2,3},{3,2},{4,5},{5,4},{6,7},{7,6},{8,9},{9,8},{10,11... | collective-permute-start | bytes 1032200 | tf_op jit(solution)/shard_map/ppermute | solution.py:1372
  639.6 8.0 %collective-permute-start.51 = (f32[43,16,128]{2,1,0:T(8,128)}, f32[43,16,128]{2,1,0:T(8,128)S(1)}, u32[]{:S(2)}, u32[]{:S(2)}) collective-permute-start(f32[43,16,128]{2,1,0:T(8,128)} %bitcast_add_fusion.19), channel_id=1, source_target_pairs={{0,2},{1,3},{2,0},{3,1},{4,6},{5,7},{6,4},{7,5},{8,10},{9,11},{10,... | collective-permute-start | bytes 1056776 | tf_op jit(solution)/shard_map/ppermute | solution.py:1372
  640.1 24.1 %collective-permute-start.53 = (f32[127,16,128]{2,1,0:T(8,128)}, f32[127,16,128]{2,1,0:T(8,128)S(1)}, u32[]{:S(2)}, u32[]{:S(2)}) collective-permute-start(f32[127,16,128]{2,1,0:T(8,128)} %pad_maximum_fusion.1), channel_id=1, source_target_pairs={{0,8},{1,9},{2,10},{3,11},{4,12},{5,13},{6,14},{7,15},{16,24},{17,... | collective-permute-start | bytes 3121160 | tf_op jit(solution)/shard_map/ppermute | solution.py:1368
  649.1 45.9 %collective-permute-start.52 = (f32[127,16,128]{2,1,0:T(8,128)S(1)}, f32[127,16,128]{2,1,0:T(8,128)S(1)}, u32[]{:S(2)}, u32[]{:S(2)}) collective-permute-start(f32[127,16,128]{2,1,0:T(8,128)S(1)} %pad_maximum_fusion.2), channel_id=1, source_target_pairs={{8,0},{9,1},{10,2},{11,3},{12,4},{13,5},{14,6},{15,7},{24,16},{25,... | collective-permute-start | bytes 3121160 | tf_op jit(solution)/shard_map/ppermute | solution.py:1368
  700.5 8.8 %collective-permute-start.55 = (f32[127,16,128]{2,1,0:T(8,128)}, f32[127,16,128]{2,1,0:T(8,128)S(1)}, u32[]{:S(2)}, u32[]{:S(2)}) collective-permute-start(f32[127,16,128]{2,1,0:T(8,128)} %get-tuple-element.417), channel_id=1, source_target_pairs={{0,16},{16,0},{1,17},{17,1},{2,18},{18,2},{3,19},{19,3},{4,20},{20... | collective-permute-start | bytes 3121160 | tf_op jit(solution)/shard_map/ppermute | solution.py:1590
  715.5 7.9 %collective-permute-start.60 = (f32[2]{0:T(128)S(1)}, f32[2]{0:T(128)S(1)}, u32[]{:S(2)}, u32[]{:S(2)}) collective-permute-start(f32[2]{0:T(128)S(1)} %add_add_fusion.2), channel_id=1, source_target_pairs={{0,8},{1,9},{2,10},{3,11},{4,12},{5,13},{6,14},{7,15},{8,0},{9,1},... | collective-permute-start | bytes 32 | tf_op jit(solution)/shard_map/ppermute | solution.py:1418
  (45 other events, 513.3 us)
Sparse Core Ops, SparseCore 0:
  29.2 121.8 all-gather.4
  154.0 75.7 all-gather.2

commit v7 on v6

--- a/solution.py
+++ b/solution.py
@@ -532,7 +532,7 @@
         grad_mixed[here, place(2)] = grad_values.astype(BF16)
         return carry
 
-    lax.fori_loop(0, images * panels, body, 0, unroll=3)
+    lax.fori_loop(0, images * panels, body, 0, unroll=4)
 
 
 def gelu_parts(value):
@@ -1568,7 +1568,7 @@
         kept = iter(kept)
         arrive(flows, [g if is_long else next(kept) for g, is_long in zip(got, long)])
         if number == 1:
-            high = Flow(dp, blocks[2], blocks[3], dp // 2, (4, 4, 2))
+            high = Flow(dp, blocks[2], blocks[3], dp // 2, (5, 5, 2))
             blocks = blocks[:2]
     low = Flow(dp, blocks[0], blocks[1], 0)
     every = [main, rest, high, low]

time: 756 us -> 757 us (level)
  transfers between devices with their start and end apart: 65 -> 65, of which waited for: 31 -> 33; matrix products, arithmetic and copies ran while one was open for 5% -> 5% of each run, Pallas kernels for 19% -> 19%
where the time goes in v7:
time: 757 us; the launch traced here: 753 us
  Pallas kernels  283 us (37%)
  waiting for transfers between devices  262 us (35%)
  starting transfers between devices  95.1 us (13%)
  other arithmetic  69.4 us (9%)
  between operations  27 us (4%)
  local copies, waits for them, and re-layouts  16.8 us (2%)
    pallas_call x1, Pallas kernels, decoder(): pl.pallas_call(lambda *refs: decoder_kernel(plan, sh, refs), out_shape=[*...  118 us
    pallas_call x5, Pallas kernels, __call__(): pl.pallas_call(functools.partial(self.kernel, len(blocks)), out_shape=[*t...  107 us
    ppermute x27, waiting for transfers between devices, send(): lax.ppermute(value, 'dp', [(i, i ^ flip) for i in range(self.dp)])  65.7 us
    add x43, other arithmetic, total_of(): total = total + term  55.6 us
    ppermute x7, waiting for transfers between devices, send(): return [lax.ppermute(payload[0], 'dp', pairs)]  50.5 us
    all_gather x1, waiting for transfers between devices, gather_decoder(): gathered = lax.all_gather(spread, ('section', 'dp'), axis=0, tiled=True)  41.1 us
    pallas_call x1, Pallas kernels, encoder(): pl.pallas_call(lambda *refs: encoder_kernel(plan, sh, refs), out_shape=[j...  37.6 us
    ppermute x27, starting transfers between devices, send(): lax.ppermute(value, 'dp', [(i, i ^ flip) for i in range(self.dp)])  36.7 us
  transfers between devices with their start and end apart: 65, of which 33 were waited for; matrix products, arithmetic and copies ran while one was open for 5% of the time, Pallas kernels for 19%

profile of v7, /device:TPU:0, one launch (start us, length us, event | category | flops | bytes accessed | tf_op | source)
XLA Modules:
  0.0 752.7 jit_solution(17495144290283824684)
XLA Ops:
  10.4 7.5 collective-permute-done.7.following
  19.4 6.8 pack_rows.1
  29.2 4.6 collective-permute-start.10
  34.5 5.1 collective-permute-done.10
  41.8 24.9 %collective-permute-done.11 = bf16[48,16,128]{2,1,0:T(8,128)(2,1)S(1)} collective-permute-done((bf16[48,16,128]{2,1,0:T(8,128)(2,1)S(1)}, bf16[48,16,128]{2,1,0:T(8,128)(2,1)S(1)}, u32[]{:S(2)}, u32[]{:S(2)}) %collective-permute-start.11) | collective-permute-done | bytes 196640 | tf_op jit(solution)/shard_map/ppermute | solution.py:1468
  68.0 8.1 %collective-permute-done.12 = bf16[48,16,128]{2,1,0:T(8,128)(2,1)S(1)} collective-permute-done((bf16[48,16,128]{2,1,0:T(8,128)(2,1)S(1)}, bf16[48,16,128]{2,1,0:T(8,128)(2,1)S(1)}, u32[]{:S(2)}, u32[]{:S(2)}) %collective-permute-start.12) | collective-permute-done | bytes 196640 | tf_op jit(solution)/shard_map/ppermute | solution.py:1468
  77.4 3.2 collective-permute-done.13
  90.3 3.8 collective-permute-start.2
  102.1 5.5 collective-permute-start.5
  107.6 3.8 collective-permute-start.6
  117.8 33.5 %all-gather.5.cloned.1.call-done = bf16[4064,16,128]{2,1,0:T(8,128)(2,1)} async-done(((bf16[127,16,128]{2,1,0:T(8,128)(2,1)}), bf16[4064,16,128]{2,1,0:T(8,128)(2,1)}) %all-gather.5.cloned.1.call-update) | async-done | bytes 16646160 | tf_op jit(solution)/shard_map/all_gather | solution.py:1519
  151.3 37.6 %encoder_forward.1 = (bf16[6,208,768]{2,1,0:T(8,128)(2,1)}, f32[672,768]{1,0:T(8,128)}, bf16[672,768]{1,0:T(8,128)(2,1)}, bf16[672,2304]{1,0:T(8,128)(2,1)}, bf1...) custom-call(s32[7]{0:T(128)} %pad_add_fusion.refs_0_, ...), custom_call_target="tpu_custom_call" | custom-call | flops 10000000000 | bytes 1048576 | tf_op jit(solution)/shard_map/encoder_forward/pallas_call | solution.py:914
  188.9 41.1 %all-gather.3.cloned.1.call-done = bf16[2048,16,128]{2,1,0:T(8,128)(2,1)} async-done(((bf16[64,16,128]{2,1,0:T(8,128)(2,1)}), bf16[2048,16,128]{2,1,0:T(8,128)(2,1)}) %all-gather.3.cloned.1.call-update) | async-done | bytes 8388624 | tf_op jit(solution)/shard_map/all_gather | solution.py:1473
  230.0 117.5 %decoder_both.1 = (f32[8,127,16,128]{3,2,1,0:T(8,128)}, f32[8,127,16,128]{3,2,1,0:T(8,128)}, f32[1,48,16,128]{3,2,1,0:T(8,128)}, f32[1,48,16,128]{3,2,1,0:T(8,12...) custom-call(s32[7]{0:T(128)} %pad_add_fusion.refs_0_, f32[1]{0:T(128)} %bitcast.3.refs_1_, ...), custom_call_target="tpu_custom_call" | custom-call | flops 32000000000 | bytes 1048576 | tf_op jit(solution)/shard_map/decoder_both/pallas_call | solution.py:1070
  348.1 4.7 collective-permute-done.17
  352.8 8.7 %collective-permute-done.16 = f32[8,127,16,128]{3,2,1,0:T(8,128)} collective-permute-done((f32[8,127,16,128]{3,2,1,0:T(8,128)}, f32[8,127,16,128]{3,2,1,0:T(8,128)}, u32[]{:S(2)}, u32[]{:S(2)}) %collective-permute-start.16) | collective-permute-done | bytes 8323104 | tf_op jit(solution)/shard_map/ppermute | solution.py:1364
  363.5 3.0 add_bitcast_fusion.6
  366.5 3.1 add_bitcast_fusion.7
  374.2 28.9 %encoder_back_fc2.1 = (f32[8,127,16,128]{3,2,1,0:T(8,128)}, f32[8,127,16,128]{3,2,1,0:T(8,128)}, f32[8,127,16,128]{3,2,1,0:T(8,128)}, f32[8,127,16,128]{3,2,1,0:...) custom-call(s32[7]{0:T(128)} %pad_add_fusion.refs_0_, bf16[2,16,127,16,128]{4,3,2,1,0:T(8,128)(2,1)} %bitcast.255, ...), custom_call_target="tpu_custom_call" | custom-call | flops 5000000000 | bytes 1048576 | tf_op jit(solution)/shard_map/encoder_back_fc2/pallas_call | solution.py:1189
  406.1 3.5 bitcast_add_fusion.6
  413.4 23.3 %encoder_back_fc1.1 = (f32[8,127,16,128]{3,2,1,0:T(8,128)}, f32[8,127,16,128]{3,2,1,0:T(8,128)}, f32[8,127,16,128]{3,2,1,0:T(8,128)}, f32[8,127,16,128]{3,2,1,0:T(8,128)}, f32[672,768]{1,0:T(8,128)}) custom-call(s32[7]{0:T(128)} %pad_add_fusion.refs_0_, ...), custom_call_target="tpu_custom_call", output_to_operand_aliasing={{0}: (6, {}), {1}: (7, {}), {2}: (8, {}), {3}: (9, {})} | custom-call | flops 4000000000 | bytes 1048576 | tf_op jit(solution)/shard_map/encoder_back_fc1/pallas_call | solution.py:1189
  443.0 2.7 collective-permute-start.27
  447.2 2.7 collective-permute-start.26
  449.9 8.2 %encoder_back_proj.1 = (f32[8,127,16,128]{3,2,1,0:T(8,128)}, f32[8,127,16,128]{3,2,1,0:T(8,128)}, bf16[672,768]{1,0:T(8,128)(2,1)}) custom-call(s32[7]{0:T(128)} %pad_add_fusion.refs_0_, bf16[2,16,127,16,128]{4,3,2,1,0:T(8,128)(2,1)} %bitcast.257, f32[672,768]{1,0:T(8,128)} %get-tuple-element.363.refs_2_, ...), custom_call_target="tpu_custom_call", output_to_operand_aliasing={{0}: (4, {}), {1}: (5, {})} | custom-call | flops 2000000000 | bytes 1048576 | tf_op jit(solution)/shard_map/encoder_back_proj/pallas_call | solution.py:1189
  458.1 4.5 collective-permute-done.27
  464.9 3.4 add_bitcast_fusion
  468.3 3.4 add_bitcast_fusion.1
  476.1 2.7 collective-permute-start.30
  481.7 24.2 %encoder_back_attention.1.refs_3_ = bf16[672,2304]{1,0:T(8,128)(2,1)} custom-call(s32[7]{0:T(128)} %pad_add_fusion.refs_0_, bf16[2,16,127,16,128]{4,3,2,1,0:T(8,128)(2,1)} %bitcast.258, bf16[672,768]{1,0:T(8,128)(2,1)} %get-tuple-element.339.refs_2_, bf16[672,2304]{1,0:T(8,128)(2,1)} %get-tuple-element.340.refs_3_), custom_call_target="tpu_custom_call" | custom-call | flops 5000000000 | bytes 1048576 | tf_op jit(solution)/shard_map/encoder_back_attention/pallas_call | solution.py:1189
  505.9 3.3 collective-permute-done.32
  509.2 6.9 collective-permute-done.30
  516.2 2.7 bitcast_add_fusion.1
  520.8 2.8 bitcast_add_fusion
  529.9 22.1 %encoder_back_qkv.1 = (f32[8,127,16,128]{3,2,1,0:T(8,128)}, f32[8,127,16,128]{3,2,1,0:T(8,128)}) custom-call(s32[7]{0:T(128)} %pad_add_fusion.refs_0_, bf16[2,16,127,16,128]{4,3,2,1,0:T(8,128)(2,1)} %bitcast.259, f32[672,768]{1,0:T(8,128)} %get-tuple-element.363.refs_2_, ...), custom_call_target="tpu_custom_call", output_to_operand_aliasing={{0}: (7, {}), {1}: (8, {})} | custom-call | flops 5000000000 | bytes 1048576 | tf_op jit(solution)/shard_map/encoder_back_qkv/pallas_call | solution.py:1189
  552.0 4.8 collective-permute-done.33
  566.0 3.5 collective-permute-done.41
  570.8 4.0 collective-permute-done.39
  584.1 2.8 collective-permute-start.45
  586.9 26.1 %collective-permute-done.43 = f32[2,2,42,16,128]{4,3,2,1,0:T(8,128)S(1)} collective-permute-done((f32[2,2,42,16,128]{4,3,2,1,0:T(8,128)S(1)}, f32[2,2,42,16,128]{4,3,2,1,0:T(8,128)S(1)}, u32[]{:S(2)}, u32[]{:S(2)}) %collective-permute-start.43) | collective-permute-done | bytes 1376288 | tf_op jit(solution)/shard_map/ppermute | solution.py:1372
  621.2 10.7 %collective-permute-done.46 = f32[2,42,16,128]{3,2,1,0:T(8,128)S(1)} collective-permute-done((f32[2,42,16,128]{3,2,1,0:T(8,128)S(1)}, f32[2,42,16,128]{3,2,1,0:T(8,128)S(1)}, u32[]{:S(2)}, u32[]{:S(2)}) %collective-permute-start.46) | collective-permute-done | bytes 688160 | tf_op jit(solution)/shard_map/ppermute | solution.py:1372
  641.3 5.3 collective-permute-start.53
  652.0 13.4 %collective-permute-done.53 = f32[127,16,128]{2,1,0:T(8,128)S(1)} collective-permute-done((f32[127,16,128]{2,1,0:T(8,128)}, f32[127,16,128]{2,1,0:T(8,128)S(1)}, u32[]{:S(2)}, u32[]{:S(2)}) %collective-permute-start.53) | collective-permute-done | bytes 1040416 | tf_op jit(solution)/shard_map/ppermute | solution.py:1368
  665.6 30.7 %collective-permute-done.52 = f32[127,16,128]{2,1,0:T(8,128)S(1)} collective-permute-done((f32[127,16,128]{2,1,0:T(8,128)S(1)}, f32[127,16,128]{2,1,0:T(8,128)S(1)}, u32[]{:S(2)}, u32[]{:S(2)}) %collective-permute-start.52) | collective-permute-done | bytes 1040416 | tf_op jit(solution)/shard_map/ppermute | solution.py:1368
  696.7 5.0 select_reduce_fusion
  716.7 4.3 collective-permute-start.61
  721.0 3.4 collective-permute-start.62
  727.8 5.9 unpack_rows.1.total
  734.9 8.2 %update_states.1 = (f32[3747,1,128]{2,1,0:T(1,128)}, f32[3747,1,128]{2,1,0:T(1,128)}, f32[3747,1,128]{2,1,0:T(1,128)}, f32[3747,1,128]{2,1,0:T(1,128)}) custom-call(f32[1]{0:T(128)} %bitcast.105.factor_ref, f32[3760,128]{1,0:T(8,128)} %copy-done.3, f32[3747,1,128]{2,1,0:T(1,128)} %bitcast.251, f32[3747,1,128]{2,1,0:T(1,128)} %bitcast.299, ...), custom_call_target="tpu_custom_call" | custom-call | tf_op jit(solution)/shard_map/update_states/pallas_call | solution.py:324
  (242 shorter events, 129.7 us)
Async XLA Ops:
  7.2 144.1 %all-gather.5.cloned.1.call-start = ((), (), s32[]{:S(2)}) async-start(), calls=%async_computation.1 | async-start | bytes 17166336 | tf_op jit(solution)/shard_map/all_gather | solution.py:1519
  8.2 9.7 %collective-permute-start.7 = (f32[384,1,128]{2,1,0:T(1,128)S(1)}, f32[384,1,128]{2,1,0:T(1,128)S(1)}, u32[]{:S(2)}, u32[]{:S(2)}) collective-permute-start(f32[384,1,128]{2,1,0:T(1,128)S(1)} %slice_bitcast_fusion), channel_id=1, source_target_pairs={{1,0},{2,1},{3,2},{4,3},{5,4},{6,5},{7,6},{8,7},{9,8},{10,9},{11,1... | collective-permute-start | bytes 589832 | tf_op jit(solution)/shard_map/ppermute | solution.py:1508
  29.1 200.9 %all-gather.3.cloned.1.call-start = ((), (), s32[]{:S(2)}) async-start(), calls=%async_computation | async-start | bytes 8650752 | tf_op jit(solution)/shard_map/all_gather | solution.py:1473
  29.2 10.4 %collective-permute-start.10 = (bf16[64,16,128]{2,1,0:T(8,128)(2,1)S(1)}, bf16[64,16,128]{2,1,0:T(8,128)(2,1)S(1)}, u32[]{:S(2)}, u32[]{:S(2)}) collective-permute-start(bf16[64,16,128]{2,1,0:T(8,128)(2,1)S(1)} %get-tuple-element.424), channel_id=1, source_target_pairs={{0,1},{1,3},{2,5},{3,7},{4,9},{5,11},{6,13},{7,15},{16,17},{17,19}... | collective-permute-start | bytes 786440 | tf_op jit(solution)/shard_map/ppermute | solution.py:1457
  40.5 26.2 %collective-permute-start.11 = (bf16[48,16,128]{2,1,0:T(8,128)(2,1)S(1)}, bf16[48,16,128]{2,1,0:T(8,128)(2,1)S(1)}, u32[]{:S(2)}, u32[]{:S(2)}) collective-permute-start(bf16[48,16,128]{2,1,0:T(8,128)(2,1)S(1)} %slice_select_fusion), channel_id=1, source_target_pairs={{8,0},{24,16}} | collective-permute-start | bytes 589832 | tf_op jit(solution)/shard_map/ppermute | solution.py:1468
  66.7 9.4 %collective-permute-start.12 = (bf16[48,16,128]{2,1,0:T(8,128)(2,1)S(1)}, bf16[48,16,128]{2,1,0:T(8,128)(2,1)S(1)}, u32[]{:S(2)}, u32[]{:S(2)}) collective-permute-start(bf16[48,16,128]{2,1,0:T(8,128)(2,1)S(1)} %fusion.22), channel_id=1, source_target_pairs={{8,12},{0,4},{24,28},{16,20}} | collective-permute-start | bytes 589832 | tf_op jit(solution)/shard_map/ppermute | solution.py:1468
  85.4 31.6 %collective-permute-start.15 = (bf16[48,16,128]{2,1,0:T(8,128)(2,1)S(1)}, bf16[48,16,128]{2,1,0:T(8,128)(2,1)S(1)}, u32[]{:S(2)}, u32[]{:S(2)}) collective-permute-start(bf16[48,16,128]{2,1,0:T(8,128)(2,1)S(1)} %add.422), channel_id=1, source_target_pairs={{0,16},{16,0},{1,17},{17,1},{2,18},{18,2},{3,19},{19,3},{4,20},{20... | collective-permute-start | bytes 589832 | tf_op jit(solution)/shard_map/ppermute | solution.py:1470
  90.3 10.5 %collective-permute-start.2 = (f32[]{:T(128)}, f32[]{:T(128)}, u32[]{:S(2)}, u32[]{:S(2)}) collective-permute-start(f32[]{:T(128)} %add.408), channel_id=1, source_target_pairs={{0,2},{1,3},{2,0},{3,1},{4,6},{5,7},{6,4},{7,5},{8,10},{9,11},{10,... | collective-permute-start | bytes 20 | tf_op jit(solution)/shard_map/ppermute | solution.py:1418
  102.1 13.5 %collective-permute-start.5 = (f32[]{:T(128)}, f32[]{:T(128)}, u32[]{:S(2)}, u32[]{:S(2)}) collective-permute-start(f32[]{:T(128)} %add.411), channel_id=1, source_target_pairs={{0,8},{1,9},{2,10},{3,11},{4,12},{5,13},{6,14},{7,15},{8,0},{9,1},... | collective-permute-start | bytes 20 | tf_op jit(solution)/shard_map/ppermute | solution.py:1418
  107.6 8.0 %collective-permute-start.6 = (f32[]{:T(128)}, f32[]{:T(128)}, u32[]{:S(2)}, u32[]{:S(2)}) collective-permute-start(f32[]{:T(128)} %add.411), channel_id=1, source_target_pairs={{0,12},{1,13},{2,14},{3,15},{4,8},{5,9},{6,10},{7,11},{8,4},{9,5},... | collective-permute-start | bytes 20 | tf_op jit(solution)/shard_map/ppermute | solution.py:1418
  347.5 14.0 %collective-permute-start.16 = (f32[8,127,16,128]{3,2,1,0:T(8,128)}, f32[8,127,16,128]{3,2,1,0:T(8,128)}, u32[]{:S(2)}, u32[]{:S(2)}) collective-permute-start(f32[8,127,16,128]{3,2,1,0:T(8,128)} %get-tuple-element.209), channel_id=1, source_target_pairs={{0,16},{16,0},{1,17},{17,1},{2,18},{18,2},{3,19},{19,3},{4,20},{20... | collective-permute-start | bytes 24969224 | tf_op jit(solution)/shard_map/ppermute | solution.py:1364
  369.6 35.0 %collective-permute-start.20 = (f32[2,2,43,16,128]{4,3,2,1,0:T(8,128)S(1)}, f32[2,2,43,16,128]{4,3,2,1,0:T(8,128)S(1)}, u32[]{:S(2)}, u32[]{:S(2)}) collective-permute-start(f32[2,2,43,16,128]{4,3,2,1,0:T(8,128)S(1)} %add_bitcast_fusion.3), channel_id=1, source_target_pairs={{0,4},{1,5},{2,6},{3,7},{4,0},{5,1},{6,2},{7,3},{8,12},{9,13},{10,... | collective-permute-start | bytes 4227080 | tf_op jit(solution)/shard_map/ppermute | solution.py:1372
  371.1 32.3 %collective-permute-start.18 = (f32[2,2,42,16,128]{4,3,2,1,0:T(8,128)}, f32[2,2,42,16,128]{4,3,2,1,0:T(8,128)}, u32[]{:S(2)}, u32[]{:S(2)}) collective-permute-start(f32[2,2,42,16,128]{4,3,2,1,0:T(8,128)} %add_bitcast_fusion.7), channel_id=1, source_target_pairs={{0,1},{1,0},{2,3},{3,2},{4,5},{5,4},{6,7},{7,6},{8,9},{9,8},{10,11... | collective-permute-start | bytes 4128776 | tf_op jit(solution)/shard_map/ppermute | solution.py:1372
  372.5 32.1 %collective-permute-start.19 = (f32[2,2,42,16,128]{4,3,2,1,0:T(8,128)}, f32[2,2,42,16,128]{4,3,2,1,0:T(8,128)}, u32[]{:S(2)}, u32[]{:S(2)}) collective-permute-start(f32[2,2,42,16,128]{4,3,2,1,0:T(8,128)} %add_bitcast_fusion.6), channel_id=1, source_target_pairs={{0,2},{1,3},{2,0},{3,1},{4,6},{5,7},{6,4},{7,5},{8,10},{9,11},{10,... | collective-permute-start | bytes 4128776 | tf_op jit(solution)/shard_map/ppermute | solution.py:1372
  409.6 27.2 %collective-permute-start.23 = (f32[2,43,16,128]{3,2,1,0:T(8,128)S(1)}, f32[2,43,16,128]{3,2,1,0:T(8,128)S(1)}, u32[]{:S(2)}, u32[]{:S(2)}) collective-permute-start(f32[2,43,16,128]{3,2,1,0:T(8,128)S(1)} %bitcast_add_fusion.3), channel_id=1, source_target_pairs={{0,1},{1,0},{2,3},{3,2},{4,5},{5,4},{6,7},{7,6},{8,9},{9,8},{10,11... | collective-permute-start | bytes 2113544 | tf_op jit(solution)/shard_map/ppermute | solution.py:1372
  410.2 26.6 %collective-permute-start.21 = (f32[2,42,16,128]{3,2,1,0:T(8,128)}, f32[2,42,16,128]{3,2,1,0:T(8,128)}, u32[]{:S(2)}, u32[]{:S(2)}) collective-permute-start(f32[2,42,16,128]{3,2,1,0:T(8,128)} %get-tuple-element.271), channel_id=1, source_target_pairs={{0,2},{1,3},{2,0},{3,1},{4,6},{5,7},{6,4},{7,5},{8,10},{9,11},{10,... | collective-permute-start | bytes 2064392 | tf_op jit(solution)/shard_map/ppermute | solution.py:1372
  411.6 25.2 %collective-permute-start.22 = (f32[2,42,16,128]{3,2,1,0:T(8,128)}, f32[2,42,16,128]{3,2,1,0:T(8,128)}, u32[]{:S(2)}, u32[]{:S(2)}) collective-permute-start(f32[2,42,16,128]{3,2,1,0:T(8,128)} %get-tuple-element.272), channel_id=1, source_target_pairs={{0,4},{1,5},{2,6},{3,7},{4,0},{5,1},{6,2},{7,3},{8,12},{9,13},{10,... | collective-permute-start | bytes 2064392 | tf_op jit(solution)/shard_map/ppermute | solution.py:1372
  412.1 24.6 %collective-permute-start.24 = (f32[48,16,128]{2,1,0:T(8,128)S(1)}, f32[48,16,128]{2,1,0:T(8,128)S(1)}, u32[]{:S(2)}, u32[]{:S(2)}) collective-permute-start(f32[48,16,128]{2,1,0:T(8,128)S(1)} %add_bitcast_fusion.9), channel_id=1, source_target_pairs={{1,0},{3,2},{5,4},{7,6},{9,8},{11,10},{13,12},{15,14},{17,16},{19,... | collective-permute-start | bytes 1179656 | tf_op jit(solution)/shard_map/ppermute | solution.py:1368
  441.6 21.0 %collective-permute-start.29 = (f32[8,127,16,128]{3,2,1,0:T(8,128)}, f32[8,127,16,128]{3,2,1,0:T(8,128)}, u32[]{:S(2)}, u32[]{:S(2)}) collective-permute-start(f32[8,127,16,128]{3,2,1,0:T(8,128)} %get-tuple-element.310), channel_id=1, source_target_pairs={{0,16},{16,0},{1,17},{17,1},{2,18},{18,2},{3,19},{19,3},{4,20},{20... | collective-permute-start | bytes 24969224 | tf_op jit(solution)/shard_map/ppermute | solution.py:1364
  441.7 20.9 %collective-permute-start.28 = (f32[48,16,128]{2,1,0:T(8,128)S(1)}, f32[48,16,128]{2,1,0:T(8,128)S(1)}, u32[]{:S(2)}, u32[]{:S(2)}) collective-permute-start(f32[48,16,128]{2,1,0:T(8,128)S(1)} %add.446), channel_id=1, source_target_pairs={{2,0},{3,1},{6,4},{7,5},{10,8},{11,9},{14,12},{15,13},{18,16},{19,... | collective-permute-start | bytes 1179656 | tf_op jit(solution)/shard_map/ppermute | solution.py:1368
  443.0 19.6 %collective-permute-start.27 = (f32[43,16,128]{2,1,0:T(8,128)}, f32[43,16,128]{2,1,0:T(8,128)S(1)}, u32[]{:S(2)}, u32[]{:S(2)}) collective-permute-start(f32[43,16,128]{2,1,0:T(8,128)} %bitcast_add_fusion.23), channel_id=1, source_target_pairs={{0,2},{1,3},{2,0},{3,1},{4,6},{5,7},{6,4},{7,5},{8,10},{9,11},{10,... | collective-permute-start | bytes 1056776 | tf_op jit(solution)/shard_map/ppermute | solution.py:1372
  445.7 12.4 %collective-permute-start.25 = (f32[42,16,128]{2,1,0:T(8,128)S(1)}, f32[42,16,128]{2,1,0:T(8,128)S(1)}, u32[]{:S(2)}, u32[]{:S(2)}) collective-permute-start(f32[42,16,128]{2,1,0:T(8,128)S(1)} %get-tuple-element.306), channel_id=1, source_target_pairs={{0,4},{1,5},{2,6},{3,7},{4,0},{5,1},{6,2},{7,3},{8,12},{9,13},{10,... | collective-permute-start | bytes 1032200 | tf_op jit(solution)/shard_map/ppermute | solution.py:1372
  447.2 10.9 %collective-permute-start.26 = (f32[42,16,128]{2,1,0:T(8,128)S(1)}, f32[42,16,128]{2,1,0:T(8,128)}, u32[]{:S(2)}, u32[]{:S(2)}) collective-permute-start(f32[42,16,128]{2,1,0:T(8,128)S(1)} %get-tuple-element.307), channel_id=1, source_target_pairs={{0,1},{1,0},{2,3},{3,2},{4,5},{5,4},{6,7},{7,6},{8,9},{9,8},{10,11... | collective-permute-start | bytes 1032200 | tf_op jit(solution)/shard_map/ppermute | solution.py:1372
  476.1 40.1 %collective-permute-start.31 = (f32[2,2,53,16,128]{4,3,2,1,0:T(8,128)}, f32[2,2,53,16,128]{4,3,2,1,0:T(8,128)}, u32[]{:S(2)}, u32[]{:S(2)}) collective-permute-start(f32[2,2,53,16,128]{4,3,2,1,0:T(8,128)} %add_bitcast_fusion), channel_id=1, source_target_pairs={{0,2},{1,3},{2,0},{3,1},{4,6},{5,7},{6,4},{7,5},{8,10},{9,11},{10,... | collective-permute-start | bytes 5210120 | tf_op jit(solution)/shard_map/ppermute | solution.py:1372
  476.1 40.1 %collective-permute-start.30 = (f32[2,2,52,16,128]{4,3,2,1,0:T(8,128)}, f32[2,2,52,16,128]{4,3,2,1,0:T(8,128)}, u32[]{:S(2)}, u32[]{:S(2)}) collective-permute-start(f32[2,2,52,16,128]{4,3,2,1,0:T(8,128)} %add_bitcast_fusion.1), channel_id=1, source_target_pairs={{0,1},{1,0},{2,3},{3,2},{4,5},{5,4},{6,7},{7,6},{8,9},{9,8},{10,11... | collective-permute-start | bytes 5111816 | tf_op jit(solution)/shard_map/ppermute | solution.py:1372
  478.8 30.5 %collective-permute-start.32 = (f32[2,2,22,16,128]{4,3,2,1,0:T(8,128)}, f32[2,2,22,16,128]{4,3,2,1,0:T(8,128)S(1)}, u32[]{:S(2)}, u32[]{:S(2)}) collective-permute-start(f32[2,2,22,16,128]{4,3,2,1,0:T(8,128)} %add_bitcast_fusion.8), channel_id=1, source_target_pairs={{0,4},{1,5},{2,6},{3,7},{4,0},{5,1},{6,2},{7,3},{8,12},{9,13},{10,... | collective-permute-start | bytes 2162696 | tf_op jit(solution)/shard_map/ppermute | solution.py:1372
  480.4 71.6 %collective-permute-start.37 = (f32[127,16,128]{2,1,0:T(8,128)}, f32[127,16,128]{2,1,0:T(8,128)S(1)}, u32[]{:S(2)}, u32[]{:S(2)}) collective-permute-start(f32[127,16,128]{2,1,0:T(8,128)} %pad_maximum_fusion), channel_id=1, source_target_pairs={{8,0},{9,1},{10,2},{11,3},{12,4},{13,5},{14,6},{15,7},{24,16},{25,... | collective-permute-start | bytes 3121160 | tf_op jit(solution)/shard_map/ppermute | solution.py:1368
  523.6 33.3 %collective-permute-start.35 = (f32[2,53,16,128]{3,2,1,0:T(8,128)}, f32[2,53,16,128]{3,2,1,0:T(8,128)S(1)}, u32[]{:S(2)}, u32[]{:S(2)}) collective-permute-start(f32[2,53,16,128]{3,2,1,0:T(8,128)} %bitcast_add_fusion), channel_id=1, source_target_pairs={{0,4},{1,5},{2,6},{3,7},{4,0},{5,1},{6,2},{7,3},{8,12},{9,13},{10,... | collective-permute-start | bytes 2605064 | tf_op jit(solution)/shard_map/ppermute | solution.py:1372
  525.1 31.8 %collective-permute-start.34 = (f32[2,52,16,128]{3,2,1,0:T(8,128)}, f32[2,52,16,128]{3,2,1,0:T(8,128)}, u32[]{:S(2)}, u32[]{:S(2)}) collective-permute-start(f32[2,52,16,128]{3,2,1,0:T(8,128)} %bitcast_add_fusion.1), channel_id=1, source_target_pairs={{0,2},{1,3},{2,0},{3,1},{4,6},{5,7},{6,4},{7,5},{8,10},{9,11},{10,... | collective-permute-start | bytes 2555912 | tf_op jit(solution)/shard_map/ppermute | solution.py:1372
  526.8 30.0 %collective-permute-start.33 = (f32[48,16,128]{2,1,0:T(8,128)S(1)}, f32[48,16,128]{2,1,0:T(8,128)}, u32[]{:S(2)}, u32[]{:S(2)}) collective-permute-start(f32[48,16,128]{2,1,0:T(8,128)S(1)} %add.459), channel_id=1, source_target_pairs={{4,0},{5,1},{6,2},{7,3},{12,8},{13,9},{14,10},{15,11},{20,16},{21,... | collective-permute-start | bytes 1179656 | tf_op jit(solution)/shard_map/ppermute | solution.py:1368
  528.1 23.9 %collective-permute-start.36 = (f32[2,22,16,128]{3,2,1,0:T(8,128)}, f32[2,22,16,128]{3,2,1,0:T(8,128)}, u32[]{:S(2)}, u32[]{:S(2)}) collective-permute-start(f32[2,22,16,128]{3,2,1,0:T(8,128)} %bitcast_add_fusion.16), channel_id=1, source_target_pairs={{0,1},{1,0},{2,3},{3,2},{4,5},{5,4},{6,7},{7,6},{8,9},{9,8},{10,11... | collective-permute-start | bytes 1081352 | tf_op jit(solution)/shard_map/ppermute | solution.py:1372
  562.5 16.5 %collective-permute-start.38 = (f32[8,127,16,128]{3,2,1,0:T(8,128)}, f32[8,127,16,128]{3,2,1,0:T(8,128)S(1)}, u32[]{:S(2)}, u32[]{:S(2)}) collective-permute-start(f32[8,127,16,128]{3,2,1,0:T(8,128)} %get-tuple-element.377), channel_id=1, source_target_pairs={{0,16},{16,0},{1,17},{17,1},{2,18},{18,2},{3,19},{19,3},{4,20},{20... | collective-permute-start | bytes 24969224 | tf_op jit(solution)/shard_map/ppermute | solution.py:1364
  562.5 12.2 %collective-permute-start.39 = (f32[52,16,128]{2,1,0:T(8,128)S(1)}, f32[52,16,128]{2,1,0:T(8,128)S(1)}, u32[]{:S(2)}, u32[]{:S(2)}) collective-permute-start(f32[52,16,128]{2,1,0:T(8,128)S(1)} %bitcast_add_fusion.14), channel_id=1, source_target_pairs={{0,4},{1,5},{2,6},{3,7},{4,0},{5,1},{6,2},{7,3},{8,12},{9,13},{10,... | collective-permute-start | bytes 1277960 | tf_op jit(solution)/shard_map/ppermute | solution.py:1372
  564.4 12.0 %collective-permute-start.40 = (f32[53,16,128]{2,1,0:T(8,128)S(1)}, f32[53,16,128]{2,1,0:T(8,128)S(1)}, u32[]{:S(2)}, u32[]{:S(2)}) collective-permute-start(f32[53,16,128]{2,1,0:T(8,128)S(1)} %bitcast_add_fusion.10), channel_id=1, source_target_pairs={{0,1},{1,0},{2,3},{3,2},{4,5},{5,4},{6,7},{7,6},{8,9},{9,8},{10,11... | collective-permute-start | bytes 1302536 | tf_op jit(solution)/shard_map/ppermute | solution.py:1372
  564.7 16.3 %collective-permute-start.42 = (f32[48,16,128]{2,1,0:T(8,128)S(1)}, f32[48,16,128]{2,1,0:T(8,128)S(1)}, u32[]{:S(2)}, u32[]{:S(2)}) collective-permute-start(f32[48,16,128]{2,1,0:T(8,128)S(1)} %add.490), channel_id=1, source_target_pairs={{0,8},{1,9},{2,10},{3,11},{4,12},{5,13},{6,14},{7,15},{16,24},{17,... | collective-permute-start | bytes 1179656 | tf_op jit(solution)/shard_map/ppermute | solution.py:1368
  581.0 31.9 %collective-permute-start.43 = (f32[2,2,42,16,128]{4,3,2,1,0:T(8,128)S(1)}, f32[2,2,42,16,128]{4,3,2,1,0:T(8,128)S(1)}, u32[]{:S(2)}, u32[]{:S(2)}) collective-permute-start(f32[2,2,42,16,128]{4,3,2,1,0:T(8,128)S(1)} %add_bitcast_fusion.5), channel_id=1, source_target_pairs={{0,1},{1,0},{2,3},{3,2},{4,5},{5,4},{6,7},{7,6},{8,9},{9,8},{10,11... | collective-permute-start | bytes 4128776 | tf_op jit(solution)/shard_map/ppermute | solution.py:1372
  582.4 31.7 %collective-permute-start.44 = (f32[2,2,42,16,128]{4,3,2,1,0:T(8,128)S(1)}, f32[2,2,42,16,128]{4,3,2,1,0:T(8,128)S(1)}, u32[]{:S(2)}, u32[]{:S(2)}) collective-permute-start(f32[2,2,42,16,128]{4,3,2,1,0:T(8,128)S(1)} %add_bitcast_fusion.4), channel_id=1, source_target_pairs={{0,2},{1,3},{2,0},{3,1},{4,6},{5,7},{6,4},{7,5},{8,10},{9,11},{10,... | collective-permute-start | bytes 4128776 | tf_op jit(solution)/shard_map/ppermute | solution.py:1372
  584.1 32.3 %collective-permute-start.45 = (f32[2,2,43,16,128]{4,3,2,1,0:T(8,128)S(1)}, f32[2,2,43,16,128]{4,3,2,1,0:T(8,128)S(1)}, u32[]{:S(2)}, u32[]{:S(2)}) collective-permute-start(f32[2,2,43,16,128]{4,3,2,1,0:T(8,128)S(1)} %add_bitcast_fusion.2), channel_id=1, source_target_pairs={{0,4},{1,5},{2,6},{3,7},{4,0},{5,1},{6,2},{7,3},{8,12},{9,13},{10,... | collective-permute-start | bytes 4227080 | tf_op jit(solution)/shard_map/ppermute | solution.py:1372
  616.6 15.3 %collective-permute-start.46 = (f32[2,42,16,128]{3,2,1,0:T(8,128)S(1)}, f32[2,42,16,128]{3,2,1,0:T(8,128)S(1)}, u32[]{:S(2)}, u32[]{:S(2)}) collective-permute-start(f32[2,42,16,128]{3,2,1,0:T(8,128)S(1)} %get-tuple-element.385), channel_id=1, source_target_pairs={{0,2},{1,3},{2,0},{3,1},{4,6},{5,7},{6,4},{7,5},{8,10},{9,11},{10,... | collective-permute-start | bytes 2064392 | tf_op jit(solution)/shard_map/ppermute | solution.py:1372
  618.4 14.9 %collective-permute-start.47 = (f32[2,42,16,128]{3,2,1,0:T(8,128)S(1)}, f32[2,42,16,128]{3,2,1,0:T(8,128)S(1)}, u32[]{:S(2)}, u32[]{:S(2)}) collective-permute-start(f32[2,42,16,128]{3,2,1,0:T(8,128)S(1)} %get-tuple-element.386), channel_id=1, source_target_pairs={{0,4},{1,5},{2,6},{3,7},{4,0},{5,1},{6,2},{7,3},{8,12},{9,13},{10,... | collective-permute-start | bytes 2064392 | tf_op jit(solution)/shard_map/ppermute | solution.py:1372
  620.2 14.7 %collective-permute-start.48 = (f32[2,43,16,128]{3,2,1,0:T(8,128)S(1)}, f32[2,43,16,128]{3,2,1,0:T(8,128)S(1)}, u32[]{:S(2)}, u32[]{:S(2)}) collective-permute-start(f32[2,43,16,128]{3,2,1,0:T(8,128)S(1)} %bitcast_add_fusion.2), channel_id=1, source_target_pairs={{0,1},{1,0},{2,3},{3,2},{4,5},{5,4},{6,7},{7,6},{8,9},{9,8},{10,11... | collective-permute-start | bytes 2113544 | tf_op jit(solution)/shard_map/ppermute | solution.py:1372
  635.9 10.7 %collective-permute-start.49 = (f32[42,16,128]{2,1,0:T(8,128)}, f32[42,16,128]{2,1,0:T(8,128)}, u32[]{:S(2)}, u32[]{:S(2)}) collective-permute-start(f32[42,16,128]{2,1,0:T(8,128)} %get-tuple-element.388), channel_id=1, source_target_pairs={{0,4},{1,5},{2,6},{3,7},{4,0},{5,1},{6,2},{7,3},{8,12},{9,13},{10,... | collective-permute-start | bytes 1032200 | tf_op jit(solution)/shard_map/ppermute | solution.py:1372
  637.1 9.6 %collective-permute-start.50 = (f32[42,16,128]{2,1,0:T(8,128)}, f32[42,16,128]{2,1,0:T(8,128)}, u32[]{:S(2)}, u32[]{:S(2)}) collective-permute-start(f32[42,16,128]{2,1,0:T(8,128)} %get-tuple-element.389), channel_id=1, source_target_pairs={{0,1},{1,0},{2,3},{3,2},{4,5},{5,4},{6,7},{7,6},{8,9},{9,8},{10,11... | collective-permute-start | bytes 1032200 | tf_op jit(solution)/shard_map/ppermute | solution.py:1372
  640.7 8.1 %collective-permute-start.51 = (f32[43,16,128]{2,1,0:T(8,128)}, f32[43,16,128]{2,1,0:T(8,128)S(1)}, u32[]{:S(2)}, u32[]{:S(2)}) collective-permute-start(f32[43,16,128]{2,1,0:T(8,128)} %bitcast_add_fusion.19), channel_id=1, source_target_pairs={{0,2},{1,3},{2,0},{3,1},{4,6},{5,7},{6,4},{7,5},{8,10},{9,11},{10,... | collective-permute-start | bytes 1056776 | tf_op jit(solution)/shard_map/ppermute | solution.py:1372
  641.3 24.1 %collective-permute-start.53 = (f32[127,16,128]{2,1,0:T(8,128)}, f32[127,16,128]{2,1,0:T(8,128)S(1)}, u32[]{:S(2)}, u32[]{:S(2)}) collective-permute-start(f32[127,16,128]{2,1,0:T(8,128)} %pad_maximum_fusion.1), channel_id=1, source_target_pairs={{0,8},{1,9},{2,10},{3,11},{4,12},{5,13},{6,14},{7,15},{16,24},{17,... | collective-permute-start | bytes 3121160 | tf_op jit(solution)/shard_map/ppermute | solution.py:1368
  650.3 45.9 %collective-permute-start.52 = (f32[127,16,128]{2,1,0:T(8,128)S(1)}, f32[127,16,128]{2,1,0:T(8,128)S(1)}, u32[]{:S(2)}, u32[]{:S(2)}) collective-permute-start(f32[127,16,128]{2,1,0:T(8,128)S(1)} %pad_maximum_fusion.2), channel_id=1, source_target_pairs={{8,0},{9,1},{10,2},{11,3},{12,4},{13,5},{14,6},{15,7},{24,16},{25,... | collective-permute-start | bytes 3121160 | tf_op jit(solution)/shard_map/ppermute | solution.py:1368
  701.7 8.8 %collective-permute-start.55 = (f32[127,16,128]{2,1,0:T(8,128)}, f32[127,16,128]{2,1,0:T(8,128)S(1)}, u32[]{:S(2)}, u32[]{:S(2)}) collective-permute-start(f32[127,16,128]{2,1,0:T(8,128)} %get-tuple-element.417), channel_id=1, source_target_pairs={{0,16},{16,0},{1,17},{17,1},{2,18},{18,2},{3,19},{19,3},{4,20},{20... | collective-permute-start | bytes 3121160 | tf_op jit(solution)/shard_map/ppermute | solution.py:1590
  716.6 7.8 %collective-permute-start.60 = (f32[2]{0:T(128)S(1)}, f32[2]{0:T(128)S(1)}, u32[]{:S(2)}, u32[]{:S(2)}) collective-permute-start(f32[2]{0:T(128)S(1)} %add_add_fusion.2), channel_id=1, source_target_pairs={{0,8},{1,9},{2,10},{3,11},{4,12},{5,13},{6,14},{7,15},{8,0},{9,1},... | collective-permute-start | bytes 32 | tf_op jit(solution)/shard_map/ppermute | solution.py:1418
  (49 other events, 568.9 us)
Sparse Core Ops, SparseCore 0:
  29.2 122.0 all-gather.4
  154.2 75.7 all-gather.2
